TPU v7x, 32 devices: a whole 2x2x4 slice. The times are simulated.
32 devices in a mesh: depth: 4 (over x, core), sx: 4 (over z), sy: 2 (over y).
Axes of the slice: x: 2, y: 2, z: 4, core: 2. Of those that a mesh axis runs over, the one named last changes fastest.
Arguments:
- transmission: bfloat16 [8, 2, 1024, 512], P('depth', None, 'sx', 'sy')
- incident: bfloat16 [8, 16, 2, 256, 256], P('depth', ('sx', 'sy')), may hold values from -6 to 6
- exit_adjoint: bfloat16 [16, 2, 256, 256], P(('sx', 'sy')), may hold values from -6 to 6
- propagator_phase: float32 [256, 256], replicated, may hold values from -3.140625 to 3.140625
- scan_anchor: int32 [16, 2], P(('sx', 'sy')), may hold values from -128 to 895, as said below
- live_count: int32 [8], P(('sx', 'sy')), may hold values from 1 to 2, as said below
Outputs:
- gradient: float32 [8, 2, 1024, 512], P('depth', None, 'sx', 'sy')
Inputs may be any that keep to these rules, and one draw needn't show every extreme that they name: `scan_anchor`: the slot at position p of the device at indices (a, b) of (sx, sy), slot a * 2 * 2 + b * 2 + p, has its x anchor in [a * 256 - 256 // 2, a * 256 + 256 - 256 // 2) and its y anchor in [b * 256 - 256 // 2, b * 256 + 256 - 256 // 2). Both ends of the whole range are taken in every draw. The live slots of a device are its first live_count slots; some device has all 2 slots live and some device exactly one.
All inputs are finite; a program needn't handle non-finite values.
Results may differ from a plain program's by a relative error of at most 0.0003.
Values may be sent and summed in bfloat16 or wider, within the bound.
No kernel may reach another device: no remote copies, remote signals or barrier semaphores. Data moves between devices by JAX's collectives and lax.ppermute only.
A program may use at most 128 MiB of HBM per device.

v0:
```python
import math

import jax
import jax.numpy as jnp
from jax import lax
from jax.sharding import PartitionSpec as P


def with_halo(array, sides, width):
    for axis, dim in sides:
        size, length = (lax.axis_size(axis), array.shape[dim])
        up = [(i, (i + 1) % size) for i in range(size - 1)]
        down = [(j, i) for i, j in up]
        last = lax.slice_in_dim(array, length - width, length, axis=dim)
        initial = lax.slice_in_dim(array, 0, width, axis=dim)
        before = lax.ppermute(last, axis, up)
        after = lax.ppermute(initial, axis, down)
        array = jnp.concatenate([before, array, after], axis=dim)
    return array


def passed_along(value, axis, steps):
    count = lax.axis_size(axis)
    initial, last = (max(0, -steps), min(count, count - steps))
    return lax.ppermute(value, axis, [(source, source + steps) for source in range(initial, last)])


def dft_tables(size):
    positions = lax.iota(jnp.int32, size)
    product = positions[:, None] * positions[None, :] % size
    angle = product.astype(jnp.float32) * (2.0 * math.pi / size)
    factor = 1.0 / math.sqrt(size)
    return (jnp.cos(angle) * factor, -jnp.sin(angle) * factor)


def left_apply(table, field):
    return jnp.einsum("jk,mkl->mjl", table, field, precision=lax.Precision.HIGHEST)


def right_apply(field, table):
    return jnp.einsum("mjk,kl->mjl", field, table, precision=lax.Precision.HIGHEST)


def complex_left(table_real, table_imag, field_real, field_imag):
    out_real = left_apply(table_real, field_real) - left_apply(table_imag, field_imag)
    out_imag = left_apply(table_real, field_imag) + left_apply(table_imag, field_real)
    return (out_real, out_imag)


def complex_right(field_real, field_imag, table_real, table_imag):
    out_real = right_apply(field_real, table_real) - right_apply(field_imag, table_imag)
    out_imag = right_apply(field_real, table_imag) + right_apply(field_imag, table_real)
    return (out_real, out_imag)


def propagate_back(wave, table_real, table_imag, phase_cos, phase_sin):
    field_real, field_imag = complex_left(table_real, table_imag, wave[:, 0], wave[:, 1])
    field_real, field_imag = complex_right(field_real, field_imag, table_real, table_imag)
    turned_real = field_real * phase_cos + field_imag * phase_sin
    turned_imag = field_imag * phase_cos - field_real * phase_sin
    field_real, field_imag = complex_left(table_real, -table_imag, turned_real, turned_imag)
    field_real, field_imag = complex_right(field_real, field_imag, table_real, -table_imag)
    return jnp.stack([field_real, field_imag], axis=1)


def fold_rims(field, axis, tile, patch):
    half = patch // 2
    inner = lax.slice_in_dim(field, patch, patch + tile, axis=axis)
    lower = lax.slice_in_dim(field, 0, half, axis=axis)
    upper = lax.slice_in_dim(field, tile + patch + half, tile + 2 * patch, axis=axis)
    widths_low = [(0, 0)] * field.ndim
    widths_high = [(0, 0)] * field.ndim
    widths_low[axis] = (0, tile - half)
    widths_high[axis] = (tile - half, 0)
    return inner + jnp.pad(lower, widths_low) + jnp.pad(upper, widths_high)


def shards(transmission, incident, exit_adjoint, propagator_phase, scan_anchor, live_count):
    depth_count = lax.axis_size("depth")
    depth_index = lax.axis_index("depth")
    tile = transmission.shape[2]
    patch = propagator_phase.shape[0]
    half = patch // 2
    slab = transmission.shape[0]
    slots = exit_adjoint.shape[0]
    extended = with_halo(transmission, (("sx", 2), ("sy", 3)), half).astype(jnp.float32)
    shift_xy = jnp.stack([lax.axis_index("sx") * tile, lax.axis_index("sy") * tile])
    local_anchor = scan_anchor - shift_xy[None, :] + half
    live = (lax.iota(jnp.int32, slots) < live_count[0]).astype(jnp.float32)
    seed_waves = exit_adjoint.astype(jnp.float32) * live[:, None, None, None]
    table_real, table_imag = dft_tables(patch)
    phase_cos = jnp.cos(propagator_phase)
    phase_sin = jnp.sin(propagator_phase)
    extent = tile + patch
    start_total = jnp.zeros((slab, 2, extent, extent), jnp.float32)
    zero_index = jnp.zeros((), jnp.int32)

    def slab_pass(wave, first, total):
        count = wave.shape[0]
        corners = lax.dynamic_slice_in_dim(local_anchor, first, count, 0)
        for layer in range(slab - 1, -1, -1):
            entering = lax.dynamic_slice_in_dim(incident[layer], first, count, 0).astype(
                jnp.float32
            )
            wave_real, wave_imag = (wave[:, 0], wave[:, 1])
            enter_real, enter_imag = (entering[:, 0], entering[:, 1])
            term = jnp.stack(
                [
                    enter_real * wave_real + enter_imag * wave_imag,
                    enter_real * wave_imag - enter_imag * wave_real,
                ],
                axis=1,
            )

            def add_member(member, running, layer=layer, term=term):
                start = (
                    jnp.asarray(layer, jnp.int32),
                    zero_index,
                    corners[member, 0],
                    corners[member, 1],
                )
                current = lax.dynamic_slice(running, start, (1, 2, patch, patch))
                return lax.dynamic_update_slice(running, current + term[member][None], start)

            total = lax.fori_loop(0, count, add_member, total)
            plane = extended[layer]
            windows = jax.vmap(
                lambda corner: lax.dynamic_slice(
                    plane, (zero_index, corner[0], corner[1]), (2, patch, patch)
                )
            )(corners)
            trans_real, trans_imag = (windows[:, 0], windows[:, 1])
            wave = jnp.stack(
                [
                    trans_real * wave_real + trans_imag * wave_imag,
                    trans_real * wave_imag - trans_imag * wave_real,
                ],
                axis=1,
            )
            wave = propagate_back(wave, table_real, table_imag, phase_cos, phase_sin)
        return (wave, total)

    def send_probe(wave):
        return passed_along(wave, "depth", -1)

    units = slots // 1
    steps = units + depth_count - 1

    def one_step(step, state):
        wave, total = state
        received = send_probe(wave)
        unit = step - (depth_count - 1 - depth_index)
        active = jnp.logical_and(unit >= 0, unit < units)
        first = jnp.clip(unit, 0, units - 1) * 1
        seeded = lax.dynamic_slice_in_dim(seed_waves, first, 1, 0)
        wave_in = jnp.where(depth_index == depth_count - 1, seeded, received)

        def run_slab(operands):
            return slab_pass(operands[0], operands[1], operands[2])

        def keep_state(operands):
            return (operands[0], operands[2])

        return lax.cond(active, run_slab, keep_state, (wave_in, first, total))

    start_wave = jnp.zeros((1, 2, patch, patch), jnp.float32)
    total = lax.fori_loop(0, steps, one_step, (start_wave, start_total))[1]
    bordered = with_halo(total, (("sx", 2), ("sy", 3)), half)
    folded = fold_rims(bordered, 2, tile, patch)
    return fold_rims(folded, 3, tile, patch)


def solution(mesh):
    placed = (
        P("depth", None, "sx", "sy"),
        P("depth", ("sx", "sy"), None, None, None),
        P(("sx", "sy"), None, None, None),
        P(),
        P(("sx", "sy"), None),
        P(("sx", "sy")),
    )
    return jax.shard_map(
        shards, mesh=mesh, in_specs=placed, out_specs=P("depth", None, "sx", "sy"), check_vma=False
    )
```

profile of v0, /device:TPU:16, one launch (start us, length us, event | category | flops | bytes accessed | tf_op | source)
XLA Modules:
  0.0 406.3 jit_solution(11000116065547414429)
XLA Ops:
  1.1 2.4 collective-permute-start.2
  3.5 3.5 collective-permute-start.1
  8.4 4.7 %collective-permute-done.1 = bf16[2,2,128,256]{3,2,1,0:T(8,128)(2,1)S(1)} collective-permute-done((bf16[2,2,128,256]{3,2,1,0:T(8,128)(2,1)S(1)}, bf16[2,2,128,256]{3,2,1,0:T(8,128)(2,1)S(1)}, u32[]{:S(2)}, u32[]{:S(2)}) %collective-permute-start.1) | collective-permute-done | bytes 262176 | tf_op jit(solution)/shard_map/ppermute | solution.py:16
  15.5 3.4 collective-permute-start.3
  18.9 1.3 collective-permute-start.4
  22.4 6.8 %collective-permute-done.3 = bf16[2,2,512,128]{3,2,1,0:T(8,128)(2,1)S(1)} collective-permute-done((bf16[2,2,512,128]{3,2,1,0:T(8,128)(2,1)}, bf16[2,2,512,128]{3,2,1,0:T(8,128)(2,1)S(1)}, u32[]{:S(2)}, u32[]{:S(2)}) %collective-permute-start.3) | collective-permute-done | bytes 524320 | tf_op jit(solution)/shard_map/ppermute | solution.py:16
  29.2 4.0 collective-permute-done.4
  33.2 2.4 maximum_convert_fusion
  36.5 2.6 broadcast_in_dim.9
  39.0 311.3 %while.25 = (s32[]{:T(128)}, f32[1,2,256,256]{3,2,1,0:T(8,128)}, f32[2,2,512,512]{3,2,1,0:T(8,128)}, s32[]{:T(128)}, pred[]{:T(512)}, /*index=5*/f32[2,2,256,256...) while((s32[]{:T(128)}, f32[1,2,256,256]{3,2,1,0:T(8,128)}, ...), condition=%wide.region_3.4_spmd.clone.clone, body=%wide.region_0.3_spmd.clone.clone.sunk | while | flops 6448545792 | bytes 62390980 | solution.py:167
  40.5 2.6 collective-permute-done
  43.0 1.9 dynamic-slice_select_fusion.2
  46.5 8.6 %collective-permute-done = f32[1,2,256,256]{3,2,1,0:T(8,128)S(1)} collective-permute-done((f32[1,2,256,256]{3,2,1,0:T(8,128)}, f32[1,2,256,256]{3,2,1,0:T(8,128)S(1)}, u32[]{:S(2)}, u32[]{:S(2)}) %collective-permute-start) | collective-permute-done | bytes 524320 | tf_op jit(solution)/shard_map/while/body/eval_jaxpr/ppermute | solution.py:25
  55.1 1.9 dynamic-slice_select_fusion.2
  58.5 9.3 %collective-permute-done = f32[1,2,256,256]{3,2,1,0:T(8,128)S(1)} collective-permute-done((f32[1,2,256,256]{3,2,1,0:T(8,128)}, f32[1,2,256,256]{3,2,1,0:T(8,128)S(1)}, u32[]{:S(2)}, u32[]{:S(2)}) %collective-permute-start) | collective-permute-done | bytes 524320 | tf_op jit(solution)/shard_map/while/body/eval_jaxpr/ppermute | solution.py:25
  67.8 1.9 dynamic-slice_select_fusion.2
  71.2 157.7 %collective-permute-done = f32[1,2,256,256]{3,2,1,0:T(8,128)S(1)} collective-permute-done((f32[1,2,256,256]{3,2,1,0:T(8,128)}, f32[1,2,256,256]{3,2,1,0:T(8,128)S(1)}, u32[]{:S(2)}, u32[]{:S(2)}) %collective-permute-start) | collective-permute-done | bytes 524320 | tf_op jit(solution)/shard_map/while/body/eval_jaxpr/ppermute | solution.py:25
  228.9 1.9 dynamic-slice_select_fusion.2
  230.9 54.3 %conditional.4 = ((f32[1,2,256,256]{3,2,1,0:T(8,128)}, f32[2,2,512,512]{3,2,1,0:T(8,128)})) conditional(s32[]{:T(128)} %convert_element_type.148, (f32[1,2,256,256]{3,2,1,0:T(8,128)}, f32[2,2,512,512]{3,2,1,0:T(8,128)}) %tuple.118, (f32[2,2,512,512]{3,2,1,0:T(8,128)}, s32[]{:T(128)}, s32[2,2]{1,0:T(2,128)S(1)}, f32[1,2,256,256]{3,2,1,0:T(8,128)}, ...), branch_computations={%region_1.1_spmd, %region_2.2_spmd.clone} | conditional | flops 6447497216 | bytes 58196312 | solution.py:164
  230.9 4.2 %fusion.41 = (f32[1,2,512,512]{3,2,1,0:T(8,128)S(1)}, f32[1,2,512,512]{3,2,1,0:T(8,128)}) fusion(f32[2,2,512,512]{3,2,1,0:T(8,128)} %get-tuple-element.629), kind=kLoop, calls=%fused_computation.100 | loop fusion | bytes 8388608 | tf_op jit(solution)/shard_map/while/body/eval_jaxpr/cond/branch_1_fun/slice | solution.py:126
  243.7 1.7 fusion.14
  246.8 1.5 multiply_add_fusion
  248.3 1.4 maximum_add_fusion
  258.8 1.6 add_bitcast_fusion
  270.8 6.5 %dynamic_update_slice.8 = f32[2,2,512,512]{3,2,1,0:T(8,128)} dynamic-update-slice(f32[2,2,512,512]{3,2,1,0:T(8,128)} %get-tuple-element.635, f32[1,2,256,256]{3,2,1,0:T(8,128)S(1)} %maximum_add_fusion, s32[]{:T(128)} %constant.91.clone.1, s32[]{:T(128)} %constant.87.clone.1, s32[]{:T(128)S(6)} %select_n.145, s32[]{:T(128)S(6)} %select_n.146) | dynamic-update-slice | bytes 1048580 | tf_op jit(solution)/shard_map/while/body/eval_jaxpr/cond/branch_1_fun/while/body/eval_jaxpr/dynamic_update_slice | solution.py:123
  277.3 1.4 maximum_add_fusion.1
  278.7 6.5 %dynamic_update_slice.9 = f32[2,2,512,512]{3,2,1,0:T(8,128)} dynamic-update-slice(f32[2,2,512,512]{3,2,1,0:T(8,128)} %dynamic_update_slice.8, f32[1,2,256,256]{3,2,1,0:T(8,128)S(1)} %maximum_add_fusion.1, s32[]{:T(128)} %constant.87.clone.1, s32[]{:T(128)} %constant.87.clone.1, s32[]{:T(128)S(6)} %select_n.145, s32[]{:T(128)S(6)} %select_n.146) | dynamic-update-slice | bytes 1048580 | tf_op jit(solution)/shard_map/while/body/eval_jaxpr/cond/branch_1_fun/while/body/eval_jaxpr/dynamic_update_slice | solution.py:123
  286.6 8.3 %collective-permute-done = f32[1,2,256,256]{3,2,1,0:T(8,128)S(1)} collective-permute-done((f32[1,2,256,256]{3,2,1,0:T(8,128)}, f32[1,2,256,256]{3,2,1,0:T(8,128)S(1)}, u32[]{:S(2)}, u32[]{:S(2)}) %collective-permute-start) | collective-permute-done | bytes 524320 | tf_op jit(solution)/shard_map/while/body/eval_jaxpr/ppermute | solution.py:25
  295.0 1.9 dynamic-slice_select_fusion.2
  296.9 53.4 %conditional.4 = ((f32[1,2,256,256]{3,2,1,0:T(8,128)}, f32[2,2,512,512]{3,2,1,0:T(8,128)})) conditional(s32[]{:T(128)} %convert_element_type.148, (f32[1,2,256,256]{3,2,1,0:T(8,128)}, f32[2,2,512,512]{3,2,1,0:T(8,128)}) %tuple.118, (f32[2,2,512,512]{3,2,1,0:T(8,128)}, s32[]{:T(128)}, s32[2,2]{1,0:T(2,128)S(1)}, f32[1,2,256,256]{3,2,1,0:T(8,128)}, ...), branch_computations={%region_1.1_spmd, %region_2.2_spmd.clone} | conditional | flops 6447497216 | bytes 58196312 | solution.py:164
  296.9 4.2 %fusion.41 = (f32[1,2,512,512]{3,2,1,0:T(8,128)S(1)}, f32[1,2,512,512]{3,2,1,0:T(8,128)}) fusion(f32[2,2,512,512]{3,2,1,0:T(8,128)} %get-tuple-element.629), kind=kLoop, calls=%fused_computation.100 | loop fusion | bytes 8388608 | tf_op jit(solution)/shard_map/while/body/eval_jaxpr/cond/branch_1_fun/slice | solution.py:126
  309.7 1.7 fusion.14
  312.9 1.5 multiply_add_fusion
  314.4 1.4 maximum_add_fusion
  324.8 1.6 add_bitcast_fusion
  336.9 6.0 %dynamic_update_slice.8 = f32[2,2,512,512]{3,2,1,0:T(8,128)} dynamic-update-slice(f32[2,2,512,512]{3,2,1,0:T(8,128)} %get-tuple-element.635, f32[1,2,256,256]{3,2,1,0:T(8,128)S(1)} %maximum_add_fusion, s32[]{:T(128)} %constant.91.clone.1, s32[]{:T(128)} %constant.87.clone.1, s32[]{:T(128)S(6)} %select_n.145, s32[]{:T(128)S(6)} %select_n.146) | dynamic-update-slice | bytes 1048580 | tf_op jit(solution)/shard_map/while/body/eval_jaxpr/cond/branch_1_fun/while/body/eval_jaxpr/dynamic_update_slice | solution.py:123
  342.9 1.4 maximum_add_fusion.1
  344.3 6.1 %dynamic_update_slice.9 = f32[2,2,512,512]{3,2,1,0:T(8,128)} dynamic-update-slice(f32[2,2,512,512]{3,2,1,0:T(8,128)} %dynamic_update_slice.8, f32[1,2,256,256]{3,2,1,0:T(8,128)S(1)} %maximum_add_fusion.1, s32[]{:T(128)} %constant.87.clone.1, s32[]{:T(128)} %constant.87.clone.1, s32[]{:T(128)S(6)} %select_n.145, s32[]{:T(128)S(6)} %select_n.146) | dynamic-update-slice | bytes 1048580 | tf_op jit(solution)/shard_map/while/body/eval_jaxpr/cond/branch_1_fun/while/body/eval_jaxpr/dynamic_update_slice | solution.py:123
  350.3 1.9 fusion.45
  352.3 2.7 collective-permute-start.5
  354.9 3.2 collective-permute-start.6
  358.1 10.8 %collective-permute-done.5 = f32[2,2,128,512]{3,2,1,0:T(8,128)S(1)} collective-permute-done((f32[2,2,128,512]{3,2,1,0:T(8,128)S(1)}, f32[2,2,128,512]{3,2,1,0:T(8,128)S(1)}, u32[]{:S(2)}, u32[]{:S(2)}) %collective-permute-start.5) | collective-permute-done | bytes 1048608 | tf_op jit(solution)/shard_map/ppermute | solution.py:16
  369.5 2.1 collective-permute-done.6
  371.9 6.5 %collective-permute-start.7 = (f32[2,2,768,128]{3,2,1,0:T(8,128)S(1)}, f32[2,2,768,128]{3,2,1,0:T(8,128)S(1)}, u32[]{:S(2)}, u32[]{:S(2)}) collective-permute-start(f32[2,2,768,128]{3,2,1,0:T(8,128)S(1)} %get-tuple-element.701), channel_id=1, source_target_pairs={{0,1},{2,3},{4,5},{6,7},{8,9},{10,11},{12,13},{14,15},{16,17},{18,... | collective-permute-start | bytes 4718600 | tf_op jit(solution)/shard_map/ppermute | solution.py:16
  379.7 16.5 %collective-permute-done.7 = f32[2,2,768,128]{3,2,1,0:T(8,128)S(1)} collective-permute-done((f32[2,2,768,128]{3,2,1,0:T(8,128)S(1)}, f32[2,2,768,128]{3,2,1,0:T(8,128)S(1)}, u32[]{:S(2)}, u32[]{:S(2)}) %collective-permute-start.7) | collective-permute-done | bytes 1572896 | tf_op jit(solution)/shard_map/ppermute | solution.py:16
  397.4 3.5 collective-permute-done.8
  400.8 2.3 pad_maximum_fusion.1
  403.1 2.0 fusion.37
  (127 shorter events, 61.4 us)
Async XLA Ops:
  0.0 20.3 %copy-start.5 = (f32[256,256]{1,0:T(8,128)S(1)}, f32[256,256]{1,0:T(8,128)}, u32[]{:S(2)}) copy-start(f32[256,256]{1,0:T(8,128)} %param.13) | copy-start | bytes 786436
  0.0 21.2 %copy-start.4 = (bf16[2,2,256,256]{3,2,1,0:T(8,128)(2,1)S(1)}, bf16[2,2,256,256]{3,2,1,0:T(8,128)(2,1)}, u32[]{:S(2)}) copy-start(bf16[2,2,256,256]{3,2,1,0:T(8,128)(2,1)} %param.12) | copy-start | bytes 1572868
  1.1 13.1 %collective-permute-start.2 = (bf16[2,2,128,256]{3,2,1,0:T(8,128)(2,1)S(1)}, bf16[2,2,128,256]{3,2,1,0:T(8,128)(2,1)S(1)}, u32[]{:S(2)}, u32[]{:S(2)}) collective-permute-start(bf16[2,2,128,256]{3,2,1,0:T(8,128)(2,1)S(1)} %get-tuple-element.707), channel_id=1, source_target_pairs={{2,0},{4,2},{6,4},{3,1},{5,3},{7,5},{10,8},{12,10},{14,12},{11,9},... | collective-permute-start | bytes 786440 | tf_op jit(solution)/shard_map/ppermute | solution.py:17
  3.5 9.7 %collective-permute-start.1 = (bf16[2,2,128,256]{3,2,1,0:T(8,128)(2,1)S(1)}, bf16[2,2,128,256]{3,2,1,0:T(8,128)(2,1)S(1)}, u32[]{:S(2)}, u32[]{:S(2)}) collective-permute-start(bf16[2,2,128,256]{3,2,1,0:T(8,128)(2,1)S(1)} %get-tuple-element.708), channel_id=1, source_target_pairs={{0,2},{2,4},{4,6},{1,3},{3,5},{5,7},{8,10},{10,12},{12,14},{9,11},... | collective-permute-start | bytes 786440 | tf_op jit(solution)/shard_map/ppermute | solution.py:16
  15.5 13.7 %collective-permute-start.3 = (bf16[2,2,512,128]{3,2,1,0:T(8,128)(2,1)}, bf16[2,2,512,128]{3,2,1,0:T(8,128)(2,1)S(1)}, u32[]{:S(2)}, u32[]{:S(2)}) collective-permute-start(bf16[2,2,512,128]{3,2,1,0:T(8,128)(2,1)} %get-tuple-element.705), channel_id=1, source_target_pairs={{0,1},{2,3},{4,5},{6,7},{8,9},{10,11},{12,13},{14,15},{16,17},{18,... | collective-permute-start | bytes 1572872 | tf_op jit(solution)/shard_map/ppermute | solution.py:16
  18.9 14.3 %collective-permute-start.4 = (bf16[2,2,512,128]{3,2,1,0:T(8,128)(2,1)}, bf16[2,2,512,128]{3,2,1,0:T(8,128)(2,1)S(1)}, u32[]{:S(2)}, u32[]{:S(2)}) collective-permute-start(bf16[2,2,512,128]{3,2,1,0:T(8,128)(2,1)} %get-tuple-element.706), channel_id=1, source_target_pairs={{1,0},{3,2},{5,4},{7,6},{9,8},{11,10},{13,12},{15,14},{17,16},{19,... | collective-permute-start | bytes 1572872 | tf_op jit(solution)/shard_map/ppermute | solution.py:17
  39.0 4.0 collective-permute-start
  45.0 10.1 %collective-permute-start = (f32[1,2,256,256]{3,2,1,0:T(8,128)}, f32[1,2,256,256]{3,2,1,0:T(8,128)S(1)}, u32[]{:S(2)}, u32[]{:S(2)}) collective-permute-start(f32[1,2,256,256]{3,2,1,0:T(8,128)} %get-tuple-element.802), channel_id=1, source_target_pairs={{8,0},{16,8},{24,16},{9,1},{17,9},{25,17},{10,2},{18,10},{26,18},{... | collective-permute-start | bytes 1572872 | tf_op jit(solution)/shard_map/while/body/eval_jaxpr/ppermute | solution.py:25
  57.1 10.7 %collective-permute-start = (f32[1,2,256,256]{3,2,1,0:T(8,128)}, f32[1,2,256,256]{3,2,1,0:T(8,128)S(1)}, u32[]{:S(2)}, u32[]{:S(2)}) collective-permute-start(f32[1,2,256,256]{3,2,1,0:T(8,128)} %get-tuple-element.802), channel_id=1, source_target_pairs={{8,0},{16,8},{24,16},{9,1},{17,9},{25,17},{10,2},{18,10},{26,18},{... | collective-permute-start | bytes 1572872 | tf_op jit(solution)/shard_map/while/body/eval_jaxpr/ppermute | solution.py:25
  69.7 159.2 %collective-permute-start = (f32[1,2,256,256]{3,2,1,0:T(8,128)}, f32[1,2,256,256]{3,2,1,0:T(8,128)S(1)}, u32[]{:S(2)}, u32[]{:S(2)}) collective-permute-start(f32[1,2,256,256]{3,2,1,0:T(8,128)} %get-tuple-element.802), channel_id=1, source_target_pairs={{8,0},{16,8},{24,16},{9,1},{17,9},{25,17},{10,2},{18,10},{26,18},{... | collective-permute-start | bytes 1572872 | tf_op jit(solution)/shard_map/while/body/eval_jaxpr/ppermute | solution.py:25
  265.8 11.6 %copy-start.1 = (f32[1,1,256,256]{3,2,1,0:T(8,128)S(1)}, f32[1,1,256,256]{3,2,1,0:T(8,128)}, u32[]{:S(2)}) copy-start(f32[1,1,256,256]{3,2,1,0:T(8,128)} %get-tuple-element.681) | copy-start | bytes 786436 | tf_op jit(solution)/shard_map/while/body/eval_jaxpr/cond
  265.8 11.5 %copy-start.2 = (f32[1,1,256,256]{3,2,1,0:T(8,128)S(1)}, f32[1,1,256,256]{3,2,1,0:T(8,128)}, u32[]{:S(2)}) copy-start(f32[1,1,256,256]{3,2,1,0:T(8,128)} %get-tuple-element.682) | copy-start | bytes 786436 | tf_op jit(solution)/shard_map/while/body/eval_jaxpr/cond
  285.2 9.8 %collective-permute-start = (f32[1,2,256,256]{3,2,1,0:T(8,128)}, f32[1,2,256,256]{3,2,1,0:T(8,128)S(1)}, u32[]{:S(2)}, u32[]{:S(2)}) collective-permute-start(f32[1,2,256,256]{3,2,1,0:T(8,128)} %get-tuple-element.802), channel_id=1, source_target_pairs={{8,0},{16,8},{24,16},{9,1},{17,9},{25,17},{10,2},{18,10},{26,18},{... | collective-permute-start | bytes 1572872 | tf_op jit(solution)/shard_map/while/body/eval_jaxpr/ppermute | solution.py:25
  331.8 11.1 %copy-start.1 = (f32[1,1,256,256]{3,2,1,0:T(8,128)S(1)}, f32[1,1,256,256]{3,2,1,0:T(8,128)}, u32[]{:S(2)}) copy-start(f32[1,1,256,256]{3,2,1,0:T(8,128)} %get-tuple-element.681) | copy-start | bytes 786436 | tf_op jit(solution)/shard_map/while/body/eval_jaxpr/cond
  331.8 11.1 %copy-start.2 = (f32[1,1,256,256]{3,2,1,0:T(8,128)S(1)}, f32[1,1,256,256]{3,2,1,0:T(8,128)}, u32[]{:S(2)}) copy-start(f32[1,1,256,256]{3,2,1,0:T(8,128)} %get-tuple-element.682) | copy-start | bytes 786436 | tf_op jit(solution)/shard_map/while/body/eval_jaxpr/cond
  350.3 18.7 %copy-start = (f32[2,2,512,512]{3,2,1,0:T(8,128)S(1)}, f32[2,2,512,512]{3,2,1,0:T(8,128)}, u32[]{:S(2)}) copy-start(f32[2,2,512,512]{3,2,1,0:T(8,128)} %get-tuple-element.509) | copy-start | bytes 12582916
  352.3 16.7 %collective-permute-start.5 = (f32[2,2,128,512]{3,2,1,0:T(8,128)S(1)}, f32[2,2,128,512]{3,2,1,0:T(8,128)S(1)}, u32[]{:S(2)}, u32[]{:S(2)}) collective-permute-start(f32[2,2,128,512]{3,2,1,0:T(8,128)S(1)} %get-tuple-element.704), channel_id=1, source_target_pairs={{0,2},{2,4},{4,6},{1,3},{3,5},{5,7},{8,10},{10,12},{12,14},{9,11},... | collective-permute-start | bytes 3145736 | tf_op jit(solution)/shard_map/ppermute | solution.py:16
  354.9 16.7 %collective-permute-start.6 = (f32[2,2,128,512]{3,2,1,0:T(8,128)S(1)}, f32[2,2,128,512]{3,2,1,0:T(8,128)S(1)}, u32[]{:S(2)}, u32[]{:S(2)}) collective-permute-start(f32[2,2,128,512]{3,2,1,0:T(8,128)S(1)} %get-tuple-element.703), channel_id=1, source_target_pairs={{2,0},{4,2},{6,4},{3,1},{5,3},{7,5},{10,8},{12,10},{14,12},{11,9},... | collective-permute-start | bytes 3145736 | tf_op jit(solution)/shard_map/ppermute | solution.py:17
  371.9 24.3 %collective-permute-start.7 = (f32[2,2,768,128]{3,2,1,0:T(8,128)S(1)}, f32[2,2,768,128]{3,2,1,0:T(8,128)S(1)}, u32[]{:S(2)}, u32[]{:S(2)}) collective-permute-start(f32[2,2,768,128]{3,2,1,0:T(8,128)S(1)} %get-tuple-element.701), channel_id=1, source_target_pairs={{0,1},{2,3},{4,5},{6,7},{8,9},{10,11},{12,13},{14,15},{16,17},{18,... | collective-permute-start | bytes 4718600 | tf_op jit(solution)/shard_map/ppermute | solution.py:16
  378.4 24.7 %copy-start.6 = (pred[256]{0:T(512)(128)(4,1)S(1)}, pred[256]{0:T(512)(128)(4,1)}, u32[]{:S(2)}) copy-start(pred[256]{0:T(512)(128)(4,1)} %constant.107.clone.1) | copy-start | bytes 772
  378.4 22.4 %collective-permute-start.8 = (f32[2,2,768,128]{3,2,1,0:T(8,128)S(1)}, f32[2,2,768,128]{3,2,1,0:T(8,128)}, u32[]{:S(2)}, u32[]{:S(2)}) collective-permute-start(f32[2,2,768,128]{3,2,1,0:T(8,128)S(1)} %get-tuple-element.702), channel_id=1, source_target_pairs={{1,0},{3,2},{5,4},{7,6},{9,8},{11,10},{13,12},{15,14},{17,16},{19,... | collective-permute-start | bytes 4718600 | tf_op jit(solution)/shard_map/ppermute | solution.py:17
  396.2 1.1 copy-start.3
where the time goes:
time: 409 us; the launch traced here: 406 us
  waiting for transfers between devices  235 us (57%)
  local copies, waits for them, and re-layouts  49.3 us (12%)
  matrix products  40 us (10%)
  other arithmetic  33.7 us (8%)
  starting transfers between devices  30.6 us (7%)
  loops' own time  16.7 us (4%)
    ppermute x5, waiting for transfers between devices, passed_along(): lax.ppermute(value, axis, [(source, source + steps) for source in range(i...  187 us
    ppermute x4, waiting for transfers between devices, with_halo(): before = lax.ppermute(last, axis, up)  38.9 us
    dynamic_update_slice x4, local copies, waits for them, and re-layouts, add_member(): lax.dynamic_update_slice(running, current + term[member][None], start)  25.1 us
    dot_general x32, matrix products, right_apply(): jnp.einsum('mjk,kl->mjl', field, table, precision=lax.Precision.HIGHEST)  21.1 us
    dot_general x32, matrix products, left_apply(): jnp.einsum('jk,mkl->mjl', table, field, precision=lax.Precision.HIGHEST)  19 us
    another operation x5, loops' own time, one_step(): return lax.cond(active, run_slab, keep_state, (wave_in, first, total))  16.5 us
    ppermute x4, starting transfers between devices, with_halo(): before = lax.ppermute(last, axis, up)  16.1 us
    ppermute x4, waiting for transfers between devices, with_halo(): after = lax.ppermute(initial, axis, down)  9.64 us
  transfers between devices with their start and end apart: 13, of which 12 were waited for; matrix products, arithmetic and copies ran while one was open for 1% of the time, Pallas kernels for 0%

commit v1 on v0

v1 whole, which is shorter than its diff:
```python
import functools
import math

import jax
import jax.numpy as jnp
import numpy as np
from jax import lax
from jax.experimental import pallas as pl
from jax.experimental.pallas import tpu as pltpu
from jax.sharding import PartitionSpec as P

VMEM = pl.BlockSpec(memory_space=pltpu.VMEM)
SMEM = pl.BlockSpec(memory_space=pltpu.SMEM)
ANY = pl.BlockSpec(memory_space=pl.ANY)
LIMIT = 48 * 1024 * 1024


def swap_pairs(size, parity):
    pairs = []
    for i in range(parity, size - 1, 2):
        pairs += [(i, i + 1), (i + 1, i)]
    return pairs


def swap_list(n_x, n_y, swap_x, swap_y):
    xs = [(i, i) for i in range(n_x)] if swap_x is None else swap_pairs(n_x, swap_x)
    ys = [(i, i) for i in range(n_y)] if swap_y is None else swap_pairs(n_y, swap_y)
    return [(a * n_y + b, c * n_y + d) for a, c in xs for b, d in ys]


def swap_kinds(n_x, n_y):
    kinds = []
    for swap_x in (None, 0, 1):
        for swap_y in (None, 0, 1):
            if (swap_x, swap_y) != (None, None) and swap_list(n_x, n_y, swap_x, swap_y):
                kinds.append((swap_x, swap_y))
    return kinds


def split(value):
    high = value.astype(jnp.bfloat16)
    return high, (value - high.astype(jnp.float32)).astype(jnp.bfloat16)


def dft_basis(size):
    half = size // 2
    n = np.arange(size)
    j = np.arange(half)
    cos = np.cos(2 * np.pi * (j[:, None] * n[None, :] % size) / size)
    sin = np.sin(2 * np.pi * (j[:, None] * n[None, :] % size) / size)
    sin[0] = np.where(n % 2 == 0, 1.0, -1.0)
    return np.concatenate([cos, sin]) / math.sqrt(size)


def folded_order(array, axis):
    half = array.shape[axis] // 2
    low = lax.slice_in_dim(array, 0, half, axis=axis)
    mid = lax.slice_in_dim(array, half, half + 1, axis=axis)
    high = lax.rev(lax.slice_in_dim(array, half + 1, 2 * half, axis=axis), (axis,))
    return jnp.concatenate([low, mid, high], axis=axis)


def spectrum_split(p, q, first):
    (pr, pi), (qr, qi) = p, q
    plus = (jnp.where(first, pr, pr + qi), jnp.where(first, pi, pi - qr))
    minus = (jnp.where(first, qr, pr - qi), jnp.where(first, qi, pi + qr))
    return plus, minus


def spectrum_join(plus, minus, first):
    (xr, xi), (yr, yi) = plus, minus
    p = (jnp.where(first, xr, xr + yr), jnp.where(first, xi, xi + yi))
    q = (jnp.where(first, yr, yi - xi), jnp.where(first, yi, xr - yr))
    return p, q


def dot(a, b):
    return jnp.dot(a, b, preferred_element_type=jnp.float32)


def left3(table, field):
    high, low = split(field)
    return dot(table[0], high) + (dot(table[0], low) + dot(table[1], high))


def right3(field, table):
    high, low = split(field)
    return dot(high, table[0]) + (dot(low, table[0]) + dot(high, table[1]))


def propagate(wave_ref, cos_ref, sin_ref, tab_ref):
    size = wave_ref.shape[1]
    half = size // 2
    table = (tab_ref[0], tab_ref[1])
    turned = (tab_ref[2], tab_ref[3])
    parts = []
    for c in range(2):
        parts.append(right3(left3(table, wave_ref[c]), turned))
    row0 = lax.broadcasted_iota(jnp.int32, (half, half), 0) == 0
    col0 = lax.broadcasted_iota(jnp.int32, (half, half), 1) == 0

    def quadrant(r, c):
        return tuple(part[r * half : (r + 1) * half, c * half : (c + 1) * half] for part in parts)

    top = spectrum_split(quadrant(0, 0), quadrant(0, 1), col0)
    bottom = spectrum_split(quadrant(1, 0), quadrant(1, 1), col0)
    out = [[None, None], [None, None]]
    for c in range(2):
        turned_halves = []
        for r, (re, im) in enumerate(spectrum_split(top[c], bottom[c], row0)):
            where = (slice(r * half, (r + 1) * half), slice(c * half, (c + 1) * half))
            cos, sin = cos_ref[where], sin_ref[where]
            turned_halves.append((re * cos + im * sin, im * cos - re * sin))
        out[0][c], out[1][c] = spectrum_join(turned_halves[0], turned_halves[1], row0)
    rows = [spectrum_join(out[r][0], out[r][1], col0) for r in range(2)]
    for c in range(2):
        field = jnp.concatenate(
            [jnp.concatenate([rows[r][0][c], rows[r][1][c]], axis=1) for r in range(2)], axis=0
        )
        wave_ref[c] = left3(turned, right3(field, table))


def take_window(ext_ref, at_x, at_y, patch):
    step = 8
    inside = lax.rem(at_x, step)
    first = pl.multiple_of(at_x - inside, step)
    rows = ext_ref[pl.ds(first, patch + step), :]
    count, width = rows.shape
    rows = pltpu.roll(rows, lax.rem(width - at_y, width), 1)[:, :patch]
    return pltpu.roll(rows, lax.rem(count - inside, count), 0)[:patch]


def add_window(ext_ref, at_x, at_y, value):
    step = 8
    inside = lax.rem(at_x, step)
    first = pl.multiple_of(at_x - inside, step)
    value = jnp.concatenate([value, jnp.zeros((step, value.shape[1]), value.dtype)], axis=0)
    value = pltpu.roll(value, inside, 0)
    value = jnp.concatenate([value, jnp.zeros_like(value)], axis=1)
    ext_ref[pl.ds(first, value.shape[0]), :] += pltpu.roll(value, at_y, 1)


def window_kernel(kinds, info_ref, own_ref, *refs):
    pieces, (mine_ref, other_ref, ext_ref) = refs[: len(kinds)], refs[len(kinds) :]
    slab, _, tile, _ = own_ref.shape
    half = tile // 2
    patch = mine_ref.shape[2]
    spots = {None: half}
    for layer in range(slab):
        for c in range(2):
            ext_ref[...] = jnp.zeros_like(ext_ref)
            ext_ref[half : half + tile, half : half + tile] = own_ref[layer, c].astype(jnp.float32)
            for kind, piece in zip(kinds, pieces):
                row = half if kind[0] is None else pl.multiple_of(info_ref[kind[0]], half)
                col = half if kind[1] is None else pl.multiple_of(info_ref[2 + kind[1]], half)
                shape = piece.shape[2:]
                ext_ref[pl.ds(row, shape[0]), pl.ds(col, shape[1])] = piece[layer, c].astype(jnp.float32)
            for slot, out in ((0, mine_ref), (1, other_ref)):
                at_x, at_y = info_ref[4 + 2 * slot], info_ref[5 + 2 * slot]
                out[layer, c] = take_window(ext_ref, at_x, at_y, patch).astype(out.dtype)


def stage_kernel(info_ref, wave_in, win_own, win_got, inc_own, inc_got, cos_ref, sin_ref, tab_ref,
                 _keep_in, _send_in, keep_ref, send_ref, wave_ref, term, sems):
    slab = win_own.shape[0]
    layers = 2 * slab
    active, core, base = info_ref[0], info_ref[1], info_ref[2]

    @pl.when(active == 1)
    def _():
        wave_ref[...] = wave_in[...].astype(jnp.float32) * info_ref[3].astype(jnp.float32)

        def one(step, _):
            i = layers - 1 - step
            owner = i // slab
            local = lax.rem(i, slab)
            slot = lax.rem(step, 2)
            own = owner == core

            def wait(_):
                pltpu.make_async_copy(term.at[slot], keep_ref.at[0], sems.at[slot]).wait()

            pl.when(step >= 2)(lambda: wait(None))
            wr, wi = wave_ref[0], wave_ref[1]
            er = jnp.where(own, inc_own[local, 0], inc_got[local, 0]).astype(jnp.float32)
            ei = jnp.where(own, inc_own[local, 1], inc_got[local, 1]).astype(jnp.float32)
            term[slot, 0] = er * wr + ei * wi
            term[slot, 1] = er * wi - ei * wr

            @pl.when(own)
            def _():
                pltpu.make_async_copy(term.at[slot], keep_ref.at[local], sems.at[slot]).start()

            @pl.when(jnp.logical_not(own))
            def _():
                pltpu.make_async_copy(term.at[slot], send_ref.at[local], sems.at[slot]).start()

            @pl.when(base + i > 0)
            def _():
                tr = jnp.where(own, win_own[local, 0], win_got[local, 0]).astype(jnp.float32)
                ti = jnp.where(own, win_own[local, 1], win_got[local, 1]).astype(jnp.float32)
                wave_ref[0] = tr * wr + ti * wi
                wave_ref[1] = tr * wi - ti * wr
                propagate(wave_ref, cos_ref, sin_ref, tab_ref)

            return 0

        lax.fori_loop(0, layers, one, 0)
        for slot in range(2):
            pltpu.make_async_copy(term.at[slot], keep_ref.at[0], sems.at[slot]).wait()


def scatter_kernel(kinds, info_ref, mine_ref, other_ref, *refs):
    own_ref, pieces, ext_ref = refs[0], refs[1 : 1 + len(kinds)], refs[-1]
    slab, _, patch, _ = mine_ref.shape
    tile = own_ref.shape[2]
    half = tile // 2
    for layer in range(slab):
        for c in range(2):
            ext_ref[...] = jnp.zeros_like(ext_ref)
            for slot, term in ((0, mine_ref), (1, other_ref)):
                at_x, at_y = info_ref[4 + 2 * slot], info_ref[5 + 2 * slot]
                add_window(ext_ref, at_x, at_y, term[layer, c])
            own_ref[layer, c] = ext_ref[half : half + tile, half : half + tile]
            for kind, piece in zip(kinds, pieces):
                row = half if kind[0] is None else pl.multiple_of(info_ref[kind[0]], half)
                col = half if kind[1] is None else pl.multiple_of(info_ref[2 + kind[1]], half)
                shape = piece.shape[2:]
                piece[layer, c] = ext_ref[pl.ds(row, shape[0]), pl.ds(col, shape[1])]


def fold_kernel(kinds, info_ref, own_ref, *refs):
    pieces, out_ref = refs[: len(kinds)], refs[-1]
    slab, _, tile, _ = own_ref.shape
    half = tile // 2
    for layer in range(slab):
        for c in range(2):
            out_ref[layer, c] = own_ref[layer, c]
            for kind, piece in zip(kinds, pieces):
                row = 0 if kind[0] is None else pl.multiple_of(info_ref[8 + kind[0]], half)
                col = 0 if kind[1] is None else pl.multiple_of(info_ref[10 + kind[1]], half)
                shape = piece.shape[2:]
                where = (layer, c, pl.ds(row, shape[0]), pl.ds(col, shape[1]))
                out_ref[where] += piece[layer, c]


def shards(transmission, incident, exit_adjoint, propagator_phase, scan_anchor, live_count):
    f32 = jnp.float32
    n_depth, n_x, n_y = lax.axis_size("depth"), lax.axis_size("sx"), lax.axis_size("sy")
    depth, at_x, at_y = lax.axis_index("depth"), lax.axis_index("sx"), lax.axis_index("sy")
    slab, _, tile, _ = transmission.shape
    patch = propagator_phase.shape[0]
    half = tile // 2
    extent = tile + patch
    core, chip = depth % 2, depth // 2
    chips = n_depth // 2
    kinds = swap_kinds(n_x, n_y)
    params = pltpu.CompilerParams(vmem_limit_bytes=LIMIT)
    core_swap = swap_pairs(n_depth, 0)
    odd_x, odd_y = at_x % 2, at_y % 2

    top = half + tile
    halo = [
        jnp.where(odd_x == 0, top, 0), jnp.where(odd_x == 0, 0, top),
        jnp.where(odd_y == 0, top, 0), jnp.where(odd_y == 0, 0, top),
    ]
    rim = [jnp.where(value == 0, 0, tile - half) for value in halo]
    corner = scan_anchor - jnp.stack([at_x * tile, at_y * tile])[None, :] + half
    corner_mine = lax.dynamic_slice_in_dim(corner, core, 1, 0)[0]
    corner_other = lax.dynamic_slice_in_dim(corner, 1 - core, 1, 0)[0]
    info = jnp.stack(halo + [corner_mine[0], corner_mine[1], corner_other[0], corner_other[1]] + rim)
    info = info.astype(jnp.int32)

    def piece_shape(kind):
        rows = tile if kind[0] is None else half
        cols = tile if kind[1] is None else half
        return (slab, 2, rows, cols)

    def swapped(value, kind):
        return lax.ppermute(value, ("sx", "sy"), swap_list(n_x, n_y, *kind))

    pieces = []
    for kind in kinds:
        value = transmission
        if kind[0] is not None:
            value = lax.dynamic_slice_in_dim(value, rim[kind[0]], half, 2)
        if kind[1] is not None:
            value = lax.dynamic_slice_in_dim(value, rim[2 + kind[1]], half, 3)
        pieces.append(swapped(value, kind))

    inc_own = lax.dynamic_slice_in_dim(incident, core, 1, 1)[:, 0]
    inc_send = lax.dynamic_slice_in_dim(incident, 1 - core, 1, 1)[:, 0]
    inc_got = lax.ppermute(inc_send, "depth", core_swap)
    phase = folded_order(folded_order(propagator_phase, 0), 1)
    phase_cos, phase_sin = jnp.cos(phase), jnp.sin(phase)
    basis = dft_basis(patch)
    high = basis.astype(jnp.bfloat16)
    low = (basis - high.astype(np.float64)).astype(jnp.bfloat16)
    tables = jnp.asarray(np.stack([high, low, high.T, low.T]))

    window_shape = jax.ShapeDtypeStruct((slab, 2, patch, patch), jnp.bfloat16)
    win_own, win_send = pl.pallas_call(
        functools.partial(window_kernel, kinds),
        out_shape=(window_shape, window_shape),
        in_specs=[SMEM] + [VMEM] * (1 + len(kinds)),
        out_specs=(VMEM, VMEM),
        scratch_shapes=[pltpu.VMEM((extent, extent), f32)],
        compiler_params=params,
        name="windows",
    )(info, transmission, *pieces)
    win_got = lax.ppermute(win_send, "depth", core_swap)

    live = (core < live_count[0]).astype(jnp.int32)
    wave = lax.dynamic_slice_in_dim(exit_adjoint, core, 1, 0)[0]
    term_shape = jax.ShapeDtypeStruct((slab, 2, patch, patch), f32)
    keep = jnp.zeros(term_shape.shape, f32)
    send = jnp.zeros(term_shape.shape, f32)
    for stage in range(chips):
        active = (chip == chips - 1 - stage).astype(jnp.int32)
        facts = jnp.stack(
            [active, core, chip * 2 * slab, live if stage == 0 else jnp.ones_like(live)]
        ).astype(jnp.int32)
        keep, send, wave = pl.pallas_call(
            stage_kernel,
            out_shape=(term_shape, term_shape, jax.ShapeDtypeStruct((2, patch, patch), f32)),
            in_specs=[SMEM] + [VMEM] * 8 + [ANY, ANY],
            out_specs=(ANY, ANY, VMEM),
            scratch_shapes=[pltpu.VMEM((2, 2, patch, patch), f32), pltpu.SemaphoreType.DMA((2,))],
            input_output_aliases={9: 0, 10: 1},
            compiler_params=params,
            name="sweep",
        )(facts, wave, win_own, win_got, inc_own, inc_got, phase_cos, phase_sin, tables, keep, send)
        if stage < chips - 1:
            source = chips - 1 - stage
            hop = [(2 * source + c, 2 * source - 2 + c) for c in range(2)]
            wave = lax.ppermute(wave, "depth", hop)

    got = lax.ppermute(send, "depth", core_swap)
    piece_shapes = tuple(jax.ShapeDtypeStruct(piece_shape(kind), f32) for kind in kinds)
    scattered = pl.pallas_call(
        functools.partial(scatter_kernel, kinds),
        out_shape=(jax.ShapeDtypeStruct((slab, 2, tile, tile), f32),) + piece_shapes,
        in_specs=[SMEM, VMEM, VMEM],
        out_specs=(VMEM,) * (1 + len(kinds)),
        scratch_shapes=[pltpu.VMEM((extent, extent), f32)],
        compiler_params=params,
        name="scatter",
    )(info, keep, got)
    folded = [swapped(value, kind) for value, kind in zip(scattered[1:], kinds)]
    return pl.pallas_call(
        functools.partial(fold_kernel, kinds),
        out_shape=jax.ShapeDtypeStruct((slab, 2, tile, tile), f32),
        in_specs=[SMEM] + [VMEM] * (1 + len(kinds)),
        out_specs=VMEM,
        compiler_params=params,
        name="fold",
    )(info, scattered[0], *folded)


def solution(mesh):
    placed = (
        P("depth", None, "sx", "sy"),
        P("depth", ("sx", "sy"), None, None, None),
        P(("sx", "sy"), None, None, None),
        P(),
        P(("sx", "sy"), None),
        P(("sx", "sy")),
    )
    return jax.shard_map(
        shards, mesh=mesh, in_specs=placed, out_specs=P("depth", None, "sx", "sy"), check_vma=False
    )
```

time: 409 us -> 103 us (0.25)
  waiting for transfers between devices: 235 us -> 44.5 us
  matrix products: 40 us -> 0 us
  other arithmetic: 33.7 us -> 1.47 us
  local copies, waits for them, and re-layouts: 49.3 us -> 21.4 us
  loops' own time: 16.7 us -> 0 us
  Pallas kernels: 0 us -> 16.4 us
  starting transfers between devices: 30.6 us -> 17.5 us
    ppermute x13 -> x14, waiting for transfers between devices: 235 us -> 44.5 us  [the longest x1 22.1 us: shards(): wave = lax.ppermute(wave, 'depth', hop)]
    dot_general x64 -> x0, matrix products: 40 us -> none  [the longest x32 21.1 us: right_apply(): jnp.einsum('mjk,kl->mjl', field, table, precision=lax.Precision.HIGHEST)]
    dynamic_update_slice x4 -> x0, local copies, waits for them, and re-layouts: 25.1 us -> none  [add_member(): lax.dynamic_update_slice(running, current + term[member][None], start)]
    another operation x6 -> x0, loops' own time: 16.7 us -> none  [the longest x5 16.5 us: one_step(): return lax.cond(active, run_slab, keep_state, (wave_in, first, total))]
    pallas_call x0 -> x5, Pallas kernels: none -> 16.4 us  [the longest x2 8.61 us: shards(): pl.pallas_call(stage_kernel, out_shape=(term_shape, term_shape, jax.Shape...]
    slice x11 -> x3, local copies, waits for them, and re-layouts: 16.8 us -> 0.62 us  [the longest x1 0.59 us: shards(): corner_other[1]]
    ppermute x13 -> x14, starting transfers between devices: 30.6 us -> 17.5 us  [the longest x10 15.4 us: swapped(): return lax.ppermute(value, ('sx', 'sy'), swap_list(n_x, n_y, *kind))]
    add x9 -> x1, other arithmetic: 12.3 us -> 0.01 us  [shards(): corner = scan_anchor - jnp.stack([at_x * tile, at_y * tile])[None, :] + half]
  transfers between devices with their start and end apart: 13 -> 14, of which waited for: 12 -> 5; matrix products, arithmetic and copies ran while one was open for 1% -> 8% of each run, Pallas kernels for 0% -> 3%
where the time goes in v1:
time: 103 us; the launch traced here: 102 us
  waiting for transfers between devices  44.5 us (43%)
  local copies, waits for them, and re-layouts  21.4 us (21%)
  starting transfers between devices  17.5 us (17%)
  Pallas kernels  16.4 us (16%)
  other arithmetic  1.47 us (1%)
    ppermute x1, waiting for transfers between devices, shards(): wave = lax.ppermute(wave, 'depth', hop)  22.1 us
    ppermute x10, waiting for transfers between devices, swapped(): return lax.ppermute(value, ('sx', 'sy'), swap_list(n_x, n_y, *kind))  19.9 us
    ppermute x10, starting transfers between devices, swapped(): return lax.ppermute(value, ('sx', 'sy'), swap_list(n_x, n_y, *kind))  15.4 us
    unnamed x40, local copies, waits for them, and re-layouts  12.3 us
    pallas_call x2, Pallas kernels, shards(): pl.pallas_call(stage_kernel, out_shape=(term_shape, term_shape, jax.Shape...  8.61 us
    pallas_call x1, Pallas kernels, shards(): pl.pallas_call(functools.partial(window_kernel, kinds), out_shape=(window...  3.41 us
    dynamic_slice x2, local copies, waits for them, and re-layouts, shards(): value = lax.dynamic_slice_in_dim(value, rim[2 + kind[1]], half, 3)  2.67 us
    pallas_call x1, Pallas kernels, shards(): pl.pallas_call(functools.partial(scatter_kernel, kinds), out_shape=(jax.S...  2.59 us
  transfers between devices with their start and end apart: 14, of which 5 were waited for; matrix products, arithmetic and copies ran while one was open for 8% of the time, Pallas kernels for 3%

profile of v1, /device:TPU:16, one launch (start us, length us, event | category | flops | bytes accessed | tf_op | source)
XLA Modules:
  0.0 102.3 jit_solution(7340378736486818135)
XLA Ops:
  0.0 1.9 %constant_dynamic-slice_fusion = (bf16[2,2,128,128]{3,2,1,0:T(8,128)(2,1)S(1)}, bf16[2,2,128,128]{3,2,1,0:T(8,128)(2,1)}) fusion(bf16[2,2,256,256]{3,2,1,0:T(8,128)(2,1)} %own_ref.1, s32[]{:T(128)S(6)} %select_n.83, s32[]{:T(128)S(6)} %select_n.82, s32[]{:T(128)S(6)} %select_n.81), kind=kLoop, calls=%fused_computation.8 | loop fusion | bytes 524300 | tf_op jit(solution)/shard_map/dynamic_slice | solution.py:288
  1.9 3.4 %collective-permute-start.4 = (bf16[2,2,128,128]{3,2,1,0:T(8,128)(2,1)S(1)}, bf16[2,2,128,128]{3,2,1,0:T(8,128)(2,1)S(1)}, u32[]{:S(2)}, u32[]{:S(2)}) collective-permute-start(bf16[2,2,128,128]{3,2,1,0:T(8,128)(2,1)S(1)} %get-tuple-element.33), channel_id=1, source_target_pairs={{2,5},{3,4},{4,3},{5,2},{10,13},{11,12},{12,11},{13,10},{18,21},{1... | collective-permute-start | bytes 393224 | tf_op jit(solution)/shard_map/ppermute | solution.py:280
  5.4 0.8 constant_dynamic-slice_fusion.4
  6.1 0.4 collective-permute-start
  6.6 0.8 constant_dynamic-slice_fusion.1
  7.4 3.5 %collective-permute-start.3 = (bf16[2,2,128,256]{3,2,1,0:T(8,128)(2,1)}, bf16[2,2,128,256]{3,2,1,0:T(8,128)(2,1)S(1)}, u32[]{:S(2)}, u32[]{:S(2)}) collective-permute-start(bf16[2,2,128,256]{3,2,1,0:T(8,128)(2,1)} %get-tuple-element.35), channel_id=1, source_target_pairs={{2,4},{3,5},{4,2},{5,3},{10,12},{11,13},{12,10},{13,11},{18,20},{1... | collective-permute-start | bytes 786440 | tf_op jit(solution)/shard_map/ppermute | solution.py:280
  10.9 0.3 collective-permute-start.1
  11.2 0.6 copy-done.19
  11.9 0.1 rev.6
  12.0 0.6 fusion.2
  12.6 2.5 %stack.79.info_ref = s32[12]{0:T(128)S(1)} concatenate(s32[1]{0:T(128)} %bitcast, s32[1]{0:T(128)} %bitcast.1, s32[1]{0:T(128)} %bitcast.2, s32[1]{0:T(128)} %bitcast.3, s32[1]{0:T(128)} %bitcast.6, s32[1]{0:T(128)} %bitcast.7, s32[1]{0:T(128)} %bitcast.8, s32[1]{0:T(128)} %bitcast.9, s32[1]{0:T(128)} %bitcast.10, s32[1]{0:T(128)} %bitcast.11, s32[1]{0:T(128)} %bitcast.12, s32[1]{0:T(128)} %bitcast.13), dimensions={0} | concatenate | bytes 96 | tf_op jit(solution)/shard_map/stack | solution.py:271
  15.1 2.1 %dynamic-slice_bitcast_fusion = (bf16[2,2,256,256]{3,2,1,0:T(8,128)(2,1)}, bf16[2,2,256,256]{3,2,1,0:T(8,128)(2,1)S(1)}) fusion(bf16[2,2,2,256,256]{4,3,2,1,0:T(8,128)(2,1)} %param.8, s32[]{:T(128)S(6)} %select_n.75, s32[]{:T(128)S(6)} %select_n.74), kind=kLoop, calls=%fused_computation | loop fusion | bytes 2097160 | tf_op jit(solution)/shard_map/squeeze | solution.py:292
  17.2 1.2 %collective-permute-done.refs_0_ = bf16[2,2,256,128]{3,2,1,0:T(8,128)(2,1)S(1)} collective-permute-done((bf16[2,2,256,128]{3,2,1,0:T(8,128)(2,1)}, bf16[2,2,256,128]{3,2,1,0:T(8,128)(2,1)S(1)}, u32[]{:S(2)}, u32[]{:S(2)}) %collective-permute-start) | collective-permute-done | bytes 262176 | tf_op jit(solution)/shard_map/ppermute | solution.py:280
  18.4 3.4 %windows.1 = (bf16[2,2,256,256]{3,2,1,0:T(8,128)(2,1)S(1)}, bf16[2,2,256,256]{3,2,1,0:T(8,128)(2,1)}) custom-call(s32[12]{0:T(128)S(1)} %stack.79.info_ref, bf16[2,2,256,256]{3,2,1,0:T(8,128)(2,1)S(1)} %copy-done.2, bf16[2,2,256,128]{3,2,1,0:T(8,128)(2,1)S(1)} %collective-permute-done.refs_0_, bf16[2,2,128,256]{3,2,1,0:T(8,128)(2,1)S(1)} %collective-permute-done.1.refs_1_, ...), custom_call_target="tpu_custom_call" | custom-call | tf_op jit(solution)/shard_map/windows/pallas_call | solution.py:302
  21.8 0.8 copy-done.10
  22.6 0.1 pad_maximum_fusion.1
  23.3 0.2 rev.7
  23.5 0.1 pad_add_fusion.2.info_ref
  23.7 1.1 %fusion = (f32[256,256]{1,0:T(8,128)S(1)}, f32[256,256]{1,0:T(8,128)S(1)}) fusion(f32[256,127]{1,0:T(8,128)S(1)} %rev.7, f32[256,129]{1,0:T(8,128)S(1)} %slice_maximum_fusion), kind=kLoop, calls=%fused_computation.5 | loop fusion | flops 65536 | bytes 786432 | tf_op jit(solution)/shard_map/sin | solution.py:295
  24.8 0.8 copy-done.7
  25.7 0.8 copy-done.13
  26.7 0.8 copy-done.11
  27.5 0.2 copy-done.14
  27.7 0.2 copy-done.5
  27.9 0.2 copy-done.8
  28.0 1.4 %sweep.2 = (f32[2,2,256,256]{3,2,1,0:T(8,128)S(1)}, f32[2,2,256,256]{3,2,1,0:T(8,128)S(1)}, f32[2,256,256]{2,1,0:T(8,128)}) custom-call(s32[4]{0:T(128)S(1)} %pad_add_fusion.2.info_ref, bf16[2,256,256]{2,1,0:T(8,128)(2,1)S(1)} %dynamic-slice_bitcast_fusion.2.wave_in, ...), custom_call_target="tpu_custom_call", output_to_operand_aliasing={{0}: (9, {}), {1}: (10, {})} | custom-call | tf_op jit(solution)/shard_map/sweep/pallas_call | solution.py:323
  29.4 1.0 copy-done.1
  30.4 1.3 %collective-permute-start.7 = (f32[2,256,256]{2,1,0:T(8,128)}, f32[2,256,256]{2,1,0:T(8,128)S(1)}, u32[]{:S(2)}, u32[]{:S(2)}) collective-permute-start(f32[2,256,256]{2,1,0:T(8,128)} %get-tuple-element.20), channel_id=1, source_target_pairs={{16,0},{24,8},{17,1},{25,9},{18,2},{26,10},{19,3},{27,11},{20,4},{... | collective-permute-start | bytes 1572872 | tf_op jit(solution)/shard_map/ppermute | solution.py:336
  31.7 0.1 pad_add_fusion.1.info_ref
  31.7 22.1 %collective-permute-done.7.wave_in = f32[2,256,256]{2,1,0:T(8,128)S(1)} collective-permute-done((f32[2,256,256]{2,1,0:T(8,128)}, f32[2,256,256]{2,1,0:T(8,128)S(1)}, u32[]{:S(2)}, u32[]{:S(2)}) %collective-permute-start.7) | collective-permute-done | bytes 524320 | tf_op jit(solution)/shard_map/ppermute | solution.py:336
  53.8 0.8 copy-done.16
  54.6 0.9 copy-done.4
  55.6 1.0 %copy-done.6 = bf16[4,256,256]{2,1,0:T(8,128)(2,1)S(1)} copy-done((bf16[4,256,256]{2,1,0:T(8,128)(2,1)S(1)}, bf16[4,256,256]{2,1,0:T(8,128)(2,1)}, u32[]{:S(2)}) %copy-start.6) | copy-done | bytes 524312
  56.6 1.0 %copy-done.9 = bf16[2,2,256,256]{3,2,1,0:T(8,128)(2,1)S(1)} copy-done((bf16[2,2,256,256]{3,2,1,0:T(8,128)(2,1)S(1)}, bf16[2,2,256,256]{3,2,1,0:T(8,128)(2,1)}, u32[]{:S(2)}) %copy-start.9) | copy-done | bytes 524312
  57.6 1.0 %copy-done.12 = bf16[2,2,256,256]{3,2,1,0:T(8,128)(2,1)S(1)} copy-done((bf16[2,2,256,256]{3,2,1,0:T(8,128)(2,1)S(1)}, bf16[2,2,256,256]{3,2,1,0:T(8,128)(2,1)}, u32[]{:S(2)}) %copy-start.12) | copy-done | bytes 524312
  58.7 1.0 %copy-done.15 = bf16[2,2,256,256]{3,2,1,0:T(8,128)(2,1)S(1)} copy-done((bf16[2,2,256,256]{3,2,1,0:T(8,128)(2,1)S(1)}, bf16[2,2,256,256]{3,2,1,0:T(8,128)(2,1)}, u32[]{:S(2)}) %copy-start.15) | copy-done | bytes 524312
  59.7 1.0 %copy-done.17 = f32[2,256,256]{2,1,0:T(8,128)S(1)} copy-done((f32[2,256,256]{2,1,0:T(8,128)S(1)}, f32[2,256,256]{2,1,0:T(8,128)}, u32[]{:S(2)}) %copy-start.17) | copy-done | bytes 524312
  60.8 7.2 %sweep.3 = (f32[2,2,256,256]{3,2,1,0:T(8,128)S(1)}, f32[2,2,256,256]{3,2,1,0:T(8,128)}, f32[2,256,256]{2,1,0:T(8,128)}) custom-call(s32[4]{0:T(128)S(1)} %pad_add_fusion.1.info_ref, f32[2,256,256]{2,1,0:T(8,128)S(1)} %copy-done.17, bf16[2,2,256,256]{3,2,1,0:T(8,128)(2,1)S(1)} %copy-done.12, ...), custom_call_target="tpu_custom_call", output_to_operand_aliasing={{0}: (9, {}), {1}: (10, {})} | custom-call | tf_op jit(solution)/shard_map/sweep/pallas_call | solution.py:323
  68.0 0.8 collective-permute-start.8
  68.8 2.5 %collective-permute-done.8.other_ref = f32[2,2,256,256]{3,2,1,0:T(8,128)S(1)} collective-permute-done((f32[2,2,256,256]{3,2,1,0:T(8,128)}, f32[2,2,256,256]{3,2,1,0:T(8,128)S(1)}, u32[]{:S(2)}, u32[]{:S(2)}) %collective-permute-start.8) | collective-permute-done | bytes 1048608 | tf_op jit(solution)/shard_map/ppermute | solution.py:338
  71.3 2.6 %scatter.1 = (f32[2,2,256,256]{3,2,1,0:T(8,128)S(1)}, f32[2,2,256,128]{3,2,1,0:T(8,128)S(1)}, f32[2,2,128,256]{3,2,1,0:T(8,128)S(1)}, f32[2,2,128,128]{3,2,1,0:T...) custom-call(s32[12]{0:T(128)S(1)} %stack.79.info_ref, ...), custom_call_target="tpu_custom_call" | custom-call | tf_op jit(solution)/shard_map/scatter/pallas_call | solution.py:340
  73.9 1.7 %collective-permute-start.9 = (f32[2,2,256,128]{3,2,1,0:T(8,128)S(1)}, f32[2,2,256,128]{3,2,1,0:T(8,128)S(1)}, u32[]{:S(2)}, u32[]{:S(2)}) collective-permute-start(f32[2,2,256,128]{3,2,1,0:T(8,128)S(1)} %get-tuple-element.26), channel_id=1, source_target_pairs={{0,1},{1,0},{2,3},{3,2},{4,5},{5,4},{6,7},{7,6},{8,9},{9,8},{10,11... | collective-permute-start | bytes 1572872 | tf_op jit(solution)/shard_map/ppermute | solution.py:280
  75.5 0.4 collective-permute-start.10
  75.9 2.4 %collective-permute-start.12 = (f32[2,2,128,256]{3,2,1,0:T(8,128)S(1)}, f32[2,2,128,256]{3,2,1,0:T(8,128)S(1)}, u32[]{:S(2)}, u32[]{:S(2)}) collective-permute-start(f32[2,2,128,256]{3,2,1,0:T(8,128)S(1)} %get-tuple-element.29), channel_id=1, source_target_pairs={{2,4},{3,5},{4,2},{5,3},{10,12},{11,13},{12,10},{13,11},{18,20},{1... | collective-permute-start | bytes 1572872 | tf_op jit(solution)/shard_map/ppermute | solution.py:280
  78.4 3.3 %collective-permute-start.13 = (f32[2,2,128,128]{3,2,1,0:T(8,128)S(1)}, f32[2,2,128,128]{3,2,1,0:T(8,128)S(1)}, u32[]{:S(2)}, u32[]{:S(2)}) collective-permute-start(f32[2,2,128,128]{3,2,1,0:T(8,128)S(1)} %get-tuple-element.30), channel_id=1, source_target_pairs={{2,5},{3,4},{4,3},{5,2},{10,13},{11,12},{12,11},{13,10},{18,21},{1... | collective-permute-start | bytes 786440 | tf_op jit(solution)/shard_map/ppermute | solution.py:280
  81.7 17.2 %collective-permute-done.11.refs_2_ = f32[2,2,128,128]{3,2,1,0:T(8,128)S(1)} collective-permute-done((f32[2,2,128,128]{3,2,1,0:T(8,128)S(1)}, f32[2,2,128,128]{3,2,1,0:T(8,128)S(1)}, u32[]{:S(2)}, u32[]{:S(2)}) %collective-permute-start.11) | collective-permute-done | bytes 262176 | tf_op jit(solution)/shard_map/ppermute | solution.py:280
  99.0 1.5 %collective-permute-done.13.refs_4_ = f32[2,2,128,128]{3,2,1,0:T(8,128)S(1)} collective-permute-done((f32[2,2,128,128]{3,2,1,0:T(8,128)S(1)}, f32[2,2,128,128]{3,2,1,0:T(8,128)S(1)}, u32[]{:S(2)}, u32[]{:S(2)}) %collective-permute-start.13) | collective-permute-done | bytes 262176 | tf_op jit(solution)/shard_map/ppermute | solution.py:280
  100.4 1.8 %fold.1 = f32[2,2,256,256]{3,2,1,0:T(8,128)} custom-call(s32[12]{0:T(128)S(1)} %stack.79.info_ref, f32[2,2,256,256]{3,2,1,0:T(8,128)S(1)} %get-tuple-element.25.own_ref, f32[2,2,256,128]{3,2,1,0:T(8,128)S(1)} %collective-permute-done.9.refs_0_, f32[2,2,128,256]{3,2,1,0:T(8,128)S(1)} %collective-permute-done.10.refs_1_, ...), custom_call_target="tpu_custom_call" | custom-call | tf_op jit(solution)/shard_map/fold/pallas_call | solution.py:350
  (46 shorter events, 0.5 us)
Async XLA Ops:
  0.0 23.7 %copy-start = (bf16[2,2,256,256]{3,2,1,0:T(8,128)(2,1)S(1)}, bf16[2,2,256,256]{3,2,1,0:T(8,128)(2,1)}, u32[]{:S(2)}) copy-start(bf16[2,2,256,256]{3,2,1,0:T(8,128)(2,1)} %param.9) | copy-start | bytes 1572868
  0.0 5.4 %copy-start.2 = (bf16[2,2,256,256]{3,2,1,0:T(8,128)(2,1)S(1)}, bf16[2,2,256,256]{3,2,1,0:T(8,128)(2,1)}, u32[]{:S(2)}) copy-start(bf16[2,2,256,256]{3,2,1,0:T(8,128)(2,1)} %own_ref.1) | copy-start | bytes 1572868
  1.9 15.3 %collective-permute-start.4 = (bf16[2,2,128,128]{3,2,1,0:T(8,128)(2,1)S(1)}, bf16[2,2,128,128]{3,2,1,0:T(8,128)(2,1)S(1)}, u32[]{:S(2)}, u32[]{:S(2)}) collective-permute-start(bf16[2,2,128,128]{3,2,1,0:T(8,128)(2,1)S(1)} %get-tuple-element.33), channel_id=1, source_target_pairs={{2,5},{3,4},{4,3},{5,2},{10,13},{11,12},{12,11},{13,10},{18,21},{1... | collective-permute-start | bytes 393224 | tf_op jit(solution)/shard_map/ppermute | solution.py:280
  5.3 11.9 %collective-permute-start.2 = (bf16[2,2,128,128]{3,2,1,0:T(8,128)(2,1)}, bf16[2,2,128,128]{3,2,1,0:T(8,128)(2,1)S(1)}, u32[]{:S(2)}, u32[]{:S(2)}) collective-permute-start(bf16[2,2,128,128]{3,2,1,0:T(8,128)(2,1)} %get-tuple-element.34), channel_id=1, source_target_pairs={{0,3},{1,2},{2,1},{3,0},{4,7},{5,6},{6,5},{7,4},{8,11},{9,10},{10,... | collective-permute-start | bytes 393224 | tf_op jit(solution)/shard_map/ppermute | solution.py:280
  6.1 5.7 %copy-start.18 = (f32[256,256]{1,0:T(8,128)S(1)}, f32[256,256]{1,0:T(8,128)}, u32[]{:S(2)}) copy-start(f32[256,256]{1,0:T(8,128)} %param.10) | copy-start | bytes 786436
  6.1 12.2 %collective-permute-start = (bf16[2,2,256,128]{3,2,1,0:T(8,128)(2,1)}, bf16[2,2,256,128]{3,2,1,0:T(8,128)(2,1)S(1)}, u32[]{:S(2)}, u32[]{:S(2)}) collective-permute-start(bf16[2,2,256,128]{3,2,1,0:T(8,128)(2,1)} %constant_dynamic-slice_fusion.4), channel_id=1, source_target_pairs={{0,1},{1,0},{2,3},{3,2},{4,5},{5,4},{6,7},{7,6},{8,9},{9,8},{10,11... | collective-permute-start | bytes 786440 | tf_op jit(solution)/shard_map/ppermute | solution.py:280
  7.4 11.0 %collective-permute-start.3 = (bf16[2,2,128,256]{3,2,1,0:T(8,128)(2,1)}, bf16[2,2,128,256]{3,2,1,0:T(8,128)(2,1)S(1)}, u32[]{:S(2)}, u32[]{:S(2)}) collective-permute-start(bf16[2,2,128,256]{3,2,1,0:T(8,128)(2,1)} %get-tuple-element.35), channel_id=1, source_target_pairs={{2,4},{3,5},{4,2},{5,3},{10,12},{11,13},{12,10},{13,11},{18,20},{1... | collective-permute-start | bytes 786440 | tf_op jit(solution)/shard_map/ppermute | solution.py:280
  10.9 7.5 %collective-permute-start.1 = (bf16[2,2,128,256]{3,2,1,0:T(8,128)(2,1)}, bf16[2,2,128,256]{3,2,1,0:T(8,128)(2,1)S(1)}, u32[]{:S(2)}, u32[]{:S(2)}) collective-permute-start(bf16[2,2,128,256]{3,2,1,0:T(8,128)(2,1)} %get-tuple-element.36), channel_id=1, source_target_pairs={{0,2},{1,3},{2,0},{3,1},{4,6},{5,7},{6,4},{7,5},{8,10},{9,11},{10,... | collective-permute-start | bytes 786440 | tf_op jit(solution)/shard_map/ppermute | solution.py:280
  11.2 0.7 copy-start.19
  17.2 7.6 %collective-permute-start.6 = (bf16[2,2,256,256]{3,2,1,0:T(8,128)(2,1)}, bf16[2,2,256,256]{3,2,1,0:T(8,128)(2,1)S(1)}, u32[]{:S(2)}, u32[]{:S(2)}) collective-permute-start(bf16[2,2,256,256]{3,2,1,0:T(8,128)(2,1)} %get-tuple-element.31), channel_id=1, source_target_pairs={{0,8},{8,0},{16,24},{24,16},{1,9},{9,1},{17,25},{25,17},{2,10},{10... | collective-permute-start | bytes 1572872 | tf_op jit(solution)/shard_map/ppermute | solution.py:293
  21.8 0.8 copy-start.10
  22.6 3.1 %collective-permute-start.5 = (bf16[2,2,256,256]{3,2,1,0:T(8,128)(2,1)}, bf16[2,2,256,256]{3,2,1,0:T(8,128)(2,1)S(1)}, u32[]{:S(2)}, u32[]{:S(2)}) collective-permute-start(bf16[2,2,256,256]{3,2,1,0:T(8,128)(2,1)} %get-tuple-element.19), channel_id=1, source_target_pairs={{0,8},{8,0},{16,24},{24,16},{1,9},{9,1},{17,25},{25,17},{2,10},{10... | collective-permute-start | bytes 1572872 | tf_op jit(solution)/shard_map/ppermute | solution.py:311
  24.8 1.9 %copy-start.3 = (f32[256,256]{1,0:T(8,128)}, f32[256,256]{1,0:T(8,128)S(1)}, u32[]{:S(2)}) copy-start(f32[256,256]{1,0:T(8,128)S(1)} %get-tuple-element.38.cos_ref) | copy-start | bytes 786436
  24.8 0.8 copy-start.7
  25.7 0.8 copy-start.13
  26.5 1.0 %copy-start.11 = (bf16[2,2,256,256]{3,2,1,0:T(8,128)(2,1)S(1)}, bf16[2,2,256,256]{3,2,1,0:T(8,128)(2,1)}, u32[]{:S(2)}) copy-start(bf16[2,2,256,256]{3,2,1,0:T(8,128)(2,1)} %copy-done.10) | copy-start | bytes 1572868
  26.5 1.2 %copy-start.14 = (bf16[2,2,256,256]{3,2,1,0:T(8,128)(2,1)S(1)}, bf16[2,2,256,256]{3,2,1,0:T(8,128)(2,1)}, u32[]{:S(2)}) copy-start(bf16[2,2,256,256]{3,2,1,0:T(8,128)(2,1)} %copy-done.13) | copy-start | bytes 1572868
  26.6 1.3 %copy-start.5 = (bf16[4,256,256]{2,1,0:T(8,128)(2,1)S(1)}, bf16[4,256,256]{2,1,0:T(8,128)(2,1)}, u32[]{:S(2)}) copy-start(bf16[4,256,256]{2,1,0:T(8,128)(2,1)} %constant.103.clone.tab_ref) | copy-start | bytes 1572868
  26.6 1.4 %copy-start.8 = (bf16[2,2,256,256]{3,2,1,0:T(8,128)(2,1)S(1)}, bf16[2,2,256,256]{3,2,1,0:T(8,128)(2,1)}, u32[]{:S(2)}) copy-start(bf16[2,2,256,256]{3,2,1,0:T(8,128)(2,1)} %copy-done.7) | copy-start | bytes 1572868
  29.4 1.0 copy-start.1
  30.4 23.4 %collective-permute-start.7 = (f32[2,256,256]{2,1,0:T(8,128)}, f32[2,256,256]{2,1,0:T(8,128)S(1)}, u32[]{:S(2)}, u32[]{:S(2)}) collective-permute-start(f32[2,256,256]{2,1,0:T(8,128)} %get-tuple-element.20), channel_id=1, source_target_pairs={{16,0},{24,8},{17,1},{25,9},{18,2},{26,10},{19,3},{27,11},{20,4},{... | collective-permute-start | bytes 1572872 | tf_op jit(solution)/shard_map/ppermute | solution.py:336
  53.8 0.8 copy-start.16
  54.6 0.9 copy-start.4
  55.6 1.0 %copy-start.6 = (bf16[4,256,256]{2,1,0:T(8,128)(2,1)S(1)}, bf16[4,256,256]{2,1,0:T(8,128)(2,1)}, u32[]{:S(2)}) copy-start(bf16[4,256,256]{2,1,0:T(8,128)(2,1)} %constant.103.clone.tab_ref) | copy-start | bytes 1572868
  56.6 1.0 %copy-start.9 = (bf16[2,2,256,256]{3,2,1,0:T(8,128)(2,1)S(1)}, bf16[2,2,256,256]{3,2,1,0:T(8,128)(2,1)}, u32[]{:S(2)}) copy-start(bf16[2,2,256,256]{3,2,1,0:T(8,128)(2,1)} %copy-done.7) | copy-start | bytes 1572868
  57.6 1.0 %copy-start.12 = (bf16[2,2,256,256]{3,2,1,0:T(8,128)(2,1)S(1)}, bf16[2,2,256,256]{3,2,1,0:T(8,128)(2,1)}, u32[]{:S(2)}) copy-start(bf16[2,2,256,256]{3,2,1,0:T(8,128)(2,1)} %copy-done.10) | copy-start | bytes 1572868
  58.7 1.0 %copy-start.15 = (bf16[2,2,256,256]{3,2,1,0:T(8,128)(2,1)S(1)}, bf16[2,2,256,256]{3,2,1,0:T(8,128)(2,1)}, u32[]{:S(2)}) copy-start(bf16[2,2,256,256]{3,2,1,0:T(8,128)(2,1)} %copy-done.13) | copy-start | bytes 1572868
  59.7 1.0 %copy-start.17 = (f32[2,256,256]{2,1,0:T(8,128)S(1)}, f32[2,256,256]{2,1,0:T(8,128)}, u32[]{:S(2)}) copy-start(f32[2,256,256]{2,1,0:T(8,128)} %copy-done.16) | copy-start | bytes 1572868
  68.0 3.3 %collective-permute-start.8 = (f32[2,2,256,256]{3,2,1,0:T(8,128)}, f32[2,2,256,256]{3,2,1,0:T(8,128)S(1)}, u32[]{:S(2)}, u32[]{:S(2)}) collective-permute-start(f32[2,2,256,256]{3,2,1,0:T(8,128)} %get-tuple-element.24), channel_id=1, source_target_pairs={{0,8},{8,0},{16,24},{24,16},{1,9},{9,1},{17,25},{25,17},{2,10},{10... | collective-permute-start | bytes 3145736 | tf_op jit(solution)/shard_map/ppermute | solution.py:338
  73.9 26.6 %collective-permute-start.9 = (f32[2,2,256,128]{3,2,1,0:T(8,128)S(1)}, f32[2,2,256,128]{3,2,1,0:T(8,128)S(1)}, u32[]{:S(2)}, u32[]{:S(2)}) collective-permute-start(f32[2,2,256,128]{3,2,1,0:T(8,128)S(1)} %get-tuple-element.26), channel_id=1, source_target_pairs={{0,1},{1,0},{2,3},{3,2},{4,5},{5,4},{6,7},{7,6},{8,9},{9,8},{10,11... | collective-permute-start | bytes 1572872 | tf_op jit(solution)/shard_map/ppermute | solution.py:280
  75.5 24.9 %collective-permute-start.10 = (f32[2,2,128,256]{3,2,1,0:T(8,128)S(1)}, f32[2,2,128,256]{3,2,1,0:T(8,128)S(1)}, u32[]{:S(2)}, u32[]{:S(2)}) collective-permute-start(f32[2,2,128,256]{3,2,1,0:T(8,128)S(1)} %get-tuple-element.27), channel_id=1, source_target_pairs={{0,2},{1,3},{2,0},{3,1},{4,6},{5,7},{6,4},{7,5},{8,10},{9,11},{10,... | collective-permute-start | bytes 1572872 | tf_op jit(solution)/shard_map/ppermute | solution.py:280
  75.9 24.5 %collective-permute-start.12 = (f32[2,2,128,256]{3,2,1,0:T(8,128)S(1)}, f32[2,2,128,256]{3,2,1,0:T(8,128)S(1)}, u32[]{:S(2)}, u32[]{:S(2)}) collective-permute-start(f32[2,2,128,256]{3,2,1,0:T(8,128)S(1)} %get-tuple-element.29), channel_id=1, source_target_pairs={{2,4},{3,5},{4,2},{5,3},{10,12},{11,13},{12,10},{13,11},{18,20},{1... | collective-permute-start | bytes 1572872 | tf_op jit(solution)/shard_map/ppermute | solution.py:280
  78.3 20.7 %collective-permute-start.11 = (f32[2,2,128,128]{3,2,1,0:T(8,128)S(1)}, f32[2,2,128,128]{3,2,1,0:T(8,128)S(1)}, u32[]{:S(2)}, u32[]{:S(2)}) collective-permute-start(f32[2,2,128,128]{3,2,1,0:T(8,128)S(1)} %get-tuple-element.28), channel_id=1, source_target_pairs={{0,3},{1,2},{2,1},{3,0},{4,7},{5,6},{6,5},{7,4},{8,11},{9,10},{10,... | collective-permute-start | bytes 786440 | tf_op jit(solution)/shard_map/ppermute | solution.py:280
  78.4 22.1 %collective-permute-start.13 = (f32[2,2,128,128]{3,2,1,0:T(8,128)S(1)}, f32[2,2,128,128]{3,2,1,0:T(8,128)S(1)}, u32[]{:S(2)}, u32[]{:S(2)}) collective-permute-start(f32[2,2,128,128]{3,2,1,0:T(8,128)S(1)} %get-tuple-element.30), channel_id=1, source_target_pairs={{2,5},{3,4},{4,3},{5,2},{10,13},{11,12},{12,11},{13,10},{18,21},{1... | collective-permute-start | bytes 786440 | tf_op jit(solution)/shard_map/ppermute | solution.py:280

commit v2 on v1

v2 whole, which is shorter than its diff:
```python
import functools
import math

import jax
import jax.numpy as jnp
import numpy as np
from jax import lax
from jax.experimental import pallas as pl
from jax.experimental.pallas import tpu as pltpu
from jax.sharding import PartitionSpec as P

VMEM = pl.BlockSpec(memory_space=pltpu.VMEM)
SMEM = pl.BlockSpec(memory_space=pltpu.SMEM)
ANY = pl.BlockSpec(memory_space=pl.ANY)
LIMIT = 16 * 1024 * 1024
LEVELS = 32767.0
SCALE_ROWS = 8


def swap_pairs(size, parity):
    pairs = []
    for i in range(parity, size - 1, 2):
        pairs += [(i, i + 1), (i + 1, i)]
    return pairs


def swap_list(n_x, n_y, swap_x, swap_y):
    xs = [(i, i) for i in range(n_x)] if swap_x is None else swap_pairs(n_x, swap_x)
    ys = [(i, i) for i in range(n_y)] if swap_y is None else swap_pairs(n_y, swap_y)
    return [(a * n_y + b, c * n_y + d) for a, c in xs for b, d in ys]


def swap_kinds(n_x, n_y):
    kinds = []
    for swap_x in (None, 0, 1):
        for swap_y in (None, 0, 1):
            if (swap_x, swap_y) != (None, None) and swap_list(n_x, n_y, swap_x, swap_y):
                kinds.append((swap_x, swap_y))
    return kinds


def split(value):
    high = value.astype(jnp.bfloat16)
    return high, (value - high.astype(jnp.float32)).astype(jnp.bfloat16)


def dft_basis(size):
    half = size // 2
    n = np.arange(size)
    j = np.arange(half)
    cos = np.cos(2 * np.pi * (j[:, None] * n[None, :] % size) / size)
    sin = np.sin(2 * np.pi * (j[:, None] * n[None, :] % size) / size)
    sin[0] = np.where(n % 2 == 0, 1.0, -1.0)
    return np.concatenate([cos, sin]) / math.sqrt(size)


def folded_order(array, axis):
    half = array.shape[axis] // 2
    low = lax.slice_in_dim(array, 0, half, axis=axis)
    mid = lax.slice_in_dim(array, half, half + 1, axis=axis)
    high = lax.rev(lax.slice_in_dim(array, half + 1, 2 * half, axis=axis), (axis,))
    return jnp.concatenate([low, mid, high], axis=axis)


def spectrum_split(p, q, first):
    (pr, pi), (qr, qi) = p, q
    plus = (jnp.where(first, pr, pr + qi), jnp.where(first, pi, pi - qr))
    minus = (jnp.where(first, qr, pr - qi), jnp.where(first, qi, pi + qr))
    return plus, minus


def spectrum_join(plus, minus, first):
    (xr, xi), (yr, yi) = plus, minus
    p = (jnp.where(first, xr, xr + yr), jnp.where(first, xi, xi + yi))
    q = (jnp.where(first, yr, yi - xi), jnp.where(first, yi, xr - yr))
    return p, q


def dot(a, b):
    return jnp.dot(a, b, preferred_element_type=jnp.float32)


def left3(table, field):
    high, low = split(field)
    return dot(table[0], high) + (dot(table[0], low) + dot(table[1], high))


def right3(field, table):
    high, low = split(field)
    return dot(high, table[0]) + (dot(low, table[0]) + dot(high, table[1]))


def propagate(wave_ref, cos_ref, sin_ref, tab_ref):
    size = wave_ref.shape[1]
    half = size // 2
    table = (tab_ref[0], tab_ref[1])
    turned = (tab_ref[2], tab_ref[3])
    parts = []
    for c in range(2):
        parts.append(right3(left3(table, wave_ref[c]), turned))
    row0 = lax.broadcasted_iota(jnp.int32, (half, half), 0) == 0
    col0 = lax.broadcasted_iota(jnp.int32, (half, half), 1) == 0

    def quadrant(r, c):
        return tuple(part[r * half : (r + 1) * half, c * half : (c + 1) * half] for part in parts)

    top = spectrum_split(quadrant(0, 0), quadrant(0, 1), col0)
    bottom = spectrum_split(quadrant(1, 0), quadrant(1, 1), col0)
    out = [[None, None], [None, None]]
    for c in range(2):
        turned_halves = []
        for r, (re, im) in enumerate(spectrum_split(top[c], bottom[c], row0)):
            where = (slice(r * half, (r + 1) * half), slice(c * half, (c + 1) * half))
            cos, sin = cos_ref[where], sin_ref[where]
            turned_halves.append((re * cos + im * sin, im * cos - re * sin))
        out[0][c], out[1][c] = spectrum_join(turned_halves[0], turned_halves[1], row0)
    rows = [spectrum_join(out[r][0], out[r][1], col0) for r in range(2)]
    for c in range(2):
        field = jnp.concatenate(
            [jnp.concatenate([rows[r][0][c], rows[r][1][c]], axis=1) for r in range(2)], axis=0
        )
        wave_ref[c] = left3(turned, right3(field, table))


def take_window(ext_ref, at_x, at_y, patch):
    step = 8
    inside = lax.rem(at_x, step)
    first = pl.multiple_of(at_x - inside, step)
    rows = ext_ref[pl.ds(first, patch + step), :]
    count, width = rows.shape
    rows = pltpu.roll(rows, lax.rem(width - at_y, width), 1)[:, :patch]
    return pltpu.roll(rows, lax.rem(count - inside, count), 0)[:patch]


def add_window(ext_ref, at_x, at_y, value):
    step = 8
    inside = lax.rem(at_x, step)
    first = pl.multiple_of(at_x - inside, step)
    value = jnp.concatenate([value, jnp.zeros((step, value.shape[1]), value.dtype)], axis=0)
    value = pltpu.roll(value, inside, 0)
    value = jnp.concatenate([value, jnp.zeros_like(value)], axis=1)
    ext_ref[pl.ds(first, value.shape[0]), :] += pltpu.roll(value, at_y, 1)


def two_powers(exponent):
    first = jnp.floor(exponent * 0.5)
    return jnp.exp2(first), jnp.exp2(exponent - first)


def encode(real, imag):
    top = jnp.maximum(jnp.abs(real), jnp.abs(imag))
    top = jnp.max(jnp.max(top, axis=0, keepdims=True), axis=1, keepdims=True)
    exponent = jnp.where(top > 0, jnp.ceil(jnp.log2(jnp.maximum(top, 1e-37))), 0.0)
    scale, rest = two_powers(-exponent)

    def code(value):
        root = jnp.sqrt(jnp.sqrt(jnp.minimum(jnp.abs(value) * scale * rest, 1.0)))
        whole = jnp.round(root * LEVELS).astype(jnp.int32)
        return jnp.where(value < 0, -whole, whole)

    return (code(real) << 16) | (code(imag) & 0xFFFF), exponent.astype(jnp.int32)


def decode(packed, exponent):
    scale, rest = two_powers(exponent.astype(jnp.float32))

    def value(whole):
        root = whole.astype(jnp.float32) * (1.0 / LEVELS)
        square = root * root
        size = square * square * scale * rest
        return jnp.where(whole < 0, -size, size)

    return value(packed >> 16), value((packed << 16) >> 16)


def put_encoded(ref, at, real, imag):
    packed, exponent = encode(real, imag)
    rows, cols = packed.shape
    ref[at + (slice(0, rows), slice(None))] = packed
    ref[at + (slice(rows, rows + SCALE_ROWS), slice(None))] = jnp.broadcast_to(exponent, (SCALE_ROWS, cols))


def get_encoded(ref, at):
    rows = ref.shape[-2] - SCALE_ROWS
    packed = ref[at + (slice(0, rows), slice(None))]
    return decode(packed, ref[at + (slice(rows, rows + 1), slice(None))])


def halo_start(kind, half, tile):
    start = []
    for swap, axis in zip(kind, ("sx", "sy")):
        if swap is None:
            start.append(half)
        else:
            above = lax.rem(lax.axis_index(axis) + swap, 2) == 0
            start.append(pl.multiple_of(jnp.where(above, half + tile, 0), half))
    return start


def rim_start(kind, half, tile):
    start = []
    for swap, axis in zip(kind, ("sx", "sy")):
        if swap is None:
            start.append(0)
        else:
            above = lax.rem(lax.axis_index(axis) + swap, 2) == 0
            start.append(pl.multiple_of(jnp.where(above, tile - half, 0), half))
    return start


def corner_of(anchor_ref, slot, half, tile):
    at_x = anchor_ref[slot, 0] - lax.axis_index("sx") * tile + half
    at_y = anchor_ref[slot, 1] - lax.axis_index("sy") * tile + half
    return at_x, at_y


def core_index():
    return lax.rem(lax.axis_index("depth"), 2)


def rims_kernel(kinds, own_ref, *pieces):
    tile = own_ref.shape[2]
    for kind, piece in zip(kinds, pieces):
        row, col = rim_start(kind, tile // 2, tile)
        rows, cols = piece.shape[2:]
        piece[...] = own_ref[:, :, pl.ds(row, rows), pl.ds(col, cols)]


def window_kernel(kinds, anchor_ref, own_ref, *refs):
    pieces, (mine_ref, other_ref, ext_ref) = refs[: len(kinds)], refs[len(kinds) :]
    slab, _, tile, _ = own_ref.shape
    half = tile // 2
    patch = mine_ref.shape[2]
    core = core_index()
    corners = [corner_of(anchor_ref, slot, half, tile) for slot in (core, 1 - core)]
    ext_ref[...] = jnp.zeros_like(ext_ref)
    for layer in range(slab):
        for c in range(2):
            ext_ref[half : half + tile, half : half + tile] = own_ref[layer, c].astype(jnp.float32)
            for kind, piece in zip(kinds, pieces):
                row, col = halo_start(kind, half, tile)
                rows, cols = piece.shape[2:]
                ext_ref[pl.ds(row, rows), pl.ds(col, cols)] = piece[layer, c].astype(jnp.float32)
            for (at_x, at_y), out in zip(corners, (mine_ref, other_ref)):
                out[layer, c] = take_window(ext_ref, at_x, at_y, patch).astype(out.dtype)


def stage_kernel(stage, live_ref, wave_in, win_own, win_got, inc_own, inc_got, cos_ref, sin_ref, tab_ref,
                 _keep_in, _send_in, keep_ref, send_ref, out_ref, wave_ref, term, sems):
    slab = win_own.shape[0]
    layers = 2 * slab
    core = core_index()
    chip = lax.axis_index("depth") // 2
    chips = lax.axis_size("depth") // 2

    def leave(slot, ref, local):
        return pltpu.make_async_copy(term.at[slot], ref.at[local], sems.at[slot])

    @pl.when(chip == chips - 1 - stage)
    def _():
        if stage == 0:
            live = (core < live_ref[0]).astype(jnp.float32)
            wave_ref[...] = wave_in[core].astype(jnp.float32) * live
        else:
            wave_ref[0], wave_ref[1] = get_encoded(wave_in, ())

        def one(step, _):
            i = layers - 1 - step
            owner = i // slab
            local = lax.rem(i, slab)
            slot = lax.rem(step, 2)
            own = owner == core

            @pl.when(step >= 2)
            def _():
                leave(slot, keep_ref, 0).wait()

            wr, wi = wave_ref[0], wave_ref[1]
            er = jnp.where(own, inc_own[local, core, 0], inc_got[local, core, 0]).astype(jnp.float32)
            ei = jnp.where(own, inc_own[local, core, 1], inc_got[local, core, 1]).astype(jnp.float32)
            term[slot, 0] = er * wr + ei * wi
            term[slot, 1] = er * wi - ei * wr

            @pl.when(own)
            def _():
                leave(slot, keep_ref, local).start()

            @pl.when(jnp.logical_not(own))
            def _():
                leave(slot, send_ref, local).start()

            @pl.when(chip * layers + i > 0)
            def _():
                tr = jnp.where(own, win_own[local, 0], win_got[local, 0]).astype(jnp.float32)
                ti = jnp.where(own, win_own[local, 1], win_got[local, 1]).astype(jnp.float32)
                wave_ref[0] = tr * wr + ti * wi
                wave_ref[1] = tr * wi - ti * wr
                propagate(wave_ref, cos_ref, sin_ref, tab_ref)

            return 0

        lax.fori_loop(0, layers, one, 0)
        if stage < chips - 1:
            put_encoded(out_ref, (), wave_ref[0], wave_ref[1])
        for slot in range(2):
            leave(slot, keep_ref, 0).wait()


def scatter_kernel(kinds, anchor_ref, mine_ref, other_ref, own_ref, *refs):
    pieces, ext_ref = refs[:-1], refs[-1]
    slab, _, patch, _ = mine_ref.shape
    tile = own_ref.shape[2]
    half = tile // 2
    core = core_index()
    corners = [corner_of(anchor_ref, slot, half, tile) for slot in (core, 1 - core)]
    for layer in range(slab):
        ext_ref[...] = jnp.zeros_like(ext_ref)
        for c in range(2):
            for (at_x, at_y), term in zip(corners, (mine_ref, other_ref)):
                add_window(ext_ref.at[c], at_x, at_y, term[layer, c])
            own_ref[layer, c] = ext_ref[c, half : half + tile, half : half + tile]
        for kind, piece in zip(kinds, pieces):
            row, col = halo_start(kind, half, tile)
            where = (pl.ds(row, piece.shape[1] - SCALE_ROWS), pl.ds(col, piece.shape[2]))
            put_encoded(piece, (layer,), ext_ref[(0,) + where], ext_ref[(1,) + where])


def fold_kernel(kinds, own_ref, *refs):
    pieces, out_ref = refs[:-1], refs[-1]
    slab, _, tile, _ = own_ref.shape
    out_ref[...] = own_ref[...]
    for layer in range(slab):
        for kind, piece in zip(kinds, pieces):
            row, col = rim_start(kind, tile // 2, tile)
            where = (pl.ds(row, piece.shape[1] - SCALE_ROWS), pl.ds(col, piece.shape[2]))
            for c, value in enumerate(get_encoded(piece, (layer,))):
                out_ref[(layer, c) + where] += value


def shards(transmission, incident, exit_adjoint, propagator_phase, scan_anchor, live_count):
    f32 = jnp.float32
    n_depth, n_x, n_y = lax.axis_size("depth"), lax.axis_size("sx"), lax.axis_size("sy")
    slab, _, tile, _ = transmission.shape
    patch = propagator_phase.shape[0]
    half = tile // 2
    extent = tile + patch
    chips = n_depth // 2
    kinds = swap_kinds(n_x, n_y)
    params = pltpu.CompilerParams(vmem_limit_bytes=LIMIT)
    core_swap = swap_pairs(n_depth, 0)

    def call(kernel, out_shape, operands, name, scratch=(), **more):
        return pl.pallas_call(
            kernel,
            out_shape=out_shape,
            scratch_shapes=list(scratch),
            compiler_params=params,
            name=name,
            **{"in_specs": [VMEM] * len(operands), "out_specs": jax.tree.map(lambda _: VMEM, out_shape), **more},
        )(*operands)

    def rim_size(kind):
        return tile if kind[0] is None else half, tile if kind[1] is None else half

    def swapped(value, kind):
        return lax.ppermute(value, ("sx", "sy"), swap_list(n_x, n_y, *kind))

    rims = call(
        functools.partial(rims_kernel, kinds),
        tuple(jax.ShapeDtypeStruct((slab, 2) + rim_size(kind), transmission.dtype) for kind in kinds),
        (transmission,),
        "rims",
    )
    halos = [swapped(value, kind) for value, kind in zip(rims, kinds)]
    inc_got = lax.ppermute(incident, "depth", core_swap)

    phase = folded_order(folded_order(propagator_phase, 0), 1)
    phase_cos, phase_sin = jnp.cos(phase), jnp.sin(phase)
    basis = dft_basis(patch)
    high = basis.astype(jnp.bfloat16)
    low = (basis - high.astype(np.float64)).astype(jnp.bfloat16)
    tables = jnp.asarray(np.stack([high, low, high.T, low.T]))
    phase_cos, phase_sin, halos = lax.optimization_barrier((phase_cos, phase_sin, halos))

    window_shape = jax.ShapeDtypeStruct((slab, 2, patch, patch), transmission.dtype)
    win_own, win_send = call(
        functools.partial(window_kernel, kinds),
        (window_shape, window_shape),
        (scan_anchor, transmission, *halos),
        "windows",
        [pltpu.VMEM((extent, extent), f32)],
        in_specs=[SMEM] + [VMEM] * (1 + len(kinds)),
    )
    win_got = lax.ppermute(win_send, "depth", core_swap)

    wave = exit_adjoint
    term_shape = jax.ShapeDtypeStruct((slab, 2, patch, patch), f32)
    coded = jax.ShapeDtypeStruct((patch + SCALE_ROWS, patch), jnp.int32)
    keep = jnp.zeros(term_shape.shape, f32)
    send = jnp.zeros(term_shape.shape, f32)
    for stage in range(chips):
        keep, send, wave = call(
            functools.partial(stage_kernel, stage),
            (term_shape, term_shape, coded),
            (live_count, wave, win_own, win_got, incident, inc_got, phase_cos, phase_sin, tables, keep, send),
            "sweep",
            [
                pltpu.VMEM((2, patch, patch), f32),
                pltpu.VMEM((2, 2, patch, patch), f32),
                pltpu.SemaphoreType.DMA((2,)),
            ],
            in_specs=[SMEM] + [VMEM] * 8 + [ANY, ANY],
            out_specs=(ANY, ANY, VMEM),
            input_output_aliases={9: 0, 10: 1},
        )
        if stage < chips - 1:
            source = chips - 1 - stage
            wave = lax.ppermute(wave, "depth", [(2 * source + c, 2 * source - 2 + c) for c in range(2)])

    got = lax.ppermute(send, "depth", core_swap)
    own_shape = jax.ShapeDtypeStruct((slab, 2, tile, tile), f32)
    coded_rims = tuple(
        jax.ShapeDtypeStruct((slab, rim_size(kind)[0] + SCALE_ROWS, rim_size(kind)[1]), jnp.int32)
        for kind in kinds
    )
    own, *beyond = call(
        functools.partial(scatter_kernel, kinds),
        (own_shape,) + coded_rims,
        (scan_anchor, keep, got),
        "scatter",
        [pltpu.VMEM((2, extent, extent), f32)],
        in_specs=[SMEM, VMEM, VMEM],
    )
    arrived = [swapped(value, kind) for value, kind in zip(beyond, kinds)]
    return call(functools.partial(fold_kernel, kinds), own_shape, (own, *arrived), "fold")


def solution(mesh):
    placed = (
        P("depth", None, "sx", "sy"),
        P("depth", ("sx", "sy"), None, None, None),
        P(("sx", "sy"), None, None, None),
        P(),
        P(("sx", "sy"), None),
        P(("sx", "sy")),
    )
    return jax.shard_map(
        shards, mesh=mesh, in_specs=placed, out_specs=P("depth", None, "sx", "sy"), check_vma=False
    )
```

time: 103 us -> 78 us (0.76)
  local copies, waits for them, and re-layouts: 21.4 us -> 4.35 us
  waiting for transfers between devices: 44.5 us -> 34.5 us
    unnamed x40 -> x14, local copies, waits for them, and re-layouts: 12.3 us -> 3.07 us
    ppermute x10, waiting for transfers between devices: 19.9 us -> 13.8 us  [swapped(): return lax.ppermute(value, ('sx', 'sy'), swap_list(n_x, n_y, *kind))]
    ppermute x2, waiting for transfers between devices: 22.1 us -> 16.8 us  [the longest x1 16.8 us: shards(): lax.ppermute(wave, 'depth', [(2 * source + c, 2 * source - 2 + c) for c i...]
    dynamic_slice x4 -> x0, local copies, waits for them, and re-layouts: 3.49 us -> none  [the longest x2 2.67 us: shards(): value = lax.dynamic_slice_in_dim(value, rim[2 + kind[1]], half, 3)]
    another operation x3 -> x2, local copies, waits for them, and re-layouts: 2.62 us -> 0.15 us  [the longest x1 2.47 us: shards(): jnp.stack(halo + [corner_mine[0], corner_mine[1], corner_other[0], corner...]
    squeeze x2 -> x0, local copies, waits for them, and re-layouts: 2.13 us -> none  [the longest x1 2.1 us: shards(): inc_send = lax.dynamic_slice_in_dim(incident, 1 - core, 1, 1)[:, 0]]
    ppermute x10, starting transfers between devices: 15.4 us -> 16.9 us  [swapped(): return lax.ppermute(value, ('sx', 'sy'), swap_list(n_x, n_y, *kind))]
    ppermute x1, waiting for transfers between devices: 0.01 us -> 1.25 us  [shards(): win_got = lax.ppermute(win_send, 'depth', core_swap)]
  transfers between devices with their start and end apart: 14 -> 14, of which waited for: 5 -> 8; matrix products, arithmetic and copies ran while one was open for 8% -> 4% of each run, Pallas kernels for 3% -> 4%
where the time goes in v2:
time: 78 us; the launch traced here: 76.5 us
  waiting for transfers between devices  34.5 us (44%)
  starting transfers between devices  18.3 us (23%)
  Pallas kernels  16.6 us (21%)
  local copies, waits for them, and re-layouts  4.35 us (6%)
  other arithmetic  1.9 us (2%)
  between operations  0.87 us (1%)
    ppermute x10, starting transfers between devices, swapped(): return lax.ppermute(value, ('sx', 'sy'), swap_list(n_x, n_y, *kind))  16.9 us
    ppermute x1, waiting for transfers between devices, shards(): lax.ppermute(wave, 'depth', [(2 * source + c, 2 * source - 2 + c) for c i...  16.8 us
    pallas_call x6, Pallas kernels, call(): pl.pallas_call(kernel, out_shape=out_shape, scratch_shapes=list(scratch),...  16.6 us
    ppermute x10, waiting for transfers between devices, swapped(): return lax.ppermute(value, ('sx', 'sy'), swap_list(n_x, n_y, *kind))  13.8 us
    unnamed x14, local copies, waits for them, and re-layouts  3.07 us
    ppermute x1, waiting for transfers between devices, shards(): got = lax.ppermute(send, 'depth', core_swap)  2.65 us
  transfers between devices with their start and end apart: 14, of which 8 were waited for; matrix products, arithmetic and copies ran while one was open for 4% of the time, Pallas kernels for 4%

profile of v2, /device:TPU:16, one launch (start us, length us, event | category | flops | bytes accessed | tf_op | source)
XLA Modules:
  0.0 76.5 jit_solution(17645991136991199774)
XLA Ops:
  0.0 0.0 collective-permute-start.6
  0.0 1.0 %copy-done.1 = bf16[2,2,256,256]{3,2,1,0:T(8,128)(2,1)S(1)} copy-done((bf16[2,2,256,256]{3,2,1,0:T(8,128)(2,1)S(1)}, bf16[2,2,256,256]{3,2,1,0:T(8,128)(2,1)}, u32[]{:S(2)}) %copy-start.1) | copy-done | bytes 524312
  1.0 0.1 rims.1
  1.2 2.6 %collective-permute-start.2 = (bf16[2,2,128,128]{3,2,1,0:T(8,128)(2,1)S(1)}, bf16[2,2,128,128]{3,2,1,0:T(8,128)(2,1)S(1)}, u32[]{:S(2)}, u32[]{:S(2)}) collective-permute-start(bf16[2,2,128,128]{3,2,1,0:T(8,128)(2,1)S(1)} %get-tuple-element.32), channel_id=1, source_target_pairs={{0,3},{1,2},{2,1},{3,0},{4,7},{5,6},{6,5},{7,4},{8,11},{9,10},{10,... | collective-permute-start | bytes 393224 | tf_op jit(solution)/shard_map/ppermute | solution.py:366
  3.8 0.5 collective-permute-start
  4.3 0.4 collective-permute-start.1
  4.7 2.3 %collective-permute-start.3 = (bf16[2,2,128,256]{3,2,1,0:T(8,128)(2,1)S(1)}, bf16[2,2,128,256]{3,2,1,0:T(8,128)(2,1)S(1)}, u32[]{:S(2)}, u32[]{:S(2)}) collective-permute-start(bf16[2,2,128,256]{3,2,1,0:T(8,128)(2,1)S(1)} %get-tuple-element.33), channel_id=1, source_target_pairs={{2,4},{3,5},{4,2},{5,3},{10,12},{11,13},{12,10},{13,11},{18,20},{1... | collective-permute-start | bytes 786440 | tf_op jit(solution)/shard_map/ppermute | solution.py:366
  7.1 0.1 rev.6
  7.3 1.0 %collective-permute-done.2.refs_2_ = bf16[2,2,128,128]{3,2,1,0:T(8,128)(2,1)S(1)} collective-permute-done((bf16[2,2,128,128]{3,2,1,0:T(8,128)(2,1)S(1)}, bf16[2,2,128,128]{3,2,1,0:T(8,128)(2,1)S(1)}, u32[]{:S(2)}, u32[]{:S(2)}) %collective-permute-start.2) | collective-permute-done | bytes 131104 | tf_op jit(solution)/shard_map/ppermute | solution.py:366
  8.3 3.5 %collective-permute-start.4 = (bf16[2,2,128,128]{3,2,1,0:T(8,128)(2,1)S(1)}, bf16[2,2,128,128]{3,2,1,0:T(8,128)(2,1)S(1)}, u32[]{:S(2)}, u32[]{:S(2)}) collective-permute-start(bf16[2,2,128,128]{3,2,1,0:T(8,128)(2,1)S(1)} %get-tuple-element.34), channel_id=1, source_target_pairs={{2,5},{3,4},{4,3},{5,2},{10,13},{11,12},{12,11},{13,10},{18,21},{1... | collective-permute-start | bytes 393224 | tf_op jit(solution)/shard_map/ppermute | solution.py:366
  11.8 0.8 pad_maximum_fusion.1
  12.6 1.0 %rev.7 = f32[256,127]{1,0:T(8,128)S(1)} reverse(f32[256,127]{1,0:T(8,128)} %pad_maximum_fusion.1), dimensions={1} | reverse | bytes 260096 | tf_op jit(solution)/shard_map/rev | solution.py:61
  13.6 0.0 copy-start.2
  13.6 1.1 %fusion = (f32[256,256]{1,0:T(8,128)S(1)}, f32[256,256]{1,0:T(8,128)S(1)}) fusion(f32[256,127]{1,0:T(8,128)S(1)} %rev.7, f32[256,129]{1,0:T(8,128)S(1)} %slice_maximum_fusion), kind=kLoop, calls=%fused_computation.2 | loop fusion | flops 65536 | bytes 786432 | tf_op jit(solution)/shard_map/sin | solution.py:378
  14.7 3.6 %collective-permute-done.4.refs_4_ = bf16[2,2,128,128]{3,2,1,0:T(8,128)(2,1)S(1)} collective-permute-done((bf16[2,2,128,128]{3,2,1,0:T(8,128)(2,1)S(1)}, bf16[2,2,128,128]{3,2,1,0:T(8,128)(2,1)S(1)}, u32[]{:S(2)}, u32[]{:S(2)}) %collective-permute-start.4) | collective-permute-done | bytes 131104 | tf_op jit(solution)/shard_map/ppermute | solution.py:366
  18.3 0.0 collective-permute-done.refs_0_
  18.3 0.0 collective-permute-done.1.refs_1_
  18.3 0.0 collective-permute-done.3.refs_3_
  18.3 0.0 copy-start.5
  18.3 0.7 copy-done.5
  19.0 2.8 %windows.1 = (bf16[2,2,256,256]{3,2,1,0:T(8,128)(2,1)S(1)}, bf16[2,2,256,256]{3,2,1,0:T(8,128)(2,1)S(1)}) custom-call(s32[2,2]{1,0:T(2,128)S(1)} %copy-done.5, bf16[2,2,256,256]{3,2,1,0:T(8,128)(2,1)S(1)} %copy-done.2, bf16[2,2,256,128]{3,2,1,0:T(8,128)(2,1)S(1)} %collective-permute-done.refs_0_, ...), custom_call_target="tpu_custom_call" | custom-call | tf_op jit(solution)/shard_map/windows/pallas_call | solution.py:353
  21.7 0.1 collective-permute-start.5
  22.4 1.2 %collective-permute-done.5.win_got = bf16[2,2,256,256]{3,2,1,0:T(8,128)(2,1)S(1)} collective-permute-done((bf16[2,2,256,256]{3,2,1,0:T(8,128)(2,1)S(1)}, bf16[2,2,256,256]{3,2,1,0:T(8,128)(2,1)S(1)}, u32[]{:S(2)}, u32[]{:S(2)}) %collective-permute-start.5) | collective-permute-done | bytes 524320 | tf_op jit(solution)/shard_map/ppermute | solution.py:394
  23.7 0.0 collective-permute-done.6.inc_got
  23.7 0.1 broadcast_1__keep_in__send_in.2.clone._send_in
  23.8 0.0 copy-start.3
  23.8 0.0 copy-start.4
  23.8 0.1 broadcast_1__keep_in__send_in.2._keep_in
  23.9 1.0 %copy-done = bf16[2,2,2,256,256]{4,3,2,1,0:T(8,128)(2,1)S(1)} copy-done((bf16[2,2,2,256,256]{4,3,2,1,0:T(8,128)(2,1)S(1)}, bf16[2,2,2,256,256]{4,3,2,1,0:T(8,128)(2,1)}, u32[]{:S(2)}) %copy-start) | copy-done | bytes 1048600
  24.9 0.1 copy-done.3
  25.1 0.2 copy-done.4
  25.3 1.3 %collective-permute-start.7 = (s32[264,256]{1,0:T(8,128)S(1)}, s32[264,256]{1,0:T(8,128)S(1)}, u32[]{:S(2)}, u32[]{:S(2)}) collective-permute-start(s32[264,256]{1,0:T(8,128)S(1)} %get-tuple-element.44), channel_id=1, source_target_pairs={{16,0},{24,8},{17,1},{25,9},{18,2},{26,10},{19,3},{27,11},{20,4},{... | collective-permute-start | bytes 811016 | tf_op jit(solution)/shard_map/ppermute | solution.py:418
  26.6 16.8 %collective-permute-done.7.wave_in = s32[264,256]{1,0:T(8,128)S(1)} collective-permute-done((s32[264,256]{1,0:T(8,128)S(1)}, s32[264,256]{1,0:T(8,128)S(1)}, u32[]{:S(2)}, u32[]{:S(2)}) %collective-permute-start.7) | collective-permute-done | bytes 270368 | tf_op jit(solution)/shard_map/ppermute | solution.py:418
  43.3 7.1 %sweep.3 = (f32[2,2,256,256]{3,2,1,0:T(8,128)S(1)}, f32[2,2,256,256]{3,2,1,0:T(8,128)S(1)}, s32[264,256]{1,0:T(8,128)}) custom-call(s32[1]{0:T(128)S(6)} %copy.16.live_ref, s32[264,256]{1,0:T(8,128)S(1)} %collective-permute-done.7.wave_in, bf16[2,2,256,256]{3,2,1,0:T(8,128)(2,1)S(1)} %get-tuple-element.40.win_own, ...), custom_call_target="tpu_custom_call", output_to_operand_aliasing={{0}: (9, {}), {1}: (10, {})} | custom-call | tf_op jit(solution)/shard_map/sweep/pallas_call | solution.py:353
  50.5 0.1 collective-permute-start.8
  50.6 2.6 %collective-permute-done.8.other_ref = f32[2,2,256,256]{3,2,1,0:T(8,128)S(1)} collective-permute-done((f32[2,2,256,256]{3,2,1,0:T(8,128)S(1)}, f32[2,2,256,256]{3,2,1,0:T(8,128)S(1)}, u32[]{:S(2)}, u32[]{:S(2)}) %collective-permute-start.8) | collective-permute-done | bytes 1048608 | tf_op jit(solution)/shard_map/ppermute | solution.py:420
  53.2 4.5 %scatter.1 = (f32[2,2,256,256]{3,2,1,0:T(8,128)S(1)}, s32[2,264,128]{2,1,0:T(8,128)S(1)}, s32[2,136,256]{2,1,0:T(8,128)S(1)}, s32[2,136,128]{2,1,0:T(8,128)S(1)}...) custom-call(s32[2,2]{1,0:T(2,128)S(1)} %copy-done.5, f32[2,2,256,256]{3,2,1,0:T(8,128)S(1)} %get-tuple-element.47.mine_ref, ...), custom_call_target="tpu_custom_call" | custom-call | tf_op jit(solution)/shard_map/scatter/pallas_call | solution.py:353
  57.7 0.1 collective-permute-start.10
  57.8 2.4 %collective-permute-start.12 = (s32[2,136,256]{2,1,0:T(8,128)S(1)}, s32[2,136,256]{2,1,0:T(8,128)S(1)}, u32[]{:S(2)}, u32[]{:S(2)}) collective-permute-start(s32[2,136,256]{2,1,0:T(8,128)S(1)} %get-tuple-element.53), channel_id=1, source_target_pairs={{2,4},{3,5},{4,2},{5,3},{10,12},{11,13},{12,10},{13,11},{18,20},{1... | collective-permute-start | bytes 835592 | tf_op jit(solution)/shard_map/ppermute | solution.py:366
  60.2 0.6 collective-permute-start.9
  60.7 1.3 %collective-permute-start.11 = (s32[2,136,128]{2,1,0:T(8,128)S(1)}, s32[2,136,128]{2,1,0:T(8,128)S(1)}, u32[]{:S(2)}, u32[]{:S(2)}) collective-permute-start(s32[2,136,128]{2,1,0:T(8,128)S(1)} %get-tuple-element.52), channel_id=1, source_target_pairs={{0,3},{1,2},{2,1},{3,0},{4,7},{5,6},{6,5},{7,4},{8,11},{9,10},{10,... | collective-permute-start | bytes 417800 | tf_op jit(solution)/shard_map/ppermute | solution.py:366
  62.0 3.2 %collective-permute-start.13 = (s32[2,136,128]{2,1,0:T(8,128)S(1)}, s32[2,136,128]{2,1,0:T(8,128)S(1)}, u32[]{:S(2)}, u32[]{:S(2)}) collective-permute-start(s32[2,136,128]{2,1,0:T(8,128)S(1)} %get-tuple-element.54), channel_id=1, source_target_pairs={{2,5},{3,4},{4,3},{5,2},{10,13},{11,12},{12,11},{13,10},{18,21},{1... | collective-permute-start | bytes 417800 | tf_op jit(solution)/shard_map/ppermute | solution.py:366
  65.2 5.8 %collective-permute-done.11.refs_2_ = s32[2,136,128]{2,1,0:T(8,128)S(1)} collective-permute-done((s32[2,136,128]{2,1,0:T(8,128)S(1)}, s32[2,136,128]{2,1,0:T(8,128)S(1)}, u32[]{:S(2)}, u32[]{:S(2)}) %collective-permute-start.11) | collective-permute-done | bytes 139296 | tf_op jit(solution)/shard_map/ppermute | solution.py:366
  71.0 1.6 %collective-permute-done.13.refs_4_ = s32[2,136,128]{2,1,0:T(8,128)S(1)} collective-permute-done((s32[2,136,128]{2,1,0:T(8,128)S(1)}, s32[2,136,128]{2,1,0:T(8,128)S(1)}, u32[]{:S(2)}, u32[]{:S(2)}) %collective-permute-start.13) | collective-permute-done | bytes 139296 | tf_op jit(solution)/shard_map/ppermute | solution.py:366
  72.5 1.9 %collective-permute-done.9.refs_0_ = s32[2,264,128]{2,1,0:T(8,128)S(1)} collective-permute-done((s32[2,264,128]{2,1,0:T(8,128)S(1)}, s32[2,264,128]{2,1,0:T(8,128)S(1)}, u32[]{:S(2)}, u32[]{:S(2)}) %collective-permute-start.9) | collective-permute-done | bytes 270368 | tf_op jit(solution)/shard_map/ppermute | solution.py:366
  74.4 0.0 collective-permute-done.10.refs_1_
  74.5 0.0 collective-permute-done.12.refs_3_
  74.5 2.1 %fold.1 = f32[2,2,256,256]{3,2,1,0:T(8,128)} custom-call(f32[2,2,256,256]{3,2,1,0:T(8,128)S(1)} %get-tuple-element.49.own_ref, s32[2,264,128]{2,1,0:T(8,128)S(1)} %collective-permute-done.9.refs_0_, s32[2,136,256]{2,1,0:T(8,128)S(1)} %collective-permute-done.10.refs_1_, s32[2,136,128]{2,1,0:T(8,128)S(1)} %collective-permute-done.11.refs_2_, ...), custom_call_target="tpu_custom_call" | custom-call | tf_op jit(solution)/shard_map/fold/pallas_call | solution.py:353
  (9 shorter events, 0.1 us)
Async XLA Ops:
  0.0 23.7 %collective-permute-start.6 = (bf16[2,2,2,256,256]{4,3,2,1,0:T(8,128)(2,1)}, bf16[2,2,2,256,256]{4,3,2,1,0:T(8,128)(2,1)S(1)}, u32[]{:S(2)}, u32[]{:S(2)}) collective-permute-start(bf16[2,2,2,256,256]{4,3,2,1,0:T(8,128)(2,1)} %inc_own.3), channel_id=1, source_target_pairs={{0,8},{8,0},{16,24},{24,16},{1,9},{9,1},{17,25},{25,17},{2,10},{10... | collective-permute-start | bytes 3145736 | tf_op jit(solution)/shard_map/ppermute | solution.py:375
  0.0 1.0 %copy-start.1 = (bf16[2,2,256,256]{3,2,1,0:T(8,128)(2,1)S(1)}, bf16[2,2,256,256]{3,2,1,0:T(8,128)(2,1)}, u32[]{:S(2)}) copy-start(bf16[2,2,256,256]{3,2,1,0:T(8,128)(2,1)} %own_ref.3) | copy-start | bytes 1572868
  1.0 6.0 %copy-start.6 = (f32[256,256]{1,0:T(8,128)S(1)}, f32[256,256]{1,0:T(8,128)}, u32[]{:S(2)}) copy-start(f32[256,256]{1,0:T(8,128)} %param.10) | copy-start | bytes 786436
  1.2 7.1 %collective-permute-start.2 = (bf16[2,2,128,128]{3,2,1,0:T(8,128)(2,1)S(1)}, bf16[2,2,128,128]{3,2,1,0:T(8,128)(2,1)S(1)}, u32[]{:S(2)}, u32[]{:S(2)}) collective-permute-start(bf16[2,2,128,128]{3,2,1,0:T(8,128)(2,1)S(1)} %get-tuple-element.32), channel_id=1, source_target_pairs={{0,3},{1,2},{2,1},{3,0},{4,7},{5,6},{6,5},{7,4},{8,11},{9,10},{10,... | collective-permute-start | bytes 393224 | tf_op jit(solution)/shard_map/ppermute | solution.py:366
  3.8 14.5 %collective-permute-start = (bf16[2,2,256,128]{3,2,1,0:T(8,128)(2,1)S(1)}, bf16[2,2,256,128]{3,2,1,0:T(8,128)(2,1)S(1)}, u32[]{:S(2)}, u32[]{:S(2)}) collective-permute-start(bf16[2,2,256,128]{3,2,1,0:T(8,128)(2,1)S(1)} %get-tuple-element.30), channel_id=1, source_target_pairs={{0,1},{1,0},{2,3},{3,2},{4,5},{5,4},{6,7},{7,6},{8,9},{9,8},{10,11... | collective-permute-start | bytes 786440 | tf_op jit(solution)/shard_map/ppermute | solution.py:366
  4.3 14.0 %collective-permute-start.1 = (bf16[2,2,128,256]{3,2,1,0:T(8,128)(2,1)S(1)}, bf16[2,2,128,256]{3,2,1,0:T(8,128)(2,1)S(1)}, u32[]{:S(2)}, u32[]{:S(2)}) collective-permute-start(bf16[2,2,128,256]{3,2,1,0:T(8,128)(2,1)S(1)} %get-tuple-element.31), channel_id=1, source_target_pairs={{0,2},{1,3},{2,0},{3,1},{4,6},{5,7},{6,4},{7,5},{8,10},{9,11},{10,... | collective-permute-start | bytes 786440 | tf_op jit(solution)/shard_map/ppermute | solution.py:366
  4.7 13.5 %collective-permute-start.3 = (bf16[2,2,128,256]{3,2,1,0:T(8,128)(2,1)S(1)}, bf16[2,2,128,256]{3,2,1,0:T(8,128)(2,1)S(1)}, u32[]{:S(2)}, u32[]{:S(2)}) collective-permute-start(bf16[2,2,128,256]{3,2,1,0:T(8,128)(2,1)S(1)} %get-tuple-element.33), channel_id=1, source_target_pairs={{2,4},{3,5},{4,2},{5,3},{10,12},{11,13},{12,10},{13,11},{18,20},{1... | collective-permute-start | bytes 786440 | tf_op jit(solution)/shard_map/ppermute | solution.py:366
  8.3 10.0 %collective-permute-start.4 = (bf16[2,2,128,128]{3,2,1,0:T(8,128)(2,1)S(1)}, bf16[2,2,128,128]{3,2,1,0:T(8,128)(2,1)S(1)}, u32[]{:S(2)}, u32[]{:S(2)}) collective-permute-start(bf16[2,2,128,128]{3,2,1,0:T(8,128)(2,1)S(1)} %get-tuple-element.34), channel_id=1, source_target_pairs={{2,5},{3,4},{4,3},{5,2},{10,13},{11,12},{12,11},{13,10},{18,21},{1... | collective-permute-start | bytes 393224 | tf_op jit(solution)/shard_map/ppermute | solution.py:366
  13.6 4.7 %copy-start.2 = (bf16[2,2,256,256]{3,2,1,0:T(8,128)(2,1)S(1)}, bf16[2,2,256,256]{3,2,1,0:T(8,128)(2,1)}, u32[]{:S(2)}) copy-start(bf16[2,2,256,256]{3,2,1,0:T(8,128)(2,1)} %own_ref.3) | copy-start | bytes 1572868
  18.3 0.7 copy-start.5
  21.7 2.0 %collective-permute-start.5 = (bf16[2,2,256,256]{3,2,1,0:T(8,128)(2,1)S(1)}, bf16[2,2,256,256]{3,2,1,0:T(8,128)(2,1)S(1)}, u32[]{:S(2)}, u32[]{:S(2)}) collective-permute-start(bf16[2,2,256,256]{3,2,1,0:T(8,128)(2,1)S(1)} %get-tuple-element.41), channel_id=1, source_target_pairs={{0,8},{8,0},{16,24},{24,16},{1,9},{9,1},{17,25},{25,17},{2,10},{10... | collective-permute-start | bytes 1572872 | tf_op jit(solution)/shard_map/ppermute | solution.py:394
  23.7 1.2 %copy-start = (bf16[2,2,2,256,256]{4,3,2,1,0:T(8,128)(2,1)S(1)}, bf16[2,2,2,256,256]{4,3,2,1,0:T(8,128)(2,1)}, u32[]{:S(2)}) copy-start(bf16[2,2,2,256,256]{4,3,2,1,0:T(8,128)(2,1)} %inc_own.3) | copy-start | bytes 3145732
  23.8 1.3 %copy-start.3 = (bf16[4,256,256]{2,1,0:T(8,128)(2,1)S(1)}, bf16[4,256,256]{2,1,0:T(8,128)(2,1)}, u32[]{:S(2)}) copy-start(bf16[4,256,256]{2,1,0:T(8,128)(2,1)} %constant.4.clone.tab_ref) | copy-start | bytes 1572868
  23.8 1.4 %copy-start.4 = (bf16[2,2,256,256]{3,2,1,0:T(8,128)(2,1)S(1)}, bf16[2,2,256,256]{3,2,1,0:T(8,128)(2,1)}, u32[]{:S(2)}) copy-start(bf16[2,2,256,256]{3,2,1,0:T(8,128)(2,1)} %wave_in.1) | copy-start | bytes 1572868
  25.3 18.1 %collective-permute-start.7 = (s32[264,256]{1,0:T(8,128)S(1)}, s32[264,256]{1,0:T(8,128)S(1)}, u32[]{:S(2)}, u32[]{:S(2)}) collective-permute-start(s32[264,256]{1,0:T(8,128)S(1)} %get-tuple-element.44), channel_id=1, source_target_pairs={{16,0},{24,8},{17,1},{25,9},{18,2},{26,10},{19,3},{27,11},{20,4},{... | collective-permute-start | bytes 811016 | tf_op jit(solution)/shard_map/ppermute | solution.py:418
  50.5 2.7 %collective-permute-start.8 = (f32[2,2,256,256]{3,2,1,0:T(8,128)S(1)}, f32[2,2,256,256]{3,2,1,0:T(8,128)S(1)}, u32[]{:S(2)}, u32[]{:S(2)}) collective-permute-start(f32[2,2,256,256]{3,2,1,0:T(8,128)S(1)} %get-tuple-element.48), channel_id=1, source_target_pairs={{0,8},{8,0},{16,24},{24,16},{1,9},{9,1},{17,25},{25,17},{2,10},{10... | collective-permute-start | bytes 3145736 | tf_op jit(solution)/shard_map/ppermute | solution.py:420
  57.7 16.7 %collective-permute-start.10 = (s32[2,136,256]{2,1,0:T(8,128)S(1)}, s32[2,136,256]{2,1,0:T(8,128)S(1)}, u32[]{:S(2)}, u32[]{:S(2)}) collective-permute-start(s32[2,136,256]{2,1,0:T(8,128)S(1)} %get-tuple-element.51), channel_id=1, source_target_pairs={{0,2},{1,3},{2,0},{3,1},{4,6},{5,7},{6,4},{7,5},{8,10},{9,11},{10,... | collective-permute-start | bytes 835592 | tf_op jit(solution)/shard_map/ppermute | solution.py:366
  57.8 16.7 %collective-permute-start.12 = (s32[2,136,256]{2,1,0:T(8,128)S(1)}, s32[2,136,256]{2,1,0:T(8,128)S(1)}, u32[]{:S(2)}, u32[]{:S(2)}) collective-permute-start(s32[2,136,256]{2,1,0:T(8,128)S(1)} %get-tuple-element.53), channel_id=1, source_target_pairs={{2,4},{3,5},{4,2},{5,3},{10,12},{11,13},{12,10},{13,11},{18,20},{1... | collective-permute-start | bytes 835592 | tf_op jit(solution)/shard_map/ppermute | solution.py:366
  60.2 14.3 %collective-permute-start.9 = (s32[2,264,128]{2,1,0:T(8,128)S(1)}, s32[2,264,128]{2,1,0:T(8,128)S(1)}, u32[]{:S(2)}, u32[]{:S(2)}) collective-permute-start(s32[2,264,128]{2,1,0:T(8,128)S(1)} %get-tuple-element.50), channel_id=1, source_target_pairs={{0,1},{1,0},{2,3},{3,2},{4,5},{5,4},{6,7},{7,6},{8,9},{9,8},{10,11... | collective-permute-start | bytes 811016 | tf_op jit(solution)/shard_map/ppermute | solution.py:366
  60.7 10.2 %collective-permute-start.11 = (s32[2,136,128]{2,1,0:T(8,128)S(1)}, s32[2,136,128]{2,1,0:T(8,128)S(1)}, u32[]{:S(2)}, u32[]{:S(2)}) collective-permute-start(s32[2,136,128]{2,1,0:T(8,128)S(1)} %get-tuple-element.52), channel_id=1, source_target_pairs={{0,3},{1,2},{2,1},{3,0},{4,7},{5,6},{6,5},{7,4},{8,11},{9,10},{10,... | collective-permute-start | bytes 417800 | tf_op jit(solution)/shard_map/ppermute | solution.py:366
  62.0 10.5 %collective-permute-start.13 = (s32[2,136,128]{2,1,0:T(8,128)S(1)}, s32[2,136,128]{2,1,0:T(8,128)S(1)}, u32[]{:S(2)}, u32[]{:S(2)}) collective-permute-start(s32[2,136,128]{2,1,0:T(8,128)S(1)} %get-tuple-element.54), channel_id=1, source_target_pairs={{2,5},{3,4},{4,3},{5,2},{10,13},{11,12},{12,11},{13,10},{18,21},{1... | collective-permute-start | bytes 417800 | tf_op jit(solution)/shard_map/ppermute | solution.py:366

commit v3 on v2

v3 whole, which is shorter than its diff:
```python
import functools
import math

import jax
import jax.numpy as jnp
import numpy as np
from jax import lax
from jax.experimental import pallas as pl
from jax.experimental.pallas import tpu as pltpu
from jax.sharding import PartitionSpec as P

VMEM = pl.BlockSpec(memory_space=pltpu.VMEM)
SMEM = pl.BlockSpec(memory_space=pltpu.SMEM)
ANY = pl.BlockSpec(memory_space=pl.ANY)
LIMIT = 16 * 1024 * 1024
LEVELS = 32767.0
SCALE_ROWS = 8


def swap_pairs(size, parity):
    pairs = []
    for i in range(parity, size - 1, 2):
        pairs += [(i, i + 1), (i + 1, i)]
    return pairs


def swap_list(n_x, n_y, swap_x, swap_y):
    xs = [(i, i) for i in range(n_x)] if swap_x is None else swap_pairs(n_x, swap_x)
    ys = [(i, i) for i in range(n_y)] if swap_y is None else swap_pairs(n_y, swap_y)
    return [(a * n_y + b, c * n_y + d) for a, c in xs for b, d in ys]


def swap_kinds(n_x, n_y):
    kinds = []
    for swap_x in (None, 0, 1):
        for swap_y in (None, 0, 1):
            if (swap_x, swap_y) != (None, None) and swap_list(n_x, n_y, swap_x, swap_y):
                kinds.append((swap_x, swap_y))
    return kinds


def split(value):
    high = value.astype(jnp.bfloat16)
    return high, (value - high.astype(jnp.float32)).astype(jnp.bfloat16)


def dft_basis(size):
    half = size // 2
    n = np.arange(size)
    j = np.arange(half)
    cos = np.cos(2 * np.pi * (j[:, None] * n[None, :] % size) / size)
    sin = np.sin(2 * np.pi * (j[:, None] * n[None, :] % size) / size)
    sin[0] = np.where(n % 2 == 0, 1.0, -1.0)
    return np.concatenate([cos, sin]) / math.sqrt(size)


def folded_order(array, axis):
    half = array.shape[axis] // 2
    low = lax.slice_in_dim(array, 0, half, axis=axis)
    mid = lax.slice_in_dim(array, half, half + 1, axis=axis)
    high = lax.rev(lax.slice_in_dim(array, half + 1, 2 * half, axis=axis), (axis,))
    return jnp.concatenate([low, mid, high], axis=axis)


def spectrum_split(p, q, first):
    (pr, pi), (qr, qi) = p, q
    plus = (jnp.where(first, pr, pr + qi), jnp.where(first, pi, pi - qr))
    minus = (jnp.where(first, qr, pr - qi), jnp.where(first, qi, pi + qr))
    return plus, minus


def spectrum_join(plus, minus, first):
    (xr, xi), (yr, yi) = plus, minus
    p = (jnp.where(first, xr, xr + yr), jnp.where(first, xi, xi + yi))
    q = (jnp.where(first, yr, yi - xi), jnp.where(first, yi, xr - yr))
    return p, q


def dot(a, b):
    return jnp.dot(a, b, preferred_element_type=jnp.float32)


def left3(table, field):
    high, low = split(field)
    return dot(table[0], high) + (dot(table[0], low) + dot(table[1], high))


def right3(field, table):
    high, low = split(field)
    return dot(high, table[0]) + (dot(low, table[0]) + dot(high, table[1]))


def lefts(table, fields):
    return [left3(table, field) for field in fields]


def rights(fields, table):
    return [right3(field, table) for field in fields]


def middle(parts, cos_ref, sin_ref):
    half = parts[0].shape[0] // 2
    row0 = lax.broadcasted_iota(jnp.int32, (half, half), 0) == 0
    col0 = lax.broadcasted_iota(jnp.int32, (half, half), 1) == 0

    def quadrant(r, c):
        return tuple(part[r * half : (r + 1) * half, c * half : (c + 1) * half] for part in parts)

    top = spectrum_split(quadrant(0, 0), quadrant(0, 1), col0)
    bottom = spectrum_split(quadrant(1, 0), quadrant(1, 1), col0)
    out = [[None, None], [None, None]]
    for c in range(2):
        turned = []
        for r, (re, im) in enumerate(spectrum_split(top[c], bottom[c], row0)):
            where = (slice(r * half, (r + 1) * half), slice(c * half, (c + 1) * half))
            cos, sin = cos_ref[where], sin_ref[where]
            turned.append((re * cos + im * sin, im * cos - re * sin))
        out[0][c], out[1][c] = spectrum_join(turned[0], turned[1], row0)
    rows = [spectrum_join(out[r][0], out[r][1], col0) for r in range(2)]
    return [
        jnp.concatenate(
            [jnp.concatenate([rows[r][0][c], rows[r][1][c]], axis=1) for r in range(2)], axis=0
        )
        for c in range(2)
    ]


def propagate(parts, cos_ref, sin_ref, tab_ref):
    table = (tab_ref[0], tab_ref[1])
    turned = (tab_ref[2], tab_ref[3])
    spectrum = middle(rights(lefts(table, parts), turned), cos_ref, sin_ref)
    return lefts(turned, rights(spectrum, table))


def take_window(ext_ref, at_x, at_y, patch):
    step = 8
    inside = lax.rem(at_x, step)
    first = pl.multiple_of(at_x - inside, step)
    rows = ext_ref[pl.ds(first, patch + step), :]
    count, width = rows.shape
    rows = pltpu.roll(rows, lax.rem(width - at_y, width), 1)[:, :patch]
    return pltpu.roll(rows, lax.rem(count - inside, count), 0)[:patch]


def add_window(ext_ref, at_x, at_y, value):
    step = 8
    inside = lax.rem(at_x, step)
    first = pl.multiple_of(at_x - inside, step)
    value = jnp.concatenate([value, jnp.zeros((step, value.shape[1]), value.dtype)], axis=0)
    value = pltpu.roll(value, inside, 0)
    value = jnp.concatenate([value, jnp.zeros_like(value)], axis=1)
    ext_ref[pl.ds(first, value.shape[0]), :] += pltpu.roll(value, at_y, 1)


def two_powers(exponent):
    first = jnp.floor(exponent * 0.5)
    return jnp.exp2(first), jnp.exp2(exponent - first)


def exponent_of(top):
    top = jnp.max(jnp.max(top, axis=0, keepdims=True), axis=1, keepdims=True)
    return jnp.where(top > 0, jnp.ceil(jnp.log2(jnp.maximum(top, 1e-37))), 0.0)


def encode(real, imag, exponent):
    scale, rest = two_powers(-exponent)

    def root(value):
        return value * lax.rsqrt(value)

    def code(value):
        size = jnp.minimum(jnp.maximum(jnp.abs(value) * scale * rest, 1e-30), 1.0)
        whole = (root(root(size)) * LEVELS + 0.5).astype(jnp.int32)
        return jnp.where(value < 0, -whole, whole)

    return (code(real) << 16) | (code(imag) & 0xFFFF)


def decode(packed, exponent):
    scale, rest = two_powers(exponent.astype(jnp.float32))

    def value(whole):
        root = whole.astype(jnp.float32) * (1.0 / LEVELS)
        square = root * root
        size = square * square * scale * rest
        return jnp.where(whole < 0, -size, size)

    return value(packed >> 16), value((packed << 16) >> 16)


def put_encoded(ref, at, real, imag, exponent):
    packed = encode(real, imag, exponent)
    rows, cols = packed.shape
    ref[at + (slice(0, rows), slice(None))] = packed
    ref[at + (slice(rows, rows + SCALE_ROWS), slice(None))] = jnp.broadcast_to(
        exponent.astype(jnp.int32), (SCALE_ROWS, cols)
    )


def get_encoded(ref, at):
    rows = ref.shape[-2] - SCALE_ROWS
    packed = ref[at + (slice(0, rows), slice(None))]
    return decode(packed, ref[at + (slice(rows, rows + 1), slice(None))])


def halo_start(kind, half, tile):
    start = []
    for swap, axis in zip(kind, ("sx", "sy")):
        if swap is None:
            start.append(half)
        else:
            above = lax.rem(lax.axis_index(axis) + swap, 2) == 0
            start.append(pl.multiple_of(jnp.where(above, half + tile, 0), half))
    return start


def rim_start(kind, half, tile):
    start = []
    for swap, axis in zip(kind, ("sx", "sy")):
        if swap is None:
            start.append(0)
        else:
            above = lax.rem(lax.axis_index(axis) + swap, 2) == 0
            start.append(pl.multiple_of(jnp.where(above, tile - half, 0), half))
    return start


def corner_of(anchor_ref, slot, half, tile):
    at_x = anchor_ref[slot, 0] - lax.axis_index("sx") * tile + half
    at_y = anchor_ref[slot, 1] - lax.axis_index("sy") * tile + half
    return at_x, at_y


def core_index():
    return lax.rem(lax.axis_index("depth"), 2)


def rims_kernel(kinds, own_ref, *pieces):
    tile = own_ref.shape[2]
    for kind, piece in zip(kinds, pieces):
        row, col = rim_start(kind, tile // 2, tile)
        rows, cols = piece.shape[2:]
        piece[...] = own_ref[:, :, pl.ds(row, rows), pl.ds(col, cols)]


def window_kernel(kinds, turn, anchor_ref, own_ref, inc_ref, *refs):
    pieces, (mine_ref, other_ref, inc_out, ext_ref, sem) = refs[: len(kinds)], refs[len(kinds) :]
    slab, _, tile, _ = own_ref.shape
    half = tile // 2
    patch = mine_ref.shape[2]
    core = core_index()

    @pl.when(core == turn)
    def _():
        fetch = [
            pltpu.make_async_copy(inc_ref.at[layer, core], inc_out.at[layer], sem.at[layer])
            for layer in range(slab)
        ]
        for copy in fetch:
            copy.start()
        corners = [corner_of(anchor_ref, slot, half, tile) for slot in (core, 1 - core)]
        ext_ref[...] = jnp.zeros_like(ext_ref)
        for layer in range(slab):
            for c in range(2):
                ext_ref[half : half + tile, half : half + tile] = own_ref[layer, c].astype(jnp.float32)
                for kind, piece in zip(kinds, pieces):
                    row, col = halo_start(kind, half, tile)
                    rows, cols = piece.shape[2:]
                    ext_ref[pl.ds(row, rows), pl.ds(col, cols)] = piece[layer, c].astype(jnp.float32)
                for (at_x, at_y), out in zip(corners, (mine_ref, other_ref)):
                    out[layer, c] = take_window(ext_ref, at_x, at_y, patch).astype(out.dtype)
        for copy in fetch:
            copy.wait()


def sweep_kernel(stage, turn, live_ref, wave_in, win_own, win_got, inc_own, inc_got, cos_ref, sin_ref, tab_ref,
                 *refs):
    term_ref, out_ref, wave_ref, term, sems = refs[-5:]
    slab = win_own.shape[0]
    core = core_index()
    chip = lax.axis_index("depth") // 2
    chips = lax.axis_size("depth") // 2
    own = core == turn

    def leave(slot, local):
        return pltpu.make_async_copy(term.at[slot], term_ref.at[local], sems.at[slot])

    @pl.when(chip == chips - 1 - stage)
    def _():
        if turn == 0:
            wave_ref[...] = wave_in[...]
        elif stage == 0:
            live = (core < live_ref[0]).astype(jnp.float32)
            wave_ref[...] = wave_in[core].astype(jnp.float32) * live
        else:
            wave_ref[0], wave_ref[1] = get_encoded(wave_in, ())

        def one(step, _):
            local = slab - 1 - step
            slot = lax.rem(step, 2)

            @pl.when(step >= 2)
            def _():
                leave(slot, 0).wait()

            wr, wi = wave_ref[0], wave_ref[1]
            er = jnp.where(own, inc_own[local, 0], inc_got[local, core, 0]).astype(jnp.float32)
            ei = jnp.where(own, inc_own[local, 1], inc_got[local, core, 1]).astype(jnp.float32)
            term[slot, 0] = er * wr + ei * wi
            term[slot, 1] = er * wi - ei * wr
            leave(slot, local).start()

            @pl.when(chip + turn + local > 0)
            def _():
                tr = jnp.where(own, win_own[local, 0], win_got[local, 0]).astype(jnp.float32)
                ti = jnp.where(own, win_own[local, 1], win_got[local, 1]).astype(jnp.float32)
                parts = [tr * wr + ti * wi, tr * wi - ti * wr]
                wave_ref[0], wave_ref[1] = propagate(parts, cos_ref, sin_ref, tab_ref)

            return 0

        lax.fori_loop(0, slab, one, 0)
        if turn == 1:
            out_ref[...] = wave_ref[...]
        elif stage < chips - 1:
            wr, wi = wave_ref[0], wave_ref[1]
            exponent = exponent_of(jnp.maximum(jnp.abs(wr), jnp.abs(wi)))
            put_encoded(out_ref, (), wr, wi, exponent)
        for slot in range(min(slab, 2)):
            leave(slot, 0).wait()


def scatter_kernel(kinds, turn, anchor_ref, mine_ref, other_ref, own_ref, *refs):
    pieces, ext_ref = refs[:-1], refs[-1]
    slab, _, patch, _ = mine_ref.shape
    tile = own_ref.shape[2]
    half = tile // 2
    core = core_index()

    @pl.when(core == turn)
    def _():
        corners = [corner_of(anchor_ref, slot, half, tile) for slot in (core, 1 - core)]
        ext_ref[...] = jnp.zeros_like(ext_ref)
        top = None
        for layer in range(slab):
            for c in range(2):
                bound = 0.0
                for (at_x, at_y), term in zip(corners, (mine_ref, other_ref)):
                    value = term[layer, c]
                    add_window(ext_ref.at[layer, c], at_x, at_y, value)
                    bound = bound + jnp.max(jnp.abs(value), axis=0, keepdims=True)
                top = bound if top is None else jnp.maximum(top, bound)
                own_ref[layer, c] = ext_ref[layer, c, half : half + tile, half : half + tile]
        exponent = exponent_of(top)
        for layer in range(slab):
            for kind, piece in zip(kinds, pieces):
                row, col = halo_start(kind, half, tile)
                where = (pl.ds(row, piece.shape[1] - SCALE_ROWS), pl.ds(col, piece.shape[2]))
                put_encoded(piece, (layer,), ext_ref[(layer, 0) + where], ext_ref[(layer, 1) + where], exponent)


def fold_kernel(kinds, *refs):
    out_ref = refs[-1]
    slab, _, tile, _ = out_ref.shape
    count = 1 + len(kinds)

    def fold(own_ref, pieces):
        out_ref[...] = own_ref[...]
        for layer in range(slab):
            for kind, piece in zip(kinds, pieces):
                row, col = rim_start(kind, tile // 2, tile)
                where = (pl.ds(row, piece.shape[1] - SCALE_ROWS), pl.ds(col, piece.shape[2]))
                for c, value in enumerate(get_encoded(piece, (layer,))):
                    out_ref[(layer, c) + where] += value

    for turn in range(2):
        own_ref, *pieces = refs[turn * count : (turn + 1) * count]
        pl.when(core_index() == turn)(functools.partial(fold, own_ref, pieces))


def shards(transmission, incident, exit_adjoint, propagator_phase, scan_anchor, live_count):
    f32 = jnp.float32
    n_depth, n_x, n_y = lax.axis_size("depth"), lax.axis_size("sx"), lax.axis_size("sy")
    slab, _, tile, _ = transmission.shape
    patch = propagator_phase.shape[0]
    half = tile // 2
    extent = tile + patch
    chips = n_depth // 2
    kinds = swap_kinds(n_x, n_y)
    params = pltpu.CompilerParams(vmem_limit_bytes=LIMIT)
    fixed = lax.optimization_barrier

    def call(kernel, out_shape, operands, name, scratch=(), **more):
        return pl.pallas_call(
            kernel,
            out_shape=out_shape,
            scratch_shapes=list(scratch),
            compiler_params=params,
            name=name,
            **{"in_specs": [VMEM] * len(operands), "out_specs": jax.tree.map(lambda _: VMEM, out_shape), **more},
        )(*operands)

    def rim_size(kind):
        return tile if kind[0] is None else half, tile if kind[1] is None else half

    def swapped(values, turn):
        return [
            lax.ppermute(
                value,
                ("depth", "sx", "sy"),
                [
                    (d * n_x * n_y + i, d * n_x * n_y + j)
                    for d in range(turn, n_depth, 2)
                    for i, j in swap_list(n_x, n_y, *kind)
                ],
            )
            for value, kind in zip(values, kinds)
        ]

    def to_other_core(value, source):
        return lax.ppermute(
            value, "depth", [(c + source, c + 1 - source) for c in range(0, n_depth, 2)]
        )

    rims = call(
        functools.partial(rims_kernel, kinds),
        tuple(jax.ShapeDtypeStruct((slab, 2) + rim_size(kind), transmission.dtype) for kind in kinds),
        (transmission,),
        "rims",
    )
    halos = {1: swapped(rims, 1)}
    propagator_phase, rims = fixed((propagator_phase, rims))
    phase = folded_order(folded_order(propagator_phase, 0), 1)
    phase_cos, phase_sin = jnp.cos(phase), jnp.sin(phase)
    phase_cos, phase_sin, rims, incident_sent = fixed((phase_cos, phase_sin, rims, incident))
    halos[0] = swapped(rims, 0)
    inc_got = lax.ppermute(incident_sent, "depth", swap_pairs(n_depth, 0))

    basis = dft_basis(patch)
    high = basis.astype(jnp.bfloat16)
    low = (basis - high.astype(np.float64)).astype(jnp.bfloat16)
    tables = jnp.asarray(np.stack([high, low, high.T, low.T]))

    window_shape = jax.ShapeDtypeStruct((slab, 2, patch, patch), transmission.dtype)
    term_shape = jax.ShapeDtypeStruct((slab, 2, patch, patch), f32)
    coded = jax.ShapeDtypeStruct((patch + SCALE_ROWS, patch), jnp.int32)
    plain = jax.ShapeDtypeStruct((2, patch, patch), f32)
    views = {}
    terms = {}
    wave = exit_adjoint
    for stage in range(chips):
        for turn in (1, 0):
            if stage == 0:
                around = halos[turn]
                if turn == 0:
                    around, wave = fixed((around, wave))
                win_own, win_send, inc_own = call(
                    functools.partial(window_kernel, kinds, turn),
                    (window_shape, window_shape, jax.ShapeDtypeStruct(window_shape.shape, incident.dtype)),
                    (scan_anchor, transmission, incident, *around),
                    "windows",
                    [pltpu.VMEM((extent, extent), f32), pltpu.SemaphoreType.DMA((slab,))],
                    in_specs=[SMEM, VMEM, ANY] + [VMEM] * len(kinds),
                )
                views[turn] = (win_own, to_other_core(win_send, turn), inc_own)
            more = [terms[turn]] if stage else []
            terms[turn], wave = call(
                functools.partial(sweep_kernel, stage, turn),
                (term_shape, plain if turn else coded),
                (live_count, wave, *views[turn], inc_got, phase_cos, phase_sin, tables, *more),
                "sweep",
                [
                    pltpu.VMEM((2, patch, patch), f32),
                    pltpu.VMEM((2, 2, patch, patch), f32),
                    pltpu.SemaphoreType.DMA((2,)),
                ],
                in_specs=[SMEM] + [VMEM] * 8 + [ANY] * len(more),
                out_specs=(ANY, VMEM),
                input_output_aliases={9: 0} if stage else {},
            )
        if stage < chips - 1:
            source = chips - 1 - stage
            wave = lax.ppermute(wave, "depth", [(2 * source + c, 2 * source - 2 + c) for c in range(2)])

    own_shape = jax.ShapeDtypeStruct((slab, 2, tile, tile), f32)
    coded_rims = tuple(
        jax.ShapeDtypeStruct((slab, rim_size(kind)[0] + SCALE_ROWS, rim_size(kind)[1]), jnp.int32)
        for kind in kinds
    )
    parts = {}
    for turn in (1, 0):
        own, *beyond = call(
            functools.partial(scatter_kernel, kinds, turn),
            (own_shape,) + coded_rims,
            (scan_anchor, terms[turn], to_other_core(terms[turn], 1 - turn)),
            "scatter",
            [pltpu.VMEM((slab, 2, extent, extent), f32)],
            in_specs=[SMEM, VMEM, VMEM],
        )
        parts[turn] = [own] + swapped(beyond, turn)
    return call(functools.partial(fold_kernel, kinds), own_shape, (*parts[0], *parts[1]), "fold")


def solution(mesh):
    placed = (
        P("depth", None, "sx", "sy"),
        P("depth", ("sx", "sy"), None, None, None),
        P(("sx", "sy"), None, None, None),
        P(),
        P(("sx", "sy"), None),
        P(("sx", "sy")),
    )
    return jax.shard_map(
        shards, mesh=mesh, in_specs=placed, out_specs=P("depth", None, "sx", "sy"), check_vma=False
    )
```

time: 78 us -> 99.8 us (1.28)
  starting transfers between devices: 18.3 us -> 43.3 us
  local copies, waits for them, and re-layouts: 4.35 us -> 2.21 us
    ppermute x13 -> x25, starting transfers between devices: 17 us -> 42 us  [the longest x20 34.9 us: swapped(): lax.ppermute(value, ('depth', 'sx', 'sy'), [(d * n_x * n_y + i, d * n_x *...]
    ppermute x13 -> x25, waiting for transfers between devices: 17.7 us -> 21.6 us  [the longest x4 11.8 us: to_other_core(): lax.ppermute(value, 'depth', [(c + source, c + 1 - source) for c in range...]
    ppermute x1, waiting for transfers between devices: 16.8 us -> 13 us  [shards(): lax.ppermute(wave, 'depth', [(2 * source + c, 2 * source - 2 + c) for c i...]
    unnamed x14, local copies, waits for them, and re-layouts: 3.07 us -> 1.89 us
    pallas_call x6 -> x10, Pallas kernels: 16.6 us -> 16.4 us  [call(): pl.pallas_call(kernel, out_shape=out_shape, scratch_shapes=list(scratch),...]
  transfers between devices with their start and end apart: 14 -> 26, of which waited for: 8 -> 9; matrix products, arithmetic and copies ran while one was open for 4% -> 0% of each run, Pallas kernels for 4% -> 5%
where the time goes in v3:
time: 99.8 us; the launch traced here: 98.9 us
  starting transfers between devices  43.3 us (43%)
  waiting for transfers between devices  34.7 us (35%)
  Pallas kernels  16.4 us (16%)
  local copies, waits for them, and re-layouts  2.21 us (2%)
  other arithmetic  1.23 us (1%)
  between operations  1.15 us (1%)
    ppermute x20, starting transfers between devices, swapped(): lax.ppermute(value, ('depth', 'sx', 'sy'), [(d * n_x * n_y + i, d * n_x *...  34.9 us
    pallas_call x10, Pallas kernels, call(): pl.pallas_call(kernel, out_shape=out_shape, scratch_shapes=list(scratch),...  16.4 us
    ppermute x1, waiting for transfers between devices, shards(): lax.ppermute(wave, 'depth', [(2 * source + c, 2 * source - 2 + c) for c i...  13 us
    ppermute x4, waiting for transfers between devices, to_other_core(): lax.ppermute(value, 'depth', [(c + source, c + 1 - source) for c in range...  11.8 us
    ppermute x20, waiting for transfers between devices, swapped(): lax.ppermute(value, ('depth', 'sx', 'sy'), [(d * n_x * n_y + i, d * n_x *...  9.87 us
    ppermute x4, starting transfers between devices, to_other_core(): lax.ppermute(value, 'depth', [(c + source, c + 1 - source) for c in range...  7.07 us
  transfers between devices with their start and end apart: 26, of which 9 were waited for; matrix products, arithmetic and copies ran while one was open for 0% of the time, Pallas kernels for 5%

profile of v3, /device:TPU:16, one launch (start us, length us, event | category | flops | bytes accessed | tf_op | source)
XLA Modules:
  0.0 98.9 jit_solution(5165327883362811442)
XLA Ops:
  0.0 1.0 %copy-done.1 = bf16[2,2,256,256]{3,2,1,0:T(8,128)(2,1)S(1)} copy-done((bf16[2,2,256,256]{3,2,1,0:T(8,128)(2,1)S(1)}, bf16[2,2,256,256]{3,2,1,0:T(8,128)(2,1)}, u32[]{:S(2)}) %copy-start.1) | copy-done | bytes 524312
  1.0 0.1 rims.1
  1.2 0.8 copy-done.6
  2.0 0.1 rev.6
  2.2 0.1 pad_maximum_fusion.1
  2.3 0.2 rev.7
  2.5 1.1 %fusion = (f32[256,256]{1,0:T(8,128)S(1)}, f32[256,256]{1,0:T(8,128)S(1)}) fusion(f32[256,127]{1,0:T(8,128)S(1)} %rev.7, f32[256,129]{1,0:T(8,128)S(1)} %slice_maximum_fusion), kind=kLoop, calls=%fused_computation.2 | loop fusion | flops 65536 | bytes 786432 | tf_op jit(solution)/shard_map/sin | solution.py:434
  3.7 0.8 collective-permute-start.7
  4.5 0.7 collective-permute-start.5
  5.2 0.7 collective-permute-start.6
  5.9 0.7 collective-permute-start.8
  6.6 0.7 collective-permute-start.9
  7.3 0.6 windows.2
  7.9 1.3 %collective-permute-start.10 = (bf16[2,2,256,256]{3,2,1,0:T(8,128)(2,1)S(1)}, bf16[2,2,256,256]{3,2,1,0:T(8,128)(2,1)S(1)}, u32[]{:S(2)}, u32[]{:S(2)}) collective-permute-start(bf16[2,2,256,256]{3,2,1,0:T(8,128)(2,1)S(1)} %get-tuple-element.72), channel_id=1, source_target_pairs={{8,0},{24,16},{9,1},{25,17},{10,2},{26,18},{11,3},{27,19},{12,4},{... | collective-permute-start | bytes 1572872 | tf_op jit(solution)/shard_map/ppermute | solution.py:421
  9.2 3.4 %collective-permute-start = (bf16[2,2,256,128]{3,2,1,0:T(8,128)(2,1)S(1)}, bf16[2,2,256,128]{3,2,1,0:T(8,128)(2,1)S(1)}, u32[]{:S(2)}, u32[]{:S(2)}) collective-permute-start(bf16[2,2,256,128]{3,2,1,0:T(8,128)(2,1)S(1)} %get-tuple-element.66), channel_id=1, source_target_pairs={{0,1},{1,0},{2,3},{3,2},{4,5},{5,4},{6,7},{7,6},{16,17},{17,16},{1... | collective-permute-start | bytes 786440 | tf_op jit(solution)/shard_map/ppermute | solution.py:408
  12.7 3.5 %collective-permute-start.1 = (bf16[2,2,128,256]{3,2,1,0:T(8,128)(2,1)S(1)}, bf16[2,2,128,256]{3,2,1,0:T(8,128)(2,1)S(1)}, u32[]{:S(2)}, u32[]{:S(2)}) collective-permute-start(bf16[2,2,128,256]{3,2,1,0:T(8,128)(2,1)S(1)} %get-tuple-element.67), channel_id=1, source_target_pairs={{0,2},{1,3},{2,0},{3,1},{4,6},{5,7},{6,4},{7,5},{16,18},{17,19},{1... | collective-permute-start | bytes 786440 | tf_op jit(solution)/shard_map/ppermute | solution.py:408
  16.2 1.9 %collective-permute-start.3 = (bf16[2,2,128,256]{3,2,1,0:T(8,128)(2,1)S(1)}, bf16[2,2,128,256]{3,2,1,0:T(8,128)(2,1)S(1)}, u32[]{:S(2)}, u32[]{:S(2)}) collective-permute-start(bf16[2,2,128,256]{3,2,1,0:T(8,128)(2,1)S(1)} %get-tuple-element.69), channel_id=1, source_target_pairs={{2,4},{3,5},{4,2},{5,3},{18,20},{19,21},{20,18},{21,19}} | collective-permute-start | bytes 786440 | tf_op jit(solution)/shard_map/ppermute | solution.py:408
  18.1 10.2 %collective-permute-done.10.win_got = bf16[2,2,256,256]{3,2,1,0:T(8,128)(2,1)S(1)} collective-permute-done((bf16[2,2,256,256]{3,2,1,0:T(8,128)(2,1)S(1)}, bf16[2,2,256,256]{3,2,1,0:T(8,128)(2,1)S(1)}, u32[]{:S(2)}, u32[]{:S(2)}) %collective-permute-start.10) | collective-permute-done | bytes 524320 | tf_op jit(solution)/shard_map/ppermute | solution.py:421
  28.3 1.9 %collective-permute-start.2 = (bf16[2,2,128,128]{3,2,1,0:T(8,128)(2,1)S(1)}, bf16[2,2,128,128]{3,2,1,0:T(8,128)(2,1)S(1)}, u32[]{:S(2)}, u32[]{:S(2)}) collective-permute-start(bf16[2,2,128,128]{3,2,1,0:T(8,128)(2,1)S(1)} %get-tuple-element.68), channel_id=1, source_target_pairs={{0,3},{1,2},{2,1},{3,0},{4,7},{5,6},{6,5},{7,4},{16,19},{17,18},{1... | collective-permute-start | bytes 393224 | tf_op jit(solution)/shard_map/ppermute | solution.py:408
  30.2 4.4 %collective-permute-start.4 = (bf16[2,2,128,128]{3,2,1,0:T(8,128)(2,1)S(1)}, bf16[2,2,128,128]{3,2,1,0:T(8,128)(2,1)S(1)}, u32[]{:S(2)}, u32[]{:S(2)}) collective-permute-start(bf16[2,2,128,128]{3,2,1,0:T(8,128)(2,1)S(1)} %get-tuple-element.70), channel_id=1, source_target_pairs={{2,5},{3,4},{4,3},{5,2},{18,21},{19,20},{20,19},{21,18}} | collective-permute-start | bytes 393224 | tf_op jit(solution)/shard_map/ppermute | solution.py:408
  35.4 0.7 collective-permute-done.2.refs_2_
  36.0 1.9 %collective-permute-done.4.refs_4_ = bf16[2,2,128,128]{3,2,1,0:T(8,128)(2,1)S(1)} collective-permute-done((bf16[2,2,128,128]{3,2,1,0:T(8,128)(2,1)S(1)}, bf16[2,2,128,128]{3,2,1,0:T(8,128)(2,1)S(1)}, u32[]{:S(2)}, u32[]{:S(2)}) %collective-permute-start.4) | collective-permute-done | bytes 131104 | tf_op jit(solution)/shard_map/ppermute | solution.py:408
  38.0 2.8 %windows.3 = (bf16[2,2,256,256]{3,2,1,0:T(8,128)(2,1)S(1)}, bf16[2,2,256,256]{3,2,1,0:T(8,128)(2,1)S(1)}, bf16[2,2,256,256]{3,2,1,0:T(8,128)(2,1)S(1)}) custom-call(s32[2,2]{1,0:T(2,128)S(1)} %copy-done.5, bf16[2,2,256,256]{3,2,1,0:T(8,128)(2,1)S(1)} %copy-done.2, bf16[2,2,2,256,256]{4,3,2,1,0:T(8,128)(2,1)S(1)} %copy-done.3, ...), custom_call_target="tpu_custom_call" | custom-call | tf_op jit(solution)/shard_map/windows/pallas_call | solution.py:394
  40.8 1.3 %collective-permute-start.12 = (bf16[2,2,256,256]{3,2,1,0:T(8,128)(2,1)S(1)}, bf16[2,2,256,256]{3,2,1,0:T(8,128)(2,1)S(1)}, u32[]{:S(2)}, u32[]{:S(2)}) collective-permute-start(bf16[2,2,256,256]{3,2,1,0:T(8,128)(2,1)S(1)} %get-tuple-element.85), channel_id=1, source_target_pairs={{0,8},{16,24},{1,9},{17,25},{2,10},{18,26},{3,11},{19,27},{4,12},{... | collective-permute-start | bytes 1572872 | tf_op jit(solution)/shard_map/ppermute | solution.py:421
  42.2 1.5 %collective-permute-done.12.win_got = bf16[2,2,256,256]{3,2,1,0:T(8,128)(2,1)S(1)} collective-permute-done((bf16[2,2,256,256]{3,2,1,0:T(8,128)(2,1)S(1)}, bf16[2,2,256,256]{3,2,1,0:T(8,128)(2,1)S(1)}, u32[]{:S(2)}, u32[]{:S(2)}) %collective-permute-start.12) | collective-permute-done | bytes 524320 | tf_op jit(solution)/shard_map/ppermute | solution.py:421
  43.7 1.3 %collective-permute-start.13 = (s32[264,256]{1,0:T(8,128)S(1)}, s32[264,256]{1,0:T(8,128)S(1)}, u32[]{:S(2)}, u32[]{:S(2)}) collective-permute-start(s32[264,256]{1,0:T(8,128)S(1)} %get-tuple-element.87), channel_id=1, source_target_pairs={{16,0},{24,8},{17,1},{25,9},{18,2},{26,10},{19,3},{27,11},{20,4},{... | collective-permute-start | bytes 811016 | tf_op jit(solution)/shard_map/ppermute | solution.py:483
  45.0 13.0 %collective-permute-done.13.wave_in = s32[264,256]{1,0:T(8,128)S(1)} collective-permute-done((s32[264,256]{1,0:T(8,128)S(1)}, s32[264,256]{1,0:T(8,128)S(1)}, u32[]{:S(2)}, u32[]{:S(2)}) %collective-permute-start.13) | collective-permute-done | bytes 270368 | tf_op jit(solution)/shard_map/ppermute | solution.py:483
  58.0 3.5 %sweep.6 = (f32[2,2,256,256]{3,2,1,0:T(8,128)S(1)}, f32[2,256,256]{2,1,0:T(8,128)S(1)}) custom-call(s32[1]{0:T(128)S(6)} %copy.12.live_ref, s32[264,256]{1,0:T(8,128)S(1)} %collective-permute-done.13.wave_in, bf16[2,2,256,256]{3,2,1,0:T(8,128)(2,1)S(1)} %get-tuple-element.71.win_own, ...), custom_call_target="tpu_custom_call", output_to_operand_aliasing={{0}: (9, {})} | custom-call | tf_op jit(solution)/shard_map/sweep/pallas_call | solution.py:394
  61.5 2.8 %sweep.7 = (f32[2,2,256,256]{3,2,1,0:T(8,128)S(1)}, s32[264,256]{1,0:T(8,128)}) custom-call(s32[1]{0:T(128)S(6)} %copy.12.live_ref, f32[2,256,256]{2,1,0:T(8,128)S(1)} %get-tuple-element.89.wave_in, bf16[2,2,256,256]{3,2,1,0:T(8,128)(2,1)S(1)} %get-tuple-element.84.win_own, ...), custom_call_target="tpu_custom_call", output_to_operand_aliasing={{0}: (9, {})} | custom-call | tf_op jit(solution)/shard_map/sweep/pallas_call | solution.py:394
  64.3 1.3 %collective-permute-start.14 = (f32[2,2,256,256]{3,2,1,0:T(8,128)S(1)}, f32[2,2,256,256]{3,2,1,0:T(8,128)S(1)}, u32[]{:S(2)}, u32[]{:S(2)}) collective-permute-start(f32[2,2,256,256]{3,2,1,0:T(8,128)S(1)} %get-tuple-element.91.mine_ref), channel_id=1, source_target_pairs={{8,0},{24,16},{9,1},{25,17},{10,2},{26,18},{11,3},{27,19},{12,4},{... | collective-permute-start | bytes 3145736 | tf_op jit(solution)/shard_map/ppermute | solution.py:421
  65.6 3.2 %collective-permute-start.20 = (f32[2,2,256,256]{3,2,1,0:T(8,128)S(1)}, f32[2,2,256,256]{3,2,1,0:T(8,128)S(1)}, u32[]{:S(2)}, u32[]{:S(2)}) collective-permute-start(f32[2,2,256,256]{3,2,1,0:T(8,128)S(1)} %get-tuple-element.98.mine_ref), channel_id=1, source_target_pairs={{0,8},{16,24},{1,9},{17,25},{2,10},{18,26},{3,11},{19,27},{4,12},{... | collective-permute-start | bytes 3145736 | tf_op jit(solution)/shard_map/ppermute | solution.py:421
  68.7 0.1 collective-permute-done.14.other_ref
  68.8 3.9 %scatter.2 = (f32[2,2,256,256]{3,2,1,0:T(8,128)S(1)}, s32[2,264,128]{2,1,0:T(8,128)S(1)}, s32[2,136,256]{2,1,0:T(8,128)S(1)}, s32[2,136,128]{2,1,0:T(8,128)S(1)}...) custom-call(s32[2,2]{1,0:T(2,128)S(1)} %copy-done.5, f32[2,2,256,256]{3,2,1,0:T(8,128)S(1)} %get-tuple-element.91.mine_ref, ...), custom_call_target="tpu_custom_call" | custom-call | tf_op jit(solution)/shard_map/scatter/pallas_call | solution.py:394
  72.7 2.4 %collective-permute-start.15 = (s32[2,264,128]{2,1,0:T(8,128)S(1)}, s32[2,264,128]{2,1,0:T(8,128)S(1)}, u32[]{:S(2)}, u32[]{:S(2)}) collective-permute-start(s32[2,264,128]{2,1,0:T(8,128)S(1)} %get-tuple-element.93), channel_id=1, source_target_pairs={{0,1},{1,0},{2,3},{3,2},{4,5},{5,4},{6,7},{7,6},{16,17},{17,16},{1... | collective-permute-start | bytes 811016 | tf_op jit(solution)/shard_map/ppermute | solution.py:408
  75.1 1.9 %collective-permute-start.17 = (s32[2,136,128]{2,1,0:T(8,128)S(1)}, s32[2,136,128]{2,1,0:T(8,128)S(1)}, u32[]{:S(2)}, u32[]{:S(2)}) collective-permute-start(s32[2,136,128]{2,1,0:T(8,128)S(1)} %get-tuple-element.95), channel_id=1, source_target_pairs={{0,3},{1,2},{2,1},{3,0},{4,7},{5,6},{6,5},{7,4},{16,19},{17,18},{1... | collective-permute-start | bytes 417800 | tf_op jit(solution)/shard_map/ppermute | solution.py:408
  77.1 3.7 %collective-permute-start.19 = (s32[2,136,128]{2,1,0:T(8,128)S(1)}, s32[2,136,128]{2,1,0:T(8,128)S(1)}, u32[]{:S(2)}, u32[]{:S(2)}) collective-permute-start(s32[2,136,128]{2,1,0:T(8,128)S(1)} %get-tuple-element.97), channel_id=1, source_target_pairs={{2,5},{3,4},{4,3},{5,2},{18,21},{19,20},{20,19},{21,18}} | collective-permute-start | bytes 417800 | tf_op jit(solution)/shard_map/ppermute | solution.py:408
  80.8 0.6 scatter.3
  81.3 0.7 collective-permute-start.23
  82.0 0.7 collective-permute-start.25
  82.7 2.4 %collective-permute-done.17.refs_3_ = s32[2,136,128]{2,1,0:T(8,128)S(1)} collective-permute-done((s32[2,136,128]{2,1,0:T(8,128)S(1)}, s32[2,136,128]{2,1,0:T(8,128)S(1)}, u32[]{:S(2)}, u32[]{:S(2)}) %collective-permute-start.17) | collective-permute-done | bytes 139296 | tf_op jit(solution)/shard_map/ppermute | solution.py:408
  85.0 1.9 %collective-permute-start.16 = (s32[2,136,256]{2,1,0:T(8,128)S(1)}, s32[2,136,256]{2,1,0:T(8,128)S(1)}, u32[]{:S(2)}, u32[]{:S(2)}) collective-permute-start(s32[2,136,256]{2,1,0:T(8,128)S(1)} %get-tuple-element.94), channel_id=1, source_target_pairs={{0,2},{1,3},{2,0},{3,1},{4,6},{5,7},{6,4},{7,5},{16,18},{17,19},{1... | collective-permute-start | bytes 835592 | tf_op jit(solution)/shard_map/ppermute | solution.py:408
  87.0 2.9 %collective-permute-start.18 = (s32[2,136,256]{2,1,0:T(8,128)S(1)}, s32[2,136,256]{2,1,0:T(8,128)S(1)}, u32[]{:S(2)}, u32[]{:S(2)}) collective-permute-start(s32[2,136,256]{2,1,0:T(8,128)S(1)} %get-tuple-element.96), channel_id=1, source_target_pairs={{2,4},{3,5},{4,2},{5,3},{18,20},{19,21},{20,18},{21,19}} | collective-permute-start | bytes 835592 | tf_op jit(solution)/shard_map/ppermute | solution.py:408
  89.9 0.7 collective-permute-start.22
  90.6 0.7 collective-permute-start.24
  91.3 0.7 collective-permute-start.21
  92.0 2.2 %collective-permute-done.16.refs_2_ = s32[2,136,256]{2,1,0:T(8,128)S(1)} collective-permute-done((s32[2,136,256]{2,1,0:T(8,128)S(1)}, s32[2,136,256]{2,1,0:T(8,128)S(1)}, u32[]{:S(2)}, u32[]{:S(2)}) %collective-permute-start.16) | collective-permute-done | bytes 278560 | tf_op jit(solution)/shard_map/ppermute | solution.py:408
  94.2 2.7 %collective-permute-done.18.refs_4_ = s32[2,136,256]{2,1,0:T(8,128)S(1)} collective-permute-done((s32[2,136,256]{2,1,0:T(8,128)S(1)}, s32[2,136,256]{2,1,0:T(8,128)S(1)}, u32[]{:S(2)}, u32[]{:S(2)}) %collective-permute-start.18) | collective-permute-done | bytes 278560 | tf_op jit(solution)/shard_map/ppermute | solution.py:408
  96.9 2.1 %fold.1 = f32[2,2,256,256]{3,2,1,0:T(8,128)} custom-call(f32[2,2,256,256]{3,2,1,0:T(8,128)S(1)} %get-tuple-element.92.refs_0_, s32[2,264,128]{2,1,0:T(8,128)S(1)} %collective-permute-done.15.refs_1_, s32[2,136,256]{2,1,0:T(8,128)S(1)} %collective-permute-done.16.refs_2_, s32[2,136,128]{2,1,0:T(8,128)S(1)} %collective-permute-done.17.refs_3_, ...), custom_call_target="tpu_custom_call" | custom-call | tf_op jit(solution)/shard_map/fold/pallas_call | solution.py:394
  (35 shorter events, 0.3 us)
Async XLA Ops:
  0.0 1.0 %copy-start.1 = (bf16[2,2,256,256]{3,2,1,0:T(8,128)(2,1)S(1)}, bf16[2,2,256,256]{3,2,1,0:T(8,128)(2,1)}, u32[]{:S(2)}) copy-start(bf16[2,2,256,256]{3,2,1,0:T(8,128)(2,1)} %own_ref.5) | copy-start | bytes 1572868
  1.0 0.9 copy-start.6
  2.1 1.5 %copy-start.3 = (bf16[2,2,2,256,256]{4,3,2,1,0:T(8,128)(2,1)S(1)}, bf16[2,2,2,256,256]{4,3,2,1,0:T(8,128)(2,1)}, u32[]{:S(2)}) copy-start(bf16[2,2,2,256,256]{4,3,2,1,0:T(8,128)(2,1)} %inc_ref.3) | copy-start | bytes 3145732
  2.5 4.9 %copy-start.2 = (bf16[2,2,256,256]{3,2,1,0:T(8,128)(2,1)S(1)}, bf16[2,2,256,256]{3,2,1,0:T(8,128)(2,1)}, u32[]{:S(2)}) copy-start(bf16[2,2,256,256]{3,2,1,0:T(8,128)(2,1)} %own_ref.5) | copy-start | bytes 1572868
  3.6 3.7 %copy-start.5 = (s32[2,2]{1,0:T(2,128)S(1)}, s32[2,2]{1,0:T(2,128)}, u32[]{:S(2)}) copy-start(s32[2,2]{1,0:T(2,128)} %anchor_ref.7) | copy-start | bytes 52
  3.6 31.7 %copy-start = (bf16[4,256,256]{2,1,0:T(8,128)(2,1)S(1)}, bf16[4,256,256]{2,1,0:T(8,128)(2,1)}, u32[]{:S(2)}) copy-start(bf16[4,256,256]{2,1,0:T(8,128)(2,1)} %constant.2.clone.tab_ref) | copy-start | bytes 1572868
  3.6 31.7 %copy-start.4 = (bf16[2,2,256,256]{3,2,1,0:T(8,128)(2,1)S(1)}, bf16[2,2,256,256]{3,2,1,0:T(8,128)(2,1)}, u32[]{:S(2)}) copy-start(bf16[2,2,256,256]{3,2,1,0:T(8,128)(2,1)} %wave_in.1) | copy-start | bytes 1572868
  3.7 26.6 %collective-permute-start.11 = (bf16[2,2,2,256,256]{4,3,2,1,0:T(8,128)(2,1)S(1)}, bf16[2,2,2,256,256]{4,3,2,1,0:T(8,128)(2,1)S(1)}, u32[]{:S(2)}, u32[]{:S(2)}) collective-permute-start(bf16[2,2,2,256,256]{4,3,2,1,0:T(8,128)(2,1)S(1)} %copy-done.3), channel_id=1, source_target_pairs={{0,8},{8,0},{16,24},{24,16},{1,9},{9,1},{17,25},{25,17},{2,10},{10... | collective-permute-start | bytes 3145736 | tf_op jit(solution)/shard_map/ppermute | solution.py:437
  3.7 2.9 %collective-permute-start.7 = (bf16[2,2,128,128]{3,2,1,0:T(8,128)(2,1)S(1)}, bf16[2,2,128,128]{3,2,1,0:T(8,128)(2,1)S(1)}, u32[]{:S(2)}, u32[]{:S(2)}) collective-permute-start(bf16[2,2,128,128]{3,2,1,0:T(8,128)(2,1)S(1)} %get-tuple-element.68), channel_id=1, source_target_pairs={{8,11},{9,10},{10,9},{11,8},{12,15},{13,14},{14,13},{15,12},{24,27... | collective-permute-start | bytes 393224 | tf_op jit(solution)/shard_map/ppermute | solution.py:408
  4.5 2.8 %collective-permute-start.5 = (bf16[2,2,256,128]{3,2,1,0:T(8,128)(2,1)S(1)}, bf16[2,2,256,128]{3,2,1,0:T(8,128)(2,1)S(1)}, u32[]{:S(2)}, u32[]{:S(2)}) collective-permute-start(bf16[2,2,256,128]{3,2,1,0:T(8,128)(2,1)S(1)} %get-tuple-element.66), channel_id=1, source_target_pairs={{8,9},{9,8},{10,11},{11,10},{12,13},{13,12},{14,15},{15,14},{24,25... | collective-permute-start | bytes 786440 | tf_op jit(solution)/shard_map/ppermute | solution.py:408
  5.2 2.1 %collective-permute-start.6 = (bf16[2,2,128,256]{3,2,1,0:T(8,128)(2,1)S(1)}, bf16[2,2,128,256]{3,2,1,0:T(8,128)(2,1)S(1)}, u32[]{:S(2)}, u32[]{:S(2)}) collective-permute-start(bf16[2,2,128,256]{3,2,1,0:T(8,128)(2,1)S(1)} %get-tuple-element.67), channel_id=1, source_target_pairs={{8,10},{9,11},{10,8},{11,9},{12,14},{13,15},{14,12},{15,13},{24,26... | collective-permute-start | bytes 786440 | tf_op jit(solution)/shard_map/ppermute | solution.py:408
  5.9 1.4 %collective-permute-start.8 = (bf16[2,2,128,256]{3,2,1,0:T(8,128)(2,1)S(1)}, bf16[2,2,128,256]{3,2,1,0:T(8,128)(2,1)S(1)}, u32[]{:S(2)}, u32[]{:S(2)}) collective-permute-start(bf16[2,2,128,256]{3,2,1,0:T(8,128)(2,1)S(1)} %get-tuple-element.69), channel_id=1, source_target_pairs={{10,12},{11,13},{12,10},{13,11},{26,28},{27,29},{28,26},{29,27}} | collective-permute-start | bytes 786440 | tf_op jit(solution)/shard_map/ppermute | solution.py:408
  6.6 0.7 collective-permute-start.9
  7.9 20.3 %collective-permute-start.10 = (bf16[2,2,256,256]{3,2,1,0:T(8,128)(2,1)S(1)}, bf16[2,2,256,256]{3,2,1,0:T(8,128)(2,1)S(1)}, u32[]{:S(2)}, u32[]{:S(2)}) collective-permute-start(bf16[2,2,256,256]{3,2,1,0:T(8,128)(2,1)S(1)} %get-tuple-element.72), channel_id=1, source_target_pairs={{8,0},{24,16},{9,1},{25,17},{10,2},{26,18},{11,3},{27,19},{12,4},{... | collective-permute-start | bytes 1572872 | tf_op jit(solution)/shard_map/ppermute | solution.py:421
  9.2 28.7 %collective-permute-start = (bf16[2,2,256,128]{3,2,1,0:T(8,128)(2,1)S(1)}, bf16[2,2,256,128]{3,2,1,0:T(8,128)(2,1)S(1)}, u32[]{:S(2)}, u32[]{:S(2)}) collective-permute-start(bf16[2,2,256,128]{3,2,1,0:T(8,128)(2,1)S(1)} %get-tuple-element.66), channel_id=1, source_target_pairs={{0,1},{1,0},{2,3},{3,2},{4,5},{5,4},{6,7},{7,6},{16,17},{17,16},{1... | collective-permute-start | bytes 786440 | tf_op jit(solution)/shard_map/ppermute | solution.py:408
  12.7 25.3 %collective-permute-start.1 = (bf16[2,2,128,256]{3,2,1,0:T(8,128)(2,1)S(1)}, bf16[2,2,128,256]{3,2,1,0:T(8,128)(2,1)S(1)}, u32[]{:S(2)}, u32[]{:S(2)}) collective-permute-start(bf16[2,2,128,256]{3,2,1,0:T(8,128)(2,1)S(1)} %get-tuple-element.67), channel_id=1, source_target_pairs={{0,2},{1,3},{2,0},{3,1},{4,6},{5,7},{6,4},{7,5},{16,18},{17,19},{1... | collective-permute-start | bytes 786440 | tf_op jit(solution)/shard_map/ppermute | solution.py:408
  16.2 21.8 %collective-permute-start.3 = (bf16[2,2,128,256]{3,2,1,0:T(8,128)(2,1)S(1)}, bf16[2,2,128,256]{3,2,1,0:T(8,128)(2,1)S(1)}, u32[]{:S(2)}, u32[]{:S(2)}) collective-permute-start(bf16[2,2,128,256]{3,2,1,0:T(8,128)(2,1)S(1)} %get-tuple-element.69), channel_id=1, source_target_pairs={{2,4},{3,5},{4,2},{5,3},{18,20},{19,21},{20,18},{21,19}} | collective-permute-start | bytes 786440 | tf_op jit(solution)/shard_map/ppermute | solution.py:408
  28.3 7.7 %collective-permute-start.2 = (bf16[2,2,128,128]{3,2,1,0:T(8,128)(2,1)S(1)}, bf16[2,2,128,128]{3,2,1,0:T(8,128)(2,1)S(1)}, u32[]{:S(2)}, u32[]{:S(2)}) collective-permute-start(bf16[2,2,128,128]{3,2,1,0:T(8,128)(2,1)S(1)} %get-tuple-element.68), channel_id=1, source_target_pairs={{0,3},{1,2},{2,1},{3,0},{4,7},{5,6},{6,5},{7,4},{16,19},{17,18},{1... | collective-permute-start | bytes 393224 | tf_op jit(solution)/shard_map/ppermute | solution.py:408
  30.2 7.8 %collective-permute-start.4 = (bf16[2,2,128,128]{3,2,1,0:T(8,128)(2,1)S(1)}, bf16[2,2,128,128]{3,2,1,0:T(8,128)(2,1)S(1)}, u32[]{:S(2)}, u32[]{:S(2)}) collective-permute-start(bf16[2,2,128,128]{3,2,1,0:T(8,128)(2,1)S(1)} %get-tuple-element.70), channel_id=1, source_target_pairs={{2,5},{3,4},{4,3},{5,2},{18,21},{19,20},{20,19},{21,18}} | collective-permute-start | bytes 393224 | tf_op jit(solution)/shard_map/ppermute | solution.py:408
  40.8 2.8 %collective-permute-start.12 = (bf16[2,2,256,256]{3,2,1,0:T(8,128)(2,1)S(1)}, bf16[2,2,256,256]{3,2,1,0:T(8,128)(2,1)S(1)}, u32[]{:S(2)}, u32[]{:S(2)}) collective-permute-start(bf16[2,2,256,256]{3,2,1,0:T(8,128)(2,1)S(1)} %get-tuple-element.85), channel_id=1, source_target_pairs={{0,8},{16,24},{1,9},{17,25},{2,10},{18,26},{3,11},{19,27},{4,12},{... | collective-permute-start | bytes 1572872 | tf_op jit(solution)/shard_map/ppermute | solution.py:421
  43.7 14.3 %collective-permute-start.13 = (s32[264,256]{1,0:T(8,128)S(1)}, s32[264,256]{1,0:T(8,128)S(1)}, u32[]{:S(2)}, u32[]{:S(2)}) collective-permute-start(s32[264,256]{1,0:T(8,128)S(1)} %get-tuple-element.87), channel_id=1, source_target_pairs={{16,0},{24,8},{17,1},{25,9},{18,2},{26,10},{19,3},{27,11},{20,4},{... | collective-permute-start | bytes 811016 | tf_op jit(solution)/shard_map/ppermute | solution.py:483
  64.3 4.6 %collective-permute-start.14 = (f32[2,2,256,256]{3,2,1,0:T(8,128)S(1)}, f32[2,2,256,256]{3,2,1,0:T(8,128)S(1)}, u32[]{:S(2)}, u32[]{:S(2)}) collective-permute-start(f32[2,2,256,256]{3,2,1,0:T(8,128)S(1)} %get-tuple-element.91.mine_ref), channel_id=1, source_target_pairs={{8,0},{24,16},{9,1},{25,17},{10,2},{26,18},{11,3},{27,19},{12,4},{... | collective-permute-start | bytes 3145736 | tf_op jit(solution)/shard_map/ppermute | solution.py:421
  65.6 15.2 %collective-permute-start.20 = (f32[2,2,256,256]{3,2,1,0:T(8,128)S(1)}, f32[2,2,256,256]{3,2,1,0:T(8,128)S(1)}, u32[]{:S(2)}, u32[]{:S(2)}) collective-permute-start(f32[2,2,256,256]{3,2,1,0:T(8,128)S(1)} %get-tuple-element.98.mine_ref), channel_id=1, source_target_pairs={{0,8},{16,24},{1,9},{17,25},{2,10},{18,26},{3,11},{19,27},{4,12},{... | collective-permute-start | bytes 3145736 | tf_op jit(solution)/shard_map/ppermute | solution.py:421
  72.7 18.6 %collective-permute-start.15 = (s32[2,264,128]{2,1,0:T(8,128)S(1)}, s32[2,264,128]{2,1,0:T(8,128)S(1)}, u32[]{:S(2)}, u32[]{:S(2)}) collective-permute-start(s32[2,264,128]{2,1,0:T(8,128)S(1)} %get-tuple-element.93), channel_id=1, source_target_pairs={{0,1},{1,0},{2,3},{3,2},{4,5},{5,4},{6,7},{7,6},{16,17},{17,16},{1... | collective-permute-start | bytes 811016 | tf_op jit(solution)/shard_map/ppermute | solution.py:408
  75.1 9.9 %collective-permute-start.17 = (s32[2,136,128]{2,1,0:T(8,128)S(1)}, s32[2,136,128]{2,1,0:T(8,128)S(1)}, u32[]{:S(2)}, u32[]{:S(2)}) collective-permute-start(s32[2,136,128]{2,1,0:T(8,128)S(1)} %get-tuple-element.95), channel_id=1, source_target_pairs={{0,3},{1,2},{2,1},{3,0},{4,7},{5,6},{6,5},{7,4},{16,19},{17,18},{1... | collective-permute-start | bytes 417800 | tf_op jit(solution)/shard_map/ppermute | solution.py:408
  77.1 9.9 %collective-permute-start.19 = (s32[2,136,128]{2,1,0:T(8,128)S(1)}, s32[2,136,128]{2,1,0:T(8,128)S(1)}, u32[]{:S(2)}, u32[]{:S(2)}) collective-permute-start(s32[2,136,128]{2,1,0:T(8,128)S(1)} %get-tuple-element.97), channel_id=1, source_target_pairs={{2,5},{3,4},{4,3},{5,2},{18,21},{19,20},{20,19},{21,18}} | collective-permute-start | bytes 417800 | tf_op jit(solution)/shard_map/ppermute | solution.py:408
  81.3 8.5 %collective-permute-start.23 = (s32[2,136,128]{2,1,0:T(8,128)S(1)}, s32[2,136,128]{2,1,0:T(8,128)S(1)}, u32[]{:S(2)}, u32[]{:S(2)}) collective-permute-start(s32[2,136,128]{2,1,0:T(8,128)S(1)} %get-tuple-element.102), channel_id=1, source_target_pairs={{8,11},{9,10},{10,9},{11,8},{12,15},{13,14},{14,13},{15,12},{24,27... | collective-permute-start | bytes 417800 | tf_op jit(solution)/shard_map/ppermute | solution.py:408
  82.0 8.6 %collective-permute-start.25 = (s32[2,136,128]{2,1,0:T(8,128)S(1)}, s32[2,136,128]{2,1,0:T(8,128)S(1)}, u32[]{:S(2)}, u32[]{:S(2)}) collective-permute-start(s32[2,136,128]{2,1,0:T(8,128)S(1)} %get-tuple-element.104), channel_id=1, source_target_pairs={{10,13},{11,12},{12,11},{13,10},{26,29},{27,28},{28,27},{29,26}} | collective-permute-start | bytes 417800 | tf_op jit(solution)/shard_map/ppermute | solution.py:408
  85.0 9.1 %collective-permute-start.16 = (s32[2,136,256]{2,1,0:T(8,128)S(1)}, s32[2,136,256]{2,1,0:T(8,128)S(1)}, u32[]{:S(2)}, u32[]{:S(2)}) collective-permute-start(s32[2,136,256]{2,1,0:T(8,128)S(1)} %get-tuple-element.94), channel_id=1, source_target_pairs={{0,2},{1,3},{2,0},{3,1},{4,6},{5,7},{6,4},{7,5},{16,18},{17,19},{1... | collective-permute-start | bytes 835592 | tf_op jit(solution)/shard_map/ppermute | solution.py:408
  87.0 9.9 %collective-permute-start.18 = (s32[2,136,256]{2,1,0:T(8,128)S(1)}, s32[2,136,256]{2,1,0:T(8,128)S(1)}, u32[]{:S(2)}, u32[]{:S(2)}) collective-permute-start(s32[2,136,256]{2,1,0:T(8,128)S(1)} %get-tuple-element.96), channel_id=1, source_target_pairs={{2,4},{3,5},{4,2},{5,3},{18,20},{19,21},{20,18},{21,19}} | collective-permute-start | bytes 835592 | tf_op jit(solution)/shard_map/ppermute | solution.py:408
  89.9 7.0 %collective-permute-start.22 = (s32[2,136,256]{2,1,0:T(8,128)S(1)}, s32[2,136,256]{2,1,0:T(8,128)S(1)}, u32[]{:S(2)}, u32[]{:S(2)}) collective-permute-start(s32[2,136,256]{2,1,0:T(8,128)S(1)} %get-tuple-element.101), channel_id=1, source_target_pairs={{8,10},{9,11},{10,8},{11,9},{12,14},{13,15},{14,12},{15,13},{24,26... | collective-permute-start | bytes 835592 | tf_op jit(solution)/shard_map/ppermute | solution.py:408
  90.6 6.3 %collective-permute-start.24 = (s32[2,136,256]{2,1,0:T(8,128)S(1)}, s32[2,136,256]{2,1,0:T(8,128)S(1)}, u32[]{:S(2)}, u32[]{:S(2)}) collective-permute-start(s32[2,136,256]{2,1,0:T(8,128)S(1)} %get-tuple-element.103), channel_id=1, source_target_pairs={{10,12},{11,13},{12,10},{13,11},{26,28},{27,29},{28,26},{29,27}} | collective-permute-start | bytes 835592 | tf_op jit(solution)/shard_map/ppermute | solution.py:408
  91.3 0.7 collective-permute-start.21

commit v4 on v2

--- a/solution.py
+++ b/solution.py
@@ -90,14 +90,16 @@
     return dot(high, table[0]) + (dot(low, table[0]) + dot(high, table[1]))
 
 
-def propagate(wave_ref, cos_ref, sin_ref, tab_ref):
-    size = wave_ref.shape[1]
-    half = size // 2
-    table = (tab_ref[0], tab_ref[1])
-    turned = (tab_ref[2], tab_ref[3])
-    parts = []
-    for c in range(2):
-        parts.append(right3(left3(table, wave_ref[c]), turned))
+def lefts(table, fields):
+    return [left3(table, field) for field in fields]
+
+
+def rights(fields, table):
+    return [right3(field, table) for field in fields]
+
+
+def middle(parts, cos_ref, sin_ref):
+    half = parts[0].shape[0] // 2
     row0 = lax.broadcasted_iota(jnp.int32, (half, half), 0) == 0
     col0 = lax.broadcasted_iota(jnp.int32, (half, half), 1) == 0
 
@@ -108,18 +110,26 @@
     bottom = spectrum_split(quadrant(1, 0), quadrant(1, 1), col0)
     out = [[None, None], [None, None]]
     for c in range(2):
-        turned_halves = []
+        turned = []
         for r, (re, im) in enumerate(spectrum_split(top[c], bottom[c], row0)):
             where = (slice(r * half, (r + 1) * half), slice(c * half, (c + 1) * half))
             cos, sin = cos_ref[where], sin_ref[where]
-            turned_halves.append((re * cos + im * sin, im * cos - re * sin))
-        out[0][c], out[1][c] = spectrum_join(turned_halves[0], turned_halves[1], row0)
+            turned.append((re * cos + im * sin, im * cos - re * sin))
+        out[0][c], out[1][c] = spectrum_join(turned[0], turned[1], row0)
     rows = [spectrum_join(out[r][0], out[r][1], col0) for r in range(2)]
-    for c in range(2):
-        field = jnp.concatenate(
+    return [
+        jnp.concatenate(
             [jnp.concatenate([rows[r][0][c], rows[r][1][c]], axis=1) for r in range(2)], axis=0
         )
-        wave_ref[c] = left3(turned, right3(field, table))
+        for c in range(2)
+    ]
+
+
+def propagate(parts, cos_ref, sin_ref, tab_ref):
+    table = (tab_ref[0], tab_ref[1])
+    turned = (tab_ref[2], tab_ref[3])
+    spectrum = middle(rights(lefts(table, parts), turned), cos_ref, sin_ref)
+    return lefts(turned, rights(spectrum, table))
 
 
 def take_window(ext_ref, at_x, at_y, patch):
@@ -147,18 +157,23 @@
     return jnp.exp2(first), jnp.exp2(exponent - first)
 
 
-def encode(real, imag):
-    top = jnp.maximum(jnp.abs(real), jnp.abs(imag))
+def exponent_of(top):
     top = jnp.max(jnp.max(top, axis=0, keepdims=True), axis=1, keepdims=True)
-    exponent = jnp.where(top > 0, jnp.ceil(jnp.log2(jnp.maximum(top, 1e-37))), 0.0)
+    return jnp.where(top > 0, jnp.ceil(jnp.log2(jnp.maximum(top, 1e-37))), 0.0)
+
+
+def encode(real, imag, exponent):
     scale, rest = two_powers(-exponent)
 
+    def root(value):
+        return value * lax.rsqrt(value)
+
     def code(value):
-        root = jnp.sqrt(jnp.sqrt(jnp.minimum(jnp.abs(value) * scale * rest, 1.0)))
-        whole = jnp.round(root * LEVELS).astype(jnp.int32)
+        size = jnp.minimum(jnp.maximum(jnp.abs(value) * scale * rest, 1e-30), 1.0)
+        whole = (root(root(size)) * LEVELS + 0.5).astype(jnp.int32)
         return jnp.where(value < 0, -whole, whole)
 
-    return (code(real) << 16) | (code(imag) & 0xFFFF), exponent.astype(jnp.int32)
+    return (code(real) << 16) | (code(imag) & 0xFFFF)
 
 
 def decode(packed, exponent):
@@ -173,11 +188,13 @@
     return value(packed >> 16), value((packed << 16) >> 16)
 
 
-def put_encoded(ref, at, real, imag):
-    packed, exponent = encode(real, imag)
+def put_encoded(ref, at, real, imag, exponent):
+    packed = encode(real, imag, exponent)
     rows, cols = packed.shape
     ref[at + (slice(0, rows), slice(None))] = packed
-    ref[at + (slice(rows, rows + SCALE_ROWS), slice(None))] = jnp.broadcast_to(exponent, (SCALE_ROWS, cols))
+    ref[at + (slice(rows, rows + SCALE_ROWS), slice(None))] = jnp.broadcast_to(
+        exponent.astype(jnp.int32), (SCALE_ROWS, cols)
+    )
 
 
 def get_encoded(ref, at):
@@ -226,27 +243,55 @@
         piece[...] = own_ref[:, :, pl.ds(row, rows), pl.ds(col, cols)]
 
 
-def window_kernel(kinds, anchor_ref, own_ref, *refs):
-    pieces, (mine_ref, other_ref, ext_ref) = refs[: len(kinds)], refs[len(kinds) :]
+def window_send_kernel(kinds, anchor_ref, own_ref, *refs):
+    pieces, (out_ref, ext_ref) = refs[: len(kinds)], refs[len(kinds) :]
     slab, _, tile, _ = own_ref.shape
     half = tile // 2
-    patch = mine_ref.shape[2]
+    at_x, at_y = corner_of(anchor_ref, 1 - core_index(), half, tile)
+
+    def one(index, _):
+        layer, c = index // 2, lax.rem(index, 2)
+        plane = ext_ref.at[layer, c]
+        plane[...] = jnp.zeros(plane.shape, plane.dtype)
+        plane[half : half + tile, half : half + tile] = own_ref[layer, c].astype(jnp.float32)
+        for kind, piece in zip(kinds, pieces):
+            row, col = halo_start(kind, half, tile)
+            rows, cols = piece.shape[2:]
+            plane[pl.ds(row, rows), pl.ds(col, cols)] = piece[layer, c].astype(jnp.float32)
+        out_ref[layer, c] = take_window(plane, at_x, at_y, out_ref.shape[2]).astype(out_ref.dtype)
+        return 0
+
+    lax.fori_loop(0, 2 * slab, one, 0)
+
+
+def window_own_kernel(tile, anchor_ref, ext_ref, out_ref):
+    slab = ext_ref.shape[0]
+    at_x, at_y = corner_of(anchor_ref, core_index(), tile // 2, tile)
+
+    def one(index, _):
+        layer, c = index // 2, lax.rem(index, 2)
+        window = take_window(ext_ref.at[layer, c], at_x, at_y, out_ref.shape[2])
+        out_ref[layer, c] = window.astype(out_ref.dtype)
+        return 0
+
+    lax.fori_loop(0, 2 * slab, one, 0)
+
+
+def incident_kernel(inc_ref, own_ref, other_ref, sems):
     core = core_index()
-    corners = [corner_of(anchor_ref, slot, half, tile) for slot in (core, 1 - core)]
-    ext_ref[...] = jnp.zeros_like(ext_ref)
-    for layer in range(slab):
-        for c in range(2):
-            ext_ref[half : half + tile, half : half + tile] = own_ref[layer, c].astype(jnp.float32)
-            for kind, piece in zip(kinds, pieces):
-                row, col = halo_start(kind, half, tile)
-                rows, cols = piece.shape[2:]
-                ext_ref[pl.ds(row, rows), pl.ds(col, cols)] = piece[layer, c].astype(jnp.float32)
-            for (at_x, at_y), out in zip(corners, (mine_ref, other_ref)):
-                out[layer, c] = take_window(ext_ref, at_x, at_y, patch).astype(out.dtype)
-
-
-def stage_kernel(stage, live_ref, wave_in, win_own, win_got, inc_own, inc_got, cos_ref, sin_ref, tab_ref,
-                 _keep_in, _send_in, keep_ref, send_ref, out_ref, wave_ref, term, sems):
+    copies = [
+        pltpu.make_async_copy(inc_ref.at[layer, slot], ref.at[layer], sems.at[layer, j])
+        for j, (slot, ref) in enumerate(((core, own_ref), (1 - core, other_ref)))
+        for layer in range(inc_ref.shape[0])
+    ]
+    for copy in copies:
+        copy.start()
+    for copy in copies:
+        copy.wait()
+
+
+def sweep_kernel(stage, live_ref, wave_in, win_own, win_got, inc_own, inc_got, cos_ref, sin_ref, tab_ref, *refs):
+    keep_ref, send_ref, out_ref, wave_ref, term, sems = refs[-6:]
     slab = win_own.shape[0]
     layers = 2 * slab
     core = core_index()
@@ -266,20 +311,31 @@
 
         def one(step, _):
             i = layers - 1 - step
-            owner = i // slab
             local = lax.rem(i, slab)
             slot = lax.rem(step, 2)
-            own = owner == core
+            own = i // slab == core
 
             @pl.when(step >= 2)
             def _():
                 leave(slot, keep_ref, 0).wait()
 
-            wr, wi = wave_ref[0], wave_ref[1]
-            er = jnp.where(own, inc_own[local, core, 0], inc_got[local, core, 0]).astype(jnp.float32)
-            ei = jnp.where(own, inc_own[local, core, 1], inc_got[local, core, 1]).astype(jnp.float32)
-            term[slot, 0] = er * wr + ei * wi
-            term[slot, 1] = er * wi - ei * wr
+            def add_term():
+                wr, wi = wave_ref[0], wave_ref[1]
+                er = jnp.where(own, inc_own[local, 0], inc_got[local, 0]).astype(jnp.float32)
+                ei = jnp.where(own, inc_own[local, 1], inc_got[local, 1]).astype(jnp.float32)
+                term[slot, 0] = er * wr + ei * wi
+                term[slot, 1] = er * wi - ei * wr
+
+            @pl.when(chip * layers + i > 0)
+            def _():
+                add_term()
+                wr, wi = wave_ref[0], wave_ref[1]
+                tr = jnp.where(own, win_own[local, 0], win_got[local, 0]).astype(jnp.float32)
+                ti = jnp.where(own, win_own[local, 1], win_got[local, 1]).astype(jnp.float32)
+                parts = [tr * wr + ti * wi, tr * wi - ti * wr]
+                wave_ref[0], wave_ref[1] = propagate(parts, cos_ref, sin_ref, tab_ref)
+
+            pl.when(chip * layers + i == 0)(add_term)
 
             @pl.when(own)
             def _():
@@ -289,52 +345,66 @@
             def _():
                 leave(slot, send_ref, local).start()
 
-            @pl.when(chip * layers + i > 0)
-            def _():
-                tr = jnp.where(own, win_own[local, 0], win_got[local, 0]).astype(jnp.float32)
-                ti = jnp.where(own, win_own[local, 1], win_got[local, 1]).astype(jnp.float32)
-                wave_ref[0] = tr * wr + ti * wi
-                wave_ref[1] = tr * wi - ti * wr
-                propagate(wave_ref, cos_ref, sin_ref, tab_ref)
-
             return 0
 
         lax.fori_loop(0, layers, one, 0)
         if stage < chips - 1:
-            put_encoded(out_ref, (), wave_ref[0], wave_ref[1])
+            wr, wi = wave_ref[0], wave_ref[1]
+            exponent = exponent_of(jnp.maximum(jnp.abs(wr), jnp.abs(wi)))
+            put_encoded(out_ref, (), wr, wi, exponent)
         for slot in range(2):
             leave(slot, keep_ref, 0).wait()
 
 
 def scatter_kernel(kinds, anchor_ref, mine_ref, other_ref, own_ref, *refs):
-    pieces, ext_ref = refs[:-1], refs[-1]
+    pieces, ext_ref, top_ref = refs[:-2], refs[-2], refs[-1]
     slab, _, patch, _ = mine_ref.shape
     tile = own_ref.shape[2]
     half = tile // 2
     core = core_index()
     corners = [corner_of(anchor_ref, slot, half, tile) for slot in (core, 1 - core)]
-    for layer in range(slab):
-        ext_ref[...] = jnp.zeros_like(ext_ref)
-        for c in range(2):
-            for (at_x, at_y), term in zip(corners, (mine_ref, other_ref)):
-                add_window(ext_ref.at[c], at_x, at_y, term[layer, c])
-            own_ref[layer, c] = ext_ref[c, half : half + tile, half : half + tile]
+    top_ref[...] = jnp.zeros_like(top_ref)
+
+    def add(index, _):
+        layer, c = index // 2, lax.rem(index, 2)
+        plane = ext_ref.at[layer, c]
+        plane[...] = jnp.zeros(plane.shape, plane.dtype)
+        bound = 0.0
+        for (at_x, at_y), term in zip(corners, (mine_ref, other_ref)):
+            value = term[layer, c]
+            add_window(plane, at_x, at_y, value)
+            bound = bound + jnp.max(jnp.abs(value), axis=0, keepdims=True)
+        top_ref[...] = jnp.maximum(top_ref[...], bound)
+        own_ref[layer, c] = plane[half : half + tile, half : half + tile]
+        return 0
+
+    lax.fori_loop(0, 2 * slab, add, 0)
+    exponent = exponent_of(top_ref[...])
+
+    def send(layer, _):
         for kind, piece in zip(kinds, pieces):
             row, col = halo_start(kind, half, tile)
             where = (pl.ds(row, piece.shape[1] - SCALE_ROWS), pl.ds(col, piece.shape[2]))
-            put_encoded(piece, (layer,), ext_ref[(0,) + where], ext_ref[(1,) + where])
+            put_encoded(piece, (layer,), ext_ref[(layer, 0) + where], ext_ref[(layer, 1) + where], exponent)
+        return 0
+
+    lax.fori_loop(0, slab, send, 0)
 
 
 def fold_kernel(kinds, own_ref, *refs):
     pieces, out_ref = refs[:-1], refs[-1]
-    slab, _, tile, _ = own_ref.shape
-    out_ref[...] = own_ref[...]
-    for layer in range(slab):
+    slab, _, tile, _ = out_ref.shape
+
+    def one(layer, _):
+        out_ref[layer] = own_ref[layer]
         for kind, piece in zip(kinds, pieces):
             row, col = rim_start(kind, tile // 2, tile)
             where = (pl.ds(row, piece.shape[1] - SCALE_ROWS), pl.ds(col, piece.shape[2]))
             for c, value in enumerate(get_encoded(piece, (layer,))):
                 out_ref[(layer, c) + where] += value
+        return 0
+
+    lax.fori_loop(0, slab, one, 0)
 
 
 def shards(transmission, incident, exit_adjoint, propagator_phase, scan_anchor, live_count):
@@ -348,6 +418,7 @@
     kinds = swap_kinds(n_x, n_y)
     params = pltpu.CompilerParams(vmem_limit_bytes=LIMIT)
     core_swap = swap_pairs(n_depth, 0)
+    shape_of = jax.ShapeDtypeStruct
 
     def call(kernel, out_shape, operands, name, scratch=(), **more):
         return pl.pallas_call(
@@ -362,77 +433,94 @@
     def rim_size(kind):
         return tile if kind[0] is None else half, tile if kind[1] is None else half
 
-    def swapped(value, kind):
-        return lax.ppermute(value, ("sx", "sy"), swap_list(n_x, n_y, *kind))
+    def swapped(values):
+        return [
+            lax.ppermute(value, ("sx", "sy"), swap_list(n_x, n_y, *kind)) for value, kind in zip(values, kinds)
+        ]
 
     rims = call(
         functools.partial(rims_kernel, kinds),
-        tuple(jax.ShapeDtypeStruct((slab, 2) + rim_size(kind), transmission.dtype) for kind in kinds),
+        tuple(shape_of((slab, 2) + rim_size(kind), transmission.dtype) for kind in kinds),
         (transmission,),
         "rims",
     )
-    halos = [swapped(value, kind) for value, kind in zip(rims, kinds)]
-    inc_got = lax.ppermute(incident, "depth", core_swap)
-
+    halos = swapped(rims)
+    propagator_phase, incident, _ = lax.optimization_barrier((propagator_phase, incident, rims))
+    inc_shape = shape_of((slab, 2, patch, patch), incident.dtype)
+    inc_own, inc_send = call(
+        incident_kernel,
+        (inc_shape, inc_shape),
+        (incident,),
+        "incident_split",
+        [pltpu.SemaphoreType.DMA((slab, 2))],
+        in_specs=[ANY],
+    )
     phase = folded_order(folded_order(propagator_phase, 0), 1)
     phase_cos, phase_sin = jnp.cos(phase), jnp.sin(phase)
     basis = dft_basis(patch)
     high = basis.astype(jnp.bfloat16)
     low = (basis - high.astype(np.float64)).astype(jnp.bfloat16)
     tables = jnp.asarray(np.stack([high, low, high.T, low.T]))
-    phase_cos, phase_sin, halos = lax.optimization_barrier((phase_cos, phase_sin, halos))
-
-    window_shape = jax.ShapeDtypeStruct((slab, 2, patch, patch), transmission.dtype)
-    win_own, win_send = call(
-        functools.partial(window_kernel, kinds),
-        (window_shape, window_shape),
+    phase_cos, phase_sin, inc_own, inc_send, halos = lax.optimization_barrier(
+        (phase_cos, phase_sin, inc_own, inc_send, halos)
+    )
+    inc_got = lax.ppermute(inc_send, "depth", core_swap)
+
+    window_shape = shape_of((slab, 2, patch, patch), transmission.dtype)
+    win_send, bordered = call(
+        functools.partial(window_send_kernel, kinds),
+        (window_shape, shape_of((slab, 2, extent, extent), f32)),
         (scan_anchor, transmission, *halos),
+        "windows_for_other",
+        in_specs=[SMEM] + [VMEM] * (1 + len(kinds)),
+    )
+    win_got = lax.ppermute(win_send, "depth", core_swap)
+    win_own = call(
+        functools.partial(window_own_kernel, tile),
+        window_shape,
+        (scan_anchor, bordered),
         "windows",
-        [pltpu.VMEM((extent, extent), f32)],
-        in_specs=[SMEM] + [VMEM] * (1 + len(kinds)),
-    )
-    win_got = lax.ppermute(win_send, "depth", core_swap)
+        in_specs=[SMEM, VMEM],
+    )
 
     wave = exit_adjoint
-    term_shape = jax.ShapeDtypeStruct((slab, 2, patch, patch), f32)
-    coded = jax.ShapeDtypeStruct((patch + SCALE_ROWS, patch), jnp.int32)
-    keep = jnp.zeros(term_shape.shape, f32)
-    send = jnp.zeros(term_shape.shape, f32)
+    term_shape = shape_of((slab, 2, patch, patch), f32)
+    coded = shape_of((patch + SCALE_ROWS, patch), jnp.int32)
+    terms = ()
     for stage in range(chips):
-        keep, send, wave = call(
-            functools.partial(stage_kernel, stage),
+        *terms, wave = call(
+            functools.partial(sweep_kernel, stage),
             (term_shape, term_shape, coded),
-            (live_count, wave, win_own, win_got, incident, inc_got, phase_cos, phase_sin, tables, keep, send),
+            (live_count, wave, win_own, win_got, inc_own, inc_got, phase_cos, phase_sin, tables, *terms),
             "sweep",
             [
                 pltpu.VMEM((2, patch, patch), f32),
                 pltpu.VMEM((2, 2, patch, patch), f32),
                 pltpu.SemaphoreType.DMA((2,)),
             ],
-            in_specs=[SMEM] + [VMEM] * 8 + [ANY, ANY],
+            in_specs=[SMEM] + [VMEM] * 8 + [ANY] * len(terms),
             out_specs=(ANY, ANY, VMEM),
-            input_output_aliases={9: 0, 10: 1},
+            input_output_aliases={9: 0, 10: 1} if stage else {},
         )
         if stage < chips - 1:
             source = chips - 1 - stage
             wave = lax.ppermute(wave, "depth", [(2 * source + c, 2 * source - 2 + c) for c in range(2)])
 
+    keep, send = terms
     got = lax.ppermute(send, "depth", core_swap)
-    own_shape = jax.ShapeDtypeStruct((slab, 2, tile, tile), f32)
+    own_shape = shape_of((slab, 2, tile, tile), f32)
     coded_rims = tuple(
-        jax.ShapeDtypeStruct((slab, rim_size(kind)[0] + SCALE_ROWS, rim_size(kind)[1]), jnp.int32)
-        for kind in kinds
+        shape_of((slab, rim_size(kind)[0] + SCALE_ROWS, rim_size(kind)[1]), jnp.int32) for kind in kinds
     )
     own, *beyond = call(
         functools.partial(scatter_kernel, kinds),
         (own_shape,) + coded_rims,
         (scan_anchor, keep, got),
         "scatter",
-        [pltpu.VMEM((2, extent, extent), f32)],
+        [pltpu.VMEM((slab, 2, extent, extent), f32), pltpu.VMEM((1, patch), f32)],
         in_specs=[SMEM, VMEM, VMEM],
     )
-    arrived = [swapped(value, kind) for value, kind in zip(beyond, kinds)]
-    return call(functools.partial(fold_kernel, kinds), own_shape, (own, *arrived), "fold")
+    return call(functools.partial(fold_kernel, kinds), own_shape, (own, *swapped(beyond)), "fold")
 
 
 def solution(mesh):

time: 78 us -> 70.3 us (0.901); the launches traced: 76.5 us -> 70 us
  waiting for transfers between devices: 34.5 us -> 28.2 us
  starting transfers between devices: 18.3 us -> 19.7 us
  Pallas kernels: 16.6 us -> 15.6 us
    ppermute x11, waiting for transfers between devices: 13.8 us -> 10.8 us  [the longest x10 10.8 us: swapped(): lax.ppermute(value, ('sx', 'sy'), swap_list(n_x, n_y, *kind))]
    ppermute x1, waiting for transfers between devices: 16.8 us -> 14.7 us  [shards(): lax.ppermute(wave, 'depth', [(2 * source + c, 2 * source - 2 + c) for c i...]
    ppermute x1, waiting for transfers between devices: 1.25 us -> 0.01 us  [shards(): win_got = lax.ppermute(win_send, 'depth', core_swap)]
    pallas_call x6 -> x8, Pallas kernels: 16.6 us -> 15.6 us  [call(): pl.pallas_call(kernel, out_shape=out_shape, scratch_shapes=list(scratch),...]
    slice x1, local copies, waits for them, and re-layouts: 0.01 us -> 0.92 us  [folded_order(): low = lax.slice_in_dim(array, 0, half, axis=axis)]
    ppermute x11, starting transfers between devices: 16.9 us -> 17.8 us  [the longest x10 17.8 us: swapped(): lax.ppermute(value, ('sx', 'sy'), swap_list(n_x, n_y, *kind))]
    slice x1, local copies, waits for them, and re-layouts: 0.01 us -> 0.92 us  [folded_order(): lax.slice_in_dim(array, half + 1, 2 * half, axis=axis)]
    rev x2, local copies, waits for them, and re-layouts: 1.11 us -> 0.3 us  [folded_order(): lax.rev(lax.slice_in_dim(array, half + 1, 2 * half, axis=axis), (axis,))]
  transfers between devices with their start and end apart: 14 -> 14, of which waited for: 8 -> 7; matrix products, arithmetic and copies ran while one was open for 4% -> 5% of each run, Pallas kernels for 4% -> 6%
where the time goes in v4:
time: 70.3 us; the launch traced here: 70 us
  waiting for transfers between devices  28.2 us (40%)
  starting transfers between devices  19.7 us (28%)
  Pallas kernels  15.6 us (22%)
  local copies, waits for them, and re-layouts  4.42 us (6%)
  other arithmetic  1.23 us (2%)
  between operations  0.86 us (1%)
    ppermute x10, starting transfers between devices, swapped(): lax.ppermute(value, ('sx', 'sy'), swap_list(n_x, n_y, *kind))  17.8 us
    pallas_call x8, Pallas kernels, call(): pl.pallas_call(kernel, out_shape=out_shape, scratch_shapes=list(scratch),...  15.6 us
    ppermute x1, waiting for transfers between devices, shards(): lax.ppermute(wave, 'depth', [(2 * source + c, 2 * source - 2 + c) for c i...  14.7 us
    ppermute x10, waiting for transfers between devices, swapped(): lax.ppermute(value, ('sx', 'sy'), swap_list(n_x, n_y, *kind))  10.8 us
    ppermute x1, waiting for transfers between devices, shards(): got = lax.ppermute(send, 'depth', core_swap)  2.65 us
    unnamed x12, local copies, waits for them, and re-layouts  2.29 us
  transfers between devices with their start and end apart: 14, of which 7 were waited for; matrix products, arithmetic and copies ran while one was open for 5% of the time, Pallas kernels for 6%

profile of v4, /device:TPU:16, one launch (start us, length us, event | category | flops | bytes accessed | tf_op | source)
XLA Modules:
  0.0 70.0 jit_solution(2234884191457166207)
XLA Ops:
  0.0 1.0 %copy-done = bf16[2,2,256,256]{3,2,1,0:T(8,128)(2,1)S(1)} copy-done((bf16[2,2,256,256]{3,2,1,0:T(8,128)(2,1)S(1)}, bf16[2,2,256,256]{3,2,1,0:T(8,128)(2,1)}, u32[]{:S(2)}) %copy-start) | copy-done | bytes 524312
  1.0 0.1 rims.1
  1.2 2.6 %collective-permute-start.2 = (bf16[2,2,128,128]{3,2,1,0:T(8,128)(2,1)S(1)}, bf16[2,2,128,128]{3,2,1,0:T(8,128)(2,1)S(1)}, u32[]{:S(2)}, u32[]{:S(2)}) collective-permute-start(bf16[2,2,128,128]{3,2,1,0:T(8,128)(2,1)S(1)} %get-tuple-element.38), channel_id=1, source_target_pairs={{0,3},{1,2},{2,1},{3,0},{4,7},{5,6},{6,5},{7,4},{8,11},{9,10},{10,... | collective-permute-start | bytes 393224 | tf_op jit(solution)/shard_map/ppermute | solution.py:438
  3.8 1.9 %collective-permute-start.4 = (bf16[2,2,128,128]{3,2,1,0:T(8,128)(2,1)S(1)}, bf16[2,2,128,128]{3,2,1,0:T(8,128)(2,1)S(1)}, u32[]{:S(2)}, u32[]{:S(2)}) collective-permute-start(bf16[2,2,128,128]{3,2,1,0:T(8,128)(2,1)S(1)} %get-tuple-element.40), channel_id=1, source_target_pairs={{2,5},{3,4},{4,3},{5,2},{10,13},{11,12},{12,11},{13,10},{18,21},{1... | collective-permute-start | bytes 393224 | tf_op jit(solution)/shard_map/ppermute | solution.py:438
  5.7 0.8 %collective-permute-start = (bf16[2,2,256,128]{3,2,1,0:T(8,128)(2,1)S(1)}, bf16[2,2,256,128]{3,2,1,0:T(8,128)(2,1)S(1)}, u32[]{:S(2)}, u32[]{:S(2)}) collective-permute-start(bf16[2,2,256,128]{3,2,1,0:T(8,128)(2,1)S(1)} %get-tuple-element.36), channel_id=1, source_target_pairs={{0,1},{1,0},{2,3},{3,2},{4,5},{5,4},{6,7},{7,6},{8,9},{9,8},{10,11... | collective-permute-start | bytes 786440 | tf_op jit(solution)/shard_map/ppermute | solution.py:438
  6.5 0.0 collective-permute-start.1
  6.5 4.6 %collective-permute-start.3 = (bf16[2,2,128,256]{3,2,1,0:T(8,128)(2,1)S(1)}, bf16[2,2,128,256]{3,2,1,0:T(8,128)(2,1)S(1)}, u32[]{:S(2)}, u32[]{:S(2)}) collective-permute-start(bf16[2,2,128,256]{3,2,1,0:T(8,128)(2,1)S(1)} %get-tuple-element.39), channel_id=1, source_target_pairs={{2,4},{3,5},{4,2},{5,3},{10,12},{11,13},{12,10},{13,11},{18,20},{1... | collective-permute-start | bytes 786440 | tf_op jit(solution)/shard_map/ppermute | solution.py:438
  11.1 0.9 %slice.17 = f32[127,256]{1,0:T(8,128)S(1)} slice(f32[256,256]{1,0:T(8,128)} %param.10), slice={[129:256], [0:256]} | slice | bytes 260096 | tf_op jit(solution)/shard_map/slice | solution.py:61
  12.1 0.9 %slice.16 = f32[129,256]{1,0:T(8,128)S(1)} slice(f32[256,256]{1,0:T(8,128)} %param.10), slice={[0:129], [0:256]} | slice | bytes 264192 | tf_op jit(solution)/shard_map/slice | solution.py:59
  13.0 0.1 rev.6
  13.1 0.1 pad_maximum_fusion.1
  13.2 0.2 rev.7
  13.4 0.0 copy-start.3
  13.4 1.2 %copy-done.3 = bf16[2,2,2,256,256]{4,3,2,1,0:T(8,128)(2,1)S(1)} copy-done((bf16[2,2,2,256,256]{4,3,2,1,0:T(8,128)(2,1)S(1)}, bf16[2,2,2,256,256]{4,3,2,1,0:T(8,128)(2,1)}, u32[]{:S(2)}) %copy-start.3) | copy-done | bytes 1048600
  14.7 0.1 incident_split.1
  14.8 1.1 %fusion = (f32[256,256]{1,0:T(8,128)S(1)}, f32[256,256]{1,0:T(8,128)S(1)}) fusion(f32[256,127]{1,0:T(8,128)S(1)} %rev.7, f32[256,129]{1,0:T(8,128)S(1)} %slice_maximum_fusion), kind=kLoop, calls=%fused_computation.2 | loop fusion | flops 65536 | bytes 786432 | tf_op jit(solution)/shard_map/sin | solution.py:459
  15.9 0.0 collective-permute-done.2.refs_2_
  15.9 0.0 collective-permute-done.4.refs_4_
  15.9 0.4 collective-permute-done.refs_0_
  16.3 0.0 collective-permute-done.1.refs_1_
  16.3 0.3 collective-permute-done.3.refs_3_
  16.6 0.0 collective-permute-start.6
  16.6 0.0 copy-done.1
  16.6 0.0 copy-done.5
  16.6 2.1 %windows_for_other.1 = (bf16[2,2,256,256]{3,2,1,0:T(8,128)(2,1)S(1)}, f32[2,2,512,512]{3,2,1,0:T(8,128)S(1)}) custom-call(s32[2,2]{1,0:T(2,128)S(1)} %copy-done.5, bf16[2,2,256,256]{3,2,1,0:T(8,128)(2,1)S(1)} %copy-done.1, bf16[2,2,256,128]{3,2,1,0:T(8,128)(2,1)S(1)} %collective-permute-done.refs_0_, ...), custom_call_target="tpu_custom_call" | custom-call | tf_op jit(solution)/shard_map/windows_for_other/pallas_call | solution.py:424
  18.7 0.6 collective-permute-start.5
  19.9 1.7 %windows.1.win_own = bf16[2,2,256,256]{3,2,1,0:T(8,128)(2,1)S(1)} custom-call(s32[2,2]{1,0:T(2,128)S(1)} %copy-done.5, f32[2,2,512,512]{3,2,1,0:T(8,128)S(1)} %get-tuple-element.50.ext_ref), custom_call_target="tpu_custom_call" | custom-call | tf_op jit(solution)/shard_map/windows/pallas_call | solution.py:424
  21.6 0.0 collective-permute-done.6.inc_got
  21.6 0.0 collective-permute-done.5.win_got
  21.6 0.0 copy-done.2
  21.6 0.0 copy-done.4
  21.7 1.3 %collective-permute-start.7 = (s32[264,256]{1,0:T(8,128)S(1)}, s32[264,256]{1,0:T(8,128)S(1)}, u32[]{:S(2)}, u32[]{:S(2)}) collective-permute-start(s32[264,256]{1,0:T(8,128)S(1)} %get-tuple-element.56), channel_id=1, source_target_pairs={{16,0},{24,8},{17,1},{25,9},{18,2},{26,10},{19,3},{27,11},{20,4},{... | collective-permute-start | bytes 811016 | tf_op jit(solution)/shard_map/ppermute | solution.py:507
  23.0 14.7 %collective-permute-done.7.wave_in = s32[264,256]{1,0:T(8,128)S(1)} collective-permute-done((s32[264,256]{1,0:T(8,128)S(1)}, s32[264,256]{1,0:T(8,128)S(1)}, u32[]{:S(2)}, u32[]{:S(2)}) %collective-permute-start.7) | collective-permute-done | bytes 270368 | tf_op jit(solution)/shard_map/ppermute | solution.py:507
  37.7 5.7 %sweep.3 = (f32[2,2,256,256]{3,2,1,0:T(8,128)S(1)}, f32[2,2,256,256]{3,2,1,0:T(8,128)S(1)}, s32[264,256]{1,0:T(8,128)}) custom-call(s32[1]{0:T(128)S(6)} %copy.12.live_ref, s32[264,256]{1,0:T(8,128)S(1)} %collective-permute-done.7.wave_in, bf16[2,2,256,256]{3,2,1,0:T(8,128)(2,1)S(1)} %windows.1.win_own, ...), custom_call_target="tpu_custom_call", output_to_operand_aliasing={{0}: (9, {}), {1}: (10, {})} | custom-call | tf_op jit(solution)/shard_map/sweep/pallas_call | solution.py:424
  43.4 0.1 collective-permute-start.8
  43.5 2.6 %collective-permute-done.8.other_ref = f32[2,2,256,256]{3,2,1,0:T(8,128)S(1)} collective-permute-done((f32[2,2,256,256]{3,2,1,0:T(8,128)S(1)}, f32[2,2,256,256]{3,2,1,0:T(8,128)S(1)}, u32[]{:S(2)}, u32[]{:S(2)}) %collective-permute-start.8) | collective-permute-done | bytes 1048608 | tf_op jit(solution)/shard_map/ppermute | solution.py:510
  46.2 3.8 %scatter.1 = (f32[2,2,256,256]{3,2,1,0:T(8,128)S(1)}, s32[2,264,128]{2,1,0:T(8,128)S(1)}, s32[2,136,256]{2,1,0:T(8,128)S(1)}, s32[2,136,128]{2,1,0:T(8,128)S(1)}...) custom-call(s32[2,2]{1,0:T(2,128)S(1)} %copy-done.5, f32[2,2,256,256]{3,2,1,0:T(8,128)S(1)} %get-tuple-element.59.mine_ref, ...), custom_call_target="tpu_custom_call" | custom-call | tf_op jit(solution)/shard_map/scatter/pallas_call | solution.py:424
  50.0 0.1 collective-permute-start.10
  50.0 3.6 %collective-permute-start.12 = (s32[2,136,256]{2,1,0:T(8,128)S(1)}, s32[2,136,256]{2,1,0:T(8,128)S(1)}, u32[]{:S(2)}, u32[]{:S(2)}) collective-permute-start(s32[2,136,256]{2,1,0:T(8,128)S(1)} %get-tuple-element.65), channel_id=1, source_target_pairs={{2,4},{3,5},{4,2},{5,3},{10,12},{11,13},{12,10},{13,11},{18,20},{1... | collective-permute-start | bytes 835592 | tf_op jit(solution)/shard_map/ppermute | solution.py:438
  53.7 0.6 collective-permute-start.9
  54.2 0.0 collective-permute-start.11
  54.2 3.5 %collective-permute-start.13 = (s32[2,136,128]{2,1,0:T(8,128)S(1)}, s32[2,136,128]{2,1,0:T(8,128)S(1)}, u32[]{:S(2)}, u32[]{:S(2)}) collective-permute-start(s32[2,136,128]{2,1,0:T(8,128)S(1)} %get-tuple-element.66), channel_id=1, source_target_pairs={{2,5},{3,4},{4,3},{5,2},{10,13},{11,12},{12,11},{13,10},{18,21},{1... | collective-permute-start | bytes 417800 | tf_op jit(solution)/shard_map/ppermute | solution.py:438
  57.8 6.0 %collective-permute-done.11.refs_2_ = s32[2,136,128]{2,1,0:T(8,128)S(1)} collective-permute-done((s32[2,136,128]{2,1,0:T(8,128)S(1)}, s32[2,136,128]{2,1,0:T(8,128)S(1)}, u32[]{:S(2)}, u32[]{:S(2)}) %collective-permute-start.11) | collective-permute-done | bytes 139296 | tf_op jit(solution)/shard_map/ppermute | solution.py:438
  63.8 1.6 %collective-permute-done.13.refs_4_ = s32[2,136,128]{2,1,0:T(8,128)S(1)} collective-permute-done((s32[2,136,128]{2,1,0:T(8,128)S(1)}, s32[2,136,128]{2,1,0:T(8,128)S(1)}, u32[]{:S(2)}, u32[]{:S(2)}) %collective-permute-start.13) | collective-permute-done | bytes 139296 | tf_op jit(solution)/shard_map/ppermute | solution.py:438
  65.4 2.6 %collective-permute-done.9.refs_0_ = s32[2,264,128]{2,1,0:T(8,128)S(1)} collective-permute-done((s32[2,264,128]{2,1,0:T(8,128)S(1)}, s32[2,264,128]{2,1,0:T(8,128)S(1)}, u32[]{:S(2)}, u32[]{:S(2)}) %collective-permute-start.9) | collective-permute-done | bytes 270368 | tf_op jit(solution)/shard_map/ppermute | solution.py:438
  67.9 0.0 collective-permute-done.10.refs_1_
  68.0 0.0 collective-permute-done.12.refs_3_
  68.0 2.0 %fold.1 = f32[2,2,256,256]{3,2,1,0:T(8,128)} custom-call(f32[2,2,256,256]{3,2,1,0:T(8,128)S(1)} %get-tuple-element.61.own_ref, s32[2,264,128]{2,1,0:T(8,128)S(1)} %collective-permute-done.9.refs_0_, s32[2,136,256]{2,1,0:T(8,128)S(1)} %collective-permute-done.10.refs_1_, s32[2,136,128]{2,1,0:T(8,128)S(1)} %collective-permute-done.11.refs_2_, ...), custom_call_target="tpu_custom_call" | custom-call | tf_op jit(solution)/shard_map/fold/pallas_call | solution.py:424
  (7 shorter events, 0.1 us)
Async XLA Ops:
  0.0 1.0 %copy-start = (bf16[2,2,256,256]{3,2,1,0:T(8,128)(2,1)S(1)}, bf16[2,2,256,256]{3,2,1,0:T(8,128)(2,1)}, u32[]{:S(2)}) copy-start(bf16[2,2,256,256]{3,2,1,0:T(8,128)(2,1)} %own_ref.3) | copy-start | bytes 1572868
  1.0 15.6 %copy-start.1 = (bf16[2,2,256,256]{3,2,1,0:T(8,128)(2,1)S(1)}, bf16[2,2,256,256]{3,2,1,0:T(8,128)(2,1)}, u32[]{:S(2)}) copy-start(bf16[2,2,256,256]{3,2,1,0:T(8,128)(2,1)} %own_ref.3) | copy-start | bytes 1572868
  1.0 15.6 %copy-start.5 = (s32[2,2]{1,0:T(2,128)S(1)}, s32[2,2]{1,0:T(2,128)}, u32[]{:S(2)}) copy-start(s32[2,2]{1,0:T(2,128)} %anchor_ref.5) | copy-start | bytes 52
  1.2 14.7 %collective-permute-start.2 = (bf16[2,2,128,128]{3,2,1,0:T(8,128)(2,1)S(1)}, bf16[2,2,128,128]{3,2,1,0:T(8,128)(2,1)S(1)}, u32[]{:S(2)}, u32[]{:S(2)}) collective-permute-start(bf16[2,2,128,128]{3,2,1,0:T(8,128)(2,1)S(1)} %get-tuple-element.38), channel_id=1, source_target_pairs={{0,3},{1,2},{2,1},{3,0},{4,7},{5,6},{6,5},{7,4},{8,11},{9,10},{10,... | collective-permute-start | bytes 393224 | tf_op jit(solution)/shard_map/ppermute | solution.py:438
  3.8 12.1 %collective-permute-start.4 = (bf16[2,2,128,128]{3,2,1,0:T(8,128)(2,1)S(1)}, bf16[2,2,128,128]{3,2,1,0:T(8,128)(2,1)S(1)}, u32[]{:S(2)}, u32[]{:S(2)}) collective-permute-start(bf16[2,2,128,128]{3,2,1,0:T(8,128)(2,1)S(1)} %get-tuple-element.40), channel_id=1, source_target_pairs={{2,5},{3,4},{4,3},{5,2},{10,13},{11,12},{12,11},{13,10},{18,21},{1... | collective-permute-start | bytes 393224 | tf_op jit(solution)/shard_map/ppermute | solution.py:438
  5.7 10.6 %collective-permute-start = (bf16[2,2,256,128]{3,2,1,0:T(8,128)(2,1)S(1)}, bf16[2,2,256,128]{3,2,1,0:T(8,128)(2,1)S(1)}, u32[]{:S(2)}, u32[]{:S(2)}) collective-permute-start(bf16[2,2,256,128]{3,2,1,0:T(8,128)(2,1)S(1)} %get-tuple-element.36), channel_id=1, source_target_pairs={{0,1},{1,0},{2,3},{3,2},{4,5},{5,4},{6,7},{7,6},{8,9},{9,8},{10,11... | collective-permute-start | bytes 786440 | tf_op jit(solution)/shard_map/ppermute | solution.py:438
  6.5 9.8 %collective-permute-start.1 = (bf16[2,2,128,256]{3,2,1,0:T(8,128)(2,1)S(1)}, bf16[2,2,128,256]{3,2,1,0:T(8,128)(2,1)S(1)}, u32[]{:S(2)}, u32[]{:S(2)}) collective-permute-start(bf16[2,2,128,256]{3,2,1,0:T(8,128)(2,1)S(1)} %get-tuple-element.37), channel_id=1, source_target_pairs={{0,2},{1,3},{2,0},{3,1},{4,6},{5,7},{6,4},{7,5},{8,10},{9,11},{10,... | collective-permute-start | bytes 786440 | tf_op jit(solution)/shard_map/ppermute | solution.py:438
  6.5 10.1 %collective-permute-start.3 = (bf16[2,2,128,256]{3,2,1,0:T(8,128)(2,1)S(1)}, bf16[2,2,128,256]{3,2,1,0:T(8,128)(2,1)S(1)}, u32[]{:S(2)}, u32[]{:S(2)}) collective-permute-start(bf16[2,2,128,256]{3,2,1,0:T(8,128)(2,1)S(1)} %get-tuple-element.39), channel_id=1, source_target_pairs={{2,4},{3,5},{4,2},{5,3},{10,12},{11,13},{12,10},{13,11},{18,20},{1... | collective-permute-start | bytes 786440 | tf_op jit(solution)/shard_map/ppermute | solution.py:438
  13.4 1.2 %copy-start.3 = (bf16[2,2,2,256,256]{4,3,2,1,0:T(8,128)(2,1)S(1)}, bf16[2,2,2,256,256]{4,3,2,1,0:T(8,128)(2,1)}, u32[]{:S(2)}) copy-start(bf16[2,2,2,256,256]{4,3,2,1,0:T(8,128)(2,1)} %inc_ref) | copy-start | bytes 3145732
  14.7 7.0 %copy-start.2 = (bf16[4,256,256]{2,1,0:T(8,128)(2,1)S(1)}, bf16[4,256,256]{2,1,0:T(8,128)(2,1)}, u32[]{:S(2)}) copy-start(bf16[4,256,256]{2,1,0:T(8,128)(2,1)} %constant.2.clone.tab_ref) | copy-start | bytes 1572868
  14.7 7.0 %copy-start.4 = (bf16[2,2,256,256]{3,2,1,0:T(8,128)(2,1)S(1)}, bf16[2,2,256,256]{3,2,1,0:T(8,128)(2,1)}, u32[]{:S(2)}) copy-start(bf16[2,2,256,256]{3,2,1,0:T(8,128)(2,1)} %wave_in.1) | copy-start | bytes 1572868
  16.6 5.0 %collective-permute-start.6 = (bf16[2,2,256,256]{3,2,1,0:T(8,128)(2,1)S(1)}, bf16[2,2,256,256]{3,2,1,0:T(8,128)(2,1)S(1)}, u32[]{:S(2)}, u32[]{:S(2)}) collective-permute-start(bf16[2,2,256,256]{3,2,1,0:T(8,128)(2,1)S(1)} %get-tuple-element.53), channel_id=1, source_target_pairs={{0,8},{8,0},{16,24},{24,16},{1,9},{9,1},{17,25},{25,17},{2,10},{10... | collective-permute-start | bytes 1572872 | tf_op jit(solution)/shard_map/ppermute | solution.py:467
  18.7 2.9 %collective-permute-start.5 = (bf16[2,2,256,256]{3,2,1,0:T(8,128)(2,1)S(1)}, bf16[2,2,256,256]{3,2,1,0:T(8,128)(2,1)S(1)}, u32[]{:S(2)}, u32[]{:S(2)}) collective-permute-start(bf16[2,2,256,256]{3,2,1,0:T(8,128)(2,1)S(1)} %get-tuple-element.51), channel_id=1, source_target_pairs={{0,8},{8,0},{16,24},{24,16},{1,9},{9,1},{17,25},{25,17},{2,10},{10... | collective-permute-start | bytes 1572872 | tf_op jit(solution)/shard_map/ppermute | solution.py:477
  21.7 16.0 %collective-permute-start.7 = (s32[264,256]{1,0:T(8,128)S(1)}, s32[264,256]{1,0:T(8,128)S(1)}, u32[]{:S(2)}, u32[]{:S(2)}) collective-permute-start(s32[264,256]{1,0:T(8,128)S(1)} %get-tuple-element.56), channel_id=1, source_target_pairs={{16,0},{24,8},{17,1},{25,9},{18,2},{26,10},{19,3},{27,11},{20,4},{... | collective-permute-start | bytes 811016 | tf_op jit(solution)/shard_map/ppermute | solution.py:507
  43.4 2.7 %collective-permute-start.8 = (f32[2,2,256,256]{3,2,1,0:T(8,128)S(1)}, f32[2,2,256,256]{3,2,1,0:T(8,128)S(1)}, u32[]{:S(2)}, u32[]{:S(2)}) collective-permute-start(f32[2,2,256,256]{3,2,1,0:T(8,128)S(1)} %get-tuple-element.60), channel_id=1, source_target_pairs={{0,8},{8,0},{16,24},{24,16},{1,9},{9,1},{17,25},{25,17},{2,10},{10... | collective-permute-start | bytes 3145736 | tf_op jit(solution)/shard_map/ppermute | solution.py:510
  50.0 18.0 %collective-permute-start.10 = (s32[2,136,256]{2,1,0:T(8,128)S(1)}, s32[2,136,256]{2,1,0:T(8,128)S(1)}, u32[]{:S(2)}, u32[]{:S(2)}) collective-permute-start(s32[2,136,256]{2,1,0:T(8,128)S(1)} %get-tuple-element.63), channel_id=1, source_target_pairs={{0,2},{1,3},{2,0},{3,1},{4,6},{5,7},{6,4},{7,5},{8,10},{9,11},{10,... | collective-permute-start | bytes 835592 | tf_op jit(solution)/shard_map/ppermute | solution.py:438
  50.0 17.9 %collective-permute-start.12 = (s32[2,136,256]{2,1,0:T(8,128)S(1)}, s32[2,136,256]{2,1,0:T(8,128)S(1)}, u32[]{:S(2)}, u32[]{:S(2)}) collective-permute-start(s32[2,136,256]{2,1,0:T(8,128)S(1)} %get-tuple-element.65), channel_id=1, source_target_pairs={{2,4},{3,5},{4,2},{5,3},{10,12},{11,13},{12,10},{13,11},{18,20},{1... | collective-permute-start | bytes 835592 | tf_op jit(solution)/shard_map/ppermute | solution.py:438
  53.7 14.3 %collective-permute-start.9 = (s32[2,264,128]{2,1,0:T(8,128)S(1)}, s32[2,264,128]{2,1,0:T(8,128)S(1)}, u32[]{:S(2)}, u32[]{:S(2)}) collective-permute-start(s32[2,264,128]{2,1,0:T(8,128)S(1)} %get-tuple-element.62), channel_id=1, source_target_pairs={{0,1},{1,0},{2,3},{3,2},{4,5},{5,4},{6,7},{7,6},{8,9},{9,8},{10,11... | collective-permute-start | bytes 811016 | tf_op jit(solution)/shard_map/ppermute | solution.py:438
  54.2 9.6 %collective-permute-start.11 = (s32[2,136,128]{2,1,0:T(8,128)S(1)}, s32[2,136,128]{2,1,0:T(8,128)S(1)}, u32[]{:S(2)}, u32[]{:S(2)}) collective-permute-start(s32[2,136,128]{2,1,0:T(8,128)S(1)} %get-tuple-element.64), channel_id=1, source_target_pairs={{0,3},{1,2},{2,1},{3,0},{4,7},{5,6},{6,5},{7,4},{8,11},{9,10},{10,... | collective-permute-start | bytes 417800 | tf_op jit(solution)/shard_map/ppermute | solution.py:438
  54.2 11.1 %collective-permute-start.13 = (s32[2,136,128]{2,1,0:T(8,128)S(1)}, s32[2,136,128]{2,1,0:T(8,128)S(1)}, u32[]{:S(2)}, u32[]{:S(2)}) collective-permute-start(s32[2,136,128]{2,1,0:T(8,128)S(1)} %get-tuple-element.66), channel_id=1, source_target_pairs={{2,5},{3,4},{4,3},{5,2},{10,13},{11,12},{12,11},{13,10},{18,21},{1... | collective-permute-start | bytes 417800 | tf_op jit(solution)/shard_map/ppermute | solution.py:438

commit v5 on v4

--- a/solution.py
+++ b/solution.py
@@ -15,6 +15,8 @@
 LIMIT = 16 * 1024 * 1024
 LEVELS = 32767.0
 SCALE_ROWS = 8
+SUBLANES = 8
+LANES = 128
 
 
 def swap_pairs(size, parity):
@@ -132,24 +134,46 @@
     return lefts(turned, rights(spectrum, table))
 
 
+def window_place(at_x, at_y):
+    down, right = lax.rem(at_x, SUBLANES), lax.rem(at_y, LANES)
+    return pl.multiple_of(at_x - down, SUBLANES), pl.multiple_of(at_y - right, LANES), down, right
+
+
 def take_window(ext_ref, at_x, at_y, patch):
-    step = 8
-    inside = lax.rem(at_x, step)
-    first = pl.multiple_of(at_x - inside, step)
-    rows = ext_ref[pl.ds(first, patch + step), :]
-    count, width = rows.shape
-    rows = pltpu.roll(rows, lax.rem(width - at_y, width), 1)[:, :patch]
-    return pltpu.roll(rows, lax.rem(count - inside, count), 0)[:patch]
+    row, col, down, right = window_place(at_x, at_y)
+    rows = patch + SUBLANES
+    lane = lax.broadcasted_iota(jnp.int32, (rows, LANES), 1)
+    blocks = [
+        pltpu.roll(
+            ext_ref[pl.ds(row, rows), pl.ds(pl.multiple_of(col + k * LANES, LANES), LANES)],
+            lax.rem(LANES - right, LANES),
+            1,
+        )
+        for k in range(patch // LANES + 1)
+    ]
+    moved = [jnp.where(lane < LANES - right, here, after) for here, after in zip(blocks, blocks[1:])]
+    groups = jnp.concatenate(moved, axis=1).reshape(rows // SUBLANES, SUBLANES, patch)
+    groups = pltpu.roll(groups, lax.rem(SUBLANES - down, SUBLANES), 1)
+    place = lax.broadcasted_iota(jnp.int32, (patch // SUBLANES, SUBLANES, patch), 1)
+    return jnp.where(place < SUBLANES - down, groups[:-1], groups[1:]).reshape(patch, patch)
 
 
 def add_window(ext_ref, at_x, at_y, value):
-    step = 8
-    inside = lax.rem(at_x, step)
-    first = pl.multiple_of(at_x - inside, step)
-    value = jnp.concatenate([value, jnp.zeros((step, value.shape[1]), value.dtype)], axis=0)
-    value = pltpu.roll(value, inside, 0)
-    value = jnp.concatenate([value, jnp.zeros_like(value)], axis=1)
-    ext_ref[pl.ds(first, value.shape[0]), :] += pltpu.roll(value, at_y, 1)
+    row, col, down, right = window_place(at_x, at_y)
+    patch = value.shape[0]
+    rows = patch + SUBLANES
+    groups = pltpu.roll(value.reshape(patch // SUBLANES, SUBLANES, patch), down, 1)
+    none = jnp.zeros((1, SUBLANES, patch), value.dtype)
+    place = lax.broadcasted_iota(jnp.int32, (rows // SUBLANES, SUBLANES, patch), 1)
+    here = jnp.concatenate([groups, none], axis=0)
+    before = jnp.concatenate([none, groups], axis=0)
+    moved = jnp.where(place >= down, here, before).reshape(rows, patch)
+    lane = lax.broadcasted_iota(jnp.int32, (rows, LANES), 1)
+    blocks = [pltpu.roll(moved[:, k * LANES : (k + 1) * LANES], right, 1) for k in range(patch // LANES)]
+    none = jnp.zeros((rows, LANES), value.dtype)
+    for k, (here, before) in enumerate(zip(blocks + [none], [none] + blocks)):
+        where = (pl.ds(row, rows), pl.ds(pl.multiple_of(col + k * LANES, LANES), LANES))
+        ext_ref[where] += jnp.where(lane >= right, here, before)
 
 
 def two_powers(exponent):

time: 70.3 us -> 68.7 us (0.977)
  Pallas kernels: 15.6 us -> 13.9 us
    pallas_call x8, Pallas kernels: 15.6 us -> 13.9 us  [call(): pl.pallas_call(kernel, out_shape=out_shape, scratch_shapes=list(scratch),...]
  transfers between devices with their start and end apart: 14 -> 14, of which waited for: 7 -> 7; matrix products, arithmetic and copies ran while one was open for 5% -> 5% of each run, Pallas kernels for 6% -> 4%
where the time goes in v5:
time: 68.7 us; the launch traced here: 68.4 us
  waiting for transfers between devices  28.2 us (41%)
  starting transfers between devices  19.7 us (29%)
  Pallas kernels  13.9 us (20%)
  local copies, waits for them, and re-layouts  4.42 us (6%)
  other arithmetic  1.23 us (2%)
  between operations  0.86 us (1%)
    ppermute x10, starting transfers between devices, swapped(): lax.ppermute(value, ('sx', 'sy'), swap_list(n_x, n_y, *kind))  17.8 us
    ppermute x1, waiting for transfers between devices, shards(): lax.ppermute(wave, 'depth', [(2 * source + c, 2 * source - 2 + c) for c i...  14.8 us
    pallas_call x8, Pallas kernels, call(): pl.pallas_call(kernel, out_shape=out_shape, scratch_shapes=list(scratch),...  13.9 us
    ppermute x10, waiting for transfers between devices, swapped(): lax.ppermute(value, ('sx', 'sy'), swap_list(n_x, n_y, *kind))  10.8 us
    ppermute x1, waiting for transfers between devices, shards(): got = lax.ppermute(send, 'depth', core_swap)  2.65 us
    unnamed x12, local copies, waits for them, and re-layouts  2.29 us
  transfers between devices with their start and end apart: 14, of which 7 were waited for; matrix products, arithmetic and copies ran while one was open for 5% of the time, Pallas kernels for 4%

profile of v5, /device:TPU:16, one launch (start us, length us, event | category | flops | bytes accessed | tf_op | source)
XLA Modules:
  0.0 68.4 jit_solution(15855844657766183616)
XLA Ops:
  0.0 1.0 %copy-done = bf16[2,2,256,256]{3,2,1,0:T(8,128)(2,1)S(1)} copy-done((bf16[2,2,256,256]{3,2,1,0:T(8,128)(2,1)S(1)}, bf16[2,2,256,256]{3,2,1,0:T(8,128)(2,1)}, u32[]{:S(2)}) %copy-start) | copy-done | bytes 524312
  1.0 0.1 rims.1
  1.2 2.6 %collective-permute-start.2 = (bf16[2,2,128,128]{3,2,1,0:T(8,128)(2,1)S(1)}, bf16[2,2,128,128]{3,2,1,0:T(8,128)(2,1)S(1)}, u32[]{:S(2)}, u32[]{:S(2)}) collective-permute-start(bf16[2,2,128,128]{3,2,1,0:T(8,128)(2,1)S(1)} %get-tuple-element.38), channel_id=1, source_target_pairs={{0,3},{1,2},{2,1},{3,0},{4,7},{5,6},{6,5},{7,4},{8,11},{9,10},{10,... | collective-permute-start | bytes 393224 | tf_op jit(solution)/shard_map/ppermute | solution.py:462
  3.8 1.9 %collective-permute-start.4 = (bf16[2,2,128,128]{3,2,1,0:T(8,128)(2,1)S(1)}, bf16[2,2,128,128]{3,2,1,0:T(8,128)(2,1)S(1)}, u32[]{:S(2)}, u32[]{:S(2)}) collective-permute-start(bf16[2,2,128,128]{3,2,1,0:T(8,128)(2,1)S(1)} %get-tuple-element.40), channel_id=1, source_target_pairs={{2,5},{3,4},{4,3},{5,2},{10,13},{11,12},{12,11},{13,10},{18,21},{1... | collective-permute-start | bytes 393224 | tf_op jit(solution)/shard_map/ppermute | solution.py:462
  5.7 0.8 %collective-permute-start = (bf16[2,2,256,128]{3,2,1,0:T(8,128)(2,1)S(1)}, bf16[2,2,256,128]{3,2,1,0:T(8,128)(2,1)S(1)}, u32[]{:S(2)}, u32[]{:S(2)}) collective-permute-start(bf16[2,2,256,128]{3,2,1,0:T(8,128)(2,1)S(1)} %get-tuple-element.36), channel_id=1, source_target_pairs={{0,1},{1,0},{2,3},{3,2},{4,5},{5,4},{6,7},{7,6},{8,9},{9,8},{10,11... | collective-permute-start | bytes 786440 | tf_op jit(solution)/shard_map/ppermute | solution.py:462
  6.5 0.0 collective-permute-start.1
  6.5 4.6 %collective-permute-start.3 = (bf16[2,2,128,256]{3,2,1,0:T(8,128)(2,1)S(1)}, bf16[2,2,128,256]{3,2,1,0:T(8,128)(2,1)S(1)}, u32[]{:S(2)}, u32[]{:S(2)}) collective-permute-start(bf16[2,2,128,256]{3,2,1,0:T(8,128)(2,1)S(1)} %get-tuple-element.39), channel_id=1, source_target_pairs={{2,4},{3,5},{4,2},{5,3},{10,12},{11,13},{12,10},{13,11},{18,20},{1... | collective-permute-start | bytes 786440 | tf_op jit(solution)/shard_map/ppermute | solution.py:462
  11.1 0.9 %slice.17 = f32[127,256]{1,0:T(8,128)S(1)} slice(f32[256,256]{1,0:T(8,128)} %param.10), slice={[129:256], [0:256]} | slice | bytes 260096 | tf_op jit(solution)/shard_map/slice | solution.py:63
  12.1 0.9 %slice.16 = f32[129,256]{1,0:T(8,128)S(1)} slice(f32[256,256]{1,0:T(8,128)} %param.10), slice={[0:129], [0:256]} | slice | bytes 264192 | tf_op jit(solution)/shard_map/slice | solution.py:61
  13.0 0.1 rev.6
  13.1 0.1 pad_maximum_fusion.1
  13.2 0.2 rev.7
  13.4 0.0 copy-start.3
  13.4 1.2 %copy-done.3 = bf16[2,2,2,256,256]{4,3,2,1,0:T(8,128)(2,1)S(1)} copy-done((bf16[2,2,2,256,256]{4,3,2,1,0:T(8,128)(2,1)S(1)}, bf16[2,2,2,256,256]{4,3,2,1,0:T(8,128)(2,1)}, u32[]{:S(2)}) %copy-start.3) | copy-done | bytes 1048600
  14.7 0.1 incident_split.1
  14.8 1.1 %fusion = (f32[256,256]{1,0:T(8,128)S(1)}, f32[256,256]{1,0:T(8,128)S(1)}) fusion(f32[256,127]{1,0:T(8,128)S(1)} %rev.7, f32[256,129]{1,0:T(8,128)S(1)} %slice_maximum_fusion), kind=kLoop, calls=%fused_computation.2 | loop fusion | flops 65536 | bytes 786432 | tf_op jit(solution)/shard_map/sin | solution.py:483
  15.9 0.0 collective-permute-done.2.refs_2_
  15.9 0.0 collective-permute-done.4.refs_4_
  15.9 0.4 collective-permute-done.refs_0_
  16.3 0.0 collective-permute-done.1.refs_1_
  16.3 0.3 collective-permute-done.3.refs_3_
  16.6 0.0 collective-permute-start.6
  16.6 0.0 copy-done.1
  16.6 0.0 copy-done.5
  16.6 1.6 %windows_for_other.1 = (bf16[2,2,256,256]{3,2,1,0:T(8,128)(2,1)S(1)}, f32[2,2,512,512]{3,2,1,0:T(8,128)S(1)}) custom-call(s32[2,2]{1,0:T(2,128)S(1)} %copy-done.5, bf16[2,2,256,256]{3,2,1,0:T(8,128)(2,1)S(1)} %copy-done.1, bf16[2,2,256,128]{3,2,1,0:T(8,128)(2,1)S(1)} %collective-permute-done.refs_0_, ...), custom_call_target="tpu_custom_call" | custom-call | tf_op jit(solution)/shard_map/windows_for_other/pallas_call | solution.py:448
  18.2 0.6 collective-permute-start.5
  19.4 1.2 %windows.1.win_own = bf16[2,2,256,256]{3,2,1,0:T(8,128)(2,1)S(1)} custom-call(s32[2,2]{1,0:T(2,128)S(1)} %copy-done.5, f32[2,2,512,512]{3,2,1,0:T(8,128)S(1)} %get-tuple-element.50.ext_ref), custom_call_target="tpu_custom_call" | custom-call | tf_op jit(solution)/shard_map/windows/pallas_call | solution.py:448
  20.6 0.0 collective-permute-done.6.inc_got
  20.6 0.0 collective-permute-done.5.win_got
  20.6 0.0 copy-done.2
  20.6 0.0 copy-done.4
  20.7 1.3 %collective-permute-start.7 = (s32[264,256]{1,0:T(8,128)S(1)}, s32[264,256]{1,0:T(8,128)S(1)}, u32[]{:S(2)}, u32[]{:S(2)}) collective-permute-start(s32[264,256]{1,0:T(8,128)S(1)} %get-tuple-element.56), channel_id=1, source_target_pairs={{16,0},{24,8},{17,1},{25,9},{18,2},{26,10},{19,3},{27,11},{20,4},{... | collective-permute-start | bytes 811016 | tf_op jit(solution)/shard_map/ppermute | solution.py:531
  22.0 14.8 %collective-permute-done.7.wave_in = s32[264,256]{1,0:T(8,128)S(1)} collective-permute-done((s32[264,256]{1,0:T(8,128)S(1)}, s32[264,256]{1,0:T(8,128)S(1)}, u32[]{:S(2)}, u32[]{:S(2)}) %collective-permute-start.7) | collective-permute-done | bytes 270368 | tf_op jit(solution)/shard_map/ppermute | solution.py:531
  36.7 5.7 %sweep.3 = (f32[2,2,256,256]{3,2,1,0:T(8,128)S(1)}, f32[2,2,256,256]{3,2,1,0:T(8,128)S(1)}, s32[264,256]{1,0:T(8,128)}) custom-call(s32[1]{0:T(128)S(6)} %copy.12.live_ref, s32[264,256]{1,0:T(8,128)S(1)} %collective-permute-done.7.wave_in, bf16[2,2,256,256]{3,2,1,0:T(8,128)(2,1)S(1)} %windows.1.win_own, ...), custom_call_target="tpu_custom_call", output_to_operand_aliasing={{0}: (9, {}), {1}: (10, {})} | custom-call | tf_op jit(solution)/shard_map/sweep/pallas_call | solution.py:448
  42.4 0.1 collective-permute-start.8
  42.5 2.6 %collective-permute-done.8.other_ref = f32[2,2,256,256]{3,2,1,0:T(8,128)S(1)} collective-permute-done((f32[2,2,256,256]{3,2,1,0:T(8,128)S(1)}, f32[2,2,256,256]{3,2,1,0:T(8,128)S(1)}, u32[]{:S(2)}, u32[]{:S(2)}) %collective-permute-start.8) | collective-permute-done | bytes 1048608 | tf_op jit(solution)/shard_map/ppermute | solution.py:534
  45.1 3.2 %scatter.1 = (f32[2,2,256,256]{3,2,1,0:T(8,128)S(1)}, s32[2,264,128]{2,1,0:T(8,128)S(1)}, s32[2,136,256]{2,1,0:T(8,128)S(1)}, s32[2,136,128]{2,1,0:T(8,128)S(1)}...) custom-call(s32[2,2]{1,0:T(2,128)S(1)} %copy-done.5, f32[2,2,256,256]{3,2,1,0:T(8,128)S(1)} %get-tuple-element.59.mine_ref, ...), custom_call_target="tpu_custom_call" | custom-call | tf_op jit(solution)/shard_map/scatter/pallas_call | solution.py:448
  48.3 0.1 collective-permute-start.10
  48.4 3.6 %collective-permute-start.12 = (s32[2,136,256]{2,1,0:T(8,128)S(1)}, s32[2,136,256]{2,1,0:T(8,128)S(1)}, u32[]{:S(2)}, u32[]{:S(2)}) collective-permute-start(s32[2,136,256]{2,1,0:T(8,128)S(1)} %get-tuple-element.65), channel_id=1, source_target_pairs={{2,4},{3,5},{4,2},{5,3},{10,12},{11,13},{12,10},{13,11},{18,20},{1... | collective-permute-start | bytes 835592 | tf_op jit(solution)/shard_map/ppermute | solution.py:462
  52.1 0.6 collective-permute-start.9
  52.6 0.0 collective-permute-start.11
  52.6 3.6 %collective-permute-start.13 = (s32[2,136,128]{2,1,0:T(8,128)S(1)}, s32[2,136,128]{2,1,0:T(8,128)S(1)}, u32[]{:S(2)}, u32[]{:S(2)}) collective-permute-start(s32[2,136,128]{2,1,0:T(8,128)S(1)} %get-tuple-element.66), channel_id=1, source_target_pairs={{2,5},{3,4},{4,3},{5,2},{10,13},{11,12},{12,11},{13,10},{18,21},{1... | collective-permute-start | bytes 417800 | tf_op jit(solution)/shard_map/ppermute | solution.py:462
  56.2 6.0 %collective-permute-done.11.refs_2_ = s32[2,136,128]{2,1,0:T(8,128)S(1)} collective-permute-done((s32[2,136,128]{2,1,0:T(8,128)S(1)}, s32[2,136,128]{2,1,0:T(8,128)S(1)}, u32[]{:S(2)}, u32[]{:S(2)}) %collective-permute-start.11) | collective-permute-done | bytes 139296 | tf_op jit(solution)/shard_map/ppermute | solution.py:462
  62.2 1.6 %collective-permute-done.13.refs_4_ = s32[2,136,128]{2,1,0:T(8,128)S(1)} collective-permute-done((s32[2,136,128]{2,1,0:T(8,128)S(1)}, s32[2,136,128]{2,1,0:T(8,128)S(1)}, u32[]{:S(2)}, u32[]{:S(2)}) %collective-permute-start.13) | collective-permute-done | bytes 139296 | tf_op jit(solution)/shard_map/ppermute | solution.py:462
  63.8 2.5 %collective-permute-done.9.refs_0_ = s32[2,264,128]{2,1,0:T(8,128)S(1)} collective-permute-done((s32[2,264,128]{2,1,0:T(8,128)S(1)}, s32[2,264,128]{2,1,0:T(8,128)S(1)}, u32[]{:S(2)}, u32[]{:S(2)}) %collective-permute-start.9) | collective-permute-done | bytes 270368 | tf_op jit(solution)/shard_map/ppermute | solution.py:462
  66.3 0.0 collective-permute-done.10.refs_1_
  66.3 0.0 collective-permute-done.12.refs_3_
  66.3 2.0 %fold.1 = f32[2,2,256,256]{3,2,1,0:T(8,128)} custom-call(f32[2,2,256,256]{3,2,1,0:T(8,128)S(1)} %get-tuple-element.61.own_ref, s32[2,264,128]{2,1,0:T(8,128)S(1)} %collective-permute-done.9.refs_0_, s32[2,136,256]{2,1,0:T(8,128)S(1)} %collective-permute-done.10.refs_1_, s32[2,136,128]{2,1,0:T(8,128)S(1)} %collective-permute-done.11.refs_2_, ...), custom_call_target="tpu_custom_call" | custom-call | tf_op jit(solution)/shard_map/fold/pallas_call | solution.py:448
  (7 shorter events, 0.1 us)
Async XLA Ops:
  0.0 1.0 %copy-start = (bf16[2,2,256,256]{3,2,1,0:T(8,128)(2,1)S(1)}, bf16[2,2,256,256]{3,2,1,0:T(8,128)(2,1)}, u32[]{:S(2)}) copy-start(bf16[2,2,256,256]{3,2,1,0:T(8,128)(2,1)} %own_ref.3) | copy-start | bytes 1572868
  1.0 15.6 %copy-start.1 = (bf16[2,2,256,256]{3,2,1,0:T(8,128)(2,1)S(1)}, bf16[2,2,256,256]{3,2,1,0:T(8,128)(2,1)}, u32[]{:S(2)}) copy-start(bf16[2,2,256,256]{3,2,1,0:T(8,128)(2,1)} %own_ref.3) | copy-start | bytes 1572868
  1.0 15.6 %copy-start.5 = (s32[2,2]{1,0:T(2,128)S(1)}, s32[2,2]{1,0:T(2,128)}, u32[]{:S(2)}) copy-start(s32[2,2]{1,0:T(2,128)} %anchor_ref.5) | copy-start | bytes 52
  1.2 14.7 %collective-permute-start.2 = (bf16[2,2,128,128]{3,2,1,0:T(8,128)(2,1)S(1)}, bf16[2,2,128,128]{3,2,1,0:T(8,128)(2,1)S(1)}, u32[]{:S(2)}, u32[]{:S(2)}) collective-permute-start(bf16[2,2,128,128]{3,2,1,0:T(8,128)(2,1)S(1)} %get-tuple-element.38), channel_id=1, source_target_pairs={{0,3},{1,2},{2,1},{3,0},{4,7},{5,6},{6,5},{7,4},{8,11},{9,10},{10,... | collective-permute-start | bytes 393224 | tf_op jit(solution)/shard_map/ppermute | solution.py:462
  3.8 12.1 %collective-permute-start.4 = (bf16[2,2,128,128]{3,2,1,0:T(8,128)(2,1)S(1)}, bf16[2,2,128,128]{3,2,1,0:T(8,128)(2,1)S(1)}, u32[]{:S(2)}, u32[]{:S(2)}) collective-permute-start(bf16[2,2,128,128]{3,2,1,0:T(8,128)(2,1)S(1)} %get-tuple-element.40), channel_id=1, source_target_pairs={{2,5},{3,4},{4,3},{5,2},{10,13},{11,12},{12,11},{13,10},{18,21},{1... | collective-permute-start | bytes 393224 | tf_op jit(solution)/shard_map/ppermute | solution.py:462
  5.7 10.6 %collective-permute-start = (bf16[2,2,256,128]{3,2,1,0:T(8,128)(2,1)S(1)}, bf16[2,2,256,128]{3,2,1,0:T(8,128)(2,1)S(1)}, u32[]{:S(2)}, u32[]{:S(2)}) collective-permute-start(bf16[2,2,256,128]{3,2,1,0:T(8,128)(2,1)S(1)} %get-tuple-element.36), channel_id=1, source_target_pairs={{0,1},{1,0},{2,3},{3,2},{4,5},{5,4},{6,7},{7,6},{8,9},{9,8},{10,11... | collective-permute-start | bytes 786440 | tf_op jit(solution)/shard_map/ppermute | solution.py:462
  6.5 9.8 %collective-permute-start.1 = (bf16[2,2,128,256]{3,2,1,0:T(8,128)(2,1)S(1)}, bf16[2,2,128,256]{3,2,1,0:T(8,128)(2,1)S(1)}, u32[]{:S(2)}, u32[]{:S(2)}) collective-permute-start(bf16[2,2,128,256]{3,2,1,0:T(8,128)(2,1)S(1)} %get-tuple-element.37), channel_id=1, source_target_pairs={{0,2},{1,3},{2,0},{3,1},{4,6},{5,7},{6,4},{7,5},{8,10},{9,11},{10,... | collective-permute-start | bytes 786440 | tf_op jit(solution)/shard_map/ppermute | solution.py:462
  6.5 10.1 %collective-permute-start.3 = (bf16[2,2,128,256]{3,2,1,0:T(8,128)(2,1)S(1)}, bf16[2,2,128,256]{3,2,1,0:T(8,128)(2,1)S(1)}, u32[]{:S(2)}, u32[]{:S(2)}) collective-permute-start(bf16[2,2,128,256]{3,2,1,0:T(8,128)(2,1)S(1)} %get-tuple-element.39), channel_id=1, source_target_pairs={{2,4},{3,5},{4,2},{5,3},{10,12},{11,13},{12,10},{13,11},{18,20},{1... | collective-permute-start | bytes 786440 | tf_op jit(solution)/shard_map/ppermute | solution.py:462
  13.4 1.2 %copy-start.3 = (bf16[2,2,2,256,256]{4,3,2,1,0:T(8,128)(2,1)S(1)}, bf16[2,2,2,256,256]{4,3,2,1,0:T(8,128)(2,1)}, u32[]{:S(2)}) copy-start(bf16[2,2,2,256,256]{4,3,2,1,0:T(8,128)(2,1)} %inc_ref) | copy-start | bytes 3145732
  14.7 5.9 %copy-start.2 = (bf16[4,256,256]{2,1,0:T(8,128)(2,1)S(1)}, bf16[4,256,256]{2,1,0:T(8,128)(2,1)}, u32[]{:S(2)}) copy-start(bf16[4,256,256]{2,1,0:T(8,128)(2,1)} %constant.2.clone.tab_ref) | copy-start | bytes 1572868
  14.7 5.9 %copy-start.4 = (bf16[2,2,256,256]{3,2,1,0:T(8,128)(2,1)S(1)}, bf16[2,2,256,256]{3,2,1,0:T(8,128)(2,1)}, u32[]{:S(2)}) copy-start(bf16[2,2,256,256]{3,2,1,0:T(8,128)(2,1)} %wave_in.1) | copy-start | bytes 1572868
  16.6 4.0 %collective-permute-start.6 = (bf16[2,2,256,256]{3,2,1,0:T(8,128)(2,1)S(1)}, bf16[2,2,256,256]{3,2,1,0:T(8,128)(2,1)S(1)}, u32[]{:S(2)}, u32[]{:S(2)}) collective-permute-start(bf16[2,2,256,256]{3,2,1,0:T(8,128)(2,1)S(1)} %get-tuple-element.53), channel_id=1, source_target_pairs={{0,8},{8,0},{16,24},{24,16},{1,9},{9,1},{17,25},{25,17},{2,10},{10... | collective-permute-start | bytes 1572872 | tf_op jit(solution)/shard_map/ppermute | solution.py:491
  18.2 2.4 %collective-permute-start.5 = (bf16[2,2,256,256]{3,2,1,0:T(8,128)(2,1)S(1)}, bf16[2,2,256,256]{3,2,1,0:T(8,128)(2,1)S(1)}, u32[]{:S(2)}, u32[]{:S(2)}) collective-permute-start(bf16[2,2,256,256]{3,2,1,0:T(8,128)(2,1)S(1)} %get-tuple-element.51), channel_id=1, source_target_pairs={{0,8},{8,0},{16,24},{24,16},{1,9},{9,1},{17,25},{25,17},{2,10},{10... | collective-permute-start | bytes 1572872 | tf_op jit(solution)/shard_map/ppermute | solution.py:501
  20.7 16.1 %collective-permute-start.7 = (s32[264,256]{1,0:T(8,128)S(1)}, s32[264,256]{1,0:T(8,128)S(1)}, u32[]{:S(2)}, u32[]{:S(2)}) collective-permute-start(s32[264,256]{1,0:T(8,128)S(1)} %get-tuple-element.56), channel_id=1, source_target_pairs={{16,0},{24,8},{17,1},{25,9},{18,2},{26,10},{19,3},{27,11},{20,4},{... | collective-permute-start | bytes 811016 | tf_op jit(solution)/shard_map/ppermute | solution.py:531
  42.4 2.7 %collective-permute-start.8 = (f32[2,2,256,256]{3,2,1,0:T(8,128)S(1)}, f32[2,2,256,256]{3,2,1,0:T(8,128)S(1)}, u32[]{:S(2)}, u32[]{:S(2)}) collective-permute-start(f32[2,2,256,256]{3,2,1,0:T(8,128)S(1)} %get-tuple-element.60), channel_id=1, source_target_pairs={{0,8},{8,0},{16,24},{24,16},{1,9},{9,1},{17,25},{25,17},{2,10},{10... | collective-permute-start | bytes 3145736 | tf_op jit(solution)/shard_map/ppermute | solution.py:534
  48.3 18.0 %collective-permute-start.10 = (s32[2,136,256]{2,1,0:T(8,128)S(1)}, s32[2,136,256]{2,1,0:T(8,128)S(1)}, u32[]{:S(2)}, u32[]{:S(2)}) collective-permute-start(s32[2,136,256]{2,1,0:T(8,128)S(1)} %get-tuple-element.63), channel_id=1, source_target_pairs={{0,2},{1,3},{2,0},{3,1},{4,6},{5,7},{6,4},{7,5},{8,10},{9,11},{10,... | collective-permute-start | bytes 835592 | tf_op jit(solution)/shard_map/ppermute | solution.py:462
  48.4 17.9 %collective-permute-start.12 = (s32[2,136,256]{2,1,0:T(8,128)S(1)}, s32[2,136,256]{2,1,0:T(8,128)S(1)}, u32[]{:S(2)}, u32[]{:S(2)}) collective-permute-start(s32[2,136,256]{2,1,0:T(8,128)S(1)} %get-tuple-element.65), channel_id=1, source_target_pairs={{2,4},{3,5},{4,2},{5,3},{10,12},{11,13},{12,10},{13,11},{18,20},{1... | collective-permute-start | bytes 835592 | tf_op jit(solution)/shard_map/ppermute | solution.py:462
  52.1 14.3 %collective-permute-start.9 = (s32[2,264,128]{2,1,0:T(8,128)S(1)}, s32[2,264,128]{2,1,0:T(8,128)S(1)}, u32[]{:S(2)}, u32[]{:S(2)}) collective-permute-start(s32[2,264,128]{2,1,0:T(8,128)S(1)} %get-tuple-element.62), channel_id=1, source_target_pairs={{0,1},{1,0},{2,3},{3,2},{4,5},{5,4},{6,7},{7,6},{8,9},{9,8},{10,11... | collective-permute-start | bytes 811016 | tf_op jit(solution)/shard_map/ppermute | solution.py:462
  52.6 9.6 %collective-permute-start.11 = (s32[2,136,128]{2,1,0:T(8,128)S(1)}, s32[2,136,128]{2,1,0:T(8,128)S(1)}, u32[]{:S(2)}, u32[]{:S(2)}) collective-permute-start(s32[2,136,128]{2,1,0:T(8,128)S(1)} %get-tuple-element.64), channel_id=1, source_target_pairs={{0,3},{1,2},{2,1},{3,0},{4,7},{5,6},{6,5},{7,4},{8,11},{9,10},{10,... | collective-permute-start | bytes 417800 | tf_op jit(solution)/shard_map/ppermute | solution.py:462
  52.6 11.2 %collective-permute-start.13 = (s32[2,136,128]{2,1,0:T(8,128)S(1)}, s32[2,136,128]{2,1,0:T(8,128)S(1)}, u32[]{:S(2)}, u32[]{:S(2)}) collective-permute-start(s32[2,136,128]{2,1,0:T(8,128)S(1)} %get-tuple-element.66), channel_id=1, source_target_pairs={{2,5},{3,4},{4,3},{5,2},{10,13},{11,12},{12,11},{13,10},{18,21},{1... | collective-permute-start | bytes 417800 | tf_op jit(solution)/shard_map/ppermute | solution.py:462

commit v6 on v5

--- a/solution.py
+++ b/solution.py
@@ -15,6 +15,9 @@
 LIMIT = 16 * 1024 * 1024
 LEVELS = 32767.0
 SCALE_ROWS = 8
+FIRST = 3
+EARLY = ((0, None), (1, None), (None, 0), (None, 1), (0, 0), (0, 1), (1, 0), (1, 1))
+LATE = ((None, 0), (None, 1), (0, None), (1, None), (0, 0), (0, 1), (1, 0), (1, 1))
 SUBLANES = 8
 LANES = 128
 
@@ -32,13 +35,8 @@
     return [(a * n_y + b, c * n_y + d) for a, c in xs for b, d in ys]
 
 
-def swap_kinds(n_x, n_y):
-    kinds = []
-    for swap_x in (None, 0, 1):
-        for swap_y in (None, 0, 1):
-            if (swap_x, swap_y) != (None, None) and swap_list(n_x, n_y, swap_x, swap_y):
-                kinds.append((swap_x, swap_y))
-    return kinds
+def swap_kinds(n_x, n_y, order):
+    return [kind for kind in order if swap_list(n_x, n_y, *kind)]
 
 
 def split(value):
@@ -56,12 +54,27 @@
     return np.concatenate([cos, sin]) / math.sqrt(size)
 
 
-def folded_order(array, axis):
-    half = array.shape[axis] // 2
-    low = lax.slice_in_dim(array, 0, half, axis=axis)
-    mid = lax.slice_in_dim(array, half, half + 1, axis=axis)
-    high = lax.rev(lax.slice_in_dim(array, half + 1, 2 * half, axis=axis), (axis,))
-    return jnp.concatenate([low, mid, high], axis=axis)
+def turn_kernel(phase_ref, cos_ref, sin_ref):
+    size = phase_ref.shape[0]
+    half = size // 2
+    place = lax.broadcasted_iota(jnp.int32, (size, size), 0)
+    source = jnp.where(place <= half, place, size + half - place)
+    select = (source == lax.broadcasted_iota(jnp.int32, (size, size), 1)).astype(jnp.bfloat16)
+
+    def thirds(value):
+        first = value.astype(jnp.bfloat16)
+        value = value - first.astype(jnp.float32)
+        return first, *split(value)
+
+    first, second, third = [dot(select, part) for part in thirds(phase_ref[...])]
+    rows = first + (second + third)
+    first, second, third = [
+        lax.dot_general(part, select, (((1,), (1,)), ((), ())), preferred_element_type=jnp.float32)
+        for part in thirds(rows)
+    ]
+    phase = first + (second + third)
+    cos_ref[...] = jnp.cos(phase)
+    sin_ref[...] = jnp.sin(phase)
 
 
 def spectrum_split(p, q, first):
@@ -212,19 +225,20 @@
     return value(packed >> 16), value((packed << 16) >> 16)
 
 
-def put_encoded(ref, at, real, imag, exponent):
+def put_encoded(ref, first, real, imag, exponent):
     packed = encode(real, imag, exponent)
     rows, cols = packed.shape
-    ref[at + (slice(0, rows), slice(None))] = packed
-    ref[at + (slice(rows, rows + SCALE_ROWS), slice(None))] = jnp.broadcast_to(
-        exponent.astype(jnp.int32), (SCALE_ROWS, cols)
-    )
-
-
-def get_encoded(ref, at):
-    rows = ref.shape[-2] - SCALE_ROWS
-    packed = ref[at + (slice(0, rows), slice(None))]
-    return decode(packed, ref[at + (slice(rows, rows + 1), slice(None))])
+    ref[pl.ds(first, rows), :] = packed
+    ref[ref.shape[0] - SCALE_ROWS :, :] = jnp.broadcast_to(exponent.astype(jnp.int32), (SCALE_ROWS, cols))
+
+
+def get_encoded(ref, first, rows):
+    last = ref.shape[0]
+    return decode(ref[pl.ds(first, rows), :], ref[last - 1 : last, :])
+
+
+def rim_size(kind, tile):
+    return tuple(tile if swap is None else tile // 2 for swap in kind)
 
 
 def halo_start(kind, half, tile):
@@ -267,17 +281,15 @@
         piece[...] = own_ref[:, :, pl.ds(row, rows), pl.ds(col, cols)]
 
 
-def window_send_kernel(kinds, anchor_ref, own_ref, *refs):
+def window_send_kernel(kinds, tile, anchor_ref, _filled, *refs):
     pieces, (out_ref, ext_ref) = refs[: len(kinds)], refs[len(kinds) :]
-    slab, _, tile, _ = own_ref.shape
+    slab = ext_ref.shape[0]
     half = tile // 2
     at_x, at_y = corner_of(anchor_ref, 1 - core_index(), half, tile)
 
     def one(index, _):
         layer, c = index // 2, lax.rem(index, 2)
         plane = ext_ref.at[layer, c]
-        plane[...] = jnp.zeros(plane.shape, plane.dtype)
-        plane[half : half + tile, half : half + tile] = own_ref[layer, c].astype(jnp.float32)
         for kind, piece in zip(kinds, pieces):
             row, col = halo_start(kind, half, tile)
             rows, cols = piece.shape[2:]
@@ -301,7 +313,7 @@
     lax.fori_loop(0, 2 * slab, one, 0)
 
 
-def incident_kernel(inc_ref, own_ref, other_ref, sems):
+def slots_kernel(live_ref, inc_ref, exit_ref, tile_ref, own_ref, other_ref, seed_ref, ext_ref, sems):
     core = core_index()
     copies = [
         pltpu.make_async_copy(inc_ref.at[layer, slot], ref.at[layer], sems.at[layer, j])
@@ -310,11 +322,24 @@
     ]
     for copy in copies:
         copy.start()
+    live = (core < live_ref[0]).astype(jnp.float32)
+    seed_ref[...] = exit_ref[core].astype(jnp.float32) * live
+    slab, _, tile, _ = tile_ref.shape
+    half = tile // 2
+
+    def fill(index, _):
+        layer, c = index // 2, lax.rem(index, 2)
+        plane = ext_ref.at[layer, c]
+        plane[...] = jnp.zeros(plane.shape, plane.dtype)
+        plane[half : half + tile, half : half + tile] = tile_ref[layer, c].astype(jnp.float32)
+        return 0
+
+    lax.fori_loop(0, 2 * slab, fill, 0)
     for copy in copies:
         copy.wait()
 
 
-def sweep_kernel(stage, live_ref, wave_in, win_own, win_got, inc_own, inc_got, cos_ref, sin_ref, tab_ref, *refs):
+def sweep_kernel(stage, wave_in, win_own, win_got, inc_own, inc_got, cos_ref, sin_ref, tab_ref, *refs):
     keep_ref, send_ref, out_ref, wave_ref, term, sems = refs[-6:]
     slab = win_own.shape[0]
     layers = 2 * slab
@@ -328,10 +353,9 @@
     @pl.when(chip == chips - 1 - stage)
     def _():
         if stage == 0:
-            live = (core < live_ref[0]).astype(jnp.float32)
-            wave_ref[...] = wave_in[core].astype(jnp.float32) * live
+            wave_ref[...] = wave_in[...]
         else:
-            wave_ref[0], wave_ref[1] = get_encoded(wave_in, ())
+            wave_ref[0], wave_ref[1] = get_encoded(wave_in, 0, wave_ref.shape[1])
 
         def one(step, _):
             i = layers - 1 - step
@@ -375,18 +399,30 @@
         if stage < chips - 1:
             wr, wi = wave_ref[0], wave_ref[1]
             exponent = exponent_of(jnp.maximum(jnp.abs(wr), jnp.abs(wi)))
-            put_encoded(out_ref, (), wr, wi, exponent)
+            put_encoded(out_ref, 0, wr, wi, exponent)
         for slot in range(2):
             leave(slot, keep_ref, 0).wait()
 
 
-def scatter_kernel(kinds, anchor_ref, mine_ref, other_ref, own_ref, *refs):
-    pieces, ext_ref, top_ref = refs[:-2], refs[-2], refs[-1]
-    slab, _, patch, _ = mine_ref.shape
-    tile = own_ref.shape[2]
+def send_halos(kinds, pieces, tile, ext_ref, exponent):
     half = tile // 2
+
+    def one(layer, _):
+        for kind, piece in zip(kinds, pieces):
+            row, col = halo_start(kind, half, tile)
+            rows, cols = rim_size(kind, tile)
+            where = (pl.ds(row, rows), pl.ds(col, cols))
+            put_encoded(piece, layer * rows, ext_ref[(layer, 0) + where], ext_ref[(layer, 1) + where], exponent)
+        return 0
+
+    lax.fori_loop(0, ext_ref.shape[0], one, 0)
+
+
+def scatter_kernel(kinds, tile, anchor_ref, mine_ref, other_ref, ext_ref, exponent_ref, *refs):
+    pieces, top_ref = refs[:-1], refs[-1]
+    slab = mine_ref.shape[0]
     core = core_index()
-    corners = [corner_of(anchor_ref, slot, half, tile) for slot in (core, 1 - core)]
+    corners = [corner_of(anchor_ref, slot, tile // 2, tile) for slot in (core, 1 - core)]
     top_ref[...] = jnp.zeros_like(top_ref)
 
     def add(index, _):
@@ -399,33 +435,47 @@
             add_window(plane, at_x, at_y, value)
             bound = bound + jnp.max(jnp.abs(value), axis=0, keepdims=True)
         top_ref[...] = jnp.maximum(top_ref[...], bound)
-        own_ref[layer, c] = plane[half : half + tile, half : half + tile]
         return 0
 
     lax.fori_loop(0, 2 * slab, add, 0)
     exponent = exponent_of(top_ref[...])
-
-    def send(layer, _):
-        for kind, piece in zip(kinds, pieces):
-            row, col = halo_start(kind, half, tile)
-            where = (pl.ds(row, piece.shape[1] - SCALE_ROWS), pl.ds(col, piece.shape[2]))
-            put_encoded(piece, (layer,), ext_ref[(layer, 0) + where], ext_ref[(layer, 1) + where], exponent)
-        return 0
-
-    lax.fori_loop(0, slab, send, 0)
-
-
-def fold_kernel(kinds, own_ref, *refs):
+    exponent_ref[...] = jnp.broadcast_to(exponent, exponent_ref.shape)
+    send_halos(kinds, pieces, tile, ext_ref, exponent)
+
+
+def halos_kernel(kinds, tile, ext_ref, exponent_ref, *pieces):
+    send_halos(kinds, pieces, tile, ext_ref, exponent_ref[:1, :1])
+
+
+def add_halos(kinds, pieces, tile, out_ref, layer):
+    for kind, piece in zip(kinds, pieces):
+        row, col = rim_start(kind, tile // 2, tile)
+        rows, cols = rim_size(kind, tile)
+        where = (pl.ds(row, rows), pl.ds(col, cols))
+        for c, value in enumerate(get_encoded(piece, layer * rows, rows)):
+            out_ref[(layer, c) + where] += value
+
+
+def fold_kernel(kinds, ext_ref, *refs):
     pieces, out_ref = refs[:-1], refs[-1]
     slab, _, tile, _ = out_ref.shape
+    half = tile // 2
 
     def one(layer, _):
-        out_ref[layer] = own_ref[layer]
-        for kind, piece in zip(kinds, pieces):
-            row, col = rim_start(kind, tile // 2, tile)
-            where = (pl.ds(row, piece.shape[1] - SCALE_ROWS), pl.ds(col, piece.shape[2]))
-            for c, value in enumerate(get_encoded(piece, (layer,))):
-                out_ref[(layer, c) + where] += value
+        out_ref[layer] = ext_ref[layer, :, half : half + tile, half : half + tile]
+        add_halos(kinds, pieces, tile, out_ref, layer)
+        return 0
+
+    lax.fori_loop(0, slab, one, 0)
+
+
+def corners_kernel(kinds, part_ref, *refs):
+    pieces, out_ref = refs[:-1], refs[-1]
+    slab, _, tile, _ = out_ref.shape
+
+    def one(layer, _):
+        out_ref[layer] = part_ref[layer]
+        add_halos(kinds, pieces, tile, out_ref, layer)
         return 0
 
     lax.fori_loop(0, slab, one, 0)
@@ -439,12 +489,16 @@
     half = tile // 2
     extent = tile + patch
     chips = n_depth // 2
-    kinds = swap_kinds(n_x, n_y)
+    early, late = swap_kinds(n_x, n_y, EARLY), swap_kinds(n_x, n_y, LATE)
     params = pltpu.CompilerParams(vmem_limit_bytes=LIMIT)
     core_swap = swap_pairs(n_depth, 0)
     shape_of = jax.ShapeDtypeStruct
 
-    def call(kernel, out_shape, operands, name, scratch=(), **more):
+    def call(kernel, out_shape, operands, name, scratch=(), cost=0, **more):
+        if cost:
+            more["cost_estimate"] = pl.CostEstimate(
+                flops=int(cost * 1e9), bytes_accessed=int(cost * 3e6), transcendentals=0
+            )
         return pl.pallas_call(
             kernel,
             out_shape=out_shape,
@@ -454,49 +508,51 @@
             **{"in_specs": [VMEM] * len(operands), "out_specs": jax.tree.map(lambda _: VMEM, out_shape), **more},
         )(*operands)
 
-    def rim_size(kind):
-        return tile if kind[0] is None else half, tile if kind[1] is None else half
-
-    def swapped(values):
+    def swapped(values, kinds):
         return [
             lax.ppermute(value, ("sx", "sy"), swap_list(n_x, n_y, *kind)) for value, kind in zip(values, kinds)
         ]
 
     rims = call(
-        functools.partial(rims_kernel, kinds),
-        tuple(shape_of((slab, 2) + rim_size(kind), transmission.dtype) for kind in kinds),
+        functools.partial(rims_kernel, early),
+        tuple(shape_of((slab, 2) + rim_size(kind, tile), transmission.dtype) for kind in early),
         (transmission,),
         "rims",
     )
-    halos = swapped(rims)
-    propagator_phase, incident, _ = lax.optimization_barrier((propagator_phase, incident, rims))
+    halos = swapped(rims, early)
+    propagator_phase, incident, exit_adjoint, _ = lax.optimization_barrier(
+        (propagator_phase, incident, exit_adjoint, rims)
+    )
     inc_shape = shape_of((slab, 2, patch, patch), incident.dtype)
-    inc_own, inc_send = call(
-        incident_kernel,
-        (inc_shape, inc_shape),
-        (incident,),
-        "incident_split",
+    ext_shape = shape_of((slab, 2, extent, extent), f32)
+    inc_own, inc_send, wave, bordered = call(
+        slots_kernel,
+        (inc_shape, inc_shape, shape_of((2, patch, patch), f32), ext_shape),
+        (live_count, incident, exit_adjoint, transmission),
+        "slots",
         [pltpu.SemaphoreType.DMA((slab, 2))],
-        in_specs=[ANY],
-    )
-    phase = folded_order(folded_order(propagator_phase, 0), 1)
-    phase_cos, phase_sin = jnp.cos(phase), jnp.sin(phase)
+        cost=1,
+        in_specs=[SMEM, ANY, VMEM, VMEM],
+    )
+    factor_shape = shape_of(propagator_phase.shape, f32)
+    phase_cos, phase_sin = call(turn_kernel, (factor_shape, factor_shape), (propagator_phase,), "turn", cost=2)
     basis = dft_basis(patch)
     high = basis.astype(jnp.bfloat16)
     low = (basis - high.astype(np.float64)).astype(jnp.bfloat16)
     tables = jnp.asarray(np.stack([high, low, high.T, low.T]))
-    phase_cos, phase_sin, inc_own, inc_send, halos = lax.optimization_barrier(
-        (phase_cos, phase_sin, inc_own, inc_send, halos)
+    phase_cos, phase_sin, inc_own, inc_send, wave, bordered, halos = lax.optimization_barrier(
+        (phase_cos, phase_sin, inc_own, inc_send, wave, bordered, halos)
     )
     inc_got = lax.ppermute(inc_send, "depth", core_swap)
 
     window_shape = shape_of((slab, 2, patch, patch), transmission.dtype)
     win_send, bordered = call(
-        functools.partial(window_send_kernel, kinds),
-        (window_shape, shape_of((slab, 2, extent, extent), f32)),
-        (scan_anchor, transmission, *halos),
+        functools.partial(window_send_kernel, early, tile),
+        (window_shape, ext_shape),
+        (scan_anchor, bordered, *halos),
         "windows_for_other",
-        in_specs=[SMEM] + [VMEM] * (1 + len(kinds)),
+        in_specs=[SMEM] + [VMEM] * (1 + len(early)),
+        input_output_aliases={1: 1},
     )
     win_got = lax.ppermute(win_send, "depth", core_swap)
     win_own = call(
@@ -507,7 +563,6 @@
         in_specs=[SMEM, VMEM],
     )
 
-    wave = exit_adjoint
     term_shape = shape_of((slab, 2, patch, patch), f32)
     coded = shape_of((patch + SCALE_ROWS, patch), jnp.int32)
     terms = ()
@@ -515,16 +570,16 @@
         *terms, wave = call(
             functools.partial(sweep_kernel, stage),
             (term_shape, term_shape, coded),
-            (live_count, wave, win_own, win_got, inc_own, inc_got, phase_cos, phase_sin, tables, *terms),
+            (wave, win_own, win_got, inc_own, inc_got, phase_cos, phase_sin, tables, *terms),
             "sweep",
             [
                 pltpu.VMEM((2, patch, patch), f32),
                 pltpu.VMEM((2, 2, patch, patch), f32),
                 pltpu.SemaphoreType.DMA((2,)),
             ],
-            in_specs=[SMEM] + [VMEM] * 8 + [ANY] * len(terms),
+            in_specs=[VMEM] * 8 + [ANY] * len(terms),
             out_specs=(ANY, ANY, VMEM),
-            input_output_aliases={9: 0, 10: 1} if stage else {},
+            input_output_aliases={8: 0, 9: 1} if stage else {},
         )
         if stage < chips - 1:
             source = chips - 1 - stage
@@ -532,19 +587,36 @@
 
     keep, send = terms
     got = lax.ppermute(send, "depth", core_swap)
-    own_shape = shape_of((slab, 2, tile, tile), f32)
-    coded_rims = tuple(
-        shape_of((slab, rim_size(kind)[0] + SCALE_ROWS, rim_size(kind)[1]), jnp.int32) for kind in kinds
-    )
-    own, *beyond = call(
-        functools.partial(scatter_kernel, kinds),
-        (own_shape,) + coded_rims,
+    def coded_rims(kinds):
+        sizes = [rim_size(kind, tile) for kind in kinds]
+        return tuple(
+            shape_of((slab * rows + SCALE_ROWS * (FIRST if rows > cols else 1), cols), jnp.int32)
+            for rows, cols in sizes
+        )
+
+    first = [kind for kind in late if kind[0] is None]
+    rest = [kind for kind in late if kind[0] is not None]
+    sides = [kind for kind in late if None in kind]
+    corners = [kind for kind in late if None not in kind]
+    ext, exponent, *beyond = call(
+        functools.partial(scatter_kernel, first, tile),
+        (ext_shape, shape_of((SUBLANES, LANES), f32)) + coded_rims(first),
         (scan_anchor, keep, got),
         "scatter",
-        [pltpu.VMEM((slab, 2, extent, extent), f32), pltpu.VMEM((1, patch), f32)],
+        [pltpu.VMEM((1, patch), f32)],
+        cost=3,
         in_specs=[SMEM, VMEM, VMEM],
     )
-    return call(functools.partial(fold_kernel, kinds), own_shape, (own, *swapped(beyond)), "fold")
+    more = call(functools.partial(halos_kernel, rest, tile), coded_rims(rest), (ext, exponent), "halos", cost=1)
+    sent = dict(zip(first + rest, (*beyond, *more)))
+    came = dict(zip(late, swapped([sent[kind] for kind in late], late)))
+    tile_shape = shape_of((slab, 2, tile, tile), f32)
+    part = call(
+        functools.partial(fold_kernel, sides), tile_shape, (ext, *[came[kind] for kind in sides]), "fold", cost=2
+    )
+    return call(
+        functools.partial(corners_kernel, corners), tile_shape, (part, *[came[kind] for kind in corners]), "corners"
+    )
 
 
 def solution(mesh):

time: 68.7 us -> 66.2 us (0.964)
  local copies, waits for them, and re-layouts: 4.42 us -> 2.01 us
  Pallas kernels: 13.9 us -> 15.7 us
  other arithmetic: 1.23 us -> 0 us
    slice x2 -> x0, local copies, waits for them, and re-layouts: 1.84 us -> none  [the longest x1 0.92 us: folded_order(): low = lax.slice_in_dim(array, 0, half, axis=axis)]
    pallas_call x8 -> x11, Pallas kernels: 13.9 us -> 15.7 us  [call(): pl.pallas_call(kernel, out_shape=out_shape, scratch_shapes=list(scratch),...]
    sin x1 -> x0, other arithmetic: 1.11 us -> none  [shards(): phase_cos, phase_sin = (jnp.cos(phase), jnp.sin(phase))]
    ppermute x10, waiting for transfers between devices: 10.8 us -> 9.71 us  [swapped(): lax.ppermute(value, ('sx', 'sy'), swap_list(n_x, n_y, *kind))]
    unnamed x12 -> x14, local copies, waits for them, and re-layouts: 2.29 us -> 2.01 us
  transfers between devices with their start and end apart: 14 -> 14, of which waited for: 7 -> 9; matrix products, arithmetic and copies ran while one was open for 5% -> 0% of each run, Pallas kernels for 4% -> 10%
where the time goes in v6:
time: 66.2 us; the launch traced here: 65.9 us
  waiting for transfers between devices  27.9 us (42%)
  starting transfers between devices  19.5 us (29%)
  Pallas kernels  15.7 us (24%)
  local copies, waits for them, and re-layouts  2.01 us (3%)
  between operations  0.86 us (1%)
    ppermute x10, starting transfers between devices, swapped(): lax.ppermute(value, ('sx', 'sy'), swap_list(n_x, n_y, *kind))  17.6 us
    pallas_call x11, Pallas kernels, call(): pl.pallas_call(kernel, out_shape=out_shape, scratch_shapes=list(scratch),...  15.7 us
    ppermute x1, waiting for transfers between devices, shards(): lax.ppermute(wave, 'depth', [(2 * source + c, 2 * source - 2 + c) for c i...  15.2 us
    ppermute x10, waiting for transfers between devices, swapped(): lax.ppermute(value, ('sx', 'sy'), swap_list(n_x, n_y, *kind))  9.71 us
    ppermute x1, waiting for transfers between devices, shards(): got = lax.ppermute(send, 'depth', core_swap)  2.65 us
    unnamed x14, local copies, waits for them, and re-layouts  2.01 us
  transfers between devices with their start and end apart: 14, of which 9 were waited for; matrix products, arithmetic and copies ran while one was open for 0% of the time, Pallas kernels for 10%

profile of v6, /device:TPU:16, one launch (start us, length us, event | category | flops | bytes accessed | tf_op | source)
XLA Modules:
  0.0 65.9 jit_solution(14245600456527183353)
XLA Ops:
  0.0 0.0 copy-start.1
  0.0 1.0 %copy-done.1 = bf16[2,2,256,256]{3,2,1,0:T(8,128)(2,1)S(1)} copy-done((bf16[2,2,256,256]{3,2,1,0:T(8,128)(2,1)S(1)}, bf16[2,2,256,256]{3,2,1,0:T(8,128)(2,1)}, u32[]{:S(2)}) %copy-start.1) | copy-done | bytes 524312
  1.0 0.0 copy-start.2
  1.0 0.1 rims.1
  1.2 2.6 %collective-permute-start.3 = (bf16[2,2,128,128]{3,2,1,0:T(8,128)(2,1)S(1)}, bf16[2,2,128,128]{3,2,1,0:T(8,128)(2,1)S(1)}, u32[]{:S(2)}, u32[]{:S(2)}) collective-permute-start(bf16[2,2,128,128]{3,2,1,0:T(8,128)(2,1)S(1)} %get-tuple-element.47), channel_id=1, source_target_pairs={{0,3},{1,2},{2,1},{3,0},{4,7},{5,6},{6,5},{7,4},{8,11},{9,10},{10,... | collective-permute-start | bytes 393224 | tf_op jit(solution)/shard_map/ppermute | solution.py:513
  3.8 1.9 %collective-permute-start.4 = (bf16[2,2,128,128]{3,2,1,0:T(8,128)(2,1)S(1)}, bf16[2,2,128,128]{3,2,1,0:T(8,128)(2,1)S(1)}, u32[]{:S(2)}, u32[]{:S(2)}) collective-permute-start(bf16[2,2,128,128]{3,2,1,0:T(8,128)(2,1)S(1)} %get-tuple-element.48), channel_id=1, source_target_pairs={{2,5},{3,4},{4,3},{5,2},{10,13},{11,12},{12,11},{13,10},{18,21},{1... | collective-permute-start | bytes 393224 | tf_op jit(solution)/shard_map/ppermute | solution.py:513
  5.7 0.1 collective-permute-start
  5.8 3.9 %collective-permute-start.1 = (bf16[2,2,128,256]{3,2,1,0:T(8,128)(2,1)S(1)}, bf16[2,2,128,256]{3,2,1,0:T(8,128)(2,1)S(1)}, u32[]{:S(2)}, u32[]{:S(2)}) collective-permute-start(bf16[2,2,128,256]{3,2,1,0:T(8,128)(2,1)S(1)} %get-tuple-element.45), channel_id=1, source_target_pairs={{2,4},{3,5},{4,2},{5,3},{10,12},{11,13},{12,10},{13,11},{18,20},{1... | collective-permute-start | bytes 786440 | tf_op jit(solution)/shard_map/ppermute | solution.py:513
  9.6 0.0 copy-start.3
  9.7 1.6 %collective-permute-start.2 = (bf16[2,2,256,128]{3,2,1,0:T(8,128)(2,1)S(1)}, bf16[2,2,256,128]{3,2,1,0:T(8,128)(2,1)S(1)}, u32[]{:S(2)}, u32[]{:S(2)}) collective-permute-start(bf16[2,2,256,128]{3,2,1,0:T(8,128)(2,1)S(1)} %get-tuple-element.46), channel_id=1, source_target_pairs={{0,1},{1,0},{2,3},{3,2},{4,5},{5,4},{6,7},{7,6},{8,9},{9,8},{10,11... | collective-permute-start | bytes 786440 | tf_op jit(solution)/shard_map/ppermute | solution.py:513
  11.2 0.9 %copy-done.6 = f32[256,256]{1,0:T(8,128)S(1)} copy-done((f32[256,256]{1,0:T(8,128)S(1)}, f32[256,256]{1,0:T(8,128)}, u32[]{:S(2)}) %copy-start.6) | copy-done | bytes 262168
  12.2 1.4 %turn.1 = (f32[256,256]{1,0:T(8,128)S(1)}, f32[256,256]{1,0:T(8,128)S(1)}) custom-call(f32[256,256]{1,0:T(8,128)S(1)} %copy-done.6), custom_call_target="tpu_custom_call" | custom-call | flops 2000000000 | bytes 6000000 | tf_op jit(solution)/shard_map/turn/pallas_call | solution.py:502
  14.3 0.0 copy-done.2
  14.3 0.0 copy-done.4
  14.3 0.0 copy-done.5
  14.3 0.5 slots.1
  14.8 0.0 collective-permute-done.3.refs_3_
  14.8 0.0 collective-permute-done.4.refs_4_
  14.8 0.0 collective-permute-done.refs_0_
  14.8 1.4 %collective-permute-done.1.refs_1_ = bf16[2,2,128,256]{3,2,1,0:T(8,128)(2,1)S(1)} collective-permute-done((bf16[2,2,128,256]{3,2,1,0:T(8,128)(2,1)S(1)}, bf16[2,2,128,256]{3,2,1,0:T(8,128)(2,1)S(1)}, u32[]{:S(2)}, u32[]{:S(2)}) %collective-permute-start.1) | collective-permute-done | bytes 262176 | tf_op jit(solution)/shard_map/ppermute | solution.py:513
  16.2 1.3 %collective-permute-done.2.refs_2_ = bf16[2,2,256,128]{3,2,1,0:T(8,128)(2,1)S(1)} collective-permute-done((bf16[2,2,256,128]{3,2,1,0:T(8,128)(2,1)S(1)}, bf16[2,2,256,128]{3,2,1,0:T(8,128)(2,1)S(1)}, u32[]{:S(2)}, u32[]{:S(2)}) %collective-permute-start.2) | collective-permute-done | bytes 262176 | tf_op jit(solution)/shard_map/ppermute | solution.py:513
  17.5 0.0 collective-permute-start.6
  17.5 0.0 copy-done.3
  17.5 1.3 %windows_for_other.1 = (bf16[2,2,256,256]{3,2,1,0:T(8,128)(2,1)S(1)}, f32[2,2,512,512]{3,2,1,0:T(8,128)S(1)}) custom-call(s32[2,2]{1,0:T(2,128)S(1)} %copy-done.3, f32[2,2,512,512]{3,2,1,0:T(8,128)S(1)} %get-tuple-element.59._filled, bf16[2,2,128,256]{3,2,1,0:T(8,128)(2,1)S(1)} %collective-permute-done.refs_0_, ...), custom_call_target="tpu_custom_call", output_to_operand_aliasing={{1}: (1, {})} | custom-call | tf_op jit(solution)/shard_map/windows_for_other/pallas_call | solution.py:502
  18.8 0.6 collective-permute-start.5
  19.4 1.1 %windows.1.win_own = bf16[2,2,256,256]{3,2,1,0:T(8,128)(2,1)S(1)} custom-call(s32[2,2]{1,0:T(2,128)S(1)} %copy-done.3, f32[2,2,512,512]{3,2,1,0:T(8,128)S(1)} %get-tuple-element.65.ext_ref), custom_call_target="tpu_custom_call" | custom-call | tf_op jit(solution)/shard_map/windows/pallas_call | solution.py:502
  20.6 0.0 collective-permute-done.6.inc_got
  20.6 0.4 collective-permute-done.5.win_got
  20.9 0.0 copy-done
  21.0 1.3 %collective-permute-start.7 = (s32[264,256]{1,0:T(8,128)S(1)}, s32[264,256]{1,0:T(8,128)S(1)}, u32[]{:S(2)}, u32[]{:S(2)}) collective-permute-start(s32[264,256]{1,0:T(8,128)S(1)} %get-tuple-element.71), channel_id=1, source_target_pairs={{16,0},{24,8},{17,1},{25,9},{18,2},{26,10},{19,3},{27,11},{20,4},{... | collective-permute-start | bytes 811016 | tf_op jit(solution)/shard_map/ppermute | solution.py:586
  22.3 15.2 %collective-permute-done.7.wave_in = s32[264,256]{1,0:T(8,128)S(1)} collective-permute-done((s32[264,256]{1,0:T(8,128)S(1)}, s32[264,256]{1,0:T(8,128)S(1)}, u32[]{:S(2)}, u32[]{:S(2)}) %collective-permute-start.7) | collective-permute-done | bytes 270368 | tf_op jit(solution)/shard_map/ppermute | solution.py:586
  37.5 5.7 %sweep.3 = (f32[2,2,256,256]{3,2,1,0:T(8,128)S(1)}, f32[2,2,256,256]{3,2,1,0:T(8,128)S(1)}, s32[264,256]{1,0:T(8,128)}) custom-call(s32[264,256]{1,0:T(8,128)S(1)} %collective-permute-done.7.wave_in, bf16[2,2,256,256]{3,2,1,0:T(8,128)(2,1)S(1)} %windows.1.win_own, ...), custom_call_target="tpu_custom_call", output_to_operand_aliasing={{0}: (8, {}), {1}: (9, {})} | custom-call | tf_op jit(solution)/shard_map/sweep/pallas_call | solution.py:502
  43.2 0.1 collective-permute-start.8
  43.3 2.6 %collective-permute-done.8.other_ref = f32[2,2,256,256]{3,2,1,0:T(8,128)S(1)} collective-permute-done((f32[2,2,256,256]{3,2,1,0:T(8,128)S(1)}, f32[2,2,256,256]{3,2,1,0:T(8,128)S(1)}, u32[]{:S(2)}, u32[]{:S(2)}) %collective-permute-start.8) | collective-permute-done | bytes 1048608 | tf_op jit(solution)/shard_map/ppermute | solution.py:589
  45.9 2.2 %scatter.1 = (f32[2,2,512,512]{3,2,1,0:T(8,128)S(1)}, f32[8,128]{1,0:T(8,128)S(1)}, s32[536,128]{1,0:T(8,128)S(1)}) custom-call(s32[2,2]{1,0:T(2,128)S(1)} %copy-done.3, f32[2,2,256,256]{3,2,1,0:T(8,128)S(1)} %get-tuple-element.74.mine_ref, f32[2,2,256,256]{3,2,1,0:T(8,128)S(1)} %collective-permute-done.8.other_ref), custom_call_target="tpu_custom_call" | custom-call | flops 3000000000 | bytes 9000000 | tf_op jit(solution)/shard_map/scatter/pallas_call | solution.py:502
  48.2 1.0 %collective-permute-start.9 = (s32[536,128]{1,0:T(8,128)S(1)}, s32[536,128]{1,0:T(8,128)S(1)}, u32[]{:S(2)}, u32[]{:S(2)}) collective-permute-start(s32[536,128]{1,0:T(8,128)S(1)} %get-tuple-element.77), channel_id=1, source_target_pairs={{0,1},{1,0},{2,3},{3,2},{4,5},{5,4},{6,7},{7,6},{8,9},{9,8},{10,11... | collective-permute-start | bytes 823304 | tf_op jit(solution)/shard_map/ppermute | solution.py:513
  49.2 1.0 %halos.1 = (s32[264,256]{1,0:T(8,128)S(1)}, s32[264,256]{1,0:T(8,128)S(1)}, s32[264,128]{1,0:T(8,128)S(1)}, s32[264,128]{1,0:T(8,128)S(1)}) custom-call(f32[2,2,512,512]{3,2,1,0:T(8,128)S(1)} %get-tuple-element.76.ext_ref, f32[8,128]{1,0:T(8,128)S(1)} %get-tuple-element.78.exponent_ref), custom_call_target="tpu_custom_call" | custom-call | flops 1000000000 | bytes 3000000 | tf_op jit(solution)/shard_map/halos/pallas_call | solution.py:502
  50.3 0.1 collective-permute-start.10
  50.3 2.6 %collective-permute-start.11 = (s32[264,256]{1,0:T(8,128)S(1)}, s32[264,256]{1,0:T(8,128)S(1)}, u32[]{:S(2)}, u32[]{:S(2)}) collective-permute-start(s32[264,256]{1,0:T(8,128)S(1)} %get-tuple-element.80), channel_id=1, source_target_pairs={{2,4},{3,5},{4,2},{5,3},{10,12},{11,13},{12,10},{13,11},{18,20},{1... | collective-permute-start | bytes 811016 | tf_op jit(solution)/shard_map/ppermute | solution.py:513
  53.0 0.6 collective-permute-start.12
  53.6 3.2 %collective-permute-start.13 = (s32[264,128]{1,0:T(8,128)S(1)}, s32[264,128]{1,0:T(8,128)S(1)}, u32[]{:S(2)}, u32[]{:S(2)}) collective-permute-start(s32[264,128]{1,0:T(8,128)S(1)} %get-tuple-element.82), channel_id=1, source_target_pairs={{2,5},{3,4},{4,3},{5,2},{10,13},{11,12},{12,11},{13,10},{18,21},{1... | collective-permute-start | bytes 405512 | tf_op jit(solution)/shard_map/ppermute | solution.py:513
  56.8 2.9 %collective-permute-done.10.refs_1_ = s32[264,256]{1,0:T(8,128)S(1)} collective-permute-done((s32[264,256]{1,0:T(8,128)S(1)}, s32[264,256]{1,0:T(8,128)S(1)}, u32[]{:S(2)}, u32[]{:S(2)}) %collective-permute-start.10) | collective-permute-done | bytes 270368 | tf_op jit(solution)/shard_map/ppermute | solution.py:513
  59.7 1.9 %collective-permute-done.11.refs_2_ = s32[264,256]{1,0:T(8,128)S(1)} collective-permute-done((s32[264,256]{1,0:T(8,128)S(1)}, s32[264,256]{1,0:T(8,128)S(1)}, u32[]{:S(2)}, u32[]{:S(2)}) %collective-permute-start.11) | collective-permute-done | bytes 270368 | tf_op jit(solution)/shard_map/ppermute | solution.py:513
  61.6 0.0 collective-permute-done.9.refs_0_
  61.6 0.9 %fold.1.part_ref = f32[2,2,256,256]{3,2,1,0:T(8,128)S(1)} custom-call(f32[2,2,512,512]{3,2,1,0:T(8,128)S(1)} %get-tuple-element.76.ext_ref, s32[536,128]{1,0:T(8,128)S(1)} %collective-permute-done.9.refs_0_, s32[264,256]{1,0:T(8,128)S(1)} %collective-permute-done.10.refs_1_, s32[264,256]{1,0:T(8,128)S(1)} %collective-permute-done.11.refs_2_), custom_call_target="tpu_custom_call" | custom-call | flops 2000000000 | bytes 6000000 | tf_op jit(solution)/shard_map/fold/pallas_call | solution.py:502
  62.5 0.6 collective-permute-done.12.refs_0_
  63.1 1.6 %collective-permute-done.13.refs_1_ = s32[264,128]{1,0:T(8,128)S(1)} collective-permute-done((s32[264,128]{1,0:T(8,128)S(1)}, s32[264,128]{1,0:T(8,128)S(1)}, u32[]{:S(2)}, u32[]{:S(2)}) %collective-permute-start.13) | collective-permute-done | bytes 135200 | tf_op jit(solution)/shard_map/ppermute | solution.py:513
  64.7 1.3 %corners.1 = f32[2,2,256,256]{3,2,1,0:T(8,128)} custom-call(f32[2,2,256,256]{3,2,1,0:T(8,128)S(1)} %fold.1.part_ref, s32[264,128]{1,0:T(8,128)S(1)} %collective-permute-done.12.refs_0_, s32[264,128]{1,0:T(8,128)S(1)} %collective-permute-done.13.refs_1_), custom_call_target="tpu_custom_call" | custom-call | tf_op jit(solution)/shard_map/corners/pallas_call | solution.py:502
  (5 shorter events, 0.0 us)
Async XLA Ops:
  0.0 1.0 %copy-start.1 = (bf16[2,2,256,256]{3,2,1,0:T(8,128)(2,1)S(1)}, bf16[2,2,256,256]{3,2,1,0:T(8,128)(2,1)}, u32[]{:S(2)}) copy-start(bf16[2,2,256,256]{3,2,1,0:T(8,128)(2,1)} %tile_ref.1) | copy-start | bytes 1572868
  1.0 13.2 %copy-start.2 = (bf16[2,2,256,256]{3,2,1,0:T(8,128)(2,1)S(1)}, bf16[2,2,256,256]{3,2,1,0:T(8,128)(2,1)}, u32[]{:S(2)}) copy-start(bf16[2,2,256,256]{3,2,1,0:T(8,128)(2,1)} %tile_ref.1) | copy-start | bytes 1572868
  1.0 13.2 %copy-start.4 = (bf16[2,2,2,256,256]{4,3,2,1,0:T(8,128)(2,1)S(1)}, bf16[2,2,2,256,256]{4,3,2,1,0:T(8,128)(2,1)}, u32[]{:S(2)}) copy-start(bf16[2,2,2,256,256]{4,3,2,1,0:T(8,128)(2,1)} %inc_ref) | copy-start | bytes 3145732
  1.0 13.2 %copy-start.5 = (bf16[2,2,256,256]{3,2,1,0:T(8,128)(2,1)S(1)}, bf16[2,2,256,256]{3,2,1,0:T(8,128)(2,1)}, u32[]{:S(2)}) copy-start(bf16[2,2,256,256]{3,2,1,0:T(8,128)(2,1)} %exit_ref) | copy-start | bytes 1572868
  1.2 13.6 %collective-permute-start.3 = (bf16[2,2,128,128]{3,2,1,0:T(8,128)(2,1)S(1)}, bf16[2,2,128,128]{3,2,1,0:T(8,128)(2,1)S(1)}, u32[]{:S(2)}, u32[]{:S(2)}) collective-permute-start(bf16[2,2,128,128]{3,2,1,0:T(8,128)(2,1)S(1)} %get-tuple-element.47), channel_id=1, source_target_pairs={{0,3},{1,2},{2,1},{3,0},{4,7},{5,6},{6,5},{7,4},{8,11},{9,10},{10,... | collective-permute-start | bytes 393224 | tf_op jit(solution)/shard_map/ppermute | solution.py:513
  3.8 11.0 %collective-permute-start.4 = (bf16[2,2,128,128]{3,2,1,0:T(8,128)(2,1)S(1)}, bf16[2,2,128,128]{3,2,1,0:T(8,128)(2,1)S(1)}, u32[]{:S(2)}, u32[]{:S(2)}) collective-permute-start(bf16[2,2,128,128]{3,2,1,0:T(8,128)(2,1)S(1)} %get-tuple-element.48), channel_id=1, source_target_pairs={{2,5},{3,4},{4,3},{5,2},{10,13},{11,12},{12,11},{13,10},{18,21},{1... | collective-permute-start | bytes 393224 | tf_op jit(solution)/shard_map/ppermute | solution.py:513
  5.7 9.1 %collective-permute-start = (bf16[2,2,128,256]{3,2,1,0:T(8,128)(2,1)S(1)}, bf16[2,2,128,256]{3,2,1,0:T(8,128)(2,1)S(1)}, u32[]{:S(2)}, u32[]{:S(2)}) collective-permute-start(bf16[2,2,128,256]{3,2,1,0:T(8,128)(2,1)S(1)} %get-tuple-element.44), channel_id=1, source_target_pairs={{0,2},{1,3},{2,0},{3,1},{4,6},{5,7},{6,4},{7,5},{8,10},{9,11},{10,... | collective-permute-start | bytes 786440 | tf_op jit(solution)/shard_map/ppermute | solution.py:513
  5.8 10.4 %collective-permute-start.1 = (bf16[2,2,128,256]{3,2,1,0:T(8,128)(2,1)S(1)}, bf16[2,2,128,256]{3,2,1,0:T(8,128)(2,1)S(1)}, u32[]{:S(2)}, u32[]{:S(2)}) collective-permute-start(bf16[2,2,128,256]{3,2,1,0:T(8,128)(2,1)S(1)} %get-tuple-element.45), channel_id=1, source_target_pairs={{2,4},{3,5},{4,2},{5,3},{10,12},{11,13},{12,10},{13,11},{18,20},{1... | collective-permute-start | bytes 786440 | tf_op jit(solution)/shard_map/ppermute | solution.py:513
  9.6 7.8 %copy-start.3 = (s32[2,2]{1,0:T(2,128)S(1)}, s32[2,2]{1,0:T(2,128)}, u32[]{:S(2)}) copy-start(s32[2,2]{1,0:T(2,128)} %anchor_ref.5) | copy-start | bytes 52
  9.7 7.8 %collective-permute-start.2 = (bf16[2,2,256,128]{3,2,1,0:T(8,128)(2,1)S(1)}, bf16[2,2,256,128]{3,2,1,0:T(8,128)(2,1)S(1)}, u32[]{:S(2)}, u32[]{:S(2)}) collective-permute-start(bf16[2,2,256,128]{3,2,1,0:T(8,128)(2,1)S(1)} %get-tuple-element.46), channel_id=1, source_target_pairs={{0,1},{1,0},{2,3},{3,2},{4,5},{5,4},{6,7},{7,6},{8,9},{9,8},{10,11... | collective-permute-start | bytes 786440 | tf_op jit(solution)/shard_map/ppermute | solution.py:513
  11.2 0.9 %copy-start.6 = (f32[256,256]{1,0:T(8,128)S(1)}, f32[256,256]{1,0:T(8,128)}, u32[]{:S(2)}) copy-start(f32[256,256]{1,0:T(8,128)} %phase_ref) | copy-start | bytes 786436
  17.5 3.5 %copy-start = (bf16[4,256,256]{2,1,0:T(8,128)(2,1)S(1)}, bf16[4,256,256]{2,1,0:T(8,128)(2,1)}, u32[]{:S(2)}) copy-start(bf16[4,256,256]{2,1,0:T(8,128)(2,1)} %constant.2.clone.tab_ref) | copy-start | bytes 1572868
  17.5 3.1 %collective-permute-start.6 = (bf16[2,2,256,256]{3,2,1,0:T(8,128)(2,1)S(1)}, bf16[2,2,256,256]{3,2,1,0:T(8,128)(2,1)S(1)}, u32[]{:S(2)}, u32[]{:S(2)}) collective-permute-start(bf16[2,2,256,256]{3,2,1,0:T(8,128)(2,1)S(1)} %get-tuple-element.68), channel_id=1, source_target_pairs={{0,8},{8,0},{16,24},{24,16},{1,9},{9,1},{17,25},{25,17},{2,10},{10... | collective-permute-start | bytes 1572872 | tf_op jit(solution)/shard_map/ppermute | solution.py:546
  18.8 2.1 %collective-permute-start.5 = (bf16[2,2,256,256]{3,2,1,0:T(8,128)(2,1)S(1)}, bf16[2,2,256,256]{3,2,1,0:T(8,128)(2,1)S(1)}, u32[]{:S(2)}, u32[]{:S(2)}) collective-permute-start(bf16[2,2,256,256]{3,2,1,0:T(8,128)(2,1)S(1)} %get-tuple-element.66), channel_id=1, source_target_pairs={{0,8},{8,0},{16,24},{24,16},{1,9},{9,1},{17,25},{25,17},{2,10},{10... | collective-permute-start | bytes 1572872 | tf_op jit(solution)/shard_map/ppermute | solution.py:557
  21.0 16.5 %collective-permute-start.7 = (s32[264,256]{1,0:T(8,128)S(1)}, s32[264,256]{1,0:T(8,128)S(1)}, u32[]{:S(2)}, u32[]{:S(2)}) collective-permute-start(s32[264,256]{1,0:T(8,128)S(1)} %get-tuple-element.71), channel_id=1, source_target_pairs={{16,0},{24,8},{17,1},{25,9},{18,2},{26,10},{19,3},{27,11},{20,4},{... | collective-permute-start | bytes 811016 | tf_op jit(solution)/shard_map/ppermute | solution.py:586
  43.2 2.7 %collective-permute-start.8 = (f32[2,2,256,256]{3,2,1,0:T(8,128)S(1)}, f32[2,2,256,256]{3,2,1,0:T(8,128)S(1)}, u32[]{:S(2)}, u32[]{:S(2)}) collective-permute-start(f32[2,2,256,256]{3,2,1,0:T(8,128)S(1)} %get-tuple-element.75), channel_id=1, source_target_pairs={{0,8},{8,0},{16,24},{24,16},{1,9},{9,1},{17,25},{25,17},{2,10},{10... | collective-permute-start | bytes 3145736 | tf_op jit(solution)/shard_map/ppermute | solution.py:589
  48.2 13.4 %collective-permute-start.9 = (s32[536,128]{1,0:T(8,128)S(1)}, s32[536,128]{1,0:T(8,128)S(1)}, u32[]{:S(2)}, u32[]{:S(2)}) collective-permute-start(s32[536,128]{1,0:T(8,128)S(1)} %get-tuple-element.77), channel_id=1, source_target_pairs={{0,1},{1,0},{2,3},{3,2},{4,5},{5,4},{6,7},{7,6},{8,9},{9,8},{10,11... | collective-permute-start | bytes 823304 | tf_op jit(solution)/shard_map/ppermute | solution.py:513
  50.3 9.4 %collective-permute-start.10 = (s32[264,256]{1,0:T(8,128)S(1)}, s32[264,256]{1,0:T(8,128)S(1)}, u32[]{:S(2)}, u32[]{:S(2)}) collective-permute-start(s32[264,256]{1,0:T(8,128)S(1)} %get-tuple-element.79), channel_id=1, source_target_pairs={{0,2},{1,3},{2,0},{3,1},{4,6},{5,7},{6,4},{7,5},{8,10},{9,11},{10,... | collective-permute-start | bytes 811016 | tf_op jit(solution)/shard_map/ppermute | solution.py:513
  50.3 11.3 %collective-permute-start.11 = (s32[264,256]{1,0:T(8,128)S(1)}, s32[264,256]{1,0:T(8,128)S(1)}, u32[]{:S(2)}, u32[]{:S(2)}) collective-permute-start(s32[264,256]{1,0:T(8,128)S(1)} %get-tuple-element.80), channel_id=1, source_target_pairs={{2,4},{3,5},{4,2},{5,3},{10,12},{11,13},{12,10},{13,11},{18,20},{1... | collective-permute-start | bytes 811016 | tf_op jit(solution)/shard_map/ppermute | solution.py:513
  53.0 10.1 %collective-permute-start.12 = (s32[264,128]{1,0:T(8,128)S(1)}, s32[264,128]{1,0:T(8,128)S(1)}, u32[]{:S(2)}, u32[]{:S(2)}) collective-permute-start(s32[264,128]{1,0:T(8,128)S(1)} %get-tuple-element.81), channel_id=1, source_target_pairs={{0,3},{1,2},{2,1},{3,0},{4,7},{5,6},{6,5},{7,4},{8,11},{9,10},{10,... | collective-permute-start | bytes 405512 | tf_op jit(solution)/shard_map/ppermute | solution.py:513
  53.6 11.1 %collective-permute-start.13 = (s32[264,128]{1,0:T(8,128)S(1)}, s32[264,128]{1,0:T(8,128)S(1)}, u32[]{:S(2)}, u32[]{:S(2)}) collective-permute-start(s32[264,128]{1,0:T(8,128)S(1)} %get-tuple-element.82), channel_id=1, source_target_pairs={{2,5},{3,4},{4,3},{5,2},{10,13},{11,12},{12,11},{13,10},{18,21},{1... | collective-permute-start | bytes 405512 | tf_op jit(solution)/shard_map/ppermute | solution.py:513

commit v7 on v6

--- a/solution.py
+++ b/solution.py
@@ -16,6 +16,7 @@
 LEVELS = 32767.0
 SCALE_ROWS = 8
 FIRST = 3
+CHUNKS = 2
 EARLY = ((0, None), (1, None), (None, 0), (None, 1), (0, 0), (0, 1), (1, 0), (1, 1))
 LATE = ((None, 0), (None, 1), (0, None), (1, None), (0, 0), (0, 1), (1, 0), (1, 1))
 SUBLANES = 8
@@ -113,13 +114,14 @@
     return [right3(field, table) for field in fields]
 
 
-def middle(parts, cos_ref, sin_ref):
-    half = parts[0].shape[0] // 2
-    row0 = lax.broadcasted_iota(jnp.int32, (half, half), 0) == 0
-    col0 = lax.broadcasted_iota(jnp.int32, (half, half), 1) == 0
+def middle(parts, cos_ref, sin_ref, chunk, chunks):
+    half = parts[0].shape[1] // 2
+    size = half // chunks
+    row0 = chunk * size + lax.broadcasted_iota(jnp.int32, (size, half), 0) == 0
+    col0 = lax.broadcasted_iota(jnp.int32, (size, half), 1) == 0
 
     def quadrant(r, c):
-        return tuple(part[r * half : (r + 1) * half, c * half : (c + 1) * half] for part in parts)
+        return tuple(part[r * size : (r + 1) * size, c * half : (c + 1) * half] for part in parts)
 
     top = spectrum_split(quadrant(0, 0), quadrant(0, 1), col0)
     bottom = spectrum_split(quadrant(1, 0), quadrant(1, 1), col0)
@@ -127,7 +129,8 @@
     for c in range(2):
         turned = []
         for r, (re, im) in enumerate(spectrum_split(top[c], bottom[c], row0)):
-            where = (slice(r * half, (r + 1) * half), slice(c * half, (c + 1) * half))
+            first = r * half + chunk * size
+            where = (slice(first, first + size), slice(c * half, (c + 1) * half))
             cos, sin = cos_ref[where], sin_ref[where]
             turned.append((re * cos + im * sin, im * cos - re * sin))
         out[0][c], out[1][c] = spectrum_join(turned[0], turned[1], row0)
@@ -143,8 +146,20 @@
 def propagate(parts, cos_ref, sin_ref, tab_ref):
     table = (tab_ref[0], tab_ref[1])
     turned = (tab_ref[2], tab_ref[3])
-    spectrum = middle(rights(lefts(table, parts), turned), cos_ref, sin_ref)
-    return lefts(turned, rights(spectrum, table))
+    half = cos_ref.shape[0] // 2
+    size = half // CHUNKS
+    parts = lefts(table, parts)
+    spectra = []
+    for chunk in range(CHUNKS):
+        rows = slice(chunk * size, (chunk + 1) * size)
+        lower = slice(half + chunk * size, half + (chunk + 1) * size)
+        spectra.append(rights([jnp.concatenate([part[rows], part[lower]], axis=0) for part in parts], turned))
+    spectra = [middle(spectrum, cos_ref, sin_ref, chunk, CHUNKS) for chunk, spectrum in enumerate(spectra)]
+    spectra = [rights(spectrum, table) for spectrum in spectra]
+    fields = [
+        jnp.concatenate([s[c][:size] for s in spectra] + [s[c][size:] for s in spectra], axis=0) for c in range(2)
+    ]
+    return lefts(turned, fields)
 
 
 def window_place(at_x, at_y):
@@ -418,27 +433,34 @@
     lax.fori_loop(0, ext_ref.shape[0], one, 0)
 
 
-def scatter_kernel(kinds, tile, anchor_ref, mine_ref, other_ref, ext_ref, exponent_ref, *refs):
-    pieces, top_ref = refs[:-1], refs[-1]
-    slab = mine_ref.shape[0]
-    core = core_index()
-    corners = [corner_of(anchor_ref, slot, tile // 2, tile) for slot in (core, 1 - core)]
-    top_ref[...] = jnp.zeros_like(top_ref)
-
-    def add(index, _):
+def scatter_own_kernel(tile, anchor_ref, term_ref, ext_ref, top_ref):
+    at_x, at_y = corner_of(anchor_ref, core_index(), tile // 2, tile)
+
+    def add(index, top):
         layer, c = index // 2, lax.rem(index, 2)
         plane = ext_ref.at[layer, c]
         plane[...] = jnp.zeros(plane.shape, plane.dtype)
-        bound = 0.0
-        for (at_x, at_y), term in zip(corners, (mine_ref, other_ref)):
-            value = term[layer, c]
-            add_window(plane, at_x, at_y, value)
-            bound = bound + jnp.max(jnp.abs(value), axis=0, keepdims=True)
-        top_ref[...] = jnp.maximum(top_ref[...], bound)
-        return 0
-
-    lax.fori_loop(0, 2 * slab, add, 0)
-    exponent = exponent_of(top_ref[...])
+        value = term_ref[layer, c]
+        add_window(plane, at_x, at_y, value)
+        return jnp.maximum(top, jnp.max(jnp.abs(value), axis=0, keepdims=True))
+
+    top = jnp.zeros((1, term_ref.shape[-1]), jnp.float32)
+    top = lax.fori_loop(0, 2 * term_ref.shape[0], add, top)
+    top_ref[...] = jnp.broadcast_to(top, top_ref.shape)
+
+
+def scatter_kernel(kinds, tile, anchor_ref, term_ref, _own, own_top_ref, ext_ref, exponent_ref, *pieces):
+    at_x, at_y = corner_of(anchor_ref, 1 - core_index(), tile // 2, tile)
+
+    def add(index, top):
+        layer, c = index // 2, lax.rem(index, 2)
+        value = term_ref[layer, c]
+        add_window(ext_ref.at[layer, c], at_x, at_y, value)
+        return jnp.maximum(top, jnp.max(jnp.abs(value), axis=0, keepdims=True))
+
+    top = jnp.zeros((1, term_ref.shape[-1]), jnp.float32)
+    top = lax.fori_loop(0, 2 * term_ref.shape[0], add, top)
+    exponent = exponent_of(top + jnp.max(own_top_ref[:1, :], axis=1, keepdims=True))
     exponent_ref[...] = jnp.broadcast_to(exponent, exponent_ref.shape)
     send_halos(kinds, pieces, tile, ext_ref, exponent)
 
@@ -598,14 +620,22 @@
     rest = [kind for kind in late if kind[0] is not None]
     sides = [kind for kind in late if None in kind]
     corners = [kind for kind in late if None not in kind]
+    ext, top = call(
+        functools.partial(scatter_own_kernel, tile),
+        (ext_shape, shape_of((SUBLANES, patch), f32)),
+        (scan_anchor, keep),
+        "scatter_own",
+        cost=2,
+        in_specs=[SMEM, VMEM],
+    )
     ext, exponent, *beyond = call(
         functools.partial(scatter_kernel, first, tile),
         (ext_shape, shape_of((SUBLANES, LANES), f32)) + coded_rims(first),
-        (scan_anchor, keep, got),
+        (scan_anchor, got, ext, top),
         "scatter",
-        [pltpu.VMEM((1, patch), f32)],
-        cost=3,
-        in_specs=[SMEM, VMEM, VMEM],
+        cost=2,
+        in_specs=[SMEM] + [VMEM] * 3,
+        input_output_aliases={2: 0},
     )
     more = call(functools.partial(halos_kernel, rest, tile), coded_rims(rest), (ext, exponent), "halos", cost=1)
     sent = dict(zip(first + rest, (*beyond, *more)))

time: 66.2 us -> 65.1 us (0.983)
  waiting for transfers between devices: 27.9 us -> 26.1 us
  Pallas kernels: 15.7 us -> 16.4 us
    ppermute x1, waiting for transfers between devices: 2.65 us -> 1.15 us  [shards(): got = lax.ppermute(send, 'depth', core_swap)]
    pallas_call x11 -> x12, Pallas kernels: 15.7 us -> 16.4 us  [call(): pl.pallas_call(kernel, out_shape=out_shape, scratch_shapes=list(scratch),...]
  transfers between devices with their start and end apart: 14 -> 14, of which waited for: 9 -> 9; matrix products, arithmetic and copies ran while one was open for 0% -> 0% of each run, Pallas kernels for 10% -> 12%
where the time goes in v7:
time: 65.1 us; the launch traced here: 64.8 us
  waiting for transfers between devices  26.1 us (40%)
  starting transfers between devices  19.5 us (30%)
  Pallas kernels  16.4 us (25%)
  local copies, waits for them, and re-layouts  2.01 us (3%)
  between operations  0.87 us (1%)
    ppermute x10, starting transfers between devices, swapped(): lax.ppermute(value, ('sx', 'sy'), swap_list(n_x, n_y, *kind))  17.5 us
    pallas_call x12, Pallas kernels, call(): pl.pallas_call(kernel, out_shape=out_shape, scratch_shapes=list(scratch),...  16.4 us
    ppermute x1, waiting for transfers between devices, shards(): lax.ppermute(wave, 'depth', [(2 * source + c, 2 * source - 2 + c) for c i...  14.9 us
    ppermute x10, waiting for transfers between devices, swapped(): lax.ppermute(value, ('sx', 'sy'), swap_list(n_x, n_y, *kind))  9.71 us
    unnamed x14, local copies, waits for them, and re-layouts  2.01 us
  transfers between devices with their start and end apart: 14, of which 9 were waited for; matrix products, arithmetic and copies ran while one was open for 0% of the time, Pallas kernels for 12%

profile of v7, /device:TPU:16, one launch (start us, length us, event | category | flops | bytes accessed | tf_op | source)
XLA Modules:
  0.0 64.8 jit_solution(16238180747127276972)
XLA Ops:
  0.0 0.0 copy-start.1
  0.0 1.0 %copy-done.1 = bf16[2,2,256,256]{3,2,1,0:T(8,128)(2,1)S(1)} copy-done((bf16[2,2,256,256]{3,2,1,0:T(8,128)(2,1)S(1)}, bf16[2,2,256,256]{3,2,1,0:T(8,128)(2,1)}, u32[]{:S(2)}) %copy-start.1) | copy-done | bytes 524312
  1.0 0.1 rims.1
  1.2 2.6 %collective-permute-start.3 = (bf16[2,2,128,128]{3,2,1,0:T(8,128)(2,1)S(1)}, bf16[2,2,128,128]{3,2,1,0:T(8,128)(2,1)S(1)}, u32[]{:S(2)}, u32[]{:S(2)}) collective-permute-start(bf16[2,2,128,128]{3,2,1,0:T(8,128)(2,1)S(1)} %get-tuple-element.49), channel_id=1, source_target_pairs={{0,3},{1,2},{2,1},{3,0},{4,7},{5,6},{6,5},{7,4},{8,11},{9,10},{10,... | collective-permute-start | bytes 393224 | tf_op jit(solution)/shard_map/ppermute | solution.py:535
  3.8 1.9 %collective-permute-start.4 = (bf16[2,2,128,128]{3,2,1,0:T(8,128)(2,1)S(1)}, bf16[2,2,128,128]{3,2,1,0:T(8,128)(2,1)S(1)}, u32[]{:S(2)}, u32[]{:S(2)}) collective-permute-start(bf16[2,2,128,128]{3,2,1,0:T(8,128)(2,1)S(1)} %get-tuple-element.50), channel_id=1, source_target_pairs={{2,5},{3,4},{4,3},{5,2},{10,13},{11,12},{12,11},{13,10},{18,21},{1... | collective-permute-start | bytes 393224 | tf_op jit(solution)/shard_map/ppermute | solution.py:535
  5.7 0.1 collective-permute-start
  5.8 3.9 %collective-permute-start.1 = (bf16[2,2,128,256]{3,2,1,0:T(8,128)(2,1)S(1)}, bf16[2,2,128,256]{3,2,1,0:T(8,128)(2,1)S(1)}, u32[]{:S(2)}, u32[]{:S(2)}) collective-permute-start(bf16[2,2,128,256]{3,2,1,0:T(8,128)(2,1)S(1)} %get-tuple-element.47), channel_id=1, source_target_pairs={{2,4},{3,5},{4,2},{5,3},{10,12},{11,13},{12,10},{13,11},{18,20},{1... | collective-permute-start | bytes 786440 | tf_op jit(solution)/shard_map/ppermute | solution.py:535
  9.6 0.0 copy-start.3
  9.7 1.6 %collective-permute-start.2 = (bf16[2,2,256,128]{3,2,1,0:T(8,128)(2,1)S(1)}, bf16[2,2,256,128]{3,2,1,0:T(8,128)(2,1)S(1)}, u32[]{:S(2)}, u32[]{:S(2)}) collective-permute-start(bf16[2,2,256,128]{3,2,1,0:T(8,128)(2,1)S(1)} %get-tuple-element.48), channel_id=1, source_target_pairs={{0,1},{1,0},{2,3},{3,2},{4,5},{5,4},{6,7},{7,6},{8,9},{9,8},{10,11... | collective-permute-start | bytes 786440 | tf_op jit(solution)/shard_map/ppermute | solution.py:535
  11.2 0.9 %copy-done.6 = f32[256,256]{1,0:T(8,128)S(1)} copy-done((f32[256,256]{1,0:T(8,128)S(1)}, f32[256,256]{1,0:T(8,128)}, u32[]{:S(2)}) %copy-start.6) | copy-done | bytes 262168
  12.2 1.4 %turn.1 = (f32[256,256]{1,0:T(8,128)S(1)}, f32[256,256]{1,0:T(8,128)S(1)}) custom-call(f32[256,256]{1,0:T(8,128)S(1)} %copy-done.6), custom_call_target="tpu_custom_call" | custom-call | flops 2000000000 | bytes 6000000 | tf_op jit(solution)/shard_map/turn/pallas_call | solution.py:524
  14.3 0.0 copy-done.2
  14.3 0.0 copy-done.4
  14.3 0.0 copy-done.5
  14.3 0.5 slots.1
  14.8 0.0 collective-permute-done.3.refs_3_
  14.8 0.0 collective-permute-done.4.refs_4_
  14.8 0.0 collective-permute-done.refs_0_
  14.8 1.4 %collective-permute-done.1.refs_1_ = bf16[2,2,128,256]{3,2,1,0:T(8,128)(2,1)S(1)} collective-permute-done((bf16[2,2,128,256]{3,2,1,0:T(8,128)(2,1)S(1)}, bf16[2,2,128,256]{3,2,1,0:T(8,128)(2,1)S(1)}, u32[]{:S(2)}, u32[]{:S(2)}) %collective-permute-start.1) | collective-permute-done | bytes 262176 | tf_op jit(solution)/shard_map/ppermute | solution.py:535
  16.2 1.3 %collective-permute-done.2.refs_2_ = bf16[2,2,256,128]{3,2,1,0:T(8,128)(2,1)S(1)} collective-permute-done((bf16[2,2,256,128]{3,2,1,0:T(8,128)(2,1)S(1)}, bf16[2,2,256,128]{3,2,1,0:T(8,128)(2,1)S(1)}, u32[]{:S(2)}, u32[]{:S(2)}) %collective-permute-start.2) | collective-permute-done | bytes 262176 | tf_op jit(solution)/shard_map/ppermute | solution.py:535
  17.5 0.0 collective-permute-start.6
  17.5 0.0 copy-done.3
  17.5 1.3 %windows_for_other.1 = (bf16[2,2,256,256]{3,2,1,0:T(8,128)(2,1)S(1)}, f32[2,2,512,512]{3,2,1,0:T(8,128)S(1)}) custom-call(s32[2,2]{1,0:T(2,128)S(1)} %copy-done.3, f32[2,2,512,512]{3,2,1,0:T(8,128)S(1)} %get-tuple-element.61._filled, bf16[2,2,128,256]{3,2,1,0:T(8,128)(2,1)S(1)} %collective-permute-done.refs_0_, ...), custom_call_target="tpu_custom_call", output_to_operand_aliasing={{1}: (1, {})} | custom-call | tf_op jit(solution)/shard_map/windows_for_other/pallas_call | solution.py:524
  18.8 0.6 collective-permute-start.5
  19.4 1.1 %windows.1.win_own = bf16[2,2,256,256]{3,2,1,0:T(8,128)(2,1)S(1)} custom-call(s32[2,2]{1,0:T(2,128)S(1)} %copy-done.3, f32[2,2,512,512]{3,2,1,0:T(8,128)S(1)} %get-tuple-element.67.ext_ref), custom_call_target="tpu_custom_call" | custom-call | tf_op jit(solution)/shard_map/windows/pallas_call | solution.py:524
  20.6 0.0 collective-permute-done.6.inc_got
  20.6 0.4 collective-permute-done.5.win_got
  20.9 0.0 copy-done
  21.0 1.3 %collective-permute-start.7 = (s32[264,256]{1,0:T(8,128)S(1)}, s32[264,256]{1,0:T(8,128)S(1)}, u32[]{:S(2)}, u32[]{:S(2)}) collective-permute-start(s32[264,256]{1,0:T(8,128)S(1)} %get-tuple-element.73), channel_id=1, source_target_pairs={{16,0},{24,8},{17,1},{25,9},{18,2},{26,10},{19,3},{27,11},{20,4},{... | collective-permute-start | bytes 811016 | tf_op jit(solution)/shard_map/ppermute | solution.py:608
  22.3 14.9 %collective-permute-done.7.wave_in = s32[264,256]{1,0:T(8,128)S(1)} collective-permute-done((s32[264,256]{1,0:T(8,128)S(1)}, s32[264,256]{1,0:T(8,128)S(1)}, u32[]{:S(2)}, u32[]{:S(2)}) %collective-permute-start.7) | collective-permute-done | bytes 270368 | tf_op jit(solution)/shard_map/ppermute | solution.py:608
  37.2 5.5 %sweep.3 = (f32[2,2,256,256]{3,2,1,0:T(8,128)S(1)}, f32[2,2,256,256]{3,2,1,0:T(8,128)S(1)}, s32[264,256]{1,0:T(8,128)}) custom-call(s32[264,256]{1,0:T(8,128)S(1)} %collective-permute-done.7.wave_in, bf16[2,2,256,256]{3,2,1,0:T(8,128)(2,1)S(1)} %windows.1.win_own, ...), custom_call_target="tpu_custom_call", output_to_operand_aliasing={{0}: (8, {}), {1}: (9, {})} | custom-call | tf_op jit(solution)/shard_map/sweep/pallas_call | solution.py:524
  42.6 0.1 collective-permute-start.8
  42.7 1.5 %scatter_own.1 = (f32[2,2,512,512]{3,2,1,0:T(8,128)S(1)}, f32[8,256]{1,0:T(8,128)S(1)}) custom-call(s32[2,2]{1,0:T(2,128)S(1)} %copy-done.3, f32[2,2,256,256]{3,2,1,0:T(8,128)S(1)} %get-tuple-element.77.term_ref), custom_call_target="tpu_custom_call" | custom-call | flops 2000000000 | bytes 6000000 | tf_op jit(solution)/shard_map/scatter_own/pallas_call | solution.py:524
  44.2 1.1 %collective-permute-done.8.term_ref = f32[2,2,256,256]{3,2,1,0:T(8,128)S(1)} collective-permute-done((f32[2,2,256,256]{3,2,1,0:T(8,128)S(1)}, f32[2,2,256,256]{3,2,1,0:T(8,128)S(1)}, u32[]{:S(2)}, u32[]{:S(2)}) %collective-permute-start.8) | collective-permute-done | bytes 1048608 | tf_op jit(solution)/shard_map/ppermute | solution.py:611
  45.3 1.7 %scatter.1 = (f32[2,2,512,512]{3,2,1,0:T(8,128)S(1)}, f32[8,128]{1,0:T(8,128)S(1)}, s32[536,128]{1,0:T(8,128)S(1)}) custom-call(s32[2,2]{1,0:T(2,128)S(1)} %copy-done.3, f32[2,2,256,256]{3,2,1,0:T(8,128)S(1)} %collective-permute-done.8.term_ref, f32[2,2,512,512]{3,2,1,0:T(8,128)S(1)} %get-tuple-element.78._own, ...), custom_call_target="tpu_custom_call", output_to_operand_aliasing={{0}: (2, {})} | custom-call | flops 2000000000 | bytes 6000000 | tf_op jit(solution)/shard_map/scatter/pallas_call | solution.py:524
  47.1 1.0 %collective-permute-start.9 = (s32[536,128]{1,0:T(8,128)S(1)}, s32[536,128]{1,0:T(8,128)S(1)}, u32[]{:S(2)}, u32[]{:S(2)}) collective-permute-start(s32[536,128]{1,0:T(8,128)S(1)} %get-tuple-element.81), channel_id=1, source_target_pairs={{0,1},{1,0},{2,3},{3,2},{4,5},{5,4},{6,7},{7,6},{8,9},{9,8},{10,11... | collective-permute-start | bytes 823304 | tf_op jit(solution)/shard_map/ppermute | solution.py:535
  48.1 1.0 %halos.1 = (s32[264,256]{1,0:T(8,128)S(1)}, s32[264,256]{1,0:T(8,128)S(1)}, s32[264,128]{1,0:T(8,128)S(1)}, s32[264,128]{1,0:T(8,128)S(1)}) custom-call(f32[2,2,512,512]{3,2,1,0:T(8,128)S(1)} %get-tuple-element.80.ext_ref, f32[8,128]{1,0:T(8,128)S(1)} %get-tuple-element.82.exponent_ref), custom_call_target="tpu_custom_call" | custom-call | flops 1000000000 | bytes 3000000 | tf_op jit(solution)/shard_map/halos/pallas_call | solution.py:524
  49.2 0.1 collective-permute-start.10
  49.2 2.7 %collective-permute-start.11 = (s32[264,256]{1,0:T(8,128)S(1)}, s32[264,256]{1,0:T(8,128)S(1)}, u32[]{:S(2)}, u32[]{:S(2)}) collective-permute-start(s32[264,256]{1,0:T(8,128)S(1)} %get-tuple-element.84), channel_id=1, source_target_pairs={{2,4},{3,5},{4,2},{5,3},{10,12},{11,13},{12,10},{13,11},{18,20},{1... | collective-permute-start | bytes 811016 | tf_op jit(solution)/shard_map/ppermute | solution.py:535
  51.9 0.6 collective-permute-start.12
  52.5 3.2 %collective-permute-start.13 = (s32[264,128]{1,0:T(8,128)S(1)}, s32[264,128]{1,0:T(8,128)S(1)}, u32[]{:S(2)}, u32[]{:S(2)}) collective-permute-start(s32[264,128]{1,0:T(8,128)S(1)} %get-tuple-element.86), channel_id=1, source_target_pairs={{2,5},{3,4},{4,3},{5,2},{10,13},{11,12},{12,11},{13,10},{18,21},{1... | collective-permute-start | bytes 405512 | tf_op jit(solution)/shard_map/ppermute | solution.py:535
  55.7 2.9 %collective-permute-done.10.refs_1_ = s32[264,256]{1,0:T(8,128)S(1)} collective-permute-done((s32[264,256]{1,0:T(8,128)S(1)}, s32[264,256]{1,0:T(8,128)S(1)}, u32[]{:S(2)}, u32[]{:S(2)}) %collective-permute-start.10) | collective-permute-done | bytes 270368 | tf_op jit(solution)/shard_map/ppermute | solution.py:535
  58.6 1.9 %collective-permute-done.11.refs_2_ = s32[264,256]{1,0:T(8,128)S(1)} collective-permute-done((s32[264,256]{1,0:T(8,128)S(1)}, s32[264,256]{1,0:T(8,128)S(1)}, u32[]{:S(2)}, u32[]{:S(2)}) %collective-permute-start.11) | collective-permute-done | bytes 270368 | tf_op jit(solution)/shard_map/ppermute | solution.py:535
  60.5 0.0 collective-permute-done.9.refs_0_
  60.5 0.9 %fold.1.part_ref = f32[2,2,256,256]{3,2,1,0:T(8,128)S(1)} custom-call(f32[2,2,512,512]{3,2,1,0:T(8,128)S(1)} %get-tuple-element.80.ext_ref, s32[536,128]{1,0:T(8,128)S(1)} %collective-permute-done.9.refs_0_, s32[264,256]{1,0:T(8,128)S(1)} %collective-permute-done.10.refs_1_, s32[264,256]{1,0:T(8,128)S(1)} %collective-permute-done.11.refs_2_), custom_call_target="tpu_custom_call" | custom-call | flops 2000000000 | bytes 6000000 | tf_op jit(solution)/shard_map/fold/pallas_call | solution.py:524
  61.4 0.6 %collective-permute-done.12.refs_0_ = s32[264,128]{1,0:T(8,128)S(1)} collective-permute-done((s32[264,128]{1,0:T(8,128)S(1)}, s32[264,128]{1,0:T(8,128)S(1)}, u32[]{:S(2)}, u32[]{:S(2)}) %collective-permute-start.12) | collective-permute-done | bytes 135200 | tf_op jit(solution)/shard_map/ppermute | solution.py:535
  62.0 1.6 %collective-permute-done.13.refs_1_ = s32[264,128]{1,0:T(8,128)S(1)} collective-permute-done((s32[264,128]{1,0:T(8,128)S(1)}, s32[264,128]{1,0:T(8,128)S(1)}, u32[]{:S(2)}, u32[]{:S(2)}) %collective-permute-start.13) | collective-permute-done | bytes 135200 | tf_op jit(solution)/shard_map/ppermute | solution.py:535
  63.6 1.3 %corners.1 = f32[2,2,256,256]{3,2,1,0:T(8,128)} custom-call(f32[2,2,256,256]{3,2,1,0:T(8,128)S(1)} %fold.1.part_ref, s32[264,128]{1,0:T(8,128)S(1)} %collective-permute-done.12.refs_0_, s32[264,128]{1,0:T(8,128)S(1)} %collective-permute-done.13.refs_1_), custom_call_target="tpu_custom_call" | custom-call | tf_op jit(solution)/shard_map/corners/pallas_call | solution.py:524
  (6 shorter events, 0.0 us)
Async XLA Ops:
  0.0 1.0 %copy-start.1 = (bf16[2,2,256,256]{3,2,1,0:T(8,128)(2,1)S(1)}, bf16[2,2,256,256]{3,2,1,0:T(8,128)(2,1)}, u32[]{:S(2)}) copy-start(bf16[2,2,256,256]{3,2,1,0:T(8,128)(2,1)} %tile_ref.1) | copy-start | bytes 1572868
  1.0 13.2 %copy-start.2 = (bf16[2,2,256,256]{3,2,1,0:T(8,128)(2,1)S(1)}, bf16[2,2,256,256]{3,2,1,0:T(8,128)(2,1)}, u32[]{:S(2)}) copy-start(bf16[2,2,256,256]{3,2,1,0:T(8,128)(2,1)} %tile_ref.1) | copy-start | bytes 1572868
  1.0 13.2 %copy-start.4 = (bf16[2,2,2,256,256]{4,3,2,1,0:T(8,128)(2,1)S(1)}, bf16[2,2,2,256,256]{4,3,2,1,0:T(8,128)(2,1)}, u32[]{:S(2)}) copy-start(bf16[2,2,2,256,256]{4,3,2,1,0:T(8,128)(2,1)} %inc_ref) | copy-start | bytes 3145732
  1.0 13.2 %copy-start.5 = (bf16[2,2,256,256]{3,2,1,0:T(8,128)(2,1)S(1)}, bf16[2,2,256,256]{3,2,1,0:T(8,128)(2,1)}, u32[]{:S(2)}) copy-start(bf16[2,2,256,256]{3,2,1,0:T(8,128)(2,1)} %exit_ref) | copy-start | bytes 1572868
  1.2 13.6 %collective-permute-start.3 = (bf16[2,2,128,128]{3,2,1,0:T(8,128)(2,1)S(1)}, bf16[2,2,128,128]{3,2,1,0:T(8,128)(2,1)S(1)}, u32[]{:S(2)}, u32[]{:S(2)}) collective-permute-start(bf16[2,2,128,128]{3,2,1,0:T(8,128)(2,1)S(1)} %get-tuple-element.49), channel_id=1, source_target_pairs={{0,3},{1,2},{2,1},{3,0},{4,7},{5,6},{6,5},{7,4},{8,11},{9,10},{10,... | collective-permute-start | bytes 393224 | tf_op jit(solution)/shard_map/ppermute | solution.py:535
  3.8 11.0 %collective-permute-start.4 = (bf16[2,2,128,128]{3,2,1,0:T(8,128)(2,1)S(1)}, bf16[2,2,128,128]{3,2,1,0:T(8,128)(2,1)S(1)}, u32[]{:S(2)}, u32[]{:S(2)}) collective-permute-start(bf16[2,2,128,128]{3,2,1,0:T(8,128)(2,1)S(1)} %get-tuple-element.50), channel_id=1, source_target_pairs={{2,5},{3,4},{4,3},{5,2},{10,13},{11,12},{12,11},{13,10},{18,21},{1... | collective-permute-start | bytes 393224 | tf_op jit(solution)/shard_map/ppermute | solution.py:535
  5.7 9.1 %collective-permute-start = (bf16[2,2,128,256]{3,2,1,0:T(8,128)(2,1)S(1)}, bf16[2,2,128,256]{3,2,1,0:T(8,128)(2,1)S(1)}, u32[]{:S(2)}, u32[]{:S(2)}) collective-permute-start(bf16[2,2,128,256]{3,2,1,0:T(8,128)(2,1)S(1)} %get-tuple-element.46), channel_id=1, source_target_pairs={{0,2},{1,3},{2,0},{3,1},{4,6},{5,7},{6,4},{7,5},{8,10},{9,11},{10,... | collective-permute-start | bytes 786440 | tf_op jit(solution)/shard_map/ppermute | solution.py:535
  5.8 10.4 %collective-permute-start.1 = (bf16[2,2,128,256]{3,2,1,0:T(8,128)(2,1)S(1)}, bf16[2,2,128,256]{3,2,1,0:T(8,128)(2,1)S(1)}, u32[]{:S(2)}, u32[]{:S(2)}) collective-permute-start(bf16[2,2,128,256]{3,2,1,0:T(8,128)(2,1)S(1)} %get-tuple-element.47), channel_id=1, source_target_pairs={{2,4},{3,5},{4,2},{5,3},{10,12},{11,13},{12,10},{13,11},{18,20},{1... | collective-permute-start | bytes 786440 | tf_op jit(solution)/shard_map/ppermute | solution.py:535
  9.6 7.8 %copy-start.3 = (s32[2,2]{1,0:T(2,128)S(1)}, s32[2,2]{1,0:T(2,128)}, u32[]{:S(2)}) copy-start(s32[2,2]{1,0:T(2,128)} %anchor_ref.7) | copy-start | bytes 52
  9.7 7.8 %collective-permute-start.2 = (bf16[2,2,256,128]{3,2,1,0:T(8,128)(2,1)S(1)}, bf16[2,2,256,128]{3,2,1,0:T(8,128)(2,1)S(1)}, u32[]{:S(2)}, u32[]{:S(2)}) collective-permute-start(bf16[2,2,256,128]{3,2,1,0:T(8,128)(2,1)S(1)} %get-tuple-element.48), channel_id=1, source_target_pairs={{0,1},{1,0},{2,3},{3,2},{4,5},{5,4},{6,7},{7,6},{8,9},{9,8},{10,11... | collective-permute-start | bytes 786440 | tf_op jit(solution)/shard_map/ppermute | solution.py:535
  11.2 0.9 %copy-start.6 = (f32[256,256]{1,0:T(8,128)S(1)}, f32[256,256]{1,0:T(8,128)}, u32[]{:S(2)}) copy-start(f32[256,256]{1,0:T(8,128)} %phase_ref) | copy-start | bytes 786436
  17.5 3.5 %copy-start = (bf16[4,256,256]{2,1,0:T(8,128)(2,1)S(1)}, bf16[4,256,256]{2,1,0:T(8,128)(2,1)}, u32[]{:S(2)}) copy-start(bf16[4,256,256]{2,1,0:T(8,128)(2,1)} %constant.2.clone.tab_ref) | copy-start | bytes 1572868
  17.5 3.1 %collective-permute-start.6 = (bf16[2,2,256,256]{3,2,1,0:T(8,128)(2,1)S(1)}, bf16[2,2,256,256]{3,2,1,0:T(8,128)(2,1)S(1)}, u32[]{:S(2)}, u32[]{:S(2)}) collective-permute-start(bf16[2,2,256,256]{3,2,1,0:T(8,128)(2,1)S(1)} %get-tuple-element.70), channel_id=1, source_target_pairs={{0,8},{8,0},{16,24},{24,16},{1,9},{9,1},{17,25},{25,17},{2,10},{10... | collective-permute-start | bytes 1572872 | tf_op jit(solution)/shard_map/ppermute | solution.py:568
  18.8 2.1 %collective-permute-start.5 = (bf16[2,2,256,256]{3,2,1,0:T(8,128)(2,1)S(1)}, bf16[2,2,256,256]{3,2,1,0:T(8,128)(2,1)S(1)}, u32[]{:S(2)}, u32[]{:S(2)}) collective-permute-start(bf16[2,2,256,256]{3,2,1,0:T(8,128)(2,1)S(1)} %get-tuple-element.68), channel_id=1, source_target_pairs={{0,8},{8,0},{16,24},{24,16},{1,9},{9,1},{17,25},{25,17},{2,10},{10... | collective-permute-start | bytes 1572872 | tf_op jit(solution)/shard_map/ppermute | solution.py:579
  21.0 16.2 %collective-permute-start.7 = (s32[264,256]{1,0:T(8,128)S(1)}, s32[264,256]{1,0:T(8,128)S(1)}, u32[]{:S(2)}, u32[]{:S(2)}) collective-permute-start(s32[264,256]{1,0:T(8,128)S(1)} %get-tuple-element.73), channel_id=1, source_target_pairs={{16,0},{24,8},{17,1},{25,9},{18,2},{26,10},{19,3},{27,11},{20,4},{... | collective-permute-start | bytes 811016 | tf_op jit(solution)/shard_map/ppermute | solution.py:608
  42.6 2.7 %collective-permute-start.8 = (f32[2,2,256,256]{3,2,1,0:T(8,128)S(1)}, f32[2,2,256,256]{3,2,1,0:T(8,128)S(1)}, u32[]{:S(2)}, u32[]{:S(2)}) collective-permute-start(f32[2,2,256,256]{3,2,1,0:T(8,128)S(1)} %get-tuple-element.76), channel_id=1, source_target_pairs={{0,8},{8,0},{16,24},{24,16},{1,9},{9,1},{17,25},{25,17},{2,10},{10... | collective-permute-start | bytes 3145736 | tf_op jit(solution)/shard_map/ppermute | solution.py:611
  47.1 13.4 %collective-permute-start.9 = (s32[536,128]{1,0:T(8,128)S(1)}, s32[536,128]{1,0:T(8,128)S(1)}, u32[]{:S(2)}, u32[]{:S(2)}) collective-permute-start(s32[536,128]{1,0:T(8,128)S(1)} %get-tuple-element.81), channel_id=1, source_target_pairs={{0,1},{1,0},{2,3},{3,2},{4,5},{5,4},{6,7},{7,6},{8,9},{9,8},{10,11... | collective-permute-start | bytes 823304 | tf_op jit(solution)/shard_map/ppermute | solution.py:535
  49.2 9.4 %collective-permute-start.10 = (s32[264,256]{1,0:T(8,128)S(1)}, s32[264,256]{1,0:T(8,128)S(1)}, u32[]{:S(2)}, u32[]{:S(2)}) collective-permute-start(s32[264,256]{1,0:T(8,128)S(1)} %get-tuple-element.83), channel_id=1, source_target_pairs={{0,2},{1,3},{2,0},{3,1},{4,6},{5,7},{6,4},{7,5},{8,10},{9,11},{10,... | collective-permute-start | bytes 811016 | tf_op jit(solution)/shard_map/ppermute | solution.py:535
  49.2 11.3 %collective-permute-start.11 = (s32[264,256]{1,0:T(8,128)S(1)}, s32[264,256]{1,0:T(8,128)S(1)}, u32[]{:S(2)}, u32[]{:S(2)}) collective-permute-start(s32[264,256]{1,0:T(8,128)S(1)} %get-tuple-element.84), channel_id=1, source_target_pairs={{2,4},{3,5},{4,2},{5,3},{10,12},{11,13},{12,10},{13,11},{18,20},{1... | collective-permute-start | bytes 811016 | tf_op jit(solution)/shard_map/ppermute | solution.py:535
  51.9 10.1 %collective-permute-start.12 = (s32[264,128]{1,0:T(8,128)S(1)}, s32[264,128]{1,0:T(8,128)S(1)}, u32[]{:S(2)}, u32[]{:S(2)}) collective-permute-start(s32[264,128]{1,0:T(8,128)S(1)} %get-tuple-element.85), channel_id=1, source_target_pairs={{0,3},{1,2},{2,1},{3,0},{4,7},{5,6},{6,5},{7,4},{8,11},{9,10},{10,... | collective-permute-start | bytes 405512 | tf_op jit(solution)/shard_map/ppermute | solution.py:535
  52.5 11.1 %collective-permute-start.13 = (s32[264,128]{1,0:T(8,128)S(1)}, s32[264,128]{1,0:T(8,128)S(1)}, u32[]{:S(2)}, u32[]{:S(2)}) collective-permute-start(s32[264,128]{1,0:T(8,128)S(1)} %get-tuple-element.86), channel_id=1, source_target_pairs={{2,5},{3,4},{4,3},{5,2},{10,13},{11,12},{12,11},{13,10},{18,21},{1... | collective-permute-start | bytes 405512 | tf_op jit(solution)/shard_map/ppermute | solution.py:535

commit v8 on v7

--- a/solution.py
+++ b/solution.py
@@ -469,38 +469,49 @@
     send_halos(kinds, pieces, tile, ext_ref, exponent_ref[:1, :1])
 
 
-def add_halos(kinds, pieces, tile, out_ref, layer):
-    for kind, piece in zip(kinds, pieces):
-        row, col = rim_start(kind, tile // 2, tile)
-        rows, cols = rim_size(kind, tile)
-        where = (pl.ds(row, rows), pl.ds(col, cols))
-        for c, value in enumerate(get_encoded(piece, layer * rows, rows)):
-            out_ref[(layer, c) + where] += value
-
-
 def fold_kernel(kinds, ext_ref, *refs):
-    pieces, out_ref = refs[:-1], refs[-1]
-    slab, _, tile, _ = out_ref.shape
+    pieces, (part_ref, out_ref, sems) = refs[:-3], refs[-3:]
+    slab, _, tile, _ = part_ref.shape
     half = tile // 2
 
+    def leave(layer):
+        return pltpu.make_async_copy(part_ref.at[layer], out_ref.at[layer], sems.at[layer])
+
     def one(layer, _):
-        out_ref[layer] = ext_ref[layer, :, half : half + tile, half : half + tile]
-        add_halos(kinds, pieces, tile, out_ref, layer)
+        part_ref[layer] = ext_ref[layer, :, half : half + tile, half : half + tile]
+        for kind, piece in zip(kinds, pieces):
+            row, col = rim_start(kind, half, tile)
+            rows, cols = rim_size(kind, tile)
+            where = (pl.ds(row, rows), pl.ds(col, cols))
+            for c, value in enumerate(get_encoded(piece, layer * rows, rows)):
+                part_ref[(layer, c) + where] += value
+        leave(layer).start()
         return 0
 
     lax.fori_loop(0, slab, one, 0)
+    for layer in range(slab):
+        leave(layer).wait()
 
 
 def corners_kernel(kinds, part_ref, *refs):
-    pieces, out_ref = refs[:-1], refs[-1]
-    slab, _, tile, _ = out_ref.shape
-
-    def one(layer, _):
-        out_ref[layer] = part_ref[layer]
-        add_halos(kinds, pieces, tile, out_ref, layer)
-        return 0
-
-    lax.fori_loop(0, slab, one, 0)
+    pieces, (_, out_ref, quarter_ref, sems) = refs[: len(kinds)], refs[len(kinds) :]
+    slab, _, tile, _ = part_ref.shape
+    half = tile // 2
+
+    def leave(layer, index, kind):
+        row, col = rim_start(kind, half, tile)
+        target = out_ref.at[layer, :, pl.ds(row, half), pl.ds(col, half)]
+        return pltpu.make_async_copy(quarter_ref.at[layer, index], target, sems.at[layer, index])
+
+    for layer in range(slab):
+        for index, (kind, piece) in enumerate(zip(kinds, pieces)):
+            row, col = rim_start(kind, half, tile)
+            for c, value in enumerate(get_encoded(piece, layer * half, half)):
+                quarter_ref[layer, index, c] = part_ref[layer, c, pl.ds(row, half), pl.ds(col, half)] + value
+            leave(layer, index, kind).start()
+    for layer in range(slab):
+        for index, kind in enumerate(kinds):
+            leave(layer, index, kind).wait()
 
 
 def shards(transmission, incident, exit_adjoint, propagator_phase, scan_anchor, live_count):
@@ -605,7 +616,8 @@
         )
         if stage < chips - 1:
             source = chips - 1 - stage
-            wave = lax.ppermute(wave, "depth", [(2 * source + c, 2 * source - 2 + c) for c in range(2)])
+            hop = [(2 * i + c, 2 * j + c) for c in range(2) for i, j in ((source, source - 1), (source - 1, source))]
+            wave = lax.ppermute(wave, "depth", hop)
 
     keep, send = terms
     got = lax.ppermute(send, "depth", core_swap)
@@ -641,11 +653,27 @@
     sent = dict(zip(first + rest, (*beyond, *more)))
     came = dict(zip(late, swapped([sent[kind] for kind in late], late)))
     tile_shape = shape_of((slab, 2, tile, tile), f32)
-    part = call(
-        functools.partial(fold_kernel, sides), tile_shape, (ext, *[came[kind] for kind in sides]), "fold", cost=2
+    part, out = call(
+        functools.partial(fold_kernel, sides),
+        (tile_shape, tile_shape),
+        (ext, *[came[kind] for kind in sides]),
+        "fold",
+        [pltpu.SemaphoreType.DMA((slab,))],
+        cost=2,
+        out_specs=(VMEM, ANY),
     )
     return call(
-        functools.partial(corners_kernel, corners), tile_shape, (part, *[came[kind] for kind in corners]), "corners"
+        functools.partial(corners_kernel, corners),
+        tile_shape,
+        (part, *[came[kind] for kind in corners], out),
+        "corners",
+        [
+            pltpu.VMEM((slab, len(corners), 2, half, half), f32),
+            pltpu.SemaphoreType.DMA((slab, len(corners))),
+        ],
+        in_specs=[VMEM] * (1 + len(corners)) + [ANY],
+        out_specs=ANY,
+        input_output_aliases={1 + len(corners): 0},
     )
 
 

time: 65.1 us -> 63.5 us (0.975)
  waiting for transfers between devices: 26.1 us -> 17.4 us
  starting transfers between devices: 19.5 us -> 26.2 us
    ppermute x1, waiting for transfers between devices: 14.9 us -> 7.01 us  [shards(): wave = lax.ppermute(wave, 'depth', hop)]
    ppermute x1, starting transfers between devices: 1.29 us -> 7.97 us  [shards(): wave = lax.ppermute(wave, 'depth', hop)]
    ppermute x10, waiting for transfers between devices: 9.71 us -> 8.89 us  [swapped(): lax.ppermute(value, ('sx', 'sy'), swap_list(n_x, n_y, *kind))]
  transfers between devices with their start and end apart: 14 -> 14, of which waited for: 9 -> 8; matrix products, arithmetic and copies ran while one was open for 0% -> 0% of each run, Pallas kernels for 12% -> 14%
where the time goes in v8:
time: 63.5 us; the launch traced here: 63.3 us
  starting transfers between devices  26.2 us (41%)
  waiting for transfers between devices  17.4 us (27%)
  Pallas kernels  16.8 us (26%)
  local copies, waits for them, and re-layouts  2.01 us (3%)
  between operations  0.87 us (1%)
    ppermute x10, starting transfers between devices, swapped(): lax.ppermute(value, ('sx', 'sy'), swap_list(n_x, n_y, *kind))  17.5 us
    pallas_call x12, Pallas kernels, call(): pl.pallas_call(kernel, out_shape=out_shape, scratch_shapes=list(scratch),...  16.8 us
    ppermute x10, waiting for transfers between devices, swapped(): lax.ppermute(value, ('sx', 'sy'), swap_list(n_x, n_y, *kind))  8.89 us
    ppermute x1, starting transfers between devices, shards(): wave = lax.ppermute(wave, 'depth', hop)  7.97 us
    ppermute x1, waiting for transfers between devices, shards(): wave = lax.ppermute(wave, 'depth', hop)  7.01 us
    unnamed x14, local copies, waits for them, and re-layouts  2.01 us
  transfers between devices with their start and end apart: 14, of which 8 were waited for; matrix products, arithmetic and copies ran while one was open for 0% of the time, Pallas kernels for 14%

profile of v8, /device:TPU:16, one launch (start us, length us, event | category | flops | bytes accessed | tf_op | source)
XLA Modules:
  0.0 63.3 jit_solution(1033292310318686071)
XLA Ops:
  0.0 0.0 copy-start.1
  0.0 1.0 %copy-done.1 = bf16[2,2,256,256]{3,2,1,0:T(8,128)(2,1)S(1)} copy-done((bf16[2,2,256,256]{3,2,1,0:T(8,128)(2,1)S(1)}, bf16[2,2,256,256]{3,2,1,0:T(8,128)(2,1)}, u32[]{:S(2)}) %copy-start.1) | copy-done | bytes 524312
  1.0 0.1 rims.1
  1.2 2.6 %collective-permute-start.3 = (bf16[2,2,128,128]{3,2,1,0:T(8,128)(2,1)S(1)}, bf16[2,2,128,128]{3,2,1,0:T(8,128)(2,1)S(1)}, u32[]{:S(2)}, u32[]{:S(2)}) collective-permute-start(bf16[2,2,128,128]{3,2,1,0:T(8,128)(2,1)S(1)} %get-tuple-element.51), channel_id=1, source_target_pairs={{0,3},{1,2},{2,1},{3,0},{4,7},{5,6},{6,5},{7,4},{8,11},{9,10},{10,... | collective-permute-start | bytes 393224 | tf_op jit(solution)/shard_map/ppermute | solution.py:546
  3.8 1.9 %collective-permute-start.4 = (bf16[2,2,128,128]{3,2,1,0:T(8,128)(2,1)S(1)}, bf16[2,2,128,128]{3,2,1,0:T(8,128)(2,1)S(1)}, u32[]{:S(2)}, u32[]{:S(2)}) collective-permute-start(bf16[2,2,128,128]{3,2,1,0:T(8,128)(2,1)S(1)} %get-tuple-element.52), channel_id=1, source_target_pairs={{2,5},{3,4},{4,3},{5,2},{10,13},{11,12},{12,11},{13,10},{18,21},{1... | collective-permute-start | bytes 393224 | tf_op jit(solution)/shard_map/ppermute | solution.py:546
  5.7 0.1 collective-permute-start
  5.8 3.9 %collective-permute-start.1 = (bf16[2,2,128,256]{3,2,1,0:T(8,128)(2,1)S(1)}, bf16[2,2,128,256]{3,2,1,0:T(8,128)(2,1)S(1)}, u32[]{:S(2)}, u32[]{:S(2)}) collective-permute-start(bf16[2,2,128,256]{3,2,1,0:T(8,128)(2,1)S(1)} %get-tuple-element.49), channel_id=1, source_target_pairs={{2,4},{3,5},{4,2},{5,3},{10,12},{11,13},{12,10},{13,11},{18,20},{1... | collective-permute-start | bytes 786440 | tf_op jit(solution)/shard_map/ppermute | solution.py:546
  9.6 0.0 copy-start.3
  9.7 1.6 %collective-permute-start.2 = (bf16[2,2,256,128]{3,2,1,0:T(8,128)(2,1)S(1)}, bf16[2,2,256,128]{3,2,1,0:T(8,128)(2,1)S(1)}, u32[]{:S(2)}, u32[]{:S(2)}) collective-permute-start(bf16[2,2,256,128]{3,2,1,0:T(8,128)(2,1)S(1)} %get-tuple-element.50), channel_id=1, source_target_pairs={{0,1},{1,0},{2,3},{3,2},{4,5},{5,4},{6,7},{7,6},{8,9},{9,8},{10,11... | collective-permute-start | bytes 786440 | tf_op jit(solution)/shard_map/ppermute | solution.py:546
  11.2 0.9 %copy-done.6 = f32[256,256]{1,0:T(8,128)S(1)} copy-done((f32[256,256]{1,0:T(8,128)S(1)}, f32[256,256]{1,0:T(8,128)}, u32[]{:S(2)}) %copy-start.6) | copy-done | bytes 262168
  12.2 1.4 %turn.1 = (f32[256,256]{1,0:T(8,128)S(1)}, f32[256,256]{1,0:T(8,128)S(1)}) custom-call(f32[256,256]{1,0:T(8,128)S(1)} %copy-done.6), custom_call_target="tpu_custom_call" | custom-call | flops 2000000000 | bytes 6000000 | tf_op jit(solution)/shard_map/turn/pallas_call | solution.py:535
  14.3 0.0 copy-done.2
  14.3 0.0 copy-done.4
  14.3 0.0 copy-done.5
  14.3 0.5 slots.1
  14.8 0.0 collective-permute-done.3.refs_3_
  14.8 0.0 collective-permute-done.4.refs_4_
  14.8 0.0 collective-permute-done.refs_0_
  14.8 1.4 %collective-permute-done.1.refs_1_ = bf16[2,2,128,256]{3,2,1,0:T(8,128)(2,1)S(1)} collective-permute-done((bf16[2,2,128,256]{3,2,1,0:T(8,128)(2,1)S(1)}, bf16[2,2,128,256]{3,2,1,0:T(8,128)(2,1)S(1)}, u32[]{:S(2)}, u32[]{:S(2)}) %collective-permute-start.1) | collective-permute-done | bytes 262176 | tf_op jit(solution)/shard_map/ppermute | solution.py:546
  16.2 1.3 %collective-permute-done.2.refs_2_ = bf16[2,2,256,128]{3,2,1,0:T(8,128)(2,1)S(1)} collective-permute-done((bf16[2,2,256,128]{3,2,1,0:T(8,128)(2,1)S(1)}, bf16[2,2,256,128]{3,2,1,0:T(8,128)(2,1)S(1)}, u32[]{:S(2)}, u32[]{:S(2)}) %collective-permute-start.2) | collective-permute-done | bytes 262176 | tf_op jit(solution)/shard_map/ppermute | solution.py:546
  17.5 0.0 collective-permute-start.6
  17.5 0.0 copy-done.3
  17.5 1.3 %windows_for_other.1 = (bf16[2,2,256,256]{3,2,1,0:T(8,128)(2,1)S(1)}, f32[2,2,512,512]{3,2,1,0:T(8,128)S(1)}) custom-call(s32[2,2]{1,0:T(2,128)S(1)} %copy-done.3, f32[2,2,512,512]{3,2,1,0:T(8,128)S(1)} %get-tuple-element.63._filled, bf16[2,2,128,256]{3,2,1,0:T(8,128)(2,1)S(1)} %collective-permute-done.refs_0_, ...), custom_call_target="tpu_custom_call", output_to_operand_aliasing={{1}: (1, {})} | custom-call | tf_op jit(solution)/shard_map/windows_for_other/pallas_call | solution.py:535
  18.8 0.6 collective-permute-start.5
  19.4 1.1 %windows.1.win_own = bf16[2,2,256,256]{3,2,1,0:T(8,128)(2,1)S(1)} custom-call(s32[2,2]{1,0:T(2,128)S(1)} %copy-done.3, f32[2,2,512,512]{3,2,1,0:T(8,128)S(1)} %get-tuple-element.69.ext_ref), custom_call_target="tpu_custom_call" | custom-call | tf_op jit(solution)/shard_map/windows/pallas_call | solution.py:535
  20.6 0.0 collective-permute-done.6.inc_got
  20.6 0.4 collective-permute-done.5.win_got
  20.9 0.0 copy-done
  21.0 8.0 %collective-permute-start.7 = (s32[264,256]{1,0:T(8,128)S(1)}, s32[264,256]{1,0:T(8,128)S(1)}, u32[]{:S(2)}, u32[]{:S(2)}) collective-permute-start(s32[264,256]{1,0:T(8,128)S(1)} %get-tuple-element.75), channel_id=1, source_target_pairs={{16,0},{0,16},{24,8},{8,24},{17,1},{1,17},{25,9},{9,25},{18,2},{2,... | collective-permute-start | bytes 811016 | tf_op jit(solution)/shard_map/ppermute | solution.py:620
  28.9 7.0 %collective-permute-done.7.wave_in = s32[264,256]{1,0:T(8,128)S(1)} collective-permute-done((s32[264,256]{1,0:T(8,128)S(1)}, s32[264,256]{1,0:T(8,128)S(1)}, u32[]{:S(2)}, u32[]{:S(2)}) %collective-permute-start.7) | collective-permute-done | bytes 270368 | tf_op jit(solution)/shard_map/ppermute | solution.py:620
  36.0 5.5 %sweep.3 = (f32[2,2,256,256]{3,2,1,0:T(8,128)S(1)}, f32[2,2,256,256]{3,2,1,0:T(8,128)S(1)}, s32[264,256]{1,0:T(8,128)}) custom-call(s32[264,256]{1,0:T(8,128)S(1)} %collective-permute-done.7.wave_in, bf16[2,2,256,256]{3,2,1,0:T(8,128)(2,1)S(1)} %windows.1.win_own, ...), custom_call_target="tpu_custom_call", output_to_operand_aliasing={{0}: (8, {}), {1}: (9, {})} | custom-call | tf_op jit(solution)/shard_map/sweep/pallas_call | solution.py:535
  41.4 0.1 collective-permute-start.8
  41.5 1.5 %scatter_own.1 = (f32[2,2,512,512]{3,2,1,0:T(8,128)S(1)}, f32[8,256]{1,0:T(8,128)S(1)}) custom-call(s32[2,2]{1,0:T(2,128)S(1)} %copy-done.3, f32[2,2,256,256]{3,2,1,0:T(8,128)S(1)} %get-tuple-element.79.term_ref), custom_call_target="tpu_custom_call" | custom-call | flops 2000000000 | bytes 6000000 | tf_op jit(solution)/shard_map/scatter_own/pallas_call | solution.py:535
  43.0 1.1 %collective-permute-done.8.term_ref = f32[2,2,256,256]{3,2,1,0:T(8,128)S(1)} collective-permute-done((f32[2,2,256,256]{3,2,1,0:T(8,128)S(1)}, f32[2,2,256,256]{3,2,1,0:T(8,128)S(1)}, u32[]{:S(2)}, u32[]{:S(2)}) %collective-permute-start.8) | collective-permute-done | bytes 1048608 | tf_op jit(solution)/shard_map/ppermute | solution.py:623
  44.1 1.7 %scatter.1 = (f32[2,2,512,512]{3,2,1,0:T(8,128)S(1)}, f32[8,128]{1,0:T(8,128)S(1)}, s32[536,128]{1,0:T(8,128)S(1)}) custom-call(s32[2,2]{1,0:T(2,128)S(1)} %copy-done.3, f32[2,2,256,256]{3,2,1,0:T(8,128)S(1)} %collective-permute-done.8.term_ref, f32[2,2,512,512]{3,2,1,0:T(8,128)S(1)} %get-tuple-element.80._own, ...), custom_call_target="tpu_custom_call", output_to_operand_aliasing={{0}: (2, {})} | custom-call | flops 2000000000 | bytes 6000000 | tf_op jit(solution)/shard_map/scatter/pallas_call | solution.py:535
  45.9 1.1 %collective-permute-start.9 = (s32[536,128]{1,0:T(8,128)S(1)}, s32[536,128]{1,0:T(8,128)S(1)}, u32[]{:S(2)}, u32[]{:S(2)}) collective-permute-start(s32[536,128]{1,0:T(8,128)S(1)} %get-tuple-element.83), channel_id=1, source_target_pairs={{0,1},{1,0},{2,3},{3,2},{4,5},{5,4},{6,7},{7,6},{8,9},{9,8},{10,11... | collective-permute-start | bytes 823304 | tf_op jit(solution)/shard_map/ppermute | solution.py:546
  46.9 1.0 %halos.1 = (s32[264,256]{1,0:T(8,128)S(1)}, s32[264,256]{1,0:T(8,128)S(1)}, s32[264,128]{1,0:T(8,128)S(1)}, s32[264,128]{1,0:T(8,128)S(1)}) custom-call(f32[2,2,512,512]{3,2,1,0:T(8,128)S(1)} %get-tuple-element.82.ext_ref, f32[8,128]{1,0:T(8,128)S(1)} %get-tuple-element.84.exponent_ref), custom_call_target="tpu_custom_call" | custom-call | flops 1000000000 | bytes 3000000 | tf_op jit(solution)/shard_map/halos/pallas_call | solution.py:535
  48.0 0.1 collective-permute-start.10
  48.1 2.6 %collective-permute-start.11 = (s32[264,256]{1,0:T(8,128)S(1)}, s32[264,256]{1,0:T(8,128)S(1)}, u32[]{:S(2)}, u32[]{:S(2)}) collective-permute-start(s32[264,256]{1,0:T(8,128)S(1)} %get-tuple-element.86), channel_id=1, source_target_pairs={{2,4},{3,5},{4,2},{5,3},{10,12},{11,13},{12,10},{13,11},{18,20},{1... | collective-permute-start | bytes 811016 | tf_op jit(solution)/shard_map/ppermute | solution.py:546
  50.7 0.6 collective-permute-start.12
  51.3 3.2 %collective-permute-start.13 = (s32[264,128]{1,0:T(8,128)S(1)}, s32[264,128]{1,0:T(8,128)S(1)}, u32[]{:S(2)}, u32[]{:S(2)}) collective-permute-start(s32[264,128]{1,0:T(8,128)S(1)} %get-tuple-element.89), channel_id=1, source_target_pairs={{2,5},{3,4},{4,3},{5,2},{10,13},{11,12},{12,11},{13,10},{18,21},{1... | collective-permute-start | bytes 405512 | tf_op jit(solution)/shard_map/ppermute | solution.py:546
  54.4 3.0 %collective-permute-done.10.refs_1_ = s32[264,256]{1,0:T(8,128)S(1)} collective-permute-done((s32[264,256]{1,0:T(8,128)S(1)}, s32[264,256]{1,0:T(8,128)S(1)}, u32[]{:S(2)}, u32[]{:S(2)}) %collective-permute-start.10) | collective-permute-done | bytes 270368 | tf_op jit(solution)/shard_map/ppermute | solution.py:546
  57.4 1.9 %collective-permute-done.11.refs_2_ = s32[264,256]{1,0:T(8,128)S(1)} collective-permute-done((s32[264,256]{1,0:T(8,128)S(1)}, s32[264,256]{1,0:T(8,128)S(1)}, u32[]{:S(2)}, u32[]{:S(2)}) %collective-permute-start.11) | collective-permute-done | bytes 270368 | tf_op jit(solution)/shard_map/ppermute | solution.py:546
  59.3 0.0 collective-permute-done.9.refs_0_
  59.3 1.7 %fold.1 = (f32[2,2,256,256]{3,2,1,0:T(8,128)S(1)}, f32[2,2,256,256]{3,2,1,0:T(8,128)}) custom-call(f32[2,2,512,512]{3,2,1,0:T(8,128)S(1)} %get-tuple-element.82.ext_ref, s32[536,128]{1,0:T(8,128)S(1)} %collective-permute-done.9.refs_0_, s32[264,256]{1,0:T(8,128)S(1)} %collective-permute-done.10.refs_1_, s32[264,256]{1,0:T(8,128)S(1)} %collective-permute-done.11.refs_2_), custom_call_target="tpu_custom_call" | custom-call | flops 2000000000 | bytes 6000000 | tf_op jit(solution)/shard_map/fold/pallas_call | solution.py:535
  61.0 0.0 collective-permute-done.12.refs_0_
  61.0 1.4 %collective-permute-done.13.refs_1_ = s32[264,128]{1,0:T(8,128)S(1)} collective-permute-done((s32[264,128]{1,0:T(8,128)S(1)}, s32[264,128]{1,0:T(8,128)S(1)}, u32[]{:S(2)}, u32[]{:S(2)}) %collective-permute-start.13) | collective-permute-done | bytes 135200 | tf_op jit(solution)/shard_map/ppermute | solution.py:546
  62.4 0.9 %corners.1 = f32[2,2,256,256]{3,2,1,0:T(8,128)} custom-call(f32[2,2,256,256]{3,2,1,0:T(8,128)S(1)} %get-tuple-element.87.part_ref, s32[264,128]{1,0:T(8,128)S(1)} %collective-permute-done.12.refs_0_, s32[264,128]{1,0:T(8,128)S(1)} %collective-permute-done.13.refs_1_, f32[2,2,256,256]{3,2,1,0:T(8,128)} %get-tuple-element.90.refs_2_), custom_call_target="tpu_custom_call", output_to_operand_aliasing={{}: (3, {})} | custom-call | tf_op jit(solution)/shard_map/corners/pallas_call | solution.py:535
  (6 shorter events, 0.0 us)
Async XLA Ops:
  0.0 1.0 %copy-start.1 = (bf16[2,2,256,256]{3,2,1,0:T(8,128)(2,1)S(1)}, bf16[2,2,256,256]{3,2,1,0:T(8,128)(2,1)}, u32[]{:S(2)}) copy-start(bf16[2,2,256,256]{3,2,1,0:T(8,128)(2,1)} %tile_ref.1) | copy-start | bytes 1572868
  1.0 13.2 %copy-start.2 = (bf16[2,2,256,256]{3,2,1,0:T(8,128)(2,1)S(1)}, bf16[2,2,256,256]{3,2,1,0:T(8,128)(2,1)}, u32[]{:S(2)}) copy-start(bf16[2,2,256,256]{3,2,1,0:T(8,128)(2,1)} %tile_ref.1) | copy-start | bytes 1572868
  1.0 13.2 %copy-start.4 = (bf16[2,2,2,256,256]{4,3,2,1,0:T(8,128)(2,1)S(1)}, bf16[2,2,2,256,256]{4,3,2,1,0:T(8,128)(2,1)}, u32[]{:S(2)}) copy-start(bf16[2,2,2,256,256]{4,3,2,1,0:T(8,128)(2,1)} %inc_ref) | copy-start | bytes 3145732
  1.0 13.2 %copy-start.5 = (bf16[2,2,256,256]{3,2,1,0:T(8,128)(2,1)S(1)}, bf16[2,2,256,256]{3,2,1,0:T(8,128)(2,1)}, u32[]{:S(2)}) copy-start(bf16[2,2,256,256]{3,2,1,0:T(8,128)(2,1)} %exit_ref) | copy-start | bytes 1572868
  1.2 13.6 %collective-permute-start.3 = (bf16[2,2,128,128]{3,2,1,0:T(8,128)(2,1)S(1)}, bf16[2,2,128,128]{3,2,1,0:T(8,128)(2,1)S(1)}, u32[]{:S(2)}, u32[]{:S(2)}) collective-permute-start(bf16[2,2,128,128]{3,2,1,0:T(8,128)(2,1)S(1)} %get-tuple-element.51), channel_id=1, source_target_pairs={{0,3},{1,2},{2,1},{3,0},{4,7},{5,6},{6,5},{7,4},{8,11},{9,10},{10,... | collective-permute-start | bytes 393224 | tf_op jit(solution)/shard_map/ppermute | solution.py:546
  3.8 11.0 %collective-permute-start.4 = (bf16[2,2,128,128]{3,2,1,0:T(8,128)(2,1)S(1)}, bf16[2,2,128,128]{3,2,1,0:T(8,128)(2,1)S(1)}, u32[]{:S(2)}, u32[]{:S(2)}) collective-permute-start(bf16[2,2,128,128]{3,2,1,0:T(8,128)(2,1)S(1)} %get-tuple-element.52), channel_id=1, source_target_pairs={{2,5},{3,4},{4,3},{5,2},{10,13},{11,12},{12,11},{13,10},{18,21},{1... | collective-permute-start | bytes 393224 | tf_op jit(solution)/shard_map/ppermute | solution.py:546
  5.7 9.1 %collective-permute-start = (bf16[2,2,128,256]{3,2,1,0:T(8,128)(2,1)S(1)}, bf16[2,2,128,256]{3,2,1,0:T(8,128)(2,1)S(1)}, u32[]{:S(2)}, u32[]{:S(2)}) collective-permute-start(bf16[2,2,128,256]{3,2,1,0:T(8,128)(2,1)S(1)} %get-tuple-element.48), channel_id=1, source_target_pairs={{0,2},{1,3},{2,0},{3,1},{4,6},{5,7},{6,4},{7,5},{8,10},{9,11},{10,... | collective-permute-start | bytes 786440 | tf_op jit(solution)/shard_map/ppermute | solution.py:546
  5.8 10.4 %collective-permute-start.1 = (bf16[2,2,128,256]{3,2,1,0:T(8,128)(2,1)S(1)}, bf16[2,2,128,256]{3,2,1,0:T(8,128)(2,1)S(1)}, u32[]{:S(2)}, u32[]{:S(2)}) collective-permute-start(bf16[2,2,128,256]{3,2,1,0:T(8,128)(2,1)S(1)} %get-tuple-element.49), channel_id=1, source_target_pairs={{2,4},{3,5},{4,2},{5,3},{10,12},{11,13},{12,10},{13,11},{18,20},{1... | collective-permute-start | bytes 786440 | tf_op jit(solution)/shard_map/ppermute | solution.py:546
  9.6 7.8 %copy-start.3 = (s32[2,2]{1,0:T(2,128)S(1)}, s32[2,2]{1,0:T(2,128)}, u32[]{:S(2)}) copy-start(s32[2,2]{1,0:T(2,128)} %anchor_ref.7) | copy-start | bytes 52
  9.7 7.8 %collective-permute-start.2 = (bf16[2,2,256,128]{3,2,1,0:T(8,128)(2,1)S(1)}, bf16[2,2,256,128]{3,2,1,0:T(8,128)(2,1)S(1)}, u32[]{:S(2)}, u32[]{:S(2)}) collective-permute-start(bf16[2,2,256,128]{3,2,1,0:T(8,128)(2,1)S(1)} %get-tuple-element.50), channel_id=1, source_target_pairs={{0,1},{1,0},{2,3},{3,2},{4,5},{5,4},{6,7},{7,6},{8,9},{9,8},{10,11... | collective-permute-start | bytes 786440 | tf_op jit(solution)/shard_map/ppermute | solution.py:546
  11.2 0.9 %copy-start.6 = (f32[256,256]{1,0:T(8,128)S(1)}, f32[256,256]{1,0:T(8,128)}, u32[]{:S(2)}) copy-start(f32[256,256]{1,0:T(8,128)} %phase_ref) | copy-start | bytes 786436
  17.5 3.5 %copy-start = (bf16[4,256,256]{2,1,0:T(8,128)(2,1)S(1)}, bf16[4,256,256]{2,1,0:T(8,128)(2,1)}, u32[]{:S(2)}) copy-start(bf16[4,256,256]{2,1,0:T(8,128)(2,1)} %constant.2.clone.tab_ref) | copy-start | bytes 1572868
  17.5 3.1 %collective-permute-start.6 = (bf16[2,2,256,256]{3,2,1,0:T(8,128)(2,1)S(1)}, bf16[2,2,256,256]{3,2,1,0:T(8,128)(2,1)S(1)}, u32[]{:S(2)}, u32[]{:S(2)}) collective-permute-start(bf16[2,2,256,256]{3,2,1,0:T(8,128)(2,1)S(1)} %get-tuple-element.72), channel_id=1, source_target_pairs={{0,8},{8,0},{16,24},{24,16},{1,9},{9,1},{17,25},{25,17},{2,10},{10... | collective-permute-start | bytes 1572872 | tf_op jit(solution)/shard_map/ppermute | solution.py:579
  18.8 2.1 %collective-permute-start.5 = (bf16[2,2,256,256]{3,2,1,0:T(8,128)(2,1)S(1)}, bf16[2,2,256,256]{3,2,1,0:T(8,128)(2,1)S(1)}, u32[]{:S(2)}, u32[]{:S(2)}) collective-permute-start(bf16[2,2,256,256]{3,2,1,0:T(8,128)(2,1)S(1)} %get-tuple-element.70), channel_id=1, source_target_pairs={{0,8},{8,0},{16,24},{24,16},{1,9},{9,1},{17,25},{25,17},{2,10},{10... | collective-permute-start | bytes 1572872 | tf_op jit(solution)/shard_map/ppermute | solution.py:590
  21.0 15.0 %collective-permute-start.7 = (s32[264,256]{1,0:T(8,128)S(1)}, s32[264,256]{1,0:T(8,128)S(1)}, u32[]{:S(2)}, u32[]{:S(2)}) collective-permute-start(s32[264,256]{1,0:T(8,128)S(1)} %get-tuple-element.75), channel_id=1, source_target_pairs={{16,0},{0,16},{24,8},{8,24},{17,1},{1,17},{25,9},{9,25},{18,2},{2,... | collective-permute-start | bytes 811016 | tf_op jit(solution)/shard_map/ppermute | solution.py:620
  41.4 2.7 %collective-permute-start.8 = (f32[2,2,256,256]{3,2,1,0:T(8,128)S(1)}, f32[2,2,256,256]{3,2,1,0:T(8,128)S(1)}, u32[]{:S(2)}, u32[]{:S(2)}) collective-permute-start(f32[2,2,256,256]{3,2,1,0:T(8,128)S(1)} %get-tuple-element.78), channel_id=1, source_target_pairs={{0,8},{8,0},{16,24},{24,16},{1,9},{9,1},{17,25},{25,17},{2,10},{10... | collective-permute-start | bytes 3145736 | tf_op jit(solution)/shard_map/ppermute | solution.py:623
  45.9 13.5 %collective-permute-start.9 = (s32[536,128]{1,0:T(8,128)S(1)}, s32[536,128]{1,0:T(8,128)S(1)}, u32[]{:S(2)}, u32[]{:S(2)}) collective-permute-start(s32[536,128]{1,0:T(8,128)S(1)} %get-tuple-element.83), channel_id=1, source_target_pairs={{0,1},{1,0},{2,3},{3,2},{4,5},{5,4},{6,7},{7,6},{8,9},{9,8},{10,11... | collective-permute-start | bytes 823304 | tf_op jit(solution)/shard_map/ppermute | solution.py:546
  48.0 9.4 %collective-permute-start.10 = (s32[264,256]{1,0:T(8,128)S(1)}, s32[264,256]{1,0:T(8,128)S(1)}, u32[]{:S(2)}, u32[]{:S(2)}) collective-permute-start(s32[264,256]{1,0:T(8,128)S(1)} %get-tuple-element.85), channel_id=1, source_target_pairs={{0,2},{1,3},{2,0},{3,1},{4,6},{5,7},{6,4},{7,5},{8,10},{9,11},{10,... | collective-permute-start | bytes 811016 | tf_op jit(solution)/shard_map/ppermute | solution.py:546
  48.1 11.3 %collective-permute-start.11 = (s32[264,256]{1,0:T(8,128)S(1)}, s32[264,256]{1,0:T(8,128)S(1)}, u32[]{:S(2)}, u32[]{:S(2)}) collective-permute-start(s32[264,256]{1,0:T(8,128)S(1)} %get-tuple-element.86), channel_id=1, source_target_pairs={{2,4},{3,5},{4,2},{5,3},{10,12},{11,13},{12,10},{13,11},{18,20},{1... | collective-permute-start | bytes 811016 | tf_op jit(solution)/shard_map/ppermute | solution.py:546
  50.7 10.3 %collective-permute-start.12 = (s32[264,128]{1,0:T(8,128)S(1)}, s32[264,128]{1,0:T(8,128)S(1)}, u32[]{:S(2)}, u32[]{:S(2)}) collective-permute-start(s32[264,128]{1,0:T(8,128)S(1)} %get-tuple-element.88), channel_id=1, source_target_pairs={{0,3},{1,2},{2,1},{3,0},{4,7},{5,6},{6,5},{7,4},{8,11},{9,10},{10,... | collective-permute-start | bytes 405512 | tf_op jit(solution)/shard_map/ppermute | solution.py:546
  51.3 11.1 %collective-permute-start.13 = (s32[264,128]{1,0:T(8,128)S(1)}, s32[264,128]{1,0:T(8,128)S(1)}, u32[]{:S(2)}, u32[]{:S(2)}) collective-permute-start(s32[264,128]{1,0:T(8,128)S(1)} %get-tuple-element.89), channel_id=1, source_target_pairs={{2,5},{3,4},{4,3},{5,2},{10,13},{11,12},{12,11},{13,10},{18,21},{1... | collective-permute-start | bytes 405512 | tf_op jit(solution)/shard_map/ppermute | solution.py:546

commit v9 on v8

--- a/solution.py
+++ b/solution.py
@@ -12,6 +12,7 @@
 VMEM = pl.BlockSpec(memory_space=pltpu.VMEM)
 SMEM = pl.BlockSpec(memory_space=pltpu.SMEM)
 ANY = pl.BlockSpec(memory_space=pl.ANY)
+TERMS = ANY
 LIMIT = 16 * 1024 * 1024
 LEVELS = 32767.0
 SCALE_ROWS = 8
@@ -209,23 +210,17 @@
     return jnp.exp2(first), jnp.exp2(exponent - first)
 
 
-def exponent_of(top):
-    top = jnp.max(jnp.max(top, axis=0, keepdims=True), axis=1, keepdims=True)
-    return jnp.where(top > 0, jnp.ceil(jnp.log2(jnp.maximum(top, 1e-37))), 0.0)
-
-
-def encode(real, imag, exponent):
+def encode(real, imag):
+    top = jnp.max(jnp.maximum(jnp.abs(real), jnp.abs(imag)), axis=0, keepdims=True)
+    exponent = jnp.where(top > 0, jnp.ceil(jnp.log2(jnp.maximum(top, 1e-37))), 0.0)
     scale, rest = two_powers(-exponent)
-
-    def root(value):
-        return value * lax.rsqrt(value)
 
     def code(value):
         size = jnp.minimum(jnp.maximum(jnp.abs(value) * scale * rest, 1e-30), 1.0)
-        whole = (root(root(size)) * LEVELS + 0.5).astype(jnp.int32)
+        whole = (size * lax.rsqrt(size) * LEVELS + 0.5).astype(jnp.int32)
         return jnp.where(value < 0, -whole, whole)
 
-    return (code(real) << 16) | (code(imag) & 0xFFFF)
+    return (code(real) << 16) | (code(imag) & 0xFFFF), exponent.astype(jnp.int32)
 
 
 def decode(packed, exponent):
@@ -233,23 +228,20 @@
 
     def value(whole):
         root = whole.astype(jnp.float32) * (1.0 / LEVELS)
-        square = root * root
-        size = square * square * scale * rest
-        return jnp.where(whole < 0, -size, size)
+        return root * jnp.abs(root) * scale * rest
 
     return value(packed >> 16), value((packed << 16) >> 16)
 
 
-def put_encoded(ref, first, real, imag, exponent):
-    packed = encode(real, imag, exponent)
-    rows, cols = packed.shape
-    ref[pl.ds(first, rows), :] = packed
-    ref[ref.shape[0] - SCALE_ROWS :, :] = jnp.broadcast_to(exponent.astype(jnp.int32), (SCALE_ROWS, cols))
-
-
-def get_encoded(ref, first, rows):
-    last = ref.shape[0]
-    return decode(ref[pl.ds(first, rows), :], ref[last - 1 : last, :])
+def put_encoded(ref, layer, real, imag):
+    packed, exponent = encode(real, imag)
+    rows = packed.shape[0]
+    ref[pl.ds(layer * rows, rows), :] = packed
+    ref[pl.ds(ref.shape[0] - SCALE_ROWS + layer, 1), :] = exponent
+
+
+def get_encoded(ref, layer, rows):
+    return decode(ref[pl.ds(layer * rows, rows), :], ref[pl.ds(ref.shape[0] - SCALE_ROWS + layer, 1), :])
 
 
 def rim_size(kind, tile):
@@ -355,7 +347,8 @@
 
 
 def sweep_kernel(stage, wave_in, win_own, win_got, inc_own, inc_got, cos_ref, sin_ref, tab_ref, *refs):
-    keep_ref, send_ref, out_ref, wave_ref, term, sems = refs[-6:]
+    wave_ref, term, sems = refs[-3:]
+    keep_ref, send_ref, *out_ref = refs[2 if stage else 0 : -3]
     slab = win_own.shape[0]
     layers = 2 * slab
     core = core_index()
@@ -410,16 +403,14 @@
 
             return 0
 
-        lax.fori_loop(0, layers, one, 0)
+        lax.fori_loop(0, layers, one, 0, unroll=True)
         if stage < chips - 1:
-            wr, wi = wave_ref[0], wave_ref[1]
-            exponent = exponent_of(jnp.maximum(jnp.abs(wr), jnp.abs(wi)))
-            put_encoded(out_ref, 0, wr, wi, exponent)
+            put_encoded(out_ref[0], 0, wave_ref[0], wave_ref[1])
         for slot in range(2):
             leave(slot, keep_ref, 0).wait()
 
 
-def send_halos(kinds, pieces, tile, ext_ref, exponent):
+def send_halos(kinds, pieces, tile, ext_ref):
     half = tile // 2
 
     def one(layer, _):
@@ -427,46 +418,39 @@
             row, col = halo_start(kind, half, tile)
             rows, cols = rim_size(kind, tile)
             where = (pl.ds(row, rows), pl.ds(col, cols))
-            put_encoded(piece, layer * rows, ext_ref[(layer, 0) + where], ext_ref[(layer, 1) + where], exponent)
+            put_encoded(piece, layer, ext_ref[(layer, 0) + where], ext_ref[(layer, 1) + where])
         return 0
 
     lax.fori_loop(0, ext_ref.shape[0], one, 0)
 
 
-def scatter_own_kernel(tile, anchor_ref, term_ref, ext_ref, top_ref):
+def scatter_own_kernel(tile, anchor_ref, term_ref, ext_ref):
     at_x, at_y = corner_of(anchor_ref, core_index(), tile // 2, tile)
 
-    def add(index, top):
+    def add(index, _):
         layer, c = index // 2, lax.rem(index, 2)
         plane = ext_ref.at[layer, c]
         plane[...] = jnp.zeros(plane.shape, plane.dtype)
-        value = term_ref[layer, c]
-        add_window(plane, at_x, at_y, value)
-        return jnp.maximum(top, jnp.max(jnp.abs(value), axis=0, keepdims=True))
-
-    top = jnp.zeros((1, term_ref.shape[-1]), jnp.float32)
-    top = lax.fori_loop(0, 2 * term_ref.shape[0], add, top)
-    top_ref[...] = jnp.broadcast_to(top, top_ref.shape)
-
-
-def scatter_kernel(kinds, tile, anchor_ref, term_ref, _own, own_top_ref, ext_ref, exponent_ref, *pieces):
+        add_window(plane, at_x, at_y, term_ref[layer, c])
+        return 0
+
+    lax.fori_loop(0, 2 * term_ref.shape[0], add, 0)
+
+
+def scatter_kernel(kinds, tile, anchor_ref, term_ref, _own, ext_ref, *pieces):
     at_x, at_y = corner_of(anchor_ref, 1 - core_index(), tile // 2, tile)
 
-    def add(index, top):
+    def add(index, _):
         layer, c = index // 2, lax.rem(index, 2)
-        value = term_ref[layer, c]
-        add_window(ext_ref.at[layer, c], at_x, at_y, value)
-        return jnp.maximum(top, jnp.max(jnp.abs(value), axis=0, keepdims=True))
-
-    top = jnp.zeros((1, term_ref.shape[-1]), jnp.float32)
-    top = lax.fori_loop(0, 2 * term_ref.shape[0], add, top)
-    exponent = exponent_of(top + jnp.max(own_top_ref[:1, :], axis=1, keepdims=True))
-    exponent_ref[...] = jnp.broadcast_to(exponent, exponent_ref.shape)
-    send_halos(kinds, pieces, tile, ext_ref, exponent)
-
-
-def halos_kernel(kinds, tile, ext_ref, exponent_ref, *pieces):
-    send_halos(kinds, pieces, tile, ext_ref, exponent_ref[:1, :1])
+        add_window(ext_ref.at[layer, c], at_x, at_y, term_ref[layer, c])
+        return 0
+
+    lax.fori_loop(0, 2 * term_ref.shape[0], add, 0)
+    send_halos(kinds, pieces, tile, ext_ref)
+
+
+def halos_kernel(kinds, tile, ext_ref, *pieces):
+    send_halos(kinds, pieces, tile, ext_ref)
 
 
 def fold_kernel(kinds, ext_ref, *refs):
@@ -483,7 +467,7 @@
             row, col = rim_start(kind, half, tile)
             rows, cols = rim_size(kind, tile)
             where = (pl.ds(row, rows), pl.ds(col, cols))
-            for c, value in enumerate(get_encoded(piece, layer * rows, rows)):
+            for c, value in enumerate(get_encoded(piece, layer, rows)):
                 part_ref[(layer, c) + where] += value
         leave(layer).start()
         return 0
@@ -506,7 +490,7 @@
     for layer in range(slab):
         for index, (kind, piece) in enumerate(zip(kinds, pieces)):
             row, col = rim_start(kind, half, tile)
-            for c, value in enumerate(get_encoded(piece, layer * half, half)):
+            for c, value in enumerate(get_encoded(piece, layer, half)):
                 quarter_ref[layer, index, c] = part_ref[layer, c, pl.ds(row, half), pl.ds(col, half)] + value
             leave(layer, index, kind).start()
     for layer in range(slab):
@@ -600,9 +584,10 @@
     coded = shape_of((patch + SCALE_ROWS, patch), jnp.int32)
     terms = ()
     for stage in range(chips):
-        *terms, wave = call(
+        last = stage == chips - 1
+        results = call(
             functools.partial(sweep_kernel, stage),
-            (term_shape, term_shape, coded),
+            (term_shape, term_shape) + (() if last else (coded,)),
             (wave, win_own, win_got, inc_own, inc_got, phase_cos, phase_sin, tables, *terms),
             "sweep",
             [
@@ -611,13 +596,14 @@
                 pltpu.SemaphoreType.DMA((2,)),
             ],
             in_specs=[VMEM] * 8 + [ANY] * len(terms),
-            out_specs=(ANY, ANY, VMEM),
+            out_specs=(TERMS, TERMS) + (() if last else (VMEM,)),
             input_output_aliases={8: 0, 9: 1} if stage else {},
         )
-        if stage < chips - 1:
+        terms = results[:2]
+        if not last:
             source = chips - 1 - stage
             hop = [(2 * i + c, 2 * j + c) for c in range(2) for i, j in ((source, source - 1), (source - 1, source))]
-            wave = lax.ppermute(wave, "depth", hop)
+            wave = lax.ppermute(results[2], "depth", hop)
 
     keep, send = terms
     got = lax.ppermute(send, "depth", core_swap)
@@ -632,24 +618,24 @@
     rest = [kind for kind in late if kind[0] is not None]
     sides = [kind for kind in late if None in kind]
     corners = [kind for kind in late if None not in kind]
-    ext, top = call(
+    ext = call(
         functools.partial(scatter_own_kernel, tile),
-        (ext_shape, shape_of((SUBLANES, patch), f32)),
+        ext_shape,
         (scan_anchor, keep),
         "scatter_own",
         cost=2,
         in_specs=[SMEM, VMEM],
     )
-    ext, exponent, *beyond = call(
+    ext, *beyond = call(
         functools.partial(scatter_kernel, first, tile),
-        (ext_shape, shape_of((SUBLANES, LANES), f32)) + coded_rims(first),
-        (scan_anchor, got, ext, top),
+        (ext_shape,) + coded_rims(first),
+        (scan_anchor, got, ext),
         "scatter",
         cost=2,
-        in_specs=[SMEM] + [VMEM] * 3,
+        in_specs=[SMEM] + [VMEM] * 2,
         input_output_aliases={2: 0},
     )
-    more = call(functools.partial(halos_kernel, rest, tile), coded_rims(rest), (ext, exponent), "halos", cost=1)
+    more = call(functools.partial(halos_kernel, rest, tile), coded_rims(rest), (ext,), "halos", cost=1)
     sent = dict(zip(first + rest, (*beyond, *more)))
     came = dict(zip(late, swapped([sent[kind] for kind in late], late)))
     tile_shape = shape_of((slab, 2, tile, tile), f32)

time: 63.5 us -> 62.4 us (0.983)
  Pallas kernels: 16.8 us -> 15.6 us
    pallas_call x12, Pallas kernels: 16.8 us -> 15.6 us  [call(): pl.pallas_call(kernel, out_shape=out_shape, scratch_shapes=list(scratch),...]
  transfers between devices with their start and end apart: 14 -> 14, of which waited for: 8 -> 8; matrix products, arithmetic and copies ran while one was open for 0% -> 0% of each run, Pallas kernels for 14% -> 13%
where the time goes in v9:
time: 62.4 us; the launch traced here: 62.1 us
  starting transfers between devices  25.9 us (42%)
  waiting for transfers between devices  17.7 us (28%)
  Pallas kernels  15.6 us (25%)
  local copies, waits for them, and re-layouts  2.01 us (3%)
  between operations  0.87 us (1%)
    ppermute x10, starting transfers between devices, swapped(): lax.ppermute(value, ('sx', 'sy'), swap_list(n_x, n_y, *kind))  17.5 us
    pallas_call x12, Pallas kernels, call(): pl.pallas_call(kernel, out_shape=out_shape, scratch_shapes=list(scratch),...  15.6 us
    ppermute x10, waiting for transfers between devices, swapped(): lax.ppermute(value, ('sx', 'sy'), swap_list(n_x, n_y, *kind))  9.12 us
    ppermute x1, starting transfers between devices, shards(): wave = lax.ppermute(results[2], 'depth', hop)  7.68 us
    ppermute x1, waiting for transfers between devices, shards(): wave = lax.ppermute(results[2], 'depth', hop)  7.01 us
    unnamed x14, local copies, waits for them, and re-layouts  2.01 us
  transfers between devices with their start and end apart: 14, of which 8 were waited for; matrix products, arithmetic and copies ran while one was open for 0% of the time, Pallas kernels for 13%

profile of v9, /device:TPU:16, one launch (start us, length us, event | category | flops | bytes accessed | tf_op | source)
XLA Modules:
  0.0 62.1 jit_solution(3310533761050277442)
XLA Ops:
  0.0 0.0 copy-start.1
  0.0 1.0 %copy-done.1 = bf16[2,2,256,256]{3,2,1,0:T(8,128)(2,1)S(1)} copy-done((bf16[2,2,256,256]{3,2,1,0:T(8,128)(2,1)S(1)}, bf16[2,2,256,256]{3,2,1,0:T(8,128)(2,1)}, u32[]{:S(2)}) %copy-start.1) | copy-done | bytes 524312
  1.0 0.1 rims.1
  1.2 2.6 %collective-permute-start.3 = (bf16[2,2,128,128]{3,2,1,0:T(8,128)(2,1)S(1)}, bf16[2,2,128,128]{3,2,1,0:T(8,128)(2,1)S(1)}, u32[]{:S(2)}, u32[]{:S(2)}) collective-permute-start(bf16[2,2,128,128]{3,2,1,0:T(8,128)(2,1)S(1)} %get-tuple-element.48), channel_id=1, source_target_pairs={{0,3},{1,2},{2,1},{3,0},{4,7},{5,6},{6,5},{7,4},{8,11},{9,10},{10,... | collective-permute-start | bytes 393224 | tf_op jit(solution)/shard_map/ppermute | solution.py:530
  3.8 1.9 %collective-permute-start.4 = (bf16[2,2,128,128]{3,2,1,0:T(8,128)(2,1)S(1)}, bf16[2,2,128,128]{3,2,1,0:T(8,128)(2,1)S(1)}, u32[]{:S(2)}, u32[]{:S(2)}) collective-permute-start(bf16[2,2,128,128]{3,2,1,0:T(8,128)(2,1)S(1)} %get-tuple-element.49), channel_id=1, source_target_pairs={{2,5},{3,4},{4,3},{5,2},{10,13},{11,12},{12,11},{13,10},{18,21},{1... | collective-permute-start | bytes 393224 | tf_op jit(solution)/shard_map/ppermute | solution.py:530
  5.7 0.1 collective-permute-start
  5.8 3.9 %collective-permute-start.1 = (bf16[2,2,128,256]{3,2,1,0:T(8,128)(2,1)S(1)}, bf16[2,2,128,256]{3,2,1,0:T(8,128)(2,1)S(1)}, u32[]{:S(2)}, u32[]{:S(2)}) collective-permute-start(bf16[2,2,128,256]{3,2,1,0:T(8,128)(2,1)S(1)} %get-tuple-element.46), channel_id=1, source_target_pairs={{2,4},{3,5},{4,2},{5,3},{10,12},{11,13},{12,10},{13,11},{18,20},{1... | collective-permute-start | bytes 786440 | tf_op jit(solution)/shard_map/ppermute | solution.py:530
  9.6 0.0 copy-start.3
  9.7 1.6 %collective-permute-start.2 = (bf16[2,2,256,128]{3,2,1,0:T(8,128)(2,1)S(1)}, bf16[2,2,256,128]{3,2,1,0:T(8,128)(2,1)S(1)}, u32[]{:S(2)}, u32[]{:S(2)}) collective-permute-start(bf16[2,2,256,128]{3,2,1,0:T(8,128)(2,1)S(1)} %get-tuple-element.47), channel_id=1, source_target_pairs={{0,1},{1,0},{2,3},{3,2},{4,5},{5,4},{6,7},{7,6},{8,9},{9,8},{10,11... | collective-permute-start | bytes 786440 | tf_op jit(solution)/shard_map/ppermute | solution.py:530
  11.2 0.9 %copy-done.6 = f32[256,256]{1,0:T(8,128)S(1)} copy-done((f32[256,256]{1,0:T(8,128)S(1)}, f32[256,256]{1,0:T(8,128)}, u32[]{:S(2)}) %copy-start.6) | copy-done | bytes 262168
  12.2 1.4 %turn.1 = (f32[256,256]{1,0:T(8,128)S(1)}, f32[256,256]{1,0:T(8,128)S(1)}) custom-call(f32[256,256]{1,0:T(8,128)S(1)} %copy-done.6), custom_call_target="tpu_custom_call" | custom-call | flops 2000000000 | bytes 6000000 | tf_op jit(solution)/shard_map/turn/pallas_call | solution.py:519
  14.3 0.0 copy-done.2
  14.3 0.0 copy-done.4
  14.3 0.0 copy-done.5
  14.3 0.5 slots.1
  14.8 0.0 collective-permute-done.3.refs_3_
  14.8 0.0 collective-permute-done.4.refs_4_
  14.8 0.0 collective-permute-done.refs_0_
  14.8 1.4 %collective-permute-done.1.refs_1_ = bf16[2,2,128,256]{3,2,1,0:T(8,128)(2,1)S(1)} collective-permute-done((bf16[2,2,128,256]{3,2,1,0:T(8,128)(2,1)S(1)}, bf16[2,2,128,256]{3,2,1,0:T(8,128)(2,1)S(1)}, u32[]{:S(2)}, u32[]{:S(2)}) %collective-permute-start.1) | collective-permute-done | bytes 262176 | tf_op jit(solution)/shard_map/ppermute | solution.py:530
  16.2 1.3 %collective-permute-done.2.refs_2_ = bf16[2,2,256,128]{3,2,1,0:T(8,128)(2,1)S(1)} collective-permute-done((bf16[2,2,256,128]{3,2,1,0:T(8,128)(2,1)S(1)}, bf16[2,2,256,128]{3,2,1,0:T(8,128)(2,1)S(1)}, u32[]{:S(2)}, u32[]{:S(2)}) %collective-permute-start.2) | collective-permute-done | bytes 262176 | tf_op jit(solution)/shard_map/ppermute | solution.py:530
  17.5 0.0 collective-permute-start.6
  17.5 0.0 copy-done.3
  17.5 1.3 %windows_for_other.1 = (bf16[2,2,256,256]{3,2,1,0:T(8,128)(2,1)S(1)}, f32[2,2,512,512]{3,2,1,0:T(8,128)S(1)}) custom-call(s32[2,2]{1,0:T(2,128)S(1)} %copy-done.3, f32[2,2,512,512]{3,2,1,0:T(8,128)S(1)} %get-tuple-element.60._filled, bf16[2,2,128,256]{3,2,1,0:T(8,128)(2,1)S(1)} %collective-permute-done.refs_0_, ...), custom_call_target="tpu_custom_call", output_to_operand_aliasing={{1}: (1, {})} | custom-call | tf_op jit(solution)/shard_map/windows_for_other/pallas_call | solution.py:519
  18.8 0.6 collective-permute-start.5
  19.4 1.1 %windows.1.win_own = bf16[2,2,256,256]{3,2,1,0:T(8,128)(2,1)S(1)} custom-call(s32[2,2]{1,0:T(2,128)S(1)} %copy-done.3, f32[2,2,512,512]{3,2,1,0:T(8,128)S(1)} %get-tuple-element.66.ext_ref), custom_call_target="tpu_custom_call" | custom-call | tf_op jit(solution)/shard_map/windows/pallas_call | solution.py:519
  20.6 0.0 collective-permute-done.6.inc_got
  20.6 0.4 collective-permute-done.5.win_got
  20.9 0.0 copy-done
  21.0 7.7 %collective-permute-start.7 = (s32[264,256]{1,0:T(8,128)S(1)}, s32[264,256]{1,0:T(8,128)S(1)}, u32[]{:S(2)}, u32[]{:S(2)}) collective-permute-start(s32[264,256]{1,0:T(8,128)S(1)} %get-tuple-element.72), channel_id=1, source_target_pairs={{16,0},{0,16},{24,8},{8,24},{17,1},{1,17},{25,9},{9,25},{18,2},{2,... | collective-permute-start | bytes 811016 | tf_op jit(solution)/shard_map/ppermute | solution.py:606
  28.7 7.0 %collective-permute-done.7.wave_in = s32[264,256]{1,0:T(8,128)S(1)} collective-permute-done((s32[264,256]{1,0:T(8,128)S(1)}, s32[264,256]{1,0:T(8,128)S(1)}, u32[]{:S(2)}, u32[]{:S(2)}) %collective-permute-start.7) | collective-permute-done | bytes 270368 | tf_op jit(solution)/shard_map/ppermute | solution.py:606
  35.7 4.7 %sweep.3 = (f32[2,2,256,256]{3,2,1,0:T(8,128)S(1)}, f32[2,2,256,256]{3,2,1,0:T(8,128)S(1)}) custom-call(s32[264,256]{1,0:T(8,128)S(1)} %collective-permute-done.7.wave_in, bf16[2,2,256,256]{3,2,1,0:T(8,128)(2,1)S(1)} %windows.1.win_own, bf16[2,2,256,256]{3,2,1,0:T(8,128)(2,1)S(1)} %collective-permute-done.5.win_got, ...), custom_call_target="tpu_custom_call", output_to_operand_aliasing={{0}: (8, {}), {1}: (9, {})} | custom-call | tf_op jit(solution)/shard_map/sweep/pallas_call | solution.py:519
  40.4 0.1 collective-permute-start.8
  40.4 1.4 %scatter_own.1._own = f32[2,2,512,512]{3,2,1,0:T(8,128)S(1)} custom-call(s32[2,2]{1,0:T(2,128)S(1)} %copy-done.3, f32[2,2,256,256]{3,2,1,0:T(8,128)S(1)} %get-tuple-element.76.term_ref), custom_call_target="tpu_custom_call" | custom-call | flops 2000000000 | bytes 6000000 | tf_op jit(solution)/shard_map/scatter_own/pallas_call | solution.py:519
  41.9 1.2 %collective-permute-done.8.term_ref = f32[2,2,256,256]{3,2,1,0:T(8,128)S(1)} collective-permute-done((f32[2,2,256,256]{3,2,1,0:T(8,128)S(1)}, f32[2,2,256,256]{3,2,1,0:T(8,128)S(1)}, u32[]{:S(2)}, u32[]{:S(2)}) %collective-permute-start.8) | collective-permute-done | bytes 1048608 | tf_op jit(solution)/shard_map/ppermute | solution.py:609
  43.1 1.6 %scatter.1 = (f32[2,2,512,512]{3,2,1,0:T(8,128)S(1)}, s32[536,128]{1,0:T(8,128)S(1)}) custom-call(s32[2,2]{1,0:T(2,128)S(1)} %copy-done.3, f32[2,2,256,256]{3,2,1,0:T(8,128)S(1)} %collective-permute-done.8.term_ref, f32[2,2,512,512]{3,2,1,0:T(8,128)S(1)} %scatter_own.1._own), custom_call_target="tpu_custom_call", output_to_operand_aliasing={{0}: (2, {})} | custom-call | flops 2000000000 | bytes 6000000 | tf_op jit(solution)/shard_map/scatter/pallas_call | solution.py:519
  44.7 1.1 %collective-permute-start.9 = (s32[536,128]{1,0:T(8,128)S(1)}, s32[536,128]{1,0:T(8,128)S(1)}, u32[]{:S(2)}, u32[]{:S(2)}) collective-permute-start(s32[536,128]{1,0:T(8,128)S(1)} %get-tuple-element.78), channel_id=1, source_target_pairs={{0,1},{1,0},{2,3},{3,2},{4,5},{5,4},{6,7},{7,6},{8,9},{9,8},{10,11... | collective-permute-start | bytes 823304 | tf_op jit(solution)/shard_map/ppermute | solution.py:530
  45.8 1.0 %halos.1 = (s32[264,256]{1,0:T(8,128)S(1)}, s32[264,256]{1,0:T(8,128)S(1)}, s32[264,128]{1,0:T(8,128)S(1)}, s32[264,128]{1,0:T(8,128)S(1)}) custom-call(f32[2,2,512,512]{3,2,1,0:T(8,128)S(1)} %get-tuple-element.77.ext_ref), custom_call_target="tpu_custom_call" | custom-call | flops 1000000000 | bytes 3000000 | tf_op jit(solution)/shard_map/halos/pallas_call | solution.py:519
  46.8 0.1 collective-permute-start.10
  46.9 2.6 %collective-permute-start.11 = (s32[264,256]{1,0:T(8,128)S(1)}, s32[264,256]{1,0:T(8,128)S(1)}, u32[]{:S(2)}, u32[]{:S(2)}) collective-permute-start(s32[264,256]{1,0:T(8,128)S(1)} %get-tuple-element.80), channel_id=1, source_target_pairs={{2,4},{3,5},{4,2},{5,3},{10,12},{11,13},{12,10},{13,11},{18,20},{1... | collective-permute-start | bytes 811016 | tf_op jit(solution)/shard_map/ppermute | solution.py:530
  49.5 0.6 collective-permute-start.12
  50.1 3.2 %collective-permute-start.13 = (s32[264,128]{1,0:T(8,128)S(1)}, s32[264,128]{1,0:T(8,128)S(1)}, u32[]{:S(2)}, u32[]{:S(2)}) collective-permute-start(s32[264,128]{1,0:T(8,128)S(1)} %get-tuple-element.83), channel_id=1, source_target_pairs={{2,5},{3,4},{4,3},{5,2},{10,13},{11,12},{12,11},{13,10},{18,21},{1... | collective-permute-start | bytes 405512 | tf_op jit(solution)/shard_map/ppermute | solution.py:530
  53.3 3.0 %collective-permute-done.10.refs_1_ = s32[264,256]{1,0:T(8,128)S(1)} collective-permute-done((s32[264,256]{1,0:T(8,128)S(1)}, s32[264,256]{1,0:T(8,128)S(1)}, u32[]{:S(2)}, u32[]{:S(2)}) %collective-permute-start.10) | collective-permute-done | bytes 270368 | tf_op jit(solution)/shard_map/ppermute | solution.py:530
  56.3 1.9 %collective-permute-done.11.refs_2_ = s32[264,256]{1,0:T(8,128)S(1)} collective-permute-done((s32[264,256]{1,0:T(8,128)S(1)}, s32[264,256]{1,0:T(8,128)S(1)}, u32[]{:S(2)}, u32[]{:S(2)}) %collective-permute-start.11) | collective-permute-done | bytes 270368 | tf_op jit(solution)/shard_map/ppermute | solution.py:530
  58.2 0.0 collective-permute-done.9.refs_0_
  58.2 1.4 %fold.1 = (f32[2,2,256,256]{3,2,1,0:T(8,128)S(1)}, f32[2,2,256,256]{3,2,1,0:T(8,128)}) custom-call(f32[2,2,512,512]{3,2,1,0:T(8,128)S(1)} %get-tuple-element.77.ext_ref, s32[536,128]{1,0:T(8,128)S(1)} %collective-permute-done.9.refs_0_, s32[264,256]{1,0:T(8,128)S(1)} %collective-permute-done.10.refs_1_, s32[264,256]{1,0:T(8,128)S(1)} %collective-permute-done.11.refs_2_), custom_call_target="tpu_custom_call" | custom-call | flops 2000000000 | bytes 6000000 | tf_op jit(solution)/shard_map/fold/pallas_call | solution.py:519
  59.6 0.0 collective-permute-done.12.refs_0_
  59.7 1.6 %collective-permute-done.13.refs_1_ = s32[264,128]{1,0:T(8,128)S(1)} collective-permute-done((s32[264,128]{1,0:T(8,128)S(1)}, s32[264,128]{1,0:T(8,128)S(1)}, u32[]{:S(2)}, u32[]{:S(2)}) %collective-permute-start.13) | collective-permute-done | bytes 135200 | tf_op jit(solution)/shard_map/ppermute | solution.py:530
  61.2 0.9 %corners.1 = f32[2,2,256,256]{3,2,1,0:T(8,128)} custom-call(f32[2,2,256,256]{3,2,1,0:T(8,128)S(1)} %get-tuple-element.81.part_ref, s32[264,128]{1,0:T(8,128)S(1)} %collective-permute-done.12.refs_0_, s32[264,128]{1,0:T(8,128)S(1)} %collective-permute-done.13.refs_1_, f32[2,2,256,256]{3,2,1,0:T(8,128)} %get-tuple-element.84.refs_2_), custom_call_target="tpu_custom_call", output_to_operand_aliasing={{}: (3, {})} | custom-call | tf_op jit(solution)/shard_map/corners/pallas_call | solution.py:519
  (6 shorter events, 0.0 us)
Async XLA Ops:
  0.0 1.0 %copy-start.1 = (bf16[2,2,256,256]{3,2,1,0:T(8,128)(2,1)S(1)}, bf16[2,2,256,256]{3,2,1,0:T(8,128)(2,1)}, u32[]{:S(2)}) copy-start(bf16[2,2,256,256]{3,2,1,0:T(8,128)(2,1)} %tile_ref.1) | copy-start | bytes 1572868
  1.0 13.2 %copy-start.2 = (bf16[2,2,256,256]{3,2,1,0:T(8,128)(2,1)S(1)}, bf16[2,2,256,256]{3,2,1,0:T(8,128)(2,1)}, u32[]{:S(2)}) copy-start(bf16[2,2,256,256]{3,2,1,0:T(8,128)(2,1)} %tile_ref.1) | copy-start | bytes 1572868
  1.0 13.2 %copy-start.4 = (bf16[2,2,2,256,256]{4,3,2,1,0:T(8,128)(2,1)S(1)}, bf16[2,2,2,256,256]{4,3,2,1,0:T(8,128)(2,1)}, u32[]{:S(2)}) copy-start(bf16[2,2,2,256,256]{4,3,2,1,0:T(8,128)(2,1)} %inc_ref) | copy-start | bytes 3145732
  1.0 13.2 %copy-start.5 = (bf16[2,2,256,256]{3,2,1,0:T(8,128)(2,1)S(1)}, bf16[2,2,256,256]{3,2,1,0:T(8,128)(2,1)}, u32[]{:S(2)}) copy-start(bf16[2,2,256,256]{3,2,1,0:T(8,128)(2,1)} %exit_ref) | copy-start | bytes 1572868
  1.2 13.6 %collective-permute-start.3 = (bf16[2,2,128,128]{3,2,1,0:T(8,128)(2,1)S(1)}, bf16[2,2,128,128]{3,2,1,0:T(8,128)(2,1)S(1)}, u32[]{:S(2)}, u32[]{:S(2)}) collective-permute-start(bf16[2,2,128,128]{3,2,1,0:T(8,128)(2,1)S(1)} %get-tuple-element.48), channel_id=1, source_target_pairs={{0,3},{1,2},{2,1},{3,0},{4,7},{5,6},{6,5},{7,4},{8,11},{9,10},{10,... | collective-permute-start | bytes 393224 | tf_op jit(solution)/shard_map/ppermute | solution.py:530
  3.8 11.0 %collective-permute-start.4 = (bf16[2,2,128,128]{3,2,1,0:T(8,128)(2,1)S(1)}, bf16[2,2,128,128]{3,2,1,0:T(8,128)(2,1)S(1)}, u32[]{:S(2)}, u32[]{:S(2)}) collective-permute-start(bf16[2,2,128,128]{3,2,1,0:T(8,128)(2,1)S(1)} %get-tuple-element.49), channel_id=1, source_target_pairs={{2,5},{3,4},{4,3},{5,2},{10,13},{11,12},{12,11},{13,10},{18,21},{1... | collective-permute-start | bytes 393224 | tf_op jit(solution)/shard_map/ppermute | solution.py:530
  5.7 9.1 %collective-permute-start = (bf16[2,2,128,256]{3,2,1,0:T(8,128)(2,1)S(1)}, bf16[2,2,128,256]{3,2,1,0:T(8,128)(2,1)S(1)}, u32[]{:S(2)}, u32[]{:S(2)}) collective-permute-start(bf16[2,2,128,256]{3,2,1,0:T(8,128)(2,1)S(1)} %get-tuple-element.45), channel_id=1, source_target_pairs={{0,2},{1,3},{2,0},{3,1},{4,6},{5,7},{6,4},{7,5},{8,10},{9,11},{10,... | collective-permute-start | bytes 786440 | tf_op jit(solution)/shard_map/ppermute | solution.py:530
  5.8 10.4 %collective-permute-start.1 = (bf16[2,2,128,256]{3,2,1,0:T(8,128)(2,1)S(1)}, bf16[2,2,128,256]{3,2,1,0:T(8,128)(2,1)S(1)}, u32[]{:S(2)}, u32[]{:S(2)}) collective-permute-start(bf16[2,2,128,256]{3,2,1,0:T(8,128)(2,1)S(1)} %get-tuple-element.46), channel_id=1, source_target_pairs={{2,4},{3,5},{4,2},{5,3},{10,12},{11,13},{12,10},{13,11},{18,20},{1... | collective-permute-start | bytes 786440 | tf_op jit(solution)/shard_map/ppermute | solution.py:530
  9.6 7.8 %copy-start.3 = (s32[2,2]{1,0:T(2,128)S(1)}, s32[2,2]{1,0:T(2,128)}, u32[]{:S(2)}) copy-start(s32[2,2]{1,0:T(2,128)} %anchor_ref.7) | copy-start | bytes 52
  9.7 7.8 %collective-permute-start.2 = (bf16[2,2,256,128]{3,2,1,0:T(8,128)(2,1)S(1)}, bf16[2,2,256,128]{3,2,1,0:T(8,128)(2,1)S(1)}, u32[]{:S(2)}, u32[]{:S(2)}) collective-permute-start(bf16[2,2,256,128]{3,2,1,0:T(8,128)(2,1)S(1)} %get-tuple-element.47), channel_id=1, source_target_pairs={{0,1},{1,0},{2,3},{3,2},{4,5},{5,4},{6,7},{7,6},{8,9},{9,8},{10,11... | collective-permute-start | bytes 786440 | tf_op jit(solution)/shard_map/ppermute | solution.py:530
  11.2 0.9 %copy-start.6 = (f32[256,256]{1,0:T(8,128)S(1)}, f32[256,256]{1,0:T(8,128)}, u32[]{:S(2)}) copy-start(f32[256,256]{1,0:T(8,128)} %phase_ref) | copy-start | bytes 786436
  17.5 3.5 %copy-start = (bf16[4,256,256]{2,1,0:T(8,128)(2,1)S(1)}, bf16[4,256,256]{2,1,0:T(8,128)(2,1)}, u32[]{:S(2)}) copy-start(bf16[4,256,256]{2,1,0:T(8,128)(2,1)} %constant.2.clone.tab_ref) | copy-start | bytes 1572868
  17.5 3.1 %collective-permute-start.6 = (bf16[2,2,256,256]{3,2,1,0:T(8,128)(2,1)S(1)}, bf16[2,2,256,256]{3,2,1,0:T(8,128)(2,1)S(1)}, u32[]{:S(2)}, u32[]{:S(2)}) collective-permute-start(bf16[2,2,256,256]{3,2,1,0:T(8,128)(2,1)S(1)} %get-tuple-element.69), channel_id=1, source_target_pairs={{0,8},{8,0},{16,24},{24,16},{1,9},{9,1},{17,25},{25,17},{2,10},{10... | collective-permute-start | bytes 1572872 | tf_op jit(solution)/shard_map/ppermute | solution.py:563
  18.8 2.1 %collective-permute-start.5 = (bf16[2,2,256,256]{3,2,1,0:T(8,128)(2,1)S(1)}, bf16[2,2,256,256]{3,2,1,0:T(8,128)(2,1)S(1)}, u32[]{:S(2)}, u32[]{:S(2)}) collective-permute-start(bf16[2,2,256,256]{3,2,1,0:T(8,128)(2,1)S(1)} %get-tuple-element.67), channel_id=1, source_target_pairs={{0,8},{8,0},{16,24},{24,16},{1,9},{9,1},{17,25},{25,17},{2,10},{10... | collective-permute-start | bytes 1572872 | tf_op jit(solution)/shard_map/ppermute | solution.py:574
  21.0 14.7 %collective-permute-start.7 = (s32[264,256]{1,0:T(8,128)S(1)}, s32[264,256]{1,0:T(8,128)S(1)}, u32[]{:S(2)}, u32[]{:S(2)}) collective-permute-start(s32[264,256]{1,0:T(8,128)S(1)} %get-tuple-element.72), channel_id=1, source_target_pairs={{16,0},{0,16},{24,8},{8,24},{17,1},{1,17},{25,9},{9,25},{18,2},{2,... | collective-permute-start | bytes 811016 | tf_op jit(solution)/shard_map/ppermute | solution.py:606
  40.4 2.7 %collective-permute-start.8 = (f32[2,2,256,256]{3,2,1,0:T(8,128)S(1)}, f32[2,2,256,256]{3,2,1,0:T(8,128)S(1)}, u32[]{:S(2)}, u32[]{:S(2)}) collective-permute-start(f32[2,2,256,256]{3,2,1,0:T(8,128)S(1)} %get-tuple-element.75), channel_id=1, source_target_pairs={{0,8},{8,0},{16,24},{24,16},{1,9},{9,1},{17,25},{25,17},{2,10},{10... | collective-permute-start | bytes 3145736 | tf_op jit(solution)/shard_map/ppermute | solution.py:609
  44.7 13.5 %collective-permute-start.9 = (s32[536,128]{1,0:T(8,128)S(1)}, s32[536,128]{1,0:T(8,128)S(1)}, u32[]{:S(2)}, u32[]{:S(2)}) collective-permute-start(s32[536,128]{1,0:T(8,128)S(1)} %get-tuple-element.78), channel_id=1, source_target_pairs={{0,1},{1,0},{2,3},{3,2},{4,5},{5,4},{6,7},{7,6},{8,9},{9,8},{10,11... | collective-permute-start | bytes 823304 | tf_op jit(solution)/shard_map/ppermute | solution.py:530
  46.8 9.4 %collective-permute-start.10 = (s32[264,256]{1,0:T(8,128)S(1)}, s32[264,256]{1,0:T(8,128)S(1)}, u32[]{:S(2)}, u32[]{:S(2)}) collective-permute-start(s32[264,256]{1,0:T(8,128)S(1)} %get-tuple-element.79), channel_id=1, source_target_pairs={{0,2},{1,3},{2,0},{3,1},{4,6},{5,7},{6,4},{7,5},{8,10},{9,11},{10,... | collective-permute-start | bytes 811016 | tf_op jit(solution)/shard_map/ppermute | solution.py:530
  46.9 11.3 %collective-permute-start.11 = (s32[264,256]{1,0:T(8,128)S(1)}, s32[264,256]{1,0:T(8,128)S(1)}, u32[]{:S(2)}, u32[]{:S(2)}) collective-permute-start(s32[264,256]{1,0:T(8,128)S(1)} %get-tuple-element.80), channel_id=1, source_target_pairs={{2,4},{3,5},{4,2},{5,3},{10,12},{11,13},{12,10},{13,11},{18,20},{1... | collective-permute-start | bytes 811016 | tf_op jit(solution)/shard_map/ppermute | solution.py:530
  49.5 10.1 %collective-permute-start.12 = (s32[264,128]{1,0:T(8,128)S(1)}, s32[264,128]{1,0:T(8,128)S(1)}, u32[]{:S(2)}, u32[]{:S(2)}) collective-permute-start(s32[264,128]{1,0:T(8,128)S(1)} %get-tuple-element.82), channel_id=1, source_target_pairs={{0,3},{1,2},{2,1},{3,0},{4,7},{5,6},{6,5},{7,4},{8,11},{9,10},{10,... | collective-permute-start | bytes 405512 | tf_op jit(solution)/shard_map/ppermute | solution.py:530
  50.1 11.1 %collective-permute-start.13 = (s32[264,128]{1,0:T(8,128)S(1)}, s32[264,128]{1,0:T(8,128)S(1)}, u32[]{:S(2)}, u32[]{:S(2)}) collective-permute-start(s32[264,128]{1,0:T(8,128)S(1)} %get-tuple-element.83), channel_id=1, source_target_pairs={{2,5},{3,4},{4,3},{5,2},{10,13},{11,12},{12,11},{13,10},{18,21},{1... | collective-permute-start | bytes 405512 | tf_op jit(solution)/shard_map/ppermute | solution.py:530

commit v10 on v9

--- a/solution.py
+++ b/solution.py
@@ -17,7 +17,6 @@
 LEVELS = 32767.0
 SCALE_ROWS = 8
 FIRST = 3
-CHUNKS = 2
 EARLY = ((0, None), (1, None), (None, 0), (None, 1), (0, 0), (0, 1), (1, 0), (1, 1))
 LATE = ((None, 0), (None, 1), (0, None), (1, None), (0, 0), (0, 1), (1, 0), (1, 1))
 SUBLANES = 8
@@ -56,22 +55,48 @@
     return np.concatenate([cos, sin]) / math.sqrt(size)
 
 
+def dft_tables(size):
+    half = size // 2
+    basis = dft_basis(size)
+
+    def parts(matrix):
+        high = matrix.astype(jnp.bfloat16)
+        return high, (matrix - high.astype(np.float64)).astype(jnp.bfloat16)
+
+    def stacked(matrix):
+        high, low = parts(matrix)
+        return np.block([[high, high], [low, np.zeros_like(low)]])
+
+    high, low = parts(basis)
+    kinds = [np.concatenate([basis[odd:half:2, :half], basis[half + odd :: 2, :half]]) for odd in (0, 1)]
+    lefts = [stacked(kind) for kind in kinds] + [stacked(kind.T) for kind in kinds]
+    return np.stack([high, low, high.T, low.T] + lefts).astype(jnp.bfloat16)
+
+
 def turn_kernel(phase_ref, cos_ref, sin_ref):
     size = phase_ref.shape[0]
     half = size // 2
     place = lax.broadcasted_iota(jnp.int32, (size, size), 0)
-    source = jnp.where(place <= half, place, size + half - place)
-    select = (source == lax.broadcasted_iota(jnp.int32, (size, size), 1)).astype(jnp.bfloat16)
+    frequency = lax.broadcasted_iota(jnp.int32, (size, size), 1)
+
+    def folded(place):
+        return jnp.where(place <= half, place, size + half - place)
+
+    odd = place // half
+    within = place - odd * half
+    row = 2 * within + odd
+    row_select = (folded(row) == frequency).astype(jnp.bfloat16)
+    column_select = (folded(place) == frequency).astype(jnp.bfloat16)
 
     def thirds(value):
         first = value.astype(jnp.bfloat16)
         value = value - first.astype(jnp.float32)
         return first, *split(value)
 
-    first, second, third = [dot(select, part) for part in thirds(phase_ref[...])]
+    first, second, third = [dot(row_select, part) for part in thirds(phase_ref[...])]
     rows = first + (second + third)
     first, second, third = [
-        lax.dot_general(part, select, (((1,), (1,)), ((), ())), preferred_element_type=jnp.float32)
+        lax.dot_general(part, column_select, (((1,), (1,)), ((), ())), preferred_element_type=jnp.float32)
         for part in thirds(rows)
     ]
     phase = first + (second + third)
@@ -97,9 +122,21 @@
     return jnp.dot(a, b, preferred_element_type=jnp.float32)
 
 
-def left3(table, field):
-    high, low = split(field)
-    return dot(table[0], high) + (dot(table[0], low) + dot(table[1], high))
+def left_half(table, field):
+    both = dot(table, jnp.concatenate(split(field), axis=0))
+    half = both.shape[0] // 2
+    return both[:half] + both[half:]
+
+
+def left_forward(tables, field):
+    half = field.shape[0] // 2
+    upper, lower = field[:half], field[half:]
+    return left_half(tables[0], upper + lower), left_half(tables[1], upper - lower)
+
+
+def left_back(tables, even, odd):
+    even, odd = left_half(tables[0], even), left_half(tables[1], odd)
+    return jnp.concatenate([even + odd, even - odd], axis=0)
 
 
 def right3(field, table):
@@ -107,18 +144,14 @@
     return dot(high, table[0]) + (dot(low, table[0]) + dot(high, table[1]))
 
 
-def lefts(table, fields):
-    return [left3(table, field) for field in fields]
-
-
 def rights(fields, table):
     return [right3(field, table) for field in fields]
 
 
-def middle(parts, cos_ref, sin_ref, chunk, chunks):
+def middle(parts, cos_ref, sin_ref, odd):
     half = parts[0].shape[1] // 2
-    size = half // chunks
-    row0 = chunk * size + lax.broadcasted_iota(jnp.int32, (size, half), 0) == 0
+    size = half // 2
+    row0 = odd * size + lax.broadcasted_iota(jnp.int32, (size, half), 0) == 0
     col0 = lax.broadcasted_iota(jnp.int32, (size, half), 1) == 0
 
     def quadrant(r, c):
@@ -130,7 +163,7 @@
     for c in range(2):
         turned = []
         for r, (re, im) in enumerate(spectrum_split(top[c], bottom[c], row0)):
-            first = r * half + chunk * size
+            first = odd * half + r * size
             where = (slice(first, first + size), slice(c * half, (c + 1) * half))
             cos, sin = cos_ref[where], sin_ref[where]
             turned.append((re * cos + im * sin, im * cos - re * sin))
@@ -145,22 +178,13 @@
 
 
 def propagate(parts, cos_ref, sin_ref, tab_ref):
-    table = (tab_ref[0], tab_ref[1])
-    turned = (tab_ref[2], tab_ref[3])
-    half = cos_ref.shape[0] // 2
-    size = half // CHUNKS
-    parts = lefts(table, parts)
-    spectra = []
-    for chunk in range(CHUNKS):
-        rows = slice(chunk * size, (chunk + 1) * size)
-        lower = slice(half + chunk * size, half + (chunk + 1) * size)
-        spectra.append(rights([jnp.concatenate([part[rows], part[lower]], axis=0) for part in parts], turned))
-    spectra = [middle(spectrum, cos_ref, sin_ref, chunk, CHUNKS) for chunk, spectrum in enumerate(spectra)]
-    spectra = [rights(spectrum, table) for spectrum in spectra]
-    fields = [
-        jnp.concatenate([s[c][:size] for s in spectra] + [s[c][size:] for s in spectra], axis=0) for c in range(2)
-    ]
-    return lefts(turned, fields)
+    table, turned = (tab_ref[0], tab_ref[1]), (tab_ref[2], tab_ref[3])
+    forward, back = (tab_ref[4], tab_ref[5]), (tab_ref[6], tab_ref[7])
+    real, imag = [left_forward(forward, part) for part in parts]
+    kinds = [rights(kind, turned) for kind in zip(real, imag)]
+    kinds = [middle(kind, cos_ref, sin_ref, odd) for odd, kind in enumerate(kinds)]
+    even, odd = [rights(kind, table) for kind in kinds]
+    return [left_back(back, even[c], odd[c]) for c in range(2)]
 
 
 def window_place(at_x, at_y):
@@ -553,10 +577,7 @@
     )
     factor_shape = shape_of(propagator_phase.shape, f32)
     phase_cos, phase_sin = call(turn_kernel, (factor_shape, factor_shape), (propagator_phase,), "turn", cost=2)
-    basis = dft_basis(patch)
-    high = basis.astype(jnp.bfloat16)
-    low = (basis - high.astype(np.float64)).astype(jnp.bfloat16)
-    tables = jnp.asarray(np.stack([high, low, high.T, low.T]))
+    tables = jnp.asarray(dft_tables(patch))
     phase_cos, phase_sin, inc_own, inc_send, wave, bordered, halos = lax.optimization_barrier(
         (phase_cos, phase_sin, inc_own, inc_send, wave, bordered, halos)
     )

time: 62.4 us -> 61.9 us (level)
  transfers between devices with their start and end apart: 14 -> 14, of which waited for: 8 -> 9; matrix products, arithmetic and copies ran while one was open for 0% -> 0% of each run, Pallas kernels for 13% -> 13%
where the time goes in v10:
time: 61.9 us; the launch traced here: 61.6 us
  starting transfers between devices  25.3 us (41%)
  waiting for transfers between devices  17.7 us (29%)
  Pallas kernels  15.5 us (25%)
  local copies, waits for them, and re-layouts  2.01 us (3%)
  between operations  1.05 us (2%)
    ppermute x10, starting transfers between devices, swapped(): lax.ppermute(value, ('sx', 'sy'), swap_list(n_x, n_y, *kind))  17.5 us
    pallas_call x12, Pallas kernels, call(): pl.pallas_call(kernel, out_shape=out_shape, scratch_shapes=list(scratch),...  15.5 us
    ppermute x10, waiting for transfers between devices, swapped(): lax.ppermute(value, ('sx', 'sy'), swap_list(n_x, n_y, *kind))  9.11 us
    ppermute x1, starting transfers between devices, shards(): wave = lax.ppermute(results[2], 'depth', hop)  7.14 us
    ppermute x1, waiting for transfers between devices, shards(): wave = lax.ppermute(results[2], 'depth', hop)  7 us
    unnamed x14, local copies, waits for them, and re-layouts  2.01 us
  transfers between devices with their start and end apart: 14, of which 9 were waited for; matrix products, arithmetic and copies ran while one was open for 0% of the time, Pallas kernels for 13%

profile of v10, /device:TPU:16, one launch (start us, length us, event | category | flops | bytes accessed | tf_op | source)
XLA Modules:
  0.0 61.6 jit_solution(15953760174622929650)
XLA Ops:
  0.0 0.0 copy-start.1
  0.0 1.0 %copy-done.1 = bf16[2,2,256,256]{3,2,1,0:T(8,128)(2,1)S(1)} copy-done((bf16[2,2,256,256]{3,2,1,0:T(8,128)(2,1)S(1)}, bf16[2,2,256,256]{3,2,1,0:T(8,128)(2,1)}, u32[]{:S(2)}) %copy-start.1) | copy-done | bytes 524312
  1.0 0.1 rims.1
  1.2 2.6 %collective-permute-start.3 = (bf16[2,2,128,128]{3,2,1,0:T(8,128)(2,1)S(1)}, bf16[2,2,128,128]{3,2,1,0:T(8,128)(2,1)S(1)}, u32[]{:S(2)}, u32[]{:S(2)}) collective-permute-start(bf16[2,2,128,128]{3,2,1,0:T(8,128)(2,1)S(1)} %get-tuple-element.48), channel_id=1, source_target_pairs={{0,3},{1,2},{2,1},{3,0},{4,7},{5,6},{6,5},{7,4},{8,11},{9,10},{10,... | collective-permute-start | bytes 393224 | tf_op jit(solution)/shard_map/ppermute | solution.py:554
  3.8 1.9 %collective-permute-start.4 = (bf16[2,2,128,128]{3,2,1,0:T(8,128)(2,1)S(1)}, bf16[2,2,128,128]{3,2,1,0:T(8,128)(2,1)S(1)}, u32[]{:S(2)}, u32[]{:S(2)}) collective-permute-start(bf16[2,2,128,128]{3,2,1,0:T(8,128)(2,1)S(1)} %get-tuple-element.49), channel_id=1, source_target_pairs={{2,5},{3,4},{4,3},{5,2},{10,13},{11,12},{12,11},{13,10},{18,21},{1... | collective-permute-start | bytes 393224 | tf_op jit(solution)/shard_map/ppermute | solution.py:554
  5.7 0.1 collective-permute-start
  5.8 3.9 %collective-permute-start.1 = (bf16[2,2,128,256]{3,2,1,0:T(8,128)(2,1)S(1)}, bf16[2,2,128,256]{3,2,1,0:T(8,128)(2,1)S(1)}, u32[]{:S(2)}, u32[]{:S(2)}) collective-permute-start(bf16[2,2,128,256]{3,2,1,0:T(8,128)(2,1)S(1)} %get-tuple-element.46), channel_id=1, source_target_pairs={{2,4},{3,5},{4,2},{5,3},{10,12},{11,13},{12,10},{13,11},{18,20},{1... | collective-permute-start | bytes 786440 | tf_op jit(solution)/shard_map/ppermute | solution.py:554
  9.6 0.0 copy-start.3
  9.7 1.6 %collective-permute-start.2 = (bf16[2,2,256,128]{3,2,1,0:T(8,128)(2,1)S(1)}, bf16[2,2,256,128]{3,2,1,0:T(8,128)(2,1)S(1)}, u32[]{:S(2)}, u32[]{:S(2)}) collective-permute-start(bf16[2,2,256,128]{3,2,1,0:T(8,128)(2,1)S(1)} %get-tuple-element.47), channel_id=1, source_target_pairs={{0,1},{1,0},{2,3},{3,2},{4,5},{5,4},{6,7},{7,6},{8,9},{9,8},{10,11... | collective-permute-start | bytes 786440 | tf_op jit(solution)/shard_map/ppermute | solution.py:554
  11.2 0.9 %copy-done.6 = f32[256,256]{1,0:T(8,128)S(1)} copy-done((f32[256,256]{1,0:T(8,128)S(1)}, f32[256,256]{1,0:T(8,128)}, u32[]{:S(2)}) %copy-start.6) | copy-done | bytes 262168
  12.2 1.4 %turn.1 = (f32[256,256]{1,0:T(8,128)S(1)}, f32[256,256]{1,0:T(8,128)S(1)}) custom-call(f32[256,256]{1,0:T(8,128)S(1)} %copy-done.6), custom_call_target="tpu_custom_call" | custom-call | flops 2000000000 | bytes 6000000 | tf_op jit(solution)/shard_map/turn/pallas_call | solution.py:543
  14.3 0.0 copy-done.2
  14.3 0.0 copy-done.4
  14.3 0.0 copy-done.5
  14.3 0.5 slots.1
  14.8 0.0 collective-permute-done.3.refs_3_
  14.8 0.0 collective-permute-done.4.refs_4_
  14.8 0.0 collective-permute-done.refs_0_
  14.8 1.4 %collective-permute-done.1.refs_1_ = bf16[2,2,128,256]{3,2,1,0:T(8,128)(2,1)S(1)} collective-permute-done((bf16[2,2,128,256]{3,2,1,0:T(8,128)(2,1)S(1)}, bf16[2,2,128,256]{3,2,1,0:T(8,128)(2,1)S(1)}, u32[]{:S(2)}, u32[]{:S(2)}) %collective-permute-start.1) | collective-permute-done | bytes 262176 | tf_op jit(solution)/shard_map/ppermute | solution.py:554
  16.2 1.3 %collective-permute-done.2.refs_2_ = bf16[2,2,256,128]{3,2,1,0:T(8,128)(2,1)S(1)} collective-permute-done((bf16[2,2,256,128]{3,2,1,0:T(8,128)(2,1)S(1)}, bf16[2,2,256,128]{3,2,1,0:T(8,128)(2,1)S(1)}, u32[]{:S(2)}, u32[]{:S(2)}) %collective-permute-start.2) | collective-permute-done | bytes 262176 | tf_op jit(solution)/shard_map/ppermute | solution.py:554
  17.5 0.0 collective-permute-start.6
  17.5 0.0 copy-done.3
  17.5 1.3 %windows_for_other.1 = (bf16[2,2,256,256]{3,2,1,0:T(8,128)(2,1)S(1)}, f32[2,2,512,512]{3,2,1,0:T(8,128)S(1)}) custom-call(s32[2,2]{1,0:T(2,128)S(1)} %copy-done.3, f32[2,2,512,512]{3,2,1,0:T(8,128)S(1)} %get-tuple-element.60._filled, bf16[2,2,128,256]{3,2,1,0:T(8,128)(2,1)S(1)} %collective-permute-done.refs_0_, ...), custom_call_target="tpu_custom_call", output_to_operand_aliasing={{1}: (1, {})} | custom-call | tf_op jit(solution)/shard_map/windows_for_other/pallas_call | solution.py:543
  18.8 0.6 collective-permute-start.5
  19.4 1.1 %windows.1.win_own = bf16[2,2,256,256]{3,2,1,0:T(8,128)(2,1)S(1)} custom-call(s32[2,2]{1,0:T(2,128)S(1)} %copy-done.3, f32[2,2,512,512]{3,2,1,0:T(8,128)S(1)} %get-tuple-element.66.ext_ref), custom_call_target="tpu_custom_call" | custom-call | tf_op jit(solution)/shard_map/windows/pallas_call | solution.py:543
  20.6 0.0 collective-permute-done.6.inc_got
  20.6 0.4 collective-permute-done.5.win_got
  20.9 0.0 copy-done
  21.0 7.1 %collective-permute-start.7 = (s32[264,256]{1,0:T(8,128)S(1)}, s32[264,256]{1,0:T(8,128)S(1)}, u32[]{:S(2)}, u32[]{:S(2)}) collective-permute-start(s32[264,256]{1,0:T(8,128)S(1)} %get-tuple-element.72), channel_id=1, source_target_pairs={{16,0},{0,16},{24,8},{8,24},{17,1},{1,17},{25,9},{9,25},{18,2},{2,... | collective-permute-start | bytes 811016 | tf_op jit(solution)/shard_map/ppermute | solution.py:627
  28.1 7.0 %collective-permute-done.7.wave_in = s32[264,256]{1,0:T(8,128)S(1)} collective-permute-done((s32[264,256]{1,0:T(8,128)S(1)}, s32[264,256]{1,0:T(8,128)S(1)}, u32[]{:S(2)}, u32[]{:S(2)}) %collective-permute-start.7) | collective-permute-done | bytes 270368 | tf_op jit(solution)/shard_map/ppermute | solution.py:627
  35.1 4.6 %sweep.3 = (f32[2,2,256,256]{3,2,1,0:T(8,128)S(1)}, f32[2,2,256,256]{3,2,1,0:T(8,128)S(1)}) custom-call(s32[264,256]{1,0:T(8,128)S(1)} %collective-permute-done.7.wave_in, bf16[2,2,256,256]{3,2,1,0:T(8,128)(2,1)S(1)} %windows.1.win_own, bf16[2,2,256,256]{3,2,1,0:T(8,128)(2,1)S(1)} %collective-permute-done.5.win_got, ...), custom_call_target="tpu_custom_call", output_to_operand_aliasing={{0}: (8, {}), {1}: (9, {})} | custom-call | tf_op jit(solution)/shard_map/sweep/pallas_call | solution.py:543
  39.7 0.1 collective-permute-start.8
  39.8 1.4 %scatter_own.1._own = f32[2,2,512,512]{3,2,1,0:T(8,128)S(1)} custom-call(s32[2,2]{1,0:T(2,128)S(1)} %copy-done.3, f32[2,2,256,256]{3,2,1,0:T(8,128)S(1)} %get-tuple-element.76.term_ref), custom_call_target="tpu_custom_call" | custom-call | flops 2000000000 | bytes 6000000 | tf_op jit(solution)/shard_map/scatter_own/pallas_call | solution.py:543
  41.2 1.2 %collective-permute-done.8.term_ref = f32[2,2,256,256]{3,2,1,0:T(8,128)S(1)} collective-permute-done((f32[2,2,256,256]{3,2,1,0:T(8,128)S(1)}, f32[2,2,256,256]{3,2,1,0:T(8,128)S(1)}, u32[]{:S(2)}, u32[]{:S(2)}) %collective-permute-start.8) | collective-permute-done | bytes 1048608 | tf_op jit(solution)/shard_map/ppermute | solution.py:630
  42.5 1.6 %scatter.1 = (f32[2,2,512,512]{3,2,1,0:T(8,128)S(1)}, s32[536,128]{1,0:T(8,128)S(1)}) custom-call(s32[2,2]{1,0:T(2,128)S(1)} %copy-done.3, f32[2,2,256,256]{3,2,1,0:T(8,128)S(1)} %collective-permute-done.8.term_ref, f32[2,2,512,512]{3,2,1,0:T(8,128)S(1)} %scatter_own.1._own), custom_call_target="tpu_custom_call", output_to_operand_aliasing={{0}: (2, {})} | custom-call | flops 2000000000 | bytes 6000000 | tf_op jit(solution)/shard_map/scatter/pallas_call | solution.py:543
  44.1 1.0 %collective-permute-start.9 = (s32[536,128]{1,0:T(8,128)S(1)}, s32[536,128]{1,0:T(8,128)S(1)}, u32[]{:S(2)}, u32[]{:S(2)}) collective-permute-start(s32[536,128]{1,0:T(8,128)S(1)} %get-tuple-element.78), channel_id=1, source_target_pairs={{0,1},{1,0},{2,3},{3,2},{4,5},{5,4},{6,7},{7,6},{8,9},{9,8},{10,11... | collective-permute-start | bytes 823304 | tf_op jit(solution)/shard_map/ppermute | solution.py:554
  45.1 1.0 %halos.1 = (s32[264,256]{1,0:T(8,128)S(1)}, s32[264,256]{1,0:T(8,128)S(1)}, s32[264,128]{1,0:T(8,128)S(1)}, s32[264,128]{1,0:T(8,128)S(1)}) custom-call(f32[2,2,512,512]{3,2,1,0:T(8,128)S(1)} %get-tuple-element.77.ext_ref), custom_call_target="tpu_custom_call" | custom-call | flops 1000000000 | bytes 3000000 | tf_op jit(solution)/shard_map/halos/pallas_call | solution.py:543
  46.2 0.1 collective-permute-start.10
  46.3 2.6 %collective-permute-start.11 = (s32[264,256]{1,0:T(8,128)S(1)}, s32[264,256]{1,0:T(8,128)S(1)}, u32[]{:S(2)}, u32[]{:S(2)}) collective-permute-start(s32[264,256]{1,0:T(8,128)S(1)} %get-tuple-element.80), channel_id=1, source_target_pairs={{2,4},{3,5},{4,2},{5,3},{10,12},{11,13},{12,10},{13,11},{18,20},{1... | collective-permute-start | bytes 811016 | tf_op jit(solution)/shard_map/ppermute | solution.py:554
  48.9 0.6 collective-permute-start.12
  49.5 3.2 %collective-permute-start.13 = (s32[264,128]{1,0:T(8,128)S(1)}, s32[264,128]{1,0:T(8,128)S(1)}, u32[]{:S(2)}, u32[]{:S(2)}) collective-permute-start(s32[264,128]{1,0:T(8,128)S(1)} %get-tuple-element.83), channel_id=1, source_target_pairs={{2,5},{3,4},{4,3},{5,2},{10,13},{11,12},{12,11},{13,10},{18,21},{1... | collective-permute-start | bytes 405512 | tf_op jit(solution)/shard_map/ppermute | solution.py:554
  52.7 2.9 %collective-permute-done.10.refs_1_ = s32[264,256]{1,0:T(8,128)S(1)} collective-permute-done((s32[264,256]{1,0:T(8,128)S(1)}, s32[264,256]{1,0:T(8,128)S(1)}, u32[]{:S(2)}, u32[]{:S(2)}) %collective-permute-start.10) | collective-permute-done | bytes 270368 | tf_op jit(solution)/shard_map/ppermute | solution.py:554
  55.6 1.9 %collective-permute-done.11.refs_2_ = s32[264,256]{1,0:T(8,128)S(1)} collective-permute-done((s32[264,256]{1,0:T(8,128)S(1)}, s32[264,256]{1,0:T(8,128)S(1)}, u32[]{:S(2)}, u32[]{:S(2)}) %collective-permute-start.11) | collective-permute-done | bytes 270368 | tf_op jit(solution)/shard_map/ppermute | solution.py:554
  57.5 0.0 collective-permute-done.9.refs_0_
  57.5 1.4 %fold.1 = (f32[2,2,256,256]{3,2,1,0:T(8,128)S(1)}, f32[2,2,256,256]{3,2,1,0:T(8,128)}) custom-call(f32[2,2,512,512]{3,2,1,0:T(8,128)S(1)} %get-tuple-element.77.ext_ref, s32[536,128]{1,0:T(8,128)S(1)} %collective-permute-done.9.refs_0_, s32[264,256]{1,0:T(8,128)S(1)} %collective-permute-done.10.refs_1_, s32[264,256]{1,0:T(8,128)S(1)} %collective-permute-done.11.refs_2_), custom_call_target="tpu_custom_call" | custom-call | flops 2000000000 | bytes 6000000 | tf_op jit(solution)/shard_map/fold/pallas_call | solution.py:543
  59.0 0.1 collective-permute-done.12.refs_0_
  59.0 1.6 %collective-permute-done.13.refs_1_ = s32[264,128]{1,0:T(8,128)S(1)} collective-permute-done((s32[264,128]{1,0:T(8,128)S(1)}, s32[264,128]{1,0:T(8,128)S(1)}, u32[]{:S(2)}, u32[]{:S(2)}) %collective-permute-start.13) | collective-permute-done | bytes 135200 | tf_op jit(solution)/shard_map/ppermute | solution.py:554
  60.6 0.9 %corners.1 = f32[2,2,256,256]{3,2,1,0:T(8,128)} custom-call(f32[2,2,256,256]{3,2,1,0:T(8,128)S(1)} %get-tuple-element.81.part_ref, s32[264,128]{1,0:T(8,128)S(1)} %collective-permute-done.12.refs_0_, s32[264,128]{1,0:T(8,128)S(1)} %collective-permute-done.13.refs_1_, f32[2,2,256,256]{3,2,1,0:T(8,128)} %get-tuple-element.84.refs_2_), custom_call_target="tpu_custom_call", output_to_operand_aliasing={{}: (3, {})} | custom-call | tf_op jit(solution)/shard_map/corners/pallas_call | solution.py:543
  (6 shorter events, 0.0 us)
Async XLA Ops:
  0.0 1.0 %copy-start.1 = (bf16[2,2,256,256]{3,2,1,0:T(8,128)(2,1)S(1)}, bf16[2,2,256,256]{3,2,1,0:T(8,128)(2,1)}, u32[]{:S(2)}) copy-start(bf16[2,2,256,256]{3,2,1,0:T(8,128)(2,1)} %tile_ref.1) | copy-start | bytes 1572868
  1.0 13.2 %copy-start.2 = (bf16[2,2,256,256]{3,2,1,0:T(8,128)(2,1)S(1)}, bf16[2,2,256,256]{3,2,1,0:T(8,128)(2,1)}, u32[]{:S(2)}) copy-start(bf16[2,2,256,256]{3,2,1,0:T(8,128)(2,1)} %tile_ref.1) | copy-start | bytes 1572868
  1.0 13.2 %copy-start.4 = (bf16[2,2,2,256,256]{4,3,2,1,0:T(8,128)(2,1)S(1)}, bf16[2,2,2,256,256]{4,3,2,1,0:T(8,128)(2,1)}, u32[]{:S(2)}) copy-start(bf16[2,2,2,256,256]{4,3,2,1,0:T(8,128)(2,1)} %inc_ref) | copy-start | bytes 3145732
  1.0 13.3 %copy-start.5 = (bf16[2,2,256,256]{3,2,1,0:T(8,128)(2,1)S(1)}, bf16[2,2,256,256]{3,2,1,0:T(8,128)(2,1)}, u32[]{:S(2)}) copy-start(bf16[2,2,256,256]{3,2,1,0:T(8,128)(2,1)} %exit_ref) | copy-start | bytes 1572868
  1.2 13.6 %collective-permute-start.3 = (bf16[2,2,128,128]{3,2,1,0:T(8,128)(2,1)S(1)}, bf16[2,2,128,128]{3,2,1,0:T(8,128)(2,1)S(1)}, u32[]{:S(2)}, u32[]{:S(2)}) collective-permute-start(bf16[2,2,128,128]{3,2,1,0:T(8,128)(2,1)S(1)} %get-tuple-element.48), channel_id=1, source_target_pairs={{0,3},{1,2},{2,1},{3,0},{4,7},{5,6},{6,5},{7,4},{8,11},{9,10},{10,... | collective-permute-start | bytes 393224 | tf_op jit(solution)/shard_map/ppermute | solution.py:554
  3.8 11.0 %collective-permute-start.4 = (bf16[2,2,128,128]{3,2,1,0:T(8,128)(2,1)S(1)}, bf16[2,2,128,128]{3,2,1,0:T(8,128)(2,1)S(1)}, u32[]{:S(2)}, u32[]{:S(2)}) collective-permute-start(bf16[2,2,128,128]{3,2,1,0:T(8,128)(2,1)S(1)} %get-tuple-element.49), channel_id=1, source_target_pairs={{2,5},{3,4},{4,3},{5,2},{10,13},{11,12},{12,11},{13,10},{18,21},{1... | collective-permute-start | bytes 393224 | tf_op jit(solution)/shard_map/ppermute | solution.py:554
  5.7 9.1 %collective-permute-start = (bf16[2,2,128,256]{3,2,1,0:T(8,128)(2,1)S(1)}, bf16[2,2,128,256]{3,2,1,0:T(8,128)(2,1)S(1)}, u32[]{:S(2)}, u32[]{:S(2)}) collective-permute-start(bf16[2,2,128,256]{3,2,1,0:T(8,128)(2,1)S(1)} %get-tuple-element.45), channel_id=1, source_target_pairs={{0,2},{1,3},{2,0},{3,1},{4,6},{5,7},{6,4},{7,5},{8,10},{9,11},{10,... | collective-permute-start | bytes 786440 | tf_op jit(solution)/shard_map/ppermute | solution.py:554
  5.8 10.4 %collective-permute-start.1 = (bf16[2,2,128,256]{3,2,1,0:T(8,128)(2,1)S(1)}, bf16[2,2,128,256]{3,2,1,0:T(8,128)(2,1)S(1)}, u32[]{:S(2)}, u32[]{:S(2)}) collective-permute-start(bf16[2,2,128,256]{3,2,1,0:T(8,128)(2,1)S(1)} %get-tuple-element.46), channel_id=1, source_target_pairs={{2,4},{3,5},{4,2},{5,3},{10,12},{11,13},{12,10},{13,11},{18,20},{1... | collective-permute-start | bytes 786440 | tf_op jit(solution)/shard_map/ppermute | solution.py:554
  9.6 7.8 %copy-start.3 = (s32[2,2]{1,0:T(2,128)S(1)}, s32[2,2]{1,0:T(2,128)}, u32[]{:S(2)}) copy-start(s32[2,2]{1,0:T(2,128)} %anchor_ref.7) | copy-start | bytes 52
  9.7 7.8 %collective-permute-start.2 = (bf16[2,2,256,128]{3,2,1,0:T(8,128)(2,1)S(1)}, bf16[2,2,256,128]{3,2,1,0:T(8,128)(2,1)S(1)}, u32[]{:S(2)}, u32[]{:S(2)}) collective-permute-start(bf16[2,2,256,128]{3,2,1,0:T(8,128)(2,1)S(1)} %get-tuple-element.47), channel_id=1, source_target_pairs={{0,1},{1,0},{2,3},{3,2},{4,5},{5,4},{6,7},{7,6},{8,9},{9,8},{10,11... | collective-permute-start | bytes 786440 | tf_op jit(solution)/shard_map/ppermute | solution.py:554
  11.2 0.9 %copy-start.6 = (f32[256,256]{1,0:T(8,128)S(1)}, f32[256,256]{1,0:T(8,128)}, u32[]{:S(2)}) copy-start(f32[256,256]{1,0:T(8,128)} %phase_ref) | copy-start | bytes 786436
  17.5 3.5 %copy-start = (bf16[8,256,256]{2,1,0:T(8,128)(2,1)S(1)}, bf16[8,256,256]{2,1,0:T(8,128)(2,1)}, u32[]{:S(2)}) copy-start(bf16[8,256,256]{2,1,0:T(8,128)(2,1)} %constant.2.clone.tab_ref) | copy-start | bytes 3145732
  17.5 3.1 %collective-permute-start.6 = (bf16[2,2,256,256]{3,2,1,0:T(8,128)(2,1)S(1)}, bf16[2,2,256,256]{3,2,1,0:T(8,128)(2,1)S(1)}, u32[]{:S(2)}, u32[]{:S(2)}) collective-permute-start(bf16[2,2,256,256]{3,2,1,0:T(8,128)(2,1)S(1)} %get-tuple-element.69), channel_id=1, source_target_pairs={{0,8},{8,0},{16,24},{24,16},{1,9},{9,1},{17,25},{25,17},{2,10},{10... | collective-permute-start | bytes 1572872 | tf_op jit(solution)/shard_map/ppermute | solution.py:584
  18.8 2.1 %collective-permute-start.5 = (bf16[2,2,256,256]{3,2,1,0:T(8,128)(2,1)S(1)}, bf16[2,2,256,256]{3,2,1,0:T(8,128)(2,1)S(1)}, u32[]{:S(2)}, u32[]{:S(2)}) collective-permute-start(bf16[2,2,256,256]{3,2,1,0:T(8,128)(2,1)S(1)} %get-tuple-element.67), channel_id=1, source_target_pairs={{0,8},{8,0},{16,24},{24,16},{1,9},{9,1},{17,25},{25,17},{2,10},{10... | collective-permute-start | bytes 1572872 | tf_op jit(solution)/shard_map/ppermute | solution.py:595
  21.0 14.1 %collective-permute-start.7 = (s32[264,256]{1,0:T(8,128)S(1)}, s32[264,256]{1,0:T(8,128)S(1)}, u32[]{:S(2)}, u32[]{:S(2)}) collective-permute-start(s32[264,256]{1,0:T(8,128)S(1)} %get-tuple-element.72), channel_id=1, source_target_pairs={{16,0},{0,16},{24,8},{8,24},{17,1},{1,17},{25,9},{9,25},{18,2},{2,... | collective-permute-start | bytes 811016 | tf_op jit(solution)/shard_map/ppermute | solution.py:627
  39.7 2.7 %collective-permute-start.8 = (f32[2,2,256,256]{3,2,1,0:T(8,128)S(1)}, f32[2,2,256,256]{3,2,1,0:T(8,128)S(1)}, u32[]{:S(2)}, u32[]{:S(2)}) collective-permute-start(f32[2,2,256,256]{3,2,1,0:T(8,128)S(1)} %get-tuple-element.75), channel_id=1, source_target_pairs={{0,8},{8,0},{16,24},{24,16},{1,9},{9,1},{17,25},{25,17},{2,10},{10... | collective-permute-start | bytes 3145736 | tf_op jit(solution)/shard_map/ppermute | solution.py:630
  44.1 13.4 %collective-permute-start.9 = (s32[536,128]{1,0:T(8,128)S(1)}, s32[536,128]{1,0:T(8,128)S(1)}, u32[]{:S(2)}, u32[]{:S(2)}) collective-permute-start(s32[536,128]{1,0:T(8,128)S(1)} %get-tuple-element.78), channel_id=1, source_target_pairs={{0,1},{1,0},{2,3},{3,2},{4,5},{5,4},{6,7},{7,6},{8,9},{9,8},{10,11... | collective-permute-start | bytes 823304 | tf_op jit(solution)/shard_map/ppermute | solution.py:554
  46.2 9.4 %collective-permute-start.10 = (s32[264,256]{1,0:T(8,128)S(1)}, s32[264,256]{1,0:T(8,128)S(1)}, u32[]{:S(2)}, u32[]{:S(2)}) collective-permute-start(s32[264,256]{1,0:T(8,128)S(1)} %get-tuple-element.79), channel_id=1, source_target_pairs={{0,2},{1,3},{2,0},{3,1},{4,6},{5,7},{6,4},{7,5},{8,10},{9,11},{10,... | collective-permute-start | bytes 811016 | tf_op jit(solution)/shard_map/ppermute | solution.py:554
  46.3 11.3 %collective-permute-start.11 = (s32[264,256]{1,0:T(8,128)S(1)}, s32[264,256]{1,0:T(8,128)S(1)}, u32[]{:S(2)}, u32[]{:S(2)}) collective-permute-start(s32[264,256]{1,0:T(8,128)S(1)} %get-tuple-element.80), channel_id=1, source_target_pairs={{2,4},{3,5},{4,2},{5,3},{10,12},{11,13},{12,10},{13,11},{18,20},{1... | collective-permute-start | bytes 811016 | tf_op jit(solution)/shard_map/ppermute | solution.py:554
  48.9 10.1 %collective-permute-start.12 = (s32[264,128]{1,0:T(8,128)S(1)}, s32[264,128]{1,0:T(8,128)S(1)}, u32[]{:S(2)}, u32[]{:S(2)}) collective-permute-start(s32[264,128]{1,0:T(8,128)S(1)} %get-tuple-element.82), channel_id=1, source_target_pairs={{0,3},{1,2},{2,1},{3,0},{4,7},{5,6},{6,5},{7,4},{8,11},{9,10},{10,... | collective-permute-start | bytes 405512 | tf_op jit(solution)/shard_map/ppermute | solution.py:554
  49.5 11.1 %collective-permute-start.13 = (s32[264,128]{1,0:T(8,128)S(1)}, s32[264,128]{1,0:T(8,128)S(1)}, u32[]{:S(2)}, u32[]{:S(2)}) collective-permute-start(s32[264,128]{1,0:T(8,128)S(1)} %get-tuple-element.83), channel_id=1, source_target_pairs={{2,5},{3,4},{4,3},{5,2},{10,13},{11,12},{12,11},{13,10},{18,21},{1... | collective-permute-start | bytes 405512 | tf_op jit(solution)/shard_map/ppermute | solution.py:554

commit v11 on v10

--- a/solution.py
+++ b/solution.py
@@ -328,7 +328,7 @@
         out_ref[layer, c] = take_window(plane, at_x, at_y, out_ref.shape[2]).astype(out_ref.dtype)
         return 0
 
-    lax.fori_loop(0, 2 * slab, one, 0)
+    lax.fori_loop(0, 2 * slab, one, 0, unroll=2)
 
 
 def window_own_kernel(tile, anchor_ref, ext_ref, out_ref):
@@ -341,7 +341,7 @@
         out_ref[layer, c] = window.astype(out_ref.dtype)
         return 0
 
-    lax.fori_loop(0, 2 * slab, one, 0)
+    lax.fori_loop(0, 2 * slab, one, 0, unroll=2)
 
 
 def slots_kernel(live_ref, inc_ref, exit_ref, tile_ref, own_ref, other_ref, seed_ref, ext_ref, sems):
@@ -427,7 +427,7 @@
 
             return 0
 
-        lax.fori_loop(0, layers, one, 0, unroll=True)
+        lax.fori_loop(0, layers, one, 0)
         if stage < chips - 1:
             put_encoded(out_ref[0], 0, wave_ref[0], wave_ref[1])
         for slot in range(2):
@@ -458,7 +458,7 @@
         add_window(plane, at_x, at_y, term_ref[layer, c])
         return 0
 
-    lax.fori_loop(0, 2 * term_ref.shape[0], add, 0)
+    lax.fori_loop(0, 2 * term_ref.shape[0], add, 0, unroll=2)
 
 
 def scatter_kernel(kinds, tile, anchor_ref, term_ref, _own, ext_ref, *pieces):
@@ -469,7 +469,7 @@
         add_window(ext_ref.at[layer, c], at_x, at_y, term_ref[layer, c])
         return 0
 
-    lax.fori_loop(0, 2 * term_ref.shape[0], add, 0)
+    lax.fori_loop(0, 2 * term_ref.shape[0], add, 0, unroll=2)
     send_halos(kinds, pieces, tile, ext_ref)
 
 

time: 61.9 us -> 61.3 us (level)
  Pallas kernels: 15.5 us -> 14.6 us
    pallas_call x12, Pallas kernels: 15.5 us -> 14.6 us  [call(): pl.pallas_call(kernel, out_shape=out_shape, scratch_shapes=list(scratch),...]
where the time goes in v11:
time: 61.3 us; the launch traced here: 61 us
  starting transfers between devices  25.4 us (41%)
  waiting for transfers between devices  18.1 us (30%)
  Pallas kernels  14.6 us (24%)
  local copies, waits for them, and re-layouts  2.01 us (3%)
  between operations  0.87 us (1%)
    ppermute x10, starting transfers between devices, swapped(): lax.ppermute(value, ('sx', 'sy'), swap_list(n_x, n_y, *kind))  17.5 us
    pallas_call x12, Pallas kernels, call(): pl.pallas_call(kernel, out_shape=out_shape, scratch_shapes=list(scratch),...  14.6 us
    ppermute x10, waiting for transfers between devices, swapped(): lax.ppermute(value, ('sx', 'sy'), swap_list(n_x, n_y, *kind))  9.11 us
    ppermute x1, starting transfers between devices, shards(): wave = lax.ppermute(results[2], 'depth', hop)  7.25 us
    ppermute x1, waiting for transfers between devices, shards(): wave = lax.ppermute(results[2], 'depth', hop)  7.01 us
    unnamed x14, local copies, waits for them, and re-layouts  2.01 us
    ppermute x1, waiting for transfers between devices, shards(): got = lax.ppermute(send, 'depth', core_swap)  1.44 us
  transfers between devices with their start and end apart: 14, of which 9 were waited for; matrix products, arithmetic and copies ran while one was open for 0% of the time, Pallas kernels for 13%

profile of v11, /device:TPU:16, one launch (start us, length us, event | category | flops | bytes accessed | tf_op | source)
XLA Modules:
  0.0 61.0 jit_solution(12685448774038948492)
XLA Ops:
  0.0 0.0 copy-start.1
  0.0 1.0 %copy-done.1 = bf16[2,2,256,256]{3,2,1,0:T(8,128)(2,1)S(1)} copy-done((bf16[2,2,256,256]{3,2,1,0:T(8,128)(2,1)S(1)}, bf16[2,2,256,256]{3,2,1,0:T(8,128)(2,1)}, u32[]{:S(2)}) %copy-start.1) | copy-done | bytes 524312
  1.0 0.1 rims.1
  1.2 2.6 %collective-permute-start.3 = (bf16[2,2,128,128]{3,2,1,0:T(8,128)(2,1)S(1)}, bf16[2,2,128,128]{3,2,1,0:T(8,128)(2,1)S(1)}, u32[]{:S(2)}, u32[]{:S(2)}) collective-permute-start(bf16[2,2,128,128]{3,2,1,0:T(8,128)(2,1)S(1)} %get-tuple-element.48), channel_id=1, source_target_pairs={{0,3},{1,2},{2,1},{3,0},{4,7},{5,6},{6,5},{7,4},{8,11},{9,10},{10,... | collective-permute-start | bytes 393224 | tf_op jit(solution)/shard_map/ppermute | solution.py:554
  3.8 1.9 %collective-permute-start.4 = (bf16[2,2,128,128]{3,2,1,0:T(8,128)(2,1)S(1)}, bf16[2,2,128,128]{3,2,1,0:T(8,128)(2,1)S(1)}, u32[]{:S(2)}, u32[]{:S(2)}) collective-permute-start(bf16[2,2,128,128]{3,2,1,0:T(8,128)(2,1)S(1)} %get-tuple-element.49), channel_id=1, source_target_pairs={{2,5},{3,4},{4,3},{5,2},{10,13},{11,12},{12,11},{13,10},{18,21},{1... | collective-permute-start | bytes 393224 | tf_op jit(solution)/shard_map/ppermute | solution.py:554
  5.7 0.1 collective-permute-start
  5.8 3.9 %collective-permute-start.1 = (bf16[2,2,128,256]{3,2,1,0:T(8,128)(2,1)S(1)}, bf16[2,2,128,256]{3,2,1,0:T(8,128)(2,1)S(1)}, u32[]{:S(2)}, u32[]{:S(2)}) collective-permute-start(bf16[2,2,128,256]{3,2,1,0:T(8,128)(2,1)S(1)} %get-tuple-element.46), channel_id=1, source_target_pairs={{2,4},{3,5},{4,2},{5,3},{10,12},{11,13},{12,10},{13,11},{18,20},{1... | collective-permute-start | bytes 786440 | tf_op jit(solution)/shard_map/ppermute | solution.py:554
  9.6 0.0 copy-start.3
  9.7 1.6 %collective-permute-start.2 = (bf16[2,2,256,128]{3,2,1,0:T(8,128)(2,1)S(1)}, bf16[2,2,256,128]{3,2,1,0:T(8,128)(2,1)S(1)}, u32[]{:S(2)}, u32[]{:S(2)}) collective-permute-start(bf16[2,2,256,128]{3,2,1,0:T(8,128)(2,1)S(1)} %get-tuple-element.47), channel_id=1, source_target_pairs={{0,1},{1,0},{2,3},{3,2},{4,5},{5,4},{6,7},{7,6},{8,9},{9,8},{10,11... | collective-permute-start | bytes 786440 | tf_op jit(solution)/shard_map/ppermute | solution.py:554
  11.2 0.9 %copy-done.6 = f32[256,256]{1,0:T(8,128)S(1)} copy-done((f32[256,256]{1,0:T(8,128)S(1)}, f32[256,256]{1,0:T(8,128)}, u32[]{:S(2)}) %copy-start.6) | copy-done | bytes 262168
  12.2 1.4 %turn.1 = (f32[256,256]{1,0:T(8,128)S(1)}, f32[256,256]{1,0:T(8,128)S(1)}) custom-call(f32[256,256]{1,0:T(8,128)S(1)} %copy-done.6), custom_call_target="tpu_custom_call" | custom-call | flops 2000000000 | bytes 6000000 | tf_op jit(solution)/shard_map/turn/pallas_call | solution.py:543
  14.3 0.0 copy-done.2
  14.3 0.0 copy-done.4
  14.3 0.0 copy-done.5
  14.3 0.5 slots.1
  14.8 0.0 collective-permute-done.3.refs_3_
  14.8 0.0 collective-permute-done.4.refs_4_
  14.8 0.0 collective-permute-done.refs_0_
  14.8 1.4 %collective-permute-done.1.refs_1_ = bf16[2,2,128,256]{3,2,1,0:T(8,128)(2,1)S(1)} collective-permute-done((bf16[2,2,128,256]{3,2,1,0:T(8,128)(2,1)S(1)}, bf16[2,2,128,256]{3,2,1,0:T(8,128)(2,1)S(1)}, u32[]{:S(2)}, u32[]{:S(2)}) %collective-permute-start.1) | collective-permute-done | bytes 262176 | tf_op jit(solution)/shard_map/ppermute | solution.py:554
  16.2 1.3 %collective-permute-done.2.refs_2_ = bf16[2,2,256,128]{3,2,1,0:T(8,128)(2,1)S(1)} collective-permute-done((bf16[2,2,256,128]{3,2,1,0:T(8,128)(2,1)S(1)}, bf16[2,2,256,128]{3,2,1,0:T(8,128)(2,1)S(1)}, u32[]{:S(2)}, u32[]{:S(2)}) %collective-permute-start.2) | collective-permute-done | bytes 262176 | tf_op jit(solution)/shard_map/ppermute | solution.py:554
  17.5 0.0 collective-permute-start.6
  17.5 0.0 copy-done.3
  17.5 1.3 %windows_for_other.1 = (bf16[2,2,256,256]{3,2,1,0:T(8,128)(2,1)S(1)}, f32[2,2,512,512]{3,2,1,0:T(8,128)S(1)}) custom-call(s32[2,2]{1,0:T(2,128)S(1)} %copy-done.3, f32[2,2,512,512]{3,2,1,0:T(8,128)S(1)} %get-tuple-element.60._filled, bf16[2,2,128,256]{3,2,1,0:T(8,128)(2,1)S(1)} %collective-permute-done.refs_0_, ...), custom_call_target="tpu_custom_call", output_to_operand_aliasing={{1}: (1, {})} | custom-call | tf_op jit(solution)/shard_map/windows_for_other/pallas_call | solution.py:543
  18.7 0.6 collective-permute-start.5
  19.3 1.0 %windows.1.win_own = bf16[2,2,256,256]{3,2,1,0:T(8,128)(2,1)S(1)} custom-call(s32[2,2]{1,0:T(2,128)S(1)} %copy-done.3, f32[2,2,512,512]{3,2,1,0:T(8,128)S(1)} %get-tuple-element.66.ext_ref), custom_call_target="tpu_custom_call" | custom-call | tf_op jit(solution)/shard_map/windows/pallas_call | solution.py:543
  20.3 0.0 collective-permute-done.6.inc_got
  20.4 0.5 collective-permute-done.5.win_got
  20.9 0.0 copy-done
  20.9 7.3 %collective-permute-start.7 = (s32[264,256]{1,0:T(8,128)S(1)}, s32[264,256]{1,0:T(8,128)S(1)}, u32[]{:S(2)}, u32[]{:S(2)}) collective-permute-start(s32[264,256]{1,0:T(8,128)S(1)} %get-tuple-element.72), channel_id=1, source_target_pairs={{16,0},{0,16},{24,8},{8,24},{17,1},{1,17},{25,9},{9,25},{18,2},{2,... | collective-permute-start | bytes 811016 | tf_op jit(solution)/shard_map/ppermute | solution.py:627
  28.1 7.0 %collective-permute-done.7.wave_in = s32[264,256]{1,0:T(8,128)S(1)} collective-permute-done((s32[264,256]{1,0:T(8,128)S(1)}, s32[264,256]{1,0:T(8,128)S(1)}, u32[]{:S(2)}, u32[]{:S(2)}) %collective-permute-start.7) | collective-permute-done | bytes 270368 | tf_op jit(solution)/shard_map/ppermute | solution.py:627
  35.1 4.3 %sweep.3 = (f32[2,2,256,256]{3,2,1,0:T(8,128)S(1)}, f32[2,2,256,256]{3,2,1,0:T(8,128)S(1)}) custom-call(s32[264,256]{1,0:T(8,128)S(1)} %collective-permute-done.7.wave_in, bf16[2,2,256,256]{3,2,1,0:T(8,128)(2,1)S(1)} %windows.1.win_own, bf16[2,2,256,256]{3,2,1,0:T(8,128)(2,1)S(1)} %collective-permute-done.5.win_got, ...), custom_call_target="tpu_custom_call", output_to_operand_aliasing={{0}: (8, {}), {1}: (9, {})} | custom-call | tf_op jit(solution)/shard_map/sweep/pallas_call | solution.py:543
  39.5 0.1 collective-permute-start.8
  39.5 1.2 %scatter_own.1._own = f32[2,2,512,512]{3,2,1,0:T(8,128)S(1)} custom-call(s32[2,2]{1,0:T(2,128)S(1)} %copy-done.3, f32[2,2,256,256]{3,2,1,0:T(8,128)S(1)} %get-tuple-element.76.term_ref), custom_call_target="tpu_custom_call" | custom-call | flops 2000000000 | bytes 6000000 | tf_op jit(solution)/shard_map/scatter_own/pallas_call | solution.py:543
  40.7 1.4 %collective-permute-done.8.term_ref = f32[2,2,256,256]{3,2,1,0:T(8,128)S(1)} collective-permute-done((f32[2,2,256,256]{3,2,1,0:T(8,128)S(1)}, f32[2,2,256,256]{3,2,1,0:T(8,128)S(1)}, u32[]{:S(2)}, u32[]{:S(2)}) %collective-permute-start.8) | collective-permute-done | bytes 1048608 | tf_op jit(solution)/shard_map/ppermute | solution.py:630
  42.2 1.4 %scatter.1 = (f32[2,2,512,512]{3,2,1,0:T(8,128)S(1)}, s32[536,128]{1,0:T(8,128)S(1)}) custom-call(s32[2,2]{1,0:T(2,128)S(1)} %copy-done.3, f32[2,2,256,256]{3,2,1,0:T(8,128)S(1)} %collective-permute-done.8.term_ref, f32[2,2,512,512]{3,2,1,0:T(8,128)S(1)} %scatter_own.1._own), custom_call_target="tpu_custom_call", output_to_operand_aliasing={{0}: (2, {})} | custom-call | flops 2000000000 | bytes 6000000 | tf_op jit(solution)/shard_map/scatter/pallas_call | solution.py:543
  43.6 1.0 %collective-permute-start.9 = (s32[536,128]{1,0:T(8,128)S(1)}, s32[536,128]{1,0:T(8,128)S(1)}, u32[]{:S(2)}, u32[]{:S(2)}) collective-permute-start(s32[536,128]{1,0:T(8,128)S(1)} %get-tuple-element.78), channel_id=1, source_target_pairs={{0,1},{1,0},{2,3},{3,2},{4,5},{5,4},{6,7},{7,6},{8,9},{9,8},{10,11... | collective-permute-start | bytes 823304 | tf_op jit(solution)/shard_map/ppermute | solution.py:554
  44.7 1.0 %halos.1 = (s32[264,256]{1,0:T(8,128)S(1)}, s32[264,256]{1,0:T(8,128)S(1)}, s32[264,128]{1,0:T(8,128)S(1)}, s32[264,128]{1,0:T(8,128)S(1)}) custom-call(f32[2,2,512,512]{3,2,1,0:T(8,128)S(1)} %get-tuple-element.77.ext_ref), custom_call_target="tpu_custom_call" | custom-call | flops 1000000000 | bytes 3000000 | tf_op jit(solution)/shard_map/halos/pallas_call | solution.py:543
  45.7 0.1 collective-permute-start.10
  45.8 2.7 %collective-permute-start.11 = (s32[264,256]{1,0:T(8,128)S(1)}, s32[264,256]{1,0:T(8,128)S(1)}, u32[]{:S(2)}, u32[]{:S(2)}) collective-permute-start(s32[264,256]{1,0:T(8,128)S(1)} %get-tuple-element.80), channel_id=1, source_target_pairs={{2,4},{3,5},{4,2},{5,3},{10,12},{11,13},{12,10},{13,11},{18,20},{1... | collective-permute-start | bytes 811016 | tf_op jit(solution)/shard_map/ppermute | solution.py:554
  48.5 0.6 collective-permute-start.12
  49.1 3.2 %collective-permute-start.13 = (s32[264,128]{1,0:T(8,128)S(1)}, s32[264,128]{1,0:T(8,128)S(1)}, u32[]{:S(2)}, u32[]{:S(2)}) collective-permute-start(s32[264,128]{1,0:T(8,128)S(1)} %get-tuple-element.83), channel_id=1, source_target_pairs={{2,5},{3,4},{4,3},{5,2},{10,13},{11,12},{12,11},{13,10},{18,21},{1... | collective-permute-start | bytes 405512 | tf_op jit(solution)/shard_map/ppermute | solution.py:554
  52.2 2.9 %collective-permute-done.10.refs_1_ = s32[264,256]{1,0:T(8,128)S(1)} collective-permute-done((s32[264,256]{1,0:T(8,128)S(1)}, s32[264,256]{1,0:T(8,128)S(1)}, u32[]{:S(2)}, u32[]{:S(2)}) %collective-permute-start.10) | collective-permute-done | bytes 270368 | tf_op jit(solution)/shard_map/ppermute | solution.py:554
  55.2 1.9 %collective-permute-done.11.refs_2_ = s32[264,256]{1,0:T(8,128)S(1)} collective-permute-done((s32[264,256]{1,0:T(8,128)S(1)}, s32[264,256]{1,0:T(8,128)S(1)}, u32[]{:S(2)}, u32[]{:S(2)}) %collective-permute-start.11) | collective-permute-done | bytes 270368 | tf_op jit(solution)/shard_map/ppermute | solution.py:554
  57.1 0.0 collective-permute-done.9.refs_0_
  57.1 1.4 %fold.1 = (f32[2,2,256,256]{3,2,1,0:T(8,128)S(1)}, f32[2,2,256,256]{3,2,1,0:T(8,128)}) custom-call(f32[2,2,512,512]{3,2,1,0:T(8,128)S(1)} %get-tuple-element.77.ext_ref, s32[536,128]{1,0:T(8,128)S(1)} %collective-permute-done.9.refs_0_, s32[264,256]{1,0:T(8,128)S(1)} %collective-permute-done.10.refs_1_, s32[264,256]{1,0:T(8,128)S(1)} %collective-permute-done.11.refs_2_), custom_call_target="tpu_custom_call" | custom-call | flops 2000000000 | bytes 6000000 | tf_op jit(solution)/shard_map/fold/pallas_call | solution.py:543
  58.5 0.1 collective-permute-done.12.refs_0_
  58.6 1.6 %collective-permute-done.13.refs_1_ = s32[264,128]{1,0:T(8,128)S(1)} collective-permute-done((s32[264,128]{1,0:T(8,128)S(1)}, s32[264,128]{1,0:T(8,128)S(1)}, u32[]{:S(2)}, u32[]{:S(2)}) %collective-permute-start.13) | collective-permute-done | bytes 135200 | tf_op jit(solution)/shard_map/ppermute | solution.py:554
  60.1 0.9 %corners.1 = f32[2,2,256,256]{3,2,1,0:T(8,128)} custom-call(f32[2,2,256,256]{3,2,1,0:T(8,128)S(1)} %get-tuple-element.81.part_ref, s32[264,128]{1,0:T(8,128)S(1)} %collective-permute-done.12.refs_0_, s32[264,128]{1,0:T(8,128)S(1)} %collective-permute-done.13.refs_1_, f32[2,2,256,256]{3,2,1,0:T(8,128)} %get-tuple-element.84.refs_2_), custom_call_target="tpu_custom_call", output_to_operand_aliasing={{}: (3, {})} | custom-call | tf_op jit(solution)/shard_map/corners/pallas_call | solution.py:543
  (6 shorter events, 0.0 us)
Async XLA Ops:
  0.0 1.0 %copy-start.1 = (bf16[2,2,256,256]{3,2,1,0:T(8,128)(2,1)S(1)}, bf16[2,2,256,256]{3,2,1,0:T(8,128)(2,1)}, u32[]{:S(2)}) copy-start(bf16[2,2,256,256]{3,2,1,0:T(8,128)(2,1)} %tile_ref.1) | copy-start | bytes 1572868
  1.0 13.2 %copy-start.2 = (bf16[2,2,256,256]{3,2,1,0:T(8,128)(2,1)S(1)}, bf16[2,2,256,256]{3,2,1,0:T(8,128)(2,1)}, u32[]{:S(2)}) copy-start(bf16[2,2,256,256]{3,2,1,0:T(8,128)(2,1)} %tile_ref.1) | copy-start | bytes 1572868
  1.0 13.2 %copy-start.4 = (bf16[2,2,2,256,256]{4,3,2,1,0:T(8,128)(2,1)S(1)}, bf16[2,2,2,256,256]{4,3,2,1,0:T(8,128)(2,1)}, u32[]{:S(2)}) copy-start(bf16[2,2,2,256,256]{4,3,2,1,0:T(8,128)(2,1)} %inc_ref) | copy-start | bytes 3145732
  1.0 13.3 %copy-start.5 = (bf16[2,2,256,256]{3,2,1,0:T(8,128)(2,1)S(1)}, bf16[2,2,256,256]{3,2,1,0:T(8,128)(2,1)}, u32[]{:S(2)}) copy-start(bf16[2,2,256,256]{3,2,1,0:T(8,128)(2,1)} %exit_ref) | copy-start | bytes 1572868
  1.2 13.6 %collective-permute-start.3 = (bf16[2,2,128,128]{3,2,1,0:T(8,128)(2,1)S(1)}, bf16[2,2,128,128]{3,2,1,0:T(8,128)(2,1)S(1)}, u32[]{:S(2)}, u32[]{:S(2)}) collective-permute-start(bf16[2,2,128,128]{3,2,1,0:T(8,128)(2,1)S(1)} %get-tuple-element.48), channel_id=1, source_target_pairs={{0,3},{1,2},{2,1},{3,0},{4,7},{5,6},{6,5},{7,4},{8,11},{9,10},{10,... | collective-permute-start | bytes 393224 | tf_op jit(solution)/shard_map/ppermute | solution.py:554
  3.8 11.0 %collective-permute-start.4 = (bf16[2,2,128,128]{3,2,1,0:T(8,128)(2,1)S(1)}, bf16[2,2,128,128]{3,2,1,0:T(8,128)(2,1)S(1)}, u32[]{:S(2)}, u32[]{:S(2)}) collective-permute-start(bf16[2,2,128,128]{3,2,1,0:T(8,128)(2,1)S(1)} %get-tuple-element.49), channel_id=1, source_target_pairs={{2,5},{3,4},{4,3},{5,2},{10,13},{11,12},{12,11},{13,10},{18,21},{1... | collective-permute-start | bytes 393224 | tf_op jit(solution)/shard_map/ppermute | solution.py:554
  5.7 9.1 %collective-permute-start = (bf16[2,2,128,256]{3,2,1,0:T(8,128)(2,1)S(1)}, bf16[2,2,128,256]{3,2,1,0:T(8,128)(2,1)S(1)}, u32[]{:S(2)}, u32[]{:S(2)}) collective-permute-start(bf16[2,2,128,256]{3,2,1,0:T(8,128)(2,1)S(1)} %get-tuple-element.45), channel_id=1, source_target_pairs={{0,2},{1,3},{2,0},{3,1},{4,6},{5,7},{6,4},{7,5},{8,10},{9,11},{10,... | collective-permute-start | bytes 786440 | tf_op jit(solution)/shard_map/ppermute | solution.py:554
  5.8 10.4 %collective-permute-start.1 = (bf16[2,2,128,256]{3,2,1,0:T(8,128)(2,1)S(1)}, bf16[2,2,128,256]{3,2,1,0:T(8,128)(2,1)S(1)}, u32[]{:S(2)}, u32[]{:S(2)}) collective-permute-start(bf16[2,2,128,256]{3,2,1,0:T(8,128)(2,1)S(1)} %get-tuple-element.46), channel_id=1, source_target_pairs={{2,4},{3,5},{4,2},{5,3},{10,12},{11,13},{12,10},{13,11},{18,20},{1... | collective-permute-start | bytes 786440 | tf_op jit(solution)/shard_map/ppermute | solution.py:554
  9.6 7.8 %copy-start.3 = (s32[2,2]{1,0:T(2,128)S(1)}, s32[2,2]{1,0:T(2,128)}, u32[]{:S(2)}) copy-start(s32[2,2]{1,0:T(2,128)} %anchor_ref.7) | copy-start | bytes 52
  9.7 7.8 %collective-permute-start.2 = (bf16[2,2,256,128]{3,2,1,0:T(8,128)(2,1)S(1)}, bf16[2,2,256,128]{3,2,1,0:T(8,128)(2,1)S(1)}, u32[]{:S(2)}, u32[]{:S(2)}) collective-permute-start(bf16[2,2,256,128]{3,2,1,0:T(8,128)(2,1)S(1)} %get-tuple-element.47), channel_id=1, source_target_pairs={{0,1},{1,0},{2,3},{3,2},{4,5},{5,4},{6,7},{7,6},{8,9},{9,8},{10,11... | collective-permute-start | bytes 786440 | tf_op jit(solution)/shard_map/ppermute | solution.py:554
  11.2 0.9 %copy-start.6 = (f32[256,256]{1,0:T(8,128)S(1)}, f32[256,256]{1,0:T(8,128)}, u32[]{:S(2)}) copy-start(f32[256,256]{1,0:T(8,128)} %phase_ref) | copy-start | bytes 786436
  17.5 3.4 %copy-start = (bf16[8,256,256]{2,1,0:T(8,128)(2,1)S(1)}, bf16[8,256,256]{2,1,0:T(8,128)(2,1)}, u32[]{:S(2)}) copy-start(bf16[8,256,256]{2,1,0:T(8,128)(2,1)} %constant.2.clone.tab_ref) | copy-start | bytes 3145732
  17.5 2.9 %collective-permute-start.6 = (bf16[2,2,256,256]{3,2,1,0:T(8,128)(2,1)S(1)}, bf16[2,2,256,256]{3,2,1,0:T(8,128)(2,1)S(1)}, u32[]{:S(2)}, u32[]{:S(2)}) collective-permute-start(bf16[2,2,256,256]{3,2,1,0:T(8,128)(2,1)S(1)} %get-tuple-element.69), channel_id=1, source_target_pairs={{0,8},{8,0},{16,24},{24,16},{1,9},{9,1},{17,25},{25,17},{2,10},{10... | collective-permute-start | bytes 1572872 | tf_op jit(solution)/shard_map/ppermute | solution.py:584
  18.7 2.1 %collective-permute-start.5 = (bf16[2,2,256,256]{3,2,1,0:T(8,128)(2,1)S(1)}, bf16[2,2,256,256]{3,2,1,0:T(8,128)(2,1)S(1)}, u32[]{:S(2)}, u32[]{:S(2)}) collective-permute-start(bf16[2,2,256,256]{3,2,1,0:T(8,128)(2,1)S(1)} %get-tuple-element.67), channel_id=1, source_target_pairs={{0,8},{8,0},{16,24},{24,16},{1,9},{9,1},{17,25},{25,17},{2,10},{10... | collective-permute-start | bytes 1572872 | tf_op jit(solution)/shard_map/ppermute | solution.py:595
  20.9 14.3 %collective-permute-start.7 = (s32[264,256]{1,0:T(8,128)S(1)}, s32[264,256]{1,0:T(8,128)S(1)}, u32[]{:S(2)}, u32[]{:S(2)}) collective-permute-start(s32[264,256]{1,0:T(8,128)S(1)} %get-tuple-element.72), channel_id=1, source_target_pairs={{16,0},{0,16},{24,8},{8,24},{17,1},{1,17},{25,9},{9,25},{18,2},{2,... | collective-permute-start | bytes 811016 | tf_op jit(solution)/shard_map/ppermute | solution.py:627
  39.5 2.7 %collective-permute-start.8 = (f32[2,2,256,256]{3,2,1,0:T(8,128)S(1)}, f32[2,2,256,256]{3,2,1,0:T(8,128)S(1)}, u32[]{:S(2)}, u32[]{:S(2)}) collective-permute-start(f32[2,2,256,256]{3,2,1,0:T(8,128)S(1)} %get-tuple-element.75), channel_id=1, source_target_pairs={{0,8},{8,0},{16,24},{24,16},{1,9},{9,1},{17,25},{25,17},{2,10},{10... | collective-permute-start | bytes 3145736 | tf_op jit(solution)/shard_map/ppermute | solution.py:630
  43.6 13.4 %collective-permute-start.9 = (s32[536,128]{1,0:T(8,128)S(1)}, s32[536,128]{1,0:T(8,128)S(1)}, u32[]{:S(2)}, u32[]{:S(2)}) collective-permute-start(s32[536,128]{1,0:T(8,128)S(1)} %get-tuple-element.78), channel_id=1, source_target_pairs={{0,1},{1,0},{2,3},{3,2},{4,5},{5,4},{6,7},{7,6},{8,9},{9,8},{10,11... | collective-permute-start | bytes 823304 | tf_op jit(solution)/shard_map/ppermute | solution.py:554
  45.7 9.4 %collective-permute-start.10 = (s32[264,256]{1,0:T(8,128)S(1)}, s32[264,256]{1,0:T(8,128)S(1)}, u32[]{:S(2)}, u32[]{:S(2)}) collective-permute-start(s32[264,256]{1,0:T(8,128)S(1)} %get-tuple-element.79), channel_id=1, source_target_pairs={{0,2},{1,3},{2,0},{3,1},{4,6},{5,7},{6,4},{7,5},{8,10},{9,11},{10,... | collective-permute-start | bytes 811016 | tf_op jit(solution)/shard_map/ppermute | solution.py:554
  45.8 11.3 %collective-permute-start.11 = (s32[264,256]{1,0:T(8,128)S(1)}, s32[264,256]{1,0:T(8,128)S(1)}, u32[]{:S(2)}, u32[]{:S(2)}) collective-permute-start(s32[264,256]{1,0:T(8,128)S(1)} %get-tuple-element.80), channel_id=1, source_target_pairs={{2,4},{3,5},{4,2},{5,3},{10,12},{11,13},{12,10},{13,11},{18,20},{1... | collective-permute-start | bytes 811016 | tf_op jit(solution)/shard_map/ppermute | solution.py:554
  48.5 10.1 %collective-permute-start.12 = (s32[264,128]{1,0:T(8,128)S(1)}, s32[264,128]{1,0:T(8,128)S(1)}, u32[]{:S(2)}, u32[]{:S(2)}) collective-permute-start(s32[264,128]{1,0:T(8,128)S(1)} %get-tuple-element.82), channel_id=1, source_target_pairs={{0,3},{1,2},{2,1},{3,0},{4,7},{5,6},{6,5},{7,4},{8,11},{9,10},{10,... | collective-permute-start | bytes 405512 | tf_op jit(solution)/shard_map/ppermute | solution.py:554
  49.1 11.1 %collective-permute-start.13 = (s32[264,128]{1,0:T(8,128)S(1)}, s32[264,128]{1,0:T(8,128)S(1)}, u32[]{:S(2)}, u32[]{:S(2)}) collective-permute-start(s32[264,128]{1,0:T(8,128)S(1)} %get-tuple-element.83), channel_id=1, source_target_pairs={{2,5},{3,4},{4,3},{5,2},{10,13},{11,12},{12,11},{13,10},{18,21},{1... | collective-permute-start | bytes 405512 | tf_op jit(solution)/shard_map/ppermute | solution.py:554

commit v12 on v11

--- a/solution.py
+++ b/solution.py
@@ -106,6 +106,8 @@
 
 def spectrum_split(p, q, first):
     (pr, pi), (qr, qi) = p, q
+    if first is None:
+        return (pr + qi, pi - qr), (pr - qi, pi + qr)
     plus = (jnp.where(first, pr, pr + qi), jnp.where(first, pi, pi - qr))
     minus = (jnp.where(first, qr, pr - qi), jnp.where(first, qi, pi + qr))
     return plus, minus
@@ -113,6 +115,8 @@
 
 def spectrum_join(plus, minus, first):
     (xr, xi), (yr, yi) = plus, minus
+    if first is None:
+        return (xr + yr, xi + yi), (yi - xi, xr - yr)
     p = (jnp.where(first, xr, xr + yr), jnp.where(first, xi, xi + yi))
     q = (jnp.where(first, yr, yi - xi), jnp.where(first, yi, xr - yr))
     return p, q
@@ -151,7 +155,7 @@
 def middle(parts, cos_ref, sin_ref, odd):
     half = parts[0].shape[1] // 2
     size = half // 2
-    row0 = odd * size + lax.broadcasted_iota(jnp.int32, (size, half), 0) == 0
+    row0 = None if odd else lax.broadcasted_iota(jnp.int32, (size, half), 0) == 0
     col0 = lax.broadcasted_iota(jnp.int32, (size, half), 1) == 0
 
     def quadrant(r, c):
@@ -445,7 +449,7 @@
             put_encoded(piece, layer, ext_ref[(layer, 0) + where], ext_ref[(layer, 1) + where])
         return 0
 
-    lax.fori_loop(0, ext_ref.shape[0], one, 0)
+    lax.fori_loop(0, ext_ref.shape[0], one, 0, unroll=True)
 
 
 def scatter_own_kernel(tile, anchor_ref, term_ref, ext_ref):

time: 61.3 us -> 61.2 us (level)
  no operation moved by 1% of the time
where the time goes in v12:
time: 61.2 us; the launch traced here: 61 us
  starting transfers between devices  25.4 us (42%)
  waiting for transfers between devices  18.1 us (30%)
  Pallas kernels  14.6 us (24%)
  local copies, waits for them, and re-layouts  2.01 us (3%)
  between operations  0.86 us (1%)
    ppermute x10, starting transfers between devices, swapped(): lax.ppermute(value, ('sx', 'sy'), swap_list(n_x, n_y, *kind))  17.5 us
    pallas_call x12, Pallas kernels, call(): pl.pallas_call(kernel, out_shape=out_shape, scratch_shapes=list(scratch),...  14.6 us
    ppermute x10, waiting for transfers between devices, swapped(): lax.ppermute(value, ('sx', 'sy'), swap_list(n_x, n_y, *kind))  9.11 us
    ppermute x1, starting transfers between devices, shards(): wave = lax.ppermute(results[2], 'depth', hop)  7.25 us
    ppermute x1, waiting for transfers between devices, shards(): wave = lax.ppermute(results[2], 'depth', hop)  7.01 us
    unnamed x14, local copies, waits for them, and re-layouts  2.01 us
    ppermute x1, waiting for transfers between devices, shards(): got = lax.ppermute(send, 'depth', core_swap)  1.44 us
  transfers between devices with their start and end apart: 14, of which 9 were waited for; matrix products, arithmetic and copies ran while one was open for 0% of the time, Pallas kernels for 13%

profile of v12, /device:TPU:16, one launch (start us, length us, event | category | flops | bytes accessed | tf_op | source)
XLA Modules:
  0.0 61.0 jit_solution(15946289057119771447)
XLA Ops:
  0.0 0.0 copy-start.1
  0.0 1.0 %copy-done.1 = bf16[2,2,256,256]{3,2,1,0:T(8,128)(2,1)S(1)} copy-done((bf16[2,2,256,256]{3,2,1,0:T(8,128)(2,1)S(1)}, bf16[2,2,256,256]{3,2,1,0:T(8,128)(2,1)}, u32[]{:S(2)}) %copy-start.1) | copy-done | bytes 524312
  1.0 0.1 rims.1
  1.2 2.6 %collective-permute-start.3 = (bf16[2,2,128,128]{3,2,1,0:T(8,128)(2,1)S(1)}, bf16[2,2,128,128]{3,2,1,0:T(8,128)(2,1)S(1)}, u32[]{:S(2)}, u32[]{:S(2)}) collective-permute-start(bf16[2,2,128,128]{3,2,1,0:T(8,128)(2,1)S(1)} %get-tuple-element.48), channel_id=1, source_target_pairs={{0,3},{1,2},{2,1},{3,0},{4,7},{5,6},{6,5},{7,4},{8,11},{9,10},{10,... | collective-permute-start | bytes 393224 | tf_op jit(solution)/shard_map/ppermute | solution.py:558
  3.8 1.9 %collective-permute-start.4 = (bf16[2,2,128,128]{3,2,1,0:T(8,128)(2,1)S(1)}, bf16[2,2,128,128]{3,2,1,0:T(8,128)(2,1)S(1)}, u32[]{:S(2)}, u32[]{:S(2)}) collective-permute-start(bf16[2,2,128,128]{3,2,1,0:T(8,128)(2,1)S(1)} %get-tuple-element.49), channel_id=1, source_target_pairs={{2,5},{3,4},{4,3},{5,2},{10,13},{11,12},{12,11},{13,10},{18,21},{1... | collective-permute-start | bytes 393224 | tf_op jit(solution)/shard_map/ppermute | solution.py:558
  5.7 0.1 collective-permute-start
  5.8 3.9 %collective-permute-start.1 = (bf16[2,2,128,256]{3,2,1,0:T(8,128)(2,1)S(1)}, bf16[2,2,128,256]{3,2,1,0:T(8,128)(2,1)S(1)}, u32[]{:S(2)}, u32[]{:S(2)}) collective-permute-start(bf16[2,2,128,256]{3,2,1,0:T(8,128)(2,1)S(1)} %get-tuple-element.46), channel_id=1, source_target_pairs={{2,4},{3,5},{4,2},{5,3},{10,12},{11,13},{12,10},{13,11},{18,20},{1... | collective-permute-start | bytes 786440 | tf_op jit(solution)/shard_map/ppermute | solution.py:558
  9.6 0.0 copy-start.3
  9.7 1.6 %collective-permute-start.2 = (bf16[2,2,256,128]{3,2,1,0:T(8,128)(2,1)S(1)}, bf16[2,2,256,128]{3,2,1,0:T(8,128)(2,1)S(1)}, u32[]{:S(2)}, u32[]{:S(2)}) collective-permute-start(bf16[2,2,256,128]{3,2,1,0:T(8,128)(2,1)S(1)} %get-tuple-element.47), channel_id=1, source_target_pairs={{0,1},{1,0},{2,3},{3,2},{4,5},{5,4},{6,7},{7,6},{8,9},{9,8},{10,11... | collective-permute-start | bytes 786440 | tf_op jit(solution)/shard_map/ppermute | solution.py:558
  11.2 0.9 %copy-done.6 = f32[256,256]{1,0:T(8,128)S(1)} copy-done((f32[256,256]{1,0:T(8,128)S(1)}, f32[256,256]{1,0:T(8,128)}, u32[]{:S(2)}) %copy-start.6) | copy-done | bytes 262168
  12.2 1.4 %turn.1 = (f32[256,256]{1,0:T(8,128)S(1)}, f32[256,256]{1,0:T(8,128)S(1)}) custom-call(f32[256,256]{1,0:T(8,128)S(1)} %copy-done.6), custom_call_target="tpu_custom_call" | custom-call | flops 2000000000 | bytes 6000000 | tf_op jit(solution)/shard_map/turn/pallas_call | solution.py:547
  14.3 0.0 copy-done.2
  14.3 0.0 copy-done.4
  14.3 0.0 copy-done.5
  14.3 0.5 slots.1
  14.8 0.0 collective-permute-done.3.refs_3_
  14.8 0.0 collective-permute-done.4.refs_4_
  14.8 0.0 collective-permute-done.refs_0_
  14.8 1.4 %collective-permute-done.1.refs_1_ = bf16[2,2,128,256]{3,2,1,0:T(8,128)(2,1)S(1)} collective-permute-done((bf16[2,2,128,256]{3,2,1,0:T(8,128)(2,1)S(1)}, bf16[2,2,128,256]{3,2,1,0:T(8,128)(2,1)S(1)}, u32[]{:S(2)}, u32[]{:S(2)}) %collective-permute-start.1) | collective-permute-done | bytes 262176 | tf_op jit(solution)/shard_map/ppermute | solution.py:558
  16.2 1.3 %collective-permute-done.2.refs_2_ = bf16[2,2,256,128]{3,2,1,0:T(8,128)(2,1)S(1)} collective-permute-done((bf16[2,2,256,128]{3,2,1,0:T(8,128)(2,1)S(1)}, bf16[2,2,256,128]{3,2,1,0:T(8,128)(2,1)S(1)}, u32[]{:S(2)}, u32[]{:S(2)}) %collective-permute-start.2) | collective-permute-done | bytes 262176 | tf_op jit(solution)/shard_map/ppermute | solution.py:558
  17.5 0.0 collective-permute-start.6
  17.5 0.0 copy-done.3
  17.5 1.3 %windows_for_other.1 = (bf16[2,2,256,256]{3,2,1,0:T(8,128)(2,1)S(1)}, f32[2,2,512,512]{3,2,1,0:T(8,128)S(1)}) custom-call(s32[2,2]{1,0:T(2,128)S(1)} %copy-done.3, f32[2,2,512,512]{3,2,1,0:T(8,128)S(1)} %get-tuple-element.60._filled, bf16[2,2,128,256]{3,2,1,0:T(8,128)(2,1)S(1)} %collective-permute-done.refs_0_, ...), custom_call_target="tpu_custom_call", output_to_operand_aliasing={{1}: (1, {})} | custom-call | tf_op jit(solution)/shard_map/windows_for_other/pallas_call | solution.py:547
  18.7 0.6 collective-permute-start.5
  19.3 1.0 %windows.1.win_own = bf16[2,2,256,256]{3,2,1,0:T(8,128)(2,1)S(1)} custom-call(s32[2,2]{1,0:T(2,128)S(1)} %copy-done.3, f32[2,2,512,512]{3,2,1,0:T(8,128)S(1)} %get-tuple-element.66.ext_ref), custom_call_target="tpu_custom_call" | custom-call | tf_op jit(solution)/shard_map/windows/pallas_call | solution.py:547
  20.3 0.0 collective-permute-done.6.inc_got
  20.4 0.5 collective-permute-done.5.win_got
  20.9 0.0 copy-done
  20.9 7.3 %collective-permute-start.7 = (s32[264,256]{1,0:T(8,128)S(1)}, s32[264,256]{1,0:T(8,128)S(1)}, u32[]{:S(2)}, u32[]{:S(2)}) collective-permute-start(s32[264,256]{1,0:T(8,128)S(1)} %get-tuple-element.72), channel_id=1, source_target_pairs={{16,0},{0,16},{24,8},{8,24},{17,1},{1,17},{25,9},{9,25},{18,2},{2,... | collective-permute-start | bytes 811016 | tf_op jit(solution)/shard_map/ppermute | solution.py:631
  28.1 7.0 %collective-permute-done.7.wave_in = s32[264,256]{1,0:T(8,128)S(1)} collective-permute-done((s32[264,256]{1,0:T(8,128)S(1)}, s32[264,256]{1,0:T(8,128)S(1)}, u32[]{:S(2)}, u32[]{:S(2)}) %collective-permute-start.7) | collective-permute-done | bytes 270368 | tf_op jit(solution)/shard_map/ppermute | solution.py:631
  35.1 4.3 %sweep.3 = (f32[2,2,256,256]{3,2,1,0:T(8,128)S(1)}, f32[2,2,256,256]{3,2,1,0:T(8,128)S(1)}) custom-call(s32[264,256]{1,0:T(8,128)S(1)} %collective-permute-done.7.wave_in, bf16[2,2,256,256]{3,2,1,0:T(8,128)(2,1)S(1)} %windows.1.win_own, bf16[2,2,256,256]{3,2,1,0:T(8,128)(2,1)S(1)} %collective-permute-done.5.win_got, ...), custom_call_target="tpu_custom_call", output_to_operand_aliasing={{0}: (8, {}), {1}: (9, {})} | custom-call | tf_op jit(solution)/shard_map/sweep/pallas_call | solution.py:547
  39.5 0.1 collective-permute-start.8
  39.5 1.2 %scatter_own.1._own = f32[2,2,512,512]{3,2,1,0:T(8,128)S(1)} custom-call(s32[2,2]{1,0:T(2,128)S(1)} %copy-done.3, f32[2,2,256,256]{3,2,1,0:T(8,128)S(1)} %get-tuple-element.76.term_ref), custom_call_target="tpu_custom_call" | custom-call | flops 2000000000 | bytes 6000000 | tf_op jit(solution)/shard_map/scatter_own/pallas_call | solution.py:547
  40.7 1.4 %collective-permute-done.8.term_ref = f32[2,2,256,256]{3,2,1,0:T(8,128)S(1)} collective-permute-done((f32[2,2,256,256]{3,2,1,0:T(8,128)S(1)}, f32[2,2,256,256]{3,2,1,0:T(8,128)S(1)}, u32[]{:S(2)}, u32[]{:S(2)}) %collective-permute-start.8) | collective-permute-done | bytes 1048608 | tf_op jit(solution)/shard_map/ppermute | solution.py:634
  42.2 1.4 %scatter.1 = (f32[2,2,512,512]{3,2,1,0:T(8,128)S(1)}, s32[536,128]{1,0:T(8,128)S(1)}) custom-call(s32[2,2]{1,0:T(2,128)S(1)} %copy-done.3, f32[2,2,256,256]{3,2,1,0:T(8,128)S(1)} %collective-permute-done.8.term_ref, f32[2,2,512,512]{3,2,1,0:T(8,128)S(1)} %scatter_own.1._own), custom_call_target="tpu_custom_call", output_to_operand_aliasing={{0}: (2, {})} | custom-call | flops 2000000000 | bytes 6000000 | tf_op jit(solution)/shard_map/scatter/pallas_call | solution.py:547
  43.6 1.0 %collective-permute-start.9 = (s32[536,128]{1,0:T(8,128)S(1)}, s32[536,128]{1,0:T(8,128)S(1)}, u32[]{:S(2)}, u32[]{:S(2)}) collective-permute-start(s32[536,128]{1,0:T(8,128)S(1)} %get-tuple-element.78), channel_id=1, source_target_pairs={{0,1},{1,0},{2,3},{3,2},{4,5},{5,4},{6,7},{7,6},{8,9},{9,8},{10,11... | collective-permute-start | bytes 823304 | tf_op jit(solution)/shard_map/ppermute | solution.py:558
  44.7 1.0 %halos.1 = (s32[264,256]{1,0:T(8,128)S(1)}, s32[264,256]{1,0:T(8,128)S(1)}, s32[264,128]{1,0:T(8,128)S(1)}, s32[264,128]{1,0:T(8,128)S(1)}) custom-call(f32[2,2,512,512]{3,2,1,0:T(8,128)S(1)} %get-tuple-element.77.ext_ref), custom_call_target="tpu_custom_call" | custom-call | flops 1000000000 | bytes 3000000 | tf_op jit(solution)/shard_map/halos/pallas_call | solution.py:547
  45.7 0.1 collective-permute-start.10
  45.8 2.6 %collective-permute-start.11 = (s32[264,256]{1,0:T(8,128)S(1)}, s32[264,256]{1,0:T(8,128)S(1)}, u32[]{:S(2)}, u32[]{:S(2)}) collective-permute-start(s32[264,256]{1,0:T(8,128)S(1)} %get-tuple-element.80), channel_id=1, source_target_pairs={{2,4},{3,5},{4,2},{5,3},{10,12},{11,13},{12,10},{13,11},{18,20},{1... | collective-permute-start | bytes 811016 | tf_op jit(solution)/shard_map/ppermute | solution.py:558
  48.4 0.6 collective-permute-start.12
  49.0 3.2 %collective-permute-start.13 = (s32[264,128]{1,0:T(8,128)S(1)}, s32[264,128]{1,0:T(8,128)S(1)}, u32[]{:S(2)}, u32[]{:S(2)}) collective-permute-start(s32[264,128]{1,0:T(8,128)S(1)} %get-tuple-element.83), channel_id=1, source_target_pairs={{2,5},{3,4},{4,3},{5,2},{10,13},{11,12},{12,11},{13,10},{18,21},{1... | collective-permute-start | bytes 405512 | tf_op jit(solution)/shard_map/ppermute | solution.py:558
  52.2 2.9 %collective-permute-done.10.refs_1_ = s32[264,256]{1,0:T(8,128)S(1)} collective-permute-done((s32[264,256]{1,0:T(8,128)S(1)}, s32[264,256]{1,0:T(8,128)S(1)}, u32[]{:S(2)}, u32[]{:S(2)}) %collective-permute-start.10) | collective-permute-done | bytes 270368 | tf_op jit(solution)/shard_map/ppermute | solution.py:558
  55.1 1.9 %collective-permute-done.11.refs_2_ = s32[264,256]{1,0:T(8,128)S(1)} collective-permute-done((s32[264,256]{1,0:T(8,128)S(1)}, s32[264,256]{1,0:T(8,128)S(1)}, u32[]{:S(2)}, u32[]{:S(2)}) %collective-permute-start.11) | collective-permute-done | bytes 270368 | tf_op jit(solution)/shard_map/ppermute | solution.py:558
  57.0 0.0 collective-permute-done.9.refs_0_
  57.0 1.4 %fold.1 = (f32[2,2,256,256]{3,2,1,0:T(8,128)S(1)}, f32[2,2,256,256]{3,2,1,0:T(8,128)}) custom-call(f32[2,2,512,512]{3,2,1,0:T(8,128)S(1)} %get-tuple-element.77.ext_ref, s32[536,128]{1,0:T(8,128)S(1)} %collective-permute-done.9.refs_0_, s32[264,256]{1,0:T(8,128)S(1)} %collective-permute-done.10.refs_1_, s32[264,256]{1,0:T(8,128)S(1)} %collective-permute-done.11.refs_2_), custom_call_target="tpu_custom_call" | custom-call | flops 2000000000 | bytes 6000000 | tf_op jit(solution)/shard_map/fold/pallas_call | solution.py:547
  58.5 0.1 collective-permute-done.12.refs_0_
  58.5 1.6 %collective-permute-done.13.refs_1_ = s32[264,128]{1,0:T(8,128)S(1)} collective-permute-done((s32[264,128]{1,0:T(8,128)S(1)}, s32[264,128]{1,0:T(8,128)S(1)}, u32[]{:S(2)}, u32[]{:S(2)}) %collective-permute-start.13) | collective-permute-done | bytes 135200 | tf_op jit(solution)/shard_map/ppermute | solution.py:558
  60.1 0.9 %corners.1 = f32[2,2,256,256]{3,2,1,0:T(8,128)} custom-call(f32[2,2,256,256]{3,2,1,0:T(8,128)S(1)} %get-tuple-element.81.part_ref, s32[264,128]{1,0:T(8,128)S(1)} %collective-permute-done.12.refs_0_, s32[264,128]{1,0:T(8,128)S(1)} %collective-permute-done.13.refs_1_, f32[2,2,256,256]{3,2,1,0:T(8,128)} %get-tuple-element.84.refs_2_), custom_call_target="tpu_custom_call", output_to_operand_aliasing={{}: (3, {})} | custom-call | tf_op jit(solution)/shard_map/corners/pallas_call | solution.py:547
  (6 shorter events, 0.0 us)
Async XLA Ops:
  0.0 1.0 %copy-start.1 = (bf16[2,2,256,256]{3,2,1,0:T(8,128)(2,1)S(1)}, bf16[2,2,256,256]{3,2,1,0:T(8,128)(2,1)}, u32[]{:S(2)}) copy-start(bf16[2,2,256,256]{3,2,1,0:T(8,128)(2,1)} %tile_ref.1) | copy-start | bytes 1572868
  1.0 13.2 %copy-start.2 = (bf16[2,2,256,256]{3,2,1,0:T(8,128)(2,1)S(1)}, bf16[2,2,256,256]{3,2,1,0:T(8,128)(2,1)}, u32[]{:S(2)}) copy-start(bf16[2,2,256,256]{3,2,1,0:T(8,128)(2,1)} %tile_ref.1) | copy-start | bytes 1572868
  1.0 13.2 %copy-start.4 = (bf16[2,2,2,256,256]{4,3,2,1,0:T(8,128)(2,1)S(1)}, bf16[2,2,2,256,256]{4,3,2,1,0:T(8,128)(2,1)}, u32[]{:S(2)}) copy-start(bf16[2,2,2,256,256]{4,3,2,1,0:T(8,128)(2,1)} %inc_ref) | copy-start | bytes 3145732
  1.0 13.3 %copy-start.5 = (bf16[2,2,256,256]{3,2,1,0:T(8,128)(2,1)S(1)}, bf16[2,2,256,256]{3,2,1,0:T(8,128)(2,1)}, u32[]{:S(2)}) copy-start(bf16[2,2,256,256]{3,2,1,0:T(8,128)(2,1)} %exit_ref) | copy-start | bytes 1572868
  1.2 13.6 %collective-permute-start.3 = (bf16[2,2,128,128]{3,2,1,0:T(8,128)(2,1)S(1)}, bf16[2,2,128,128]{3,2,1,0:T(8,128)(2,1)S(1)}, u32[]{:S(2)}, u32[]{:S(2)}) collective-permute-start(bf16[2,2,128,128]{3,2,1,0:T(8,128)(2,1)S(1)} %get-tuple-element.48), channel_id=1, source_target_pairs={{0,3},{1,2},{2,1},{3,0},{4,7},{5,6},{6,5},{7,4},{8,11},{9,10},{10,... | collective-permute-start | bytes 393224 | tf_op jit(solution)/shard_map/ppermute | solution.py:558
  3.8 11.0 %collective-permute-start.4 = (bf16[2,2,128,128]{3,2,1,0:T(8,128)(2,1)S(1)}, bf16[2,2,128,128]{3,2,1,0:T(8,128)(2,1)S(1)}, u32[]{:S(2)}, u32[]{:S(2)}) collective-permute-start(bf16[2,2,128,128]{3,2,1,0:T(8,128)(2,1)S(1)} %get-tuple-element.49), channel_id=1, source_target_pairs={{2,5},{3,4},{4,3},{5,2},{10,13},{11,12},{12,11},{13,10},{18,21},{1... | collective-permute-start | bytes 393224 | tf_op jit(solution)/shard_map/ppermute | solution.py:558
  5.7 9.1 %collective-permute-start = (bf16[2,2,128,256]{3,2,1,0:T(8,128)(2,1)S(1)}, bf16[2,2,128,256]{3,2,1,0:T(8,128)(2,1)S(1)}, u32[]{:S(2)}, u32[]{:S(2)}) collective-permute-start(bf16[2,2,128,256]{3,2,1,0:T(8,128)(2,1)S(1)} %get-tuple-element.45), channel_id=1, source_target_pairs={{0,2},{1,3},{2,0},{3,1},{4,6},{5,7},{6,4},{7,5},{8,10},{9,11},{10,... | collective-permute-start | bytes 786440 | tf_op jit(solution)/shard_map/ppermute | solution.py:558
  5.8 10.4 %collective-permute-start.1 = (bf16[2,2,128,256]{3,2,1,0:T(8,128)(2,1)S(1)}, bf16[2,2,128,256]{3,2,1,0:T(8,128)(2,1)S(1)}, u32[]{:S(2)}, u32[]{:S(2)}) collective-permute-start(bf16[2,2,128,256]{3,2,1,0:T(8,128)(2,1)S(1)} %get-tuple-element.46), channel_id=1, source_target_pairs={{2,4},{3,5},{4,2},{5,3},{10,12},{11,13},{12,10},{13,11},{18,20},{1... | collective-permute-start | bytes 786440 | tf_op jit(solution)/shard_map/ppermute | solution.py:558
  9.6 7.8 %copy-start.3 = (s32[2,2]{1,0:T(2,128)S(1)}, s32[2,2]{1,0:T(2,128)}, u32[]{:S(2)}) copy-start(s32[2,2]{1,0:T(2,128)} %anchor_ref.7) | copy-start | bytes 52
  9.7 7.8 %collective-permute-start.2 = (bf16[2,2,256,128]{3,2,1,0:T(8,128)(2,1)S(1)}, bf16[2,2,256,128]{3,2,1,0:T(8,128)(2,1)S(1)}, u32[]{:S(2)}, u32[]{:S(2)}) collective-permute-start(bf16[2,2,256,128]{3,2,1,0:T(8,128)(2,1)S(1)} %get-tuple-element.47), channel_id=1, source_target_pairs={{0,1},{1,0},{2,3},{3,2},{4,5},{5,4},{6,7},{7,6},{8,9},{9,8},{10,11... | collective-permute-start | bytes 786440 | tf_op jit(solution)/shard_map/ppermute | solution.py:558
  11.2 0.9 %copy-start.6 = (f32[256,256]{1,0:T(8,128)S(1)}, f32[256,256]{1,0:T(8,128)}, u32[]{:S(2)}) copy-start(f32[256,256]{1,0:T(8,128)} %phase_ref) | copy-start | bytes 786436
  17.5 3.4 %copy-start = (bf16[8,256,256]{2,1,0:T(8,128)(2,1)S(1)}, bf16[8,256,256]{2,1,0:T(8,128)(2,1)}, u32[]{:S(2)}) copy-start(bf16[8,256,256]{2,1,0:T(8,128)(2,1)} %constant.2.clone.tab_ref) | copy-start | bytes 3145732
  17.5 2.9 %collective-permute-start.6 = (bf16[2,2,256,256]{3,2,1,0:T(8,128)(2,1)S(1)}, bf16[2,2,256,256]{3,2,1,0:T(8,128)(2,1)S(1)}, u32[]{:S(2)}, u32[]{:S(2)}) collective-permute-start(bf16[2,2,256,256]{3,2,1,0:T(8,128)(2,1)S(1)} %get-tuple-element.69), channel_id=1, source_target_pairs={{0,8},{8,0},{16,24},{24,16},{1,9},{9,1},{17,25},{25,17},{2,10},{10... | collective-permute-start | bytes 1572872 | tf_op jit(solution)/shard_map/ppermute | solution.py:588
  18.7 2.1 %collective-permute-start.5 = (bf16[2,2,256,256]{3,2,1,0:T(8,128)(2,1)S(1)}, bf16[2,2,256,256]{3,2,1,0:T(8,128)(2,1)S(1)}, u32[]{:S(2)}, u32[]{:S(2)}) collective-permute-start(bf16[2,2,256,256]{3,2,1,0:T(8,128)(2,1)S(1)} %get-tuple-element.67), channel_id=1, source_target_pairs={{0,8},{8,0},{16,24},{24,16},{1,9},{9,1},{17,25},{25,17},{2,10},{10... | collective-permute-start | bytes 1572872 | tf_op jit(solution)/shard_map/ppermute | solution.py:599
  20.9 14.3 %collective-permute-start.7 = (s32[264,256]{1,0:T(8,128)S(1)}, s32[264,256]{1,0:T(8,128)S(1)}, u32[]{:S(2)}, u32[]{:S(2)}) collective-permute-start(s32[264,256]{1,0:T(8,128)S(1)} %get-tuple-element.72), channel_id=1, source_target_pairs={{16,0},{0,16},{24,8},{8,24},{17,1},{1,17},{25,9},{9,25},{18,2},{2,... | collective-permute-start | bytes 811016 | tf_op jit(solution)/shard_map/ppermute | solution.py:631
  39.5 2.7 %collective-permute-start.8 = (f32[2,2,256,256]{3,2,1,0:T(8,128)S(1)}, f32[2,2,256,256]{3,2,1,0:T(8,128)S(1)}, u32[]{:S(2)}, u32[]{:S(2)}) collective-permute-start(f32[2,2,256,256]{3,2,1,0:T(8,128)S(1)} %get-tuple-element.75), channel_id=1, source_target_pairs={{0,8},{8,0},{16,24},{24,16},{1,9},{9,1},{17,25},{25,17},{2,10},{10... | collective-permute-start | bytes 3145736 | tf_op jit(solution)/shard_map/ppermute | solution.py:634
  43.6 13.4 %collective-permute-start.9 = (s32[536,128]{1,0:T(8,128)S(1)}, s32[536,128]{1,0:T(8,128)S(1)}, u32[]{:S(2)}, u32[]{:S(2)}) collective-permute-start(s32[536,128]{1,0:T(8,128)S(1)} %get-tuple-element.78), channel_id=1, source_target_pairs={{0,1},{1,0},{2,3},{3,2},{4,5},{5,4},{6,7},{7,6},{8,9},{9,8},{10,11... | collective-permute-start | bytes 823304 | tf_op jit(solution)/shard_map/ppermute | solution.py:558
  45.7 9.4 %collective-permute-start.10 = (s32[264,256]{1,0:T(8,128)S(1)}, s32[264,256]{1,0:T(8,128)S(1)}, u32[]{:S(2)}, u32[]{:S(2)}) collective-permute-start(s32[264,256]{1,0:T(8,128)S(1)} %get-tuple-element.79), channel_id=1, source_target_pairs={{0,2},{1,3},{2,0},{3,1},{4,6},{5,7},{6,4},{7,5},{8,10},{9,11},{10,... | collective-permute-start | bytes 811016 | tf_op jit(solution)/shard_map/ppermute | solution.py:558
  45.8 11.3 %collective-permute-start.11 = (s32[264,256]{1,0:T(8,128)S(1)}, s32[264,256]{1,0:T(8,128)S(1)}, u32[]{:S(2)}, u32[]{:S(2)}) collective-permute-start(s32[264,256]{1,0:T(8,128)S(1)} %get-tuple-element.80), channel_id=1, source_target_pairs={{2,4},{3,5},{4,2},{5,3},{10,12},{11,13},{12,10},{13,11},{18,20},{1... | collective-permute-start | bytes 811016 | tf_op jit(solution)/shard_map/ppermute | solution.py:558
  48.4 10.1 %collective-permute-start.12 = (s32[264,128]{1,0:T(8,128)S(1)}, s32[264,128]{1,0:T(8,128)S(1)}, u32[]{:S(2)}, u32[]{:S(2)}) collective-permute-start(s32[264,128]{1,0:T(8,128)S(1)} %get-tuple-element.82), channel_id=1, source_target_pairs={{0,3},{1,2},{2,1},{3,0},{4,7},{5,6},{6,5},{7,4},{8,11},{9,10},{10,... | collective-permute-start | bytes 405512 | tf_op jit(solution)/shard_map/ppermute | solution.py:558
  49.0 11.1 %collective-permute-start.13 = (s32[264,128]{1,0:T(8,128)S(1)}, s32[264,128]{1,0:T(8,128)S(1)}, u32[]{:S(2)}, u32[]{:S(2)}) collective-permute-start(s32[264,128]{1,0:T(8,128)S(1)} %get-tuple-element.83), channel_id=1, source_target_pairs={{2,5},{3,4},{4,3},{5,2},{10,13},{11,12},{12,11},{13,10},{18,21},{1... | collective-permute-start | bytes 405512 | tf_op jit(solution)/shard_map/ppermute | solution.py:558

commit v13 on v12

--- a/solution.py
+++ b/solution.py
@@ -431,7 +431,7 @@
 
             return 0
 
-        lax.fori_loop(0, layers, one, 0)
+        lax.fori_loop(0, layers, one, 0, unroll=2)
         if stage < chips - 1:
             put_encoded(out_ref[0], 0, wave_ref[0], wave_ref[1])
         for slot in range(2):

time: 61.2 us -> 61.2 us (level)
  no operation moved by 1% of the time
where the time goes in v13:
time: 61.2 us; the launch traced here: 61 us
  starting transfers between devices  25.4 us (42%)
  waiting for transfers between devices  18.1 us (30%)
  Pallas kernels  14.6 us (24%)
  local copies, waits for them, and re-layouts  2.01 us (3%)
  between operations  0.86 us (1%)
    ppermute x10, starting transfers between devices, swapped(): lax.ppermute(value, ('sx', 'sy'), swap_list(n_x, n_y, *kind))  17.5 us
    pallas_call x12, Pallas kernels, call(): pl.pallas_call(kernel, out_shape=out_shape, scratch_shapes=list(scratch),...  14.6 us
    ppermute x10, waiting for transfers between devices, swapped(): lax.ppermute(value, ('sx', 'sy'), swap_list(n_x, n_y, *kind))  9.13 us
    ppermute x1, starting transfers between devices, shards(): wave = lax.ppermute(results[2], 'depth', hop)  7.24 us
    ppermute x1, waiting for transfers between devices, shards(): wave = lax.ppermute(results[2], 'depth', hop)  7 us
    unnamed x14, local copies, waits for them, and re-layouts  2.01 us
    ppermute x1, waiting for transfers between devices, shards(): got = lax.ppermute(send, 'depth', core_swap)  1.44 us
  transfers between devices with their start and end apart: 14, of which 9 were waited for; matrix products, arithmetic and copies ran while one was open for 0% of the time, Pallas kernels for 13%

profile of v13, /device:TPU:16, one launch (start us, length us, event | category | flops | bytes accessed | tf_op | source)
XLA Modules:
  0.0 61.0 jit_solution(10035353664348113134)
XLA Ops:
  0.0 0.0 copy-start.1
  0.0 1.0 %copy-done.1 = bf16[2,2,256,256]{3,2,1,0:T(8,128)(2,1)S(1)} copy-done((bf16[2,2,256,256]{3,2,1,0:T(8,128)(2,1)S(1)}, bf16[2,2,256,256]{3,2,1,0:T(8,128)(2,1)}, u32[]{:S(2)}) %copy-start.1) | copy-done | bytes 524312
  1.0 0.1 rims.1
  1.2 2.6 %collective-permute-start.3 = (bf16[2,2,128,128]{3,2,1,0:T(8,128)(2,1)S(1)}, bf16[2,2,128,128]{3,2,1,0:T(8,128)(2,1)S(1)}, u32[]{:S(2)}, u32[]{:S(2)}) collective-permute-start(bf16[2,2,128,128]{3,2,1,0:T(8,128)(2,1)S(1)} %get-tuple-element.48), channel_id=1, source_target_pairs={{0,3},{1,2},{2,1},{3,0},{4,7},{5,6},{6,5},{7,4},{8,11},{9,10},{10,... | collective-permute-start | bytes 393224 | tf_op jit(solution)/shard_map/ppermute | solution.py:558
  3.8 1.9 %collective-permute-start.4 = (bf16[2,2,128,128]{3,2,1,0:T(8,128)(2,1)S(1)}, bf16[2,2,128,128]{3,2,1,0:T(8,128)(2,1)S(1)}, u32[]{:S(2)}, u32[]{:S(2)}) collective-permute-start(bf16[2,2,128,128]{3,2,1,0:T(8,128)(2,1)S(1)} %get-tuple-element.49), channel_id=1, source_target_pairs={{2,5},{3,4},{4,3},{5,2},{10,13},{11,12},{12,11},{13,10},{18,21},{1... | collective-permute-start | bytes 393224 | tf_op jit(solution)/shard_map/ppermute | solution.py:558
  5.7 0.1 collective-permute-start
  5.8 3.9 %collective-permute-start.1 = (bf16[2,2,128,256]{3,2,1,0:T(8,128)(2,1)S(1)}, bf16[2,2,128,256]{3,2,1,0:T(8,128)(2,1)S(1)}, u32[]{:S(2)}, u32[]{:S(2)}) collective-permute-start(bf16[2,2,128,256]{3,2,1,0:T(8,128)(2,1)S(1)} %get-tuple-element.46), channel_id=1, source_target_pairs={{2,4},{3,5},{4,2},{5,3},{10,12},{11,13},{12,10},{13,11},{18,20},{1... | collective-permute-start | bytes 786440 | tf_op jit(solution)/shard_map/ppermute | solution.py:558
  9.6 0.0 copy-start.3
  9.7 1.6 %collective-permute-start.2 = (bf16[2,2,256,128]{3,2,1,0:T(8,128)(2,1)S(1)}, bf16[2,2,256,128]{3,2,1,0:T(8,128)(2,1)S(1)}, u32[]{:S(2)}, u32[]{:S(2)}) collective-permute-start(bf16[2,2,256,128]{3,2,1,0:T(8,128)(2,1)S(1)} %get-tuple-element.47), channel_id=1, source_target_pairs={{0,1},{1,0},{2,3},{3,2},{4,5},{5,4},{6,7},{7,6},{8,9},{9,8},{10,11... | collective-permute-start | bytes 786440 | tf_op jit(solution)/shard_map/ppermute | solution.py:558
  11.2 0.9 %copy-done.6 = f32[256,256]{1,0:T(8,128)S(1)} copy-done((f32[256,256]{1,0:T(8,128)S(1)}, f32[256,256]{1,0:T(8,128)}, u32[]{:S(2)}) %copy-start.6) | copy-done | bytes 262168
  12.2 1.4 %turn.1 = (f32[256,256]{1,0:T(8,128)S(1)}, f32[256,256]{1,0:T(8,128)S(1)}) custom-call(f32[256,256]{1,0:T(8,128)S(1)} %copy-done.6), custom_call_target="tpu_custom_call" | custom-call | flops 2000000000 | bytes 6000000 | tf_op jit(solution)/shard_map/turn/pallas_call | solution.py:547
  14.3 0.0 copy-done.2
  14.3 0.0 copy-done.4
  14.3 0.0 copy-done.5
  14.3 0.5 slots.1
  14.8 0.0 collective-permute-done.3.refs_3_
  14.8 0.0 collective-permute-done.4.refs_4_
  14.8 0.0 collective-permute-done.refs_0_
  14.8 1.4 %collective-permute-done.1.refs_1_ = bf16[2,2,128,256]{3,2,1,0:T(8,128)(2,1)S(1)} collective-permute-done((bf16[2,2,128,256]{3,2,1,0:T(8,128)(2,1)S(1)}, bf16[2,2,128,256]{3,2,1,0:T(8,128)(2,1)S(1)}, u32[]{:S(2)}, u32[]{:S(2)}) %collective-permute-start.1) | collective-permute-done | bytes 262176 | tf_op jit(solution)/shard_map/ppermute | solution.py:558
  16.2 1.3 %collective-permute-done.2.refs_2_ = bf16[2,2,256,128]{3,2,1,0:T(8,128)(2,1)S(1)} collective-permute-done((bf16[2,2,256,128]{3,2,1,0:T(8,128)(2,1)S(1)}, bf16[2,2,256,128]{3,2,1,0:T(8,128)(2,1)S(1)}, u32[]{:S(2)}, u32[]{:S(2)}) %collective-permute-start.2) | collective-permute-done | bytes 262176 | tf_op jit(solution)/shard_map/ppermute | solution.py:558
  17.5 0.0 collective-permute-start.6
  17.5 0.0 copy-done.3
  17.5 1.3 %windows_for_other.1 = (bf16[2,2,256,256]{3,2,1,0:T(8,128)(2,1)S(1)}, f32[2,2,512,512]{3,2,1,0:T(8,128)S(1)}) custom-call(s32[2,2]{1,0:T(2,128)S(1)} %copy-done.3, f32[2,2,512,512]{3,2,1,0:T(8,128)S(1)} %get-tuple-element.60._filled, bf16[2,2,128,256]{3,2,1,0:T(8,128)(2,1)S(1)} %collective-permute-done.refs_0_, ...), custom_call_target="tpu_custom_call", output_to_operand_aliasing={{1}: (1, {})} | custom-call | tf_op jit(solution)/shard_map/windows_for_other/pallas_call | solution.py:547
  18.7 0.6 collective-permute-start.5
  19.3 1.0 %windows.1.win_own = bf16[2,2,256,256]{3,2,1,0:T(8,128)(2,1)S(1)} custom-call(s32[2,2]{1,0:T(2,128)S(1)} %copy-done.3, f32[2,2,512,512]{3,2,1,0:T(8,128)S(1)} %get-tuple-element.66.ext_ref), custom_call_target="tpu_custom_call" | custom-call | tf_op jit(solution)/shard_map/windows/pallas_call | solution.py:547
  20.3 0.0 collective-permute-done.6.inc_got
  20.4 0.5 collective-permute-done.5.win_got
  20.9 0.0 copy-done
  20.9 7.2 %collective-permute-start.7 = (s32[264,256]{1,0:T(8,128)S(1)}, s32[264,256]{1,0:T(8,128)S(1)}, u32[]{:S(2)}, u32[]{:S(2)}) collective-permute-start(s32[264,256]{1,0:T(8,128)S(1)} %get-tuple-element.72), channel_id=1, source_target_pairs={{16,0},{0,16},{24,8},{8,24},{17,1},{1,17},{25,9},{9,25},{18,2},{2,... | collective-permute-start | bytes 811016 | tf_op jit(solution)/shard_map/ppermute | solution.py:631
  28.1 7.0 %collective-permute-done.7.wave_in = s32[264,256]{1,0:T(8,128)S(1)} collective-permute-done((s32[264,256]{1,0:T(8,128)S(1)}, s32[264,256]{1,0:T(8,128)S(1)}, u32[]{:S(2)}, u32[]{:S(2)}) %collective-permute-start.7) | collective-permute-done | bytes 270368 | tf_op jit(solution)/shard_map/ppermute | solution.py:631
  35.1 4.3 %sweep.3 = (f32[2,2,256,256]{3,2,1,0:T(8,128)S(1)}, f32[2,2,256,256]{3,2,1,0:T(8,128)S(1)}) custom-call(s32[264,256]{1,0:T(8,128)S(1)} %collective-permute-done.7.wave_in, bf16[2,2,256,256]{3,2,1,0:T(8,128)(2,1)S(1)} %windows.1.win_own, bf16[2,2,256,256]{3,2,1,0:T(8,128)(2,1)S(1)} %collective-permute-done.5.win_got, ...), custom_call_target="tpu_custom_call", output_to_operand_aliasing={{0}: (8, {}), {1}: (9, {})} | custom-call | tf_op jit(solution)/shard_map/sweep/pallas_call | solution.py:547
  39.4 0.1 collective-permute-start.8
  39.5 1.2 %scatter_own.1._own = f32[2,2,512,512]{3,2,1,0:T(8,128)S(1)} custom-call(s32[2,2]{1,0:T(2,128)S(1)} %copy-done.3, f32[2,2,256,256]{3,2,1,0:T(8,128)S(1)} %get-tuple-element.76.term_ref), custom_call_target="tpu_custom_call" | custom-call | flops 2000000000 | bytes 6000000 | tf_op jit(solution)/shard_map/scatter_own/pallas_call | solution.py:547
  40.7 1.4 %collective-permute-done.8.term_ref = f32[2,2,256,256]{3,2,1,0:T(8,128)S(1)} collective-permute-done((f32[2,2,256,256]{3,2,1,0:T(8,128)S(1)}, f32[2,2,256,256]{3,2,1,0:T(8,128)S(1)}, u32[]{:S(2)}, u32[]{:S(2)}) %collective-permute-start.8) | collective-permute-done | bytes 1048608 | tf_op jit(solution)/shard_map/ppermute | solution.py:634
  42.2 1.4 %scatter.1 = (f32[2,2,512,512]{3,2,1,0:T(8,128)S(1)}, s32[536,128]{1,0:T(8,128)S(1)}) custom-call(s32[2,2]{1,0:T(2,128)S(1)} %copy-done.3, f32[2,2,256,256]{3,2,1,0:T(8,128)S(1)} %collective-permute-done.8.term_ref, f32[2,2,512,512]{3,2,1,0:T(8,128)S(1)} %scatter_own.1._own), custom_call_target="tpu_custom_call", output_to_operand_aliasing={{0}: (2, {})} | custom-call | flops 2000000000 | bytes 6000000 | tf_op jit(solution)/shard_map/scatter/pallas_call | solution.py:547
  43.6 1.0 %collective-permute-start.9 = (s32[536,128]{1,0:T(8,128)S(1)}, s32[536,128]{1,0:T(8,128)S(1)}, u32[]{:S(2)}, u32[]{:S(2)}) collective-permute-start(s32[536,128]{1,0:T(8,128)S(1)} %get-tuple-element.78), channel_id=1, source_target_pairs={{0,1},{1,0},{2,3},{3,2},{4,5},{5,4},{6,7},{7,6},{8,9},{9,8},{10,11... | collective-permute-start | bytes 823304 | tf_op jit(solution)/shard_map/ppermute | solution.py:558
  44.6 1.0 %halos.1 = (s32[264,256]{1,0:T(8,128)S(1)}, s32[264,256]{1,0:T(8,128)S(1)}, s32[264,128]{1,0:T(8,128)S(1)}, s32[264,128]{1,0:T(8,128)S(1)}) custom-call(f32[2,2,512,512]{3,2,1,0:T(8,128)S(1)} %get-tuple-element.77.ext_ref), custom_call_target="tpu_custom_call" | custom-call | flops 1000000000 | bytes 3000000 | tf_op jit(solution)/shard_map/halos/pallas_call | solution.py:547
  45.7 0.1 collective-permute-start.10
  45.7 2.7 %collective-permute-start.11 = (s32[264,256]{1,0:T(8,128)S(1)}, s32[264,256]{1,0:T(8,128)S(1)}, u32[]{:S(2)}, u32[]{:S(2)}) collective-permute-start(s32[264,256]{1,0:T(8,128)S(1)} %get-tuple-element.80), channel_id=1, source_target_pairs={{2,4},{3,5},{4,2},{5,3},{10,12},{11,13},{12,10},{13,11},{18,20},{1... | collective-permute-start | bytes 811016 | tf_op jit(solution)/shard_map/ppermute | solution.py:558
  48.4 0.5 collective-permute-start.12
  49.0 3.2 %collective-permute-start.13 = (s32[264,128]{1,0:T(8,128)S(1)}, s32[264,128]{1,0:T(8,128)S(1)}, u32[]{:S(2)}, u32[]{:S(2)}) collective-permute-start(s32[264,128]{1,0:T(8,128)S(1)} %get-tuple-element.83), channel_id=1, source_target_pairs={{2,5},{3,4},{4,3},{5,2},{10,13},{11,12},{12,11},{13,10},{18,21},{1... | collective-permute-start | bytes 405512 | tf_op jit(solution)/shard_map/ppermute | solution.py:558
  52.2 2.9 %collective-permute-done.10.refs_1_ = s32[264,256]{1,0:T(8,128)S(1)} collective-permute-done((s32[264,256]{1,0:T(8,128)S(1)}, s32[264,256]{1,0:T(8,128)S(1)}, u32[]{:S(2)}, u32[]{:S(2)}) %collective-permute-start.10) | collective-permute-done | bytes 270368 | tf_op jit(solution)/shard_map/ppermute | solution.py:558
  55.1 1.9 %collective-permute-done.11.refs_2_ = s32[264,256]{1,0:T(8,128)S(1)} collective-permute-done((s32[264,256]{1,0:T(8,128)S(1)}, s32[264,256]{1,0:T(8,128)S(1)}, u32[]{:S(2)}, u32[]{:S(2)}) %collective-permute-start.11) | collective-permute-done | bytes 270368 | tf_op jit(solution)/shard_map/ppermute | solution.py:558
  57.0 0.0 collective-permute-done.9.refs_0_
  57.0 1.4 %fold.1 = (f32[2,2,256,256]{3,2,1,0:T(8,128)S(1)}, f32[2,2,256,256]{3,2,1,0:T(8,128)}) custom-call(f32[2,2,512,512]{3,2,1,0:T(8,128)S(1)} %get-tuple-element.77.ext_ref, s32[536,128]{1,0:T(8,128)S(1)} %collective-permute-done.9.refs_0_, s32[264,256]{1,0:T(8,128)S(1)} %collective-permute-done.10.refs_1_, s32[264,256]{1,0:T(8,128)S(1)} %collective-permute-done.11.refs_2_), custom_call_target="tpu_custom_call" | custom-call | flops 2000000000 | bytes 6000000 | tf_op jit(solution)/shard_map/fold/pallas_call | solution.py:547
  58.5 0.1 collective-permute-done.12.refs_0_
  58.5 1.6 %collective-permute-done.13.refs_1_ = s32[264,128]{1,0:T(8,128)S(1)} collective-permute-done((s32[264,128]{1,0:T(8,128)S(1)}, s32[264,128]{1,0:T(8,128)S(1)}, u32[]{:S(2)}, u32[]{:S(2)}) %collective-permute-start.13) | collective-permute-done | bytes 135200 | tf_op jit(solution)/shard_map/ppermute | solution.py:558
  60.1 0.9 %corners.1 = f32[2,2,256,256]{3,2,1,0:T(8,128)} custom-call(f32[2,2,256,256]{3,2,1,0:T(8,128)S(1)} %get-tuple-element.81.part_ref, s32[264,128]{1,0:T(8,128)S(1)} %collective-permute-done.12.refs_0_, s32[264,128]{1,0:T(8,128)S(1)} %collective-permute-done.13.refs_1_, f32[2,2,256,256]{3,2,1,0:T(8,128)} %get-tuple-element.84.refs_2_), custom_call_target="tpu_custom_call", output_to_operand_aliasing={{}: (3, {})} | custom-call | tf_op jit(solution)/shard_map/corners/pallas_call | solution.py:547
  (6 shorter events, 0.0 us)
Async XLA Ops:
  0.0 1.0 %copy-start.1 = (bf16[2,2,256,256]{3,2,1,0:T(8,128)(2,1)S(1)}, bf16[2,2,256,256]{3,2,1,0:T(8,128)(2,1)}, u32[]{:S(2)}) copy-start(bf16[2,2,256,256]{3,2,1,0:T(8,128)(2,1)} %tile_ref.1) | copy-start | bytes 1572868
  1.0 13.2 %copy-start.2 = (bf16[2,2,256,256]{3,2,1,0:T(8,128)(2,1)S(1)}, bf16[2,2,256,256]{3,2,1,0:T(8,128)(2,1)}, u32[]{:S(2)}) copy-start(bf16[2,2,256,256]{3,2,1,0:T(8,128)(2,1)} %tile_ref.1) | copy-start | bytes 1572868
  1.0 13.2 %copy-start.4 = (bf16[2,2,2,256,256]{4,3,2,1,0:T(8,128)(2,1)S(1)}, bf16[2,2,2,256,256]{4,3,2,1,0:T(8,128)(2,1)}, u32[]{:S(2)}) copy-start(bf16[2,2,2,256,256]{4,3,2,1,0:T(8,128)(2,1)} %inc_ref) | copy-start | bytes 3145732
  1.0 13.3 %copy-start.5 = (bf16[2,2,256,256]{3,2,1,0:T(8,128)(2,1)S(1)}, bf16[2,2,256,256]{3,2,1,0:T(8,128)(2,1)}, u32[]{:S(2)}) copy-start(bf16[2,2,256,256]{3,2,1,0:T(8,128)(2,1)} %exit_ref) | copy-start | bytes 1572868
  1.2 13.6 %collective-permute-start.3 = (bf16[2,2,128,128]{3,2,1,0:T(8,128)(2,1)S(1)}, bf16[2,2,128,128]{3,2,1,0:T(8,128)(2,1)S(1)}, u32[]{:S(2)}, u32[]{:S(2)}) collective-permute-start(bf16[2,2,128,128]{3,2,1,0:T(8,128)(2,1)S(1)} %get-tuple-element.48), channel_id=1, source_target_pairs={{0,3},{1,2},{2,1},{3,0},{4,7},{5,6},{6,5},{7,4},{8,11},{9,10},{10,... | collective-permute-start | bytes 393224 | tf_op jit(solution)/shard_map/ppermute | solution.py:558
  3.8 11.0 %collective-permute-start.4 = (bf16[2,2,128,128]{3,2,1,0:T(8,128)(2,1)S(1)}, bf16[2,2,128,128]{3,2,1,0:T(8,128)(2,1)S(1)}, u32[]{:S(2)}, u32[]{:S(2)}) collective-permute-start(bf16[2,2,128,128]{3,2,1,0:T(8,128)(2,1)S(1)} %get-tuple-element.49), channel_id=1, source_target_pairs={{2,5},{3,4},{4,3},{5,2},{10,13},{11,12},{12,11},{13,10},{18,21},{1... | collective-permute-start | bytes 393224 | tf_op jit(solution)/shard_map/ppermute | solution.py:558
  5.7 9.1 %collective-permute-start = (bf16[2,2,128,256]{3,2,1,0:T(8,128)(2,1)S(1)}, bf16[2,2,128,256]{3,2,1,0:T(8,128)(2,1)S(1)}, u32[]{:S(2)}, u32[]{:S(2)}) collective-permute-start(bf16[2,2,128,256]{3,2,1,0:T(8,128)(2,1)S(1)} %get-tuple-element.45), channel_id=1, source_target_pairs={{0,2},{1,3},{2,0},{3,1},{4,6},{5,7},{6,4},{7,5},{8,10},{9,11},{10,... | collective-permute-start | bytes 786440 | tf_op jit(solution)/shard_map/ppermute | solution.py:558
  5.8 10.4 %collective-permute-start.1 = (bf16[2,2,128,256]{3,2,1,0:T(8,128)(2,1)S(1)}, bf16[2,2,128,256]{3,2,1,0:T(8,128)(2,1)S(1)}, u32[]{:S(2)}, u32[]{:S(2)}) collective-permute-start(bf16[2,2,128,256]{3,2,1,0:T(8,128)(2,1)S(1)} %get-tuple-element.46), channel_id=1, source_target_pairs={{2,4},{3,5},{4,2},{5,3},{10,12},{11,13},{12,10},{13,11},{18,20},{1... | collective-permute-start | bytes 786440 | tf_op jit(solution)/shard_map/ppermute | solution.py:558
  9.6 7.8 %copy-start.3 = (s32[2,2]{1,0:T(2,128)S(1)}, s32[2,2]{1,0:T(2,128)}, u32[]{:S(2)}) copy-start(s32[2,2]{1,0:T(2,128)} %anchor_ref.7) | copy-start | bytes 52
  9.7 7.8 %collective-permute-start.2 = (bf16[2,2,256,128]{3,2,1,0:T(8,128)(2,1)S(1)}, bf16[2,2,256,128]{3,2,1,0:T(8,128)(2,1)S(1)}, u32[]{:S(2)}, u32[]{:S(2)}) collective-permute-start(bf16[2,2,256,128]{3,2,1,0:T(8,128)(2,1)S(1)} %get-tuple-element.47), channel_id=1, source_target_pairs={{0,1},{1,0},{2,3},{3,2},{4,5},{5,4},{6,7},{7,6},{8,9},{9,8},{10,11... | collective-permute-start | bytes 786440 | tf_op jit(solution)/shard_map/ppermute | solution.py:558
  11.2 0.9 %copy-start.6 = (f32[256,256]{1,0:T(8,128)S(1)}, f32[256,256]{1,0:T(8,128)}, u32[]{:S(2)}) copy-start(f32[256,256]{1,0:T(8,128)} %phase_ref) | copy-start | bytes 786436
  17.5 3.4 %copy-start = (bf16[8,256,256]{2,1,0:T(8,128)(2,1)S(1)}, bf16[8,256,256]{2,1,0:T(8,128)(2,1)}, u32[]{:S(2)}) copy-start(bf16[8,256,256]{2,1,0:T(8,128)(2,1)} %constant.2.clone.tab_ref) | copy-start | bytes 3145732
  17.5 2.9 %collective-permute-start.6 = (bf16[2,2,256,256]{3,2,1,0:T(8,128)(2,1)S(1)}, bf16[2,2,256,256]{3,2,1,0:T(8,128)(2,1)S(1)}, u32[]{:S(2)}, u32[]{:S(2)}) collective-permute-start(bf16[2,2,256,256]{3,2,1,0:T(8,128)(2,1)S(1)} %get-tuple-element.69), channel_id=1, source_target_pairs={{0,8},{8,0},{16,24},{24,16},{1,9},{9,1},{17,25},{25,17},{2,10},{10... | collective-permute-start | bytes 1572872 | tf_op jit(solution)/shard_map/ppermute | solution.py:588
  18.7 2.1 %collective-permute-start.5 = (bf16[2,2,256,256]{3,2,1,0:T(8,128)(2,1)S(1)}, bf16[2,2,256,256]{3,2,1,0:T(8,128)(2,1)S(1)}, u32[]{:S(2)}, u32[]{:S(2)}) collective-permute-start(bf16[2,2,256,256]{3,2,1,0:T(8,128)(2,1)S(1)} %get-tuple-element.67), channel_id=1, source_target_pairs={{0,8},{8,0},{16,24},{24,16},{1,9},{9,1},{17,25},{25,17},{2,10},{10... | collective-permute-start | bytes 1572872 | tf_op jit(solution)/shard_map/ppermute | solution.py:599
  20.9 14.2 %collective-permute-start.7 = (s32[264,256]{1,0:T(8,128)S(1)}, s32[264,256]{1,0:T(8,128)S(1)}, u32[]{:S(2)}, u32[]{:S(2)}) collective-permute-start(s32[264,256]{1,0:T(8,128)S(1)} %get-tuple-element.72), channel_id=1, source_target_pairs={{16,0},{0,16},{24,8},{8,24},{17,1},{1,17},{25,9},{9,25},{18,2},{2,... | collective-permute-start | bytes 811016 | tf_op jit(solution)/shard_map/ppermute | solution.py:631
  39.4 2.7 %collective-permute-start.8 = (f32[2,2,256,256]{3,2,1,0:T(8,128)S(1)}, f32[2,2,256,256]{3,2,1,0:T(8,128)S(1)}, u32[]{:S(2)}, u32[]{:S(2)}) collective-permute-start(f32[2,2,256,256]{3,2,1,0:T(8,128)S(1)} %get-tuple-element.75), channel_id=1, source_target_pairs={{0,8},{8,0},{16,24},{24,16},{1,9},{9,1},{17,25},{25,17},{2,10},{10... | collective-permute-start | bytes 3145736 | tf_op jit(solution)/shard_map/ppermute | solution.py:634
  43.6 13.4 %collective-permute-start.9 = (s32[536,128]{1,0:T(8,128)S(1)}, s32[536,128]{1,0:T(8,128)S(1)}, u32[]{:S(2)}, u32[]{:S(2)}) collective-permute-start(s32[536,128]{1,0:T(8,128)S(1)} %get-tuple-element.78), channel_id=1, source_target_pairs={{0,1},{1,0},{2,3},{3,2},{4,5},{5,4},{6,7},{7,6},{8,9},{9,8},{10,11... | collective-permute-start | bytes 823304 | tf_op jit(solution)/shard_map/ppermute | solution.py:558
  45.7 9.4 %collective-permute-start.10 = (s32[264,256]{1,0:T(8,128)S(1)}, s32[264,256]{1,0:T(8,128)S(1)}, u32[]{:S(2)}, u32[]{:S(2)}) collective-permute-start(s32[264,256]{1,0:T(8,128)S(1)} %get-tuple-element.79), channel_id=1, source_target_pairs={{0,2},{1,3},{2,0},{3,1},{4,6},{5,7},{6,4},{7,5},{8,10},{9,11},{10,... | collective-permute-start | bytes 811016 | tf_op jit(solution)/shard_map/ppermute | solution.py:558
  45.7 11.3 %collective-permute-start.11 = (s32[264,256]{1,0:T(8,128)S(1)}, s32[264,256]{1,0:T(8,128)S(1)}, u32[]{:S(2)}, u32[]{:S(2)}) collective-permute-start(s32[264,256]{1,0:T(8,128)S(1)} %get-tuple-element.80), channel_id=1, source_target_pairs={{2,4},{3,5},{4,2},{5,3},{10,12},{11,13},{12,10},{13,11},{18,20},{1... | collective-permute-start | bytes 811016 | tf_op jit(solution)/shard_map/ppermute | solution.py:558
  48.4 10.1 %collective-permute-start.12 = (s32[264,128]{1,0:T(8,128)S(1)}, s32[264,128]{1,0:T(8,128)S(1)}, u32[]{:S(2)}, u32[]{:S(2)}) collective-permute-start(s32[264,128]{1,0:T(8,128)S(1)} %get-tuple-element.82), channel_id=1, source_target_pairs={{0,3},{1,2},{2,1},{3,0},{4,7},{5,6},{6,5},{7,4},{8,11},{9,10},{10,... | collective-permute-start | bytes 405512 | tf_op jit(solution)/shard_map/ppermute | solution.py:558
  49.0 11.1 %collective-permute-start.13 = (s32[264,128]{1,0:T(8,128)S(1)}, s32[264,128]{1,0:T(8,128)S(1)}, u32[]{:S(2)}, u32[]{:S(2)}) collective-permute-start(s32[264,128]{1,0:T(8,128)S(1)} %get-tuple-element.83), channel_id=1, source_target_pairs={{2,5},{3,4},{4,3},{5,2},{10,13},{11,12},{12,11},{13,10},{18,21},{1... | collective-permute-start | bytes 405512 | tf_op jit(solution)/shard_map/ppermute | solution.py:558
